TPU v7x, 32 devices: a whole 2x2x4 slice. The times are simulated.
32 devices in a mesh: section: 2 (over core), seq: 16 (over z, y, x).
Axes of the slice: x: 2, y: 2, z: 4, core: 2. Of those that a mesh axis runs over, the one named last changes fastest.
Arguments:
- io_pair: bfloat16 [2, 2, 2048, 512], P('section', None, 'seq'), may hold values from -6 to 6
- lengths: int32 [2], replicated, may hold values from 1024 to 2048, as said below
- filters: bfloat16 [2048, 24], P('seq'), may hold values from -0.125 to 0.125
- stu_maps: bfloat16 [26112, 512], P(('section', 'seq')), may hold values from -0.0390625 to 0.0390625
- attn_proj: bfloat16 [1536, 512], P(('section', 'seq')), may hold values from -0.25 to 0.25
- attn_out: bfloat16 [512, 512], P(('section', 'seq')), may hold values from -2 to 2
- norm_gains: bfloat16 [2, 2, 512], P('section', None, 'seq'), may hold values from 0.5 to 1.5
- mlp_gate: bfloat16 [2, 512, 2048], P('section', 'seq'), may hold values from -0.25 to 0.25
- mlp_up: bfloat16 [2, 512, 2048], P('section', 'seq'), may hold values from -0.25 to 0.25
- mlp_down: bfloat16 [2, 2048, 512], P('section', 'seq'), may hold values from -0.125 to 0.125
Outputs:
- result_pair: bfloat16 [2, 2, 2048, 512], P('section', None, 'seq')
- stu_maps_grad: float32 [26112, 512], P(('section', 'seq'))
- attn_proj_grad: float32 [1536, 512], P(('section', 'seq'))
- attn_out_grad: float32 [512, 512], P(('section', 'seq'))
- norm_gains_grad: float32 [2, 2, 512], P('section', None, 'seq')
- mlp_gate_grad: float32 [2, 512, 2048], P('section', 'seq')
- mlp_up_grad: float32 [2, 512, 2048], P('section', 'seq')
- mlp_down_grad: float32 [2, 2048, 512], P('section', 'seq')
Inputs may be any that keep to these rules, and one draw needn't show every extreme that they name: `lengths`: valid length of each micro-batch's sequence; at least one equals 2048.
All inputs are finite; a program needn't handle non-finite values.
Results may differ from a plain program's by a relative error of at most 0.035.
Values may be sent and summed in bfloat16 or wider, within the bound.
A program may use at most 384 MiB of HBM per device.

v0:
```python
import math

import jax
import jax.numpy as jnp
from jax import lax
from jax.sharding import PartitionSpec as P

ORDER = 3
HEAD_DIM = 64
WINDOW = 512


EPSILON = 1e-05
BIG_NEGATIVE = -1e30


def shortened(array):
    return jax.tree.map(lambda a: a.astype(jnp.bfloat16) if a.dtype == jnp.float32 else a, array)


def shifted(block, axis, distance):
    devices = range(lax.axis_size(axis))
    route = [(i - distance, i) for i in devices if i - distance in devices]
    return lax.ppermute(block, axis, route)


def phase_table(first_index, second_index, period):
    product = first_index[:, None] * second_index[None, :] % period
    angles = product.astype(jnp.float32) * (2.0 * math.pi / period)
    return (jnp.cos(angles), jnp.sin(angles))


def exact_dot(formula, left, right):
    return jnp.einsum(
        formula, left, right, precision=lax.Precision.HIGHEST, preferred_element_type=jnp.float32
    )


def norm_forward(values, weights):
    factor = lax.rsqrt(jnp.mean(values * values, axis=-1, keepdims=True) + EPSILON)
    return (values * factor * weights, factor)


def norm_backward(values, factor, weights, upstream):
    weighted = upstream * weights
    gain_grad = jnp.sum(upstream * values * factor, axis=0)
    correction = jnp.mean(weighted * values, axis=-1, keepdims=True)
    return (factor * weighted - values * factor * factor * factor * correction, gain_grad)


def mlp_forward(middle, gain, w_gate, w_up, w_down):
    normed, factor = norm_forward(middle, gain)
    inputs = normed.astype(jnp.bfloat16)
    gate_rows = jnp.dot(inputs, w_gate, preferred_element_type=jnp.float32)
    up_rows = jnp.dot(inputs, w_up, preferred_element_type=jnp.float32)
    active = (jax.nn.silu(gate_rows) * up_rows).astype(jnp.bfloat16)
    branch = jnp.dot(active, w_down, preferred_element_type=jnp.float32)
    return (branch, (factor, inputs, gate_rows, up_rows, active))


def mlp_backward(middle, gain, w_gate, w_up, w_down, saved, upstream):
    factor, inputs, gate_rows, up_rows, active = saved
    branch_grad = upstream.astype(jnp.bfloat16)
    down_grad = jnp.einsum("tf,td->fd", active, branch_grad, preferred_element_type=jnp.float32)
    active_grad = jnp.einsum("td,fd->tf", branch_grad, w_down, preferred_element_type=jnp.float32)
    sigmoid = jax.nn.sigmoid(gate_rows)
    slope = sigmoid * (1.0 + gate_rows * (1.0 - sigmoid))
    gate_grad = (active_grad * up_rows * slope).astype(jnp.bfloat16)
    up_grad = (active_grad * gate_rows * sigmoid).astype(jnp.bfloat16)
    gate_w_grad = jnp.einsum("td,tf->df", inputs, gate_grad, preferred_element_type=jnp.float32)
    up_w_grad = jnp.einsum("td,tf->df", inputs, up_grad, preferred_element_type=jnp.float32)
    normed_grad = jnp.einsum("tf,df->td", gate_grad, w_gate, preferred_element_type=jnp.float32)
    normed_grad = normed_grad + jnp.einsum(
        "tf,df->td", up_grad, w_up, preferred_element_type=jnp.float32
    )
    middle_grad, gain_grad = norm_backward(middle, factor, gain, normed_grad)
    return (upstream + middle_grad, gain_grad, gate_w_grad, up_w_grad, down_grad)


def body(
    io_pair, lengths, filters, stu_maps, attn_proj, attn_out, norm_gains, mlp_gate, mlp_up, mlp_down
):
    devices = lax.axis_size("seq")
    place = lax.axis_index("seq")
    first = lax.axis_index("section") == 0
    batches = io_pair.shape[1]
    tok_rows = io_pair.shape[2]
    width = io_pair.shape[3]
    part_rows = tok_rows // devices
    span = 2 * devices
    period = span * tok_rows
    heads = width // HEAD_DIM
    reach = WINDOW // tok_rows
    score_scale = HEAD_DIM ** (-0.5)
    maps_spectral, maps_triple, maps_output = (
        lax.all_gather(stu_maps, ("section", "seq"), axis=0, tiled=True),
        lax.all_gather(attn_proj, ("section", "seq"), axis=0, tiled=True),
        lax.all_gather(attn_out, ("section", "seq"), axis=0, tiled=True),
    )
    section_gains, section_gate, section_up, section_down = (
        lax.all_gather(norm_gains, "seq", axis=2, tiled=True),
        lax.all_gather(mlp_gate, "seq", axis=1, tiled=True),
        lax.all_gather(mlp_up, "seq", axis=1, tiled=True),
        lax.all_gather(mlp_down, "seq", axis=1, tiled=True),
    )
    gains = section_gains[0].astype(jnp.float32)
    w_gate = section_gate[0]
    w_up = section_up[0]
    w_down = section_down[0]
    proj_blocks = maps_triple.reshape(3, width, width)
    filter_count = maps_spectral.shape[0] // width
    group_size = 3
    group_count = filter_count // group_size
    block_index = jnp.arange(devices, dtype=jnp.int32)
    span_index = jnp.arange(span, dtype=jnp.int32)
    row_index = jnp.arange(tok_rows, dtype=jnp.int32)
    global_rows = place * tok_rows + row_index
    cos_block, sin_block = phase_table(span_index, block_index, span)
    cos_twist, sin_twist = phase_table(
        span_index, place * part_rows + jnp.arange(part_rows, dtype=jnp.int32), period
    )
    cos_row, sin_row = phase_table(row_index, row_index, tok_rows)
    own_span = 2 * place + jnp.arange(2, dtype=jnp.int32)
    cos_back, sin_back = phase_table(own_span, row_index, period)
    own_freq = (own_span[:, None] + span * row_index[None, :]).reshape(-1)
    shift_cos, shift_sin = phase_table(own_freq, jnp.arange(ORDER, dtype=jnp.int32), period)
    alternate = (1 - 2 * (global_rows % 2)).astype(jnp.bfloat16)
    filter_pair = jnp.concatenate([filters, filters * alternate[:, None]], 1)

    def finish_spectrum(blocks):
        real_part = exact_dot("fd,dsc->fsc", cos_block, blocks)
        imag_part = -exact_dot("fd,dsc->fsc", sin_block, blocks)
        twist_real = real_part * cos_twist[:, :, None] + imag_part * sin_twist[:, :, None]
        twist_imag = imag_part * cos_twist[:, :, None] - real_part * sin_twist[:, :, None]
        moved_real, moved_imag = (
            lax.all_to_all(
                twist_real.astype(jnp.bfloat16), "seq", split_axis=0, concat_axis=1, tiled=True
            ).astype(twist_real.dtype),
            lax.all_to_all(
                twist_imag.astype(jnp.bfloat16), "seq", split_axis=0, concat_axis=1, tiled=True
            ).astype(twist_imag.dtype),
        )
        out_real = exact_dot("ts,asc->atc", cos_row, moved_real) + exact_dot(
            "ts,asc->atc", sin_row, moved_imag
        )
        out_imag = exact_dot("ts,asc->atc", cos_row, moved_imag) - exact_dot(
            "ts,asc->atc", sin_row, moved_real
        )
        return (out_real, out_imag)

    def to_time(real_part, imag_part):
        v_real = exact_dot("ts,atc->asc", cos_row, real_part) - exact_dot(
            "ts,atc->asc", sin_row, imag_part
        )
        v_imag = exact_dot("ts,atc->asc", cos_row, imag_part) + exact_dot(
            "ts,atc->asc", sin_row, real_part
        )
        twist_real = v_real * cos_back[:, :, None] - v_imag * sin_back[:, :, None]
        twist_imag = v_imag * cos_back[:, :, None] + v_real * sin_back[:, :, None]
        moved_real, moved_imag = (
            lax.all_to_all(
                twist_real.astype(jnp.bfloat16), "seq", split_axis=1, concat_axis=0, tiled=True
            ).astype(twist_real.dtype),
            lax.all_to_all(
                twist_imag.astype(jnp.bfloat16), "seq", split_axis=1, concat_axis=0, tiled=True
            ).astype(twist_imag.dtype),
        )
        summed = exact_dot("fd,fsc->dsc", cos_block, moved_real) - exact_dot(
            "fd,fsc->dsc", sin_block, moved_imag
        )
        return lax.all_to_all(
            (summed / period).astype(jnp.bfloat16), "seq", split_axis=0, concat_axis=1, tiled=True
        ).astype(jnp.float32)[0]

    def spectral_inputs(signal):
        moved_signal, moved_filter = (
            lax.all_to_all(signal[None], "seq", split_axis=1, concat_axis=0, tiled=True),
            lax.all_to_all(filter_pair[None], "seq", split_axis=1, concat_axis=0, tiled=True),
        )
        joined = jnp.concatenate(
            [moved_signal.astype(jnp.float32), moved_filter.astype(jnp.float32)], 2
        )
        out_real, out_imag = finish_spectrum(joined)
        u_real = out_real[:, :, :width].reshape(2 * tok_rows, width)
        u_imag = out_imag[:, :, :width].reshape(2 * tok_rows, width)
        f_real = jnp.concatenate([out_real[:, :, width:].reshape(2 * tok_rows, -1), shift_cos], 1)
        f_imag = jnp.concatenate([out_imag[:, :, width:].reshape(2 * tok_rows, -1), -shift_sin], 1)
        return (u_real, u_imag, f_real, f_imag)

    def mix_rows(u_real, u_imag, f_real, f_imag):
        a_real = f_real[:, :, None] * u_real[:, None, :] - f_imag[:, :, None] * u_imag[:, None, :]
        a_imag = f_real[:, :, None] * u_imag[:, None, :] + f_imag[:, :, None] * u_real[:, None, :]
        stacked = jnp.concatenate([a_real, a_imag], 0).astype(jnp.bfloat16)
        return stacked.reshape(4 * tok_rows, filter_count * width)

    def spectral_backward(kept, incoming, mask_rows):
        hidden = kept[0]
        middle = kept[1]
        upstream = incoming.astype(jnp.float32) * mask_rows
        branch, saved = mlp_forward(middle, gains[1], w_gate, w_up, w_down)
        middle_grad, gain_two, gate_grad, up_grad, down_grad = mlp_backward(
            middle, gains[1], w_gate, w_up, w_down, saved, upstream
        )
        normed, factor = norm_forward(hidden, gains[0])
        u_real, u_imag, f_real, f_imag = spectral_inputs(normed.astype(jnp.bfloat16))
        mixed = mix_rows(u_real, u_imag, f_real, f_imag)
        moved_grad = lax.all_to_all(
            shortened(middle_grad[None]), "seq", split_axis=1, concat_axis=0, tiled=True
        )
        grad_real, grad_imag = finish_spectrum(moved_grad)
        spectrum_grad = jnp.concatenate(
            [grad_real.reshape(2 * tok_rows, width), grad_imag.reshape(2 * tok_rows, width)], 0
        )
        spectrum_grad = (spectrum_grad / period).astype(jnp.bfloat16)
        group_cols = group_size * width

        def one_group(carry, group_number):
            real_acc, imag_acc = carry
            map_block = lax.dynamic_slice_in_dim(
                maps_spectral, group_number * group_cols, group_cols, 0
            )
            mixed_block = lax.dynamic_slice_in_dim(mixed, group_number * group_cols, group_cols, 1)
            filt_real = lax.dynamic_slice_in_dim(f_real, group_number * group_size, group_size, 1)
            filt_imag = lax.dynamic_slice_in_dim(f_imag, group_number * group_size, group_size, 1)
            block_grad = jnp.einsum(
                "rd,kd->rk", spectrum_grad, map_block, preferred_element_type=jnp.float32
            )
            block_grad = block_grad.reshape(2, 2 * tok_rows, group_size, width)
            real_acc = (
                real_acc
                + exact_dot("rc,rci->ri", filt_real, block_grad[0])
                + exact_dot("rc,rci->ri", filt_imag, block_grad[1])
            )
            imag_acc = (
                imag_acc
                + exact_dot("rc,rci->ri", filt_real, block_grad[1])
                - exact_dot("rc,rci->ri", filt_imag, block_grad[0])
            )
            weight_block = jnp.einsum(
                "rk,rd->kd", mixed_block, spectrum_grad, preferred_element_type=jnp.float32
            )
            return ((real_acc, imag_acc), weight_block)

        start_acc = jnp.zeros((2 * tok_rows, width), jnp.float32)
        (real_grad, imag_grad), weight_blocks = lax.scan(
            one_group, (start_acc, start_acc), jnp.arange(group_count, dtype=jnp.int32)
        )
        maps_grad = weight_blocks.reshape(filter_count * width, width)
        signal_grad = (
            to_time(real_grad.reshape(2, tok_rows, width), imag_grad.reshape(2, tok_rows, width))
            * period
        )
        hidden_grad, gain_one = norm_backward(hidden, factor, gains[0], signal_grad)
        inputs_grad = (mask_rows * (middle_grad + hidden_grad)).astype(jnp.bfloat16)
        return (
            inputs_grad,
            (maps_grad, jnp.stack([gain_one, gain_two]), gate_grad, up_grad, down_grad),
        )

    spectral_total = jnp.zeros(maps_spectral.shape, jnp.float32)
    triple_total = jnp.zeros(maps_triple.shape, jnp.float32)
    output_total = jnp.zeros(maps_output.shape, jnp.float32)
    gain_total = jnp.zeros((2, width), jnp.float32)
    gate_total = jnp.zeros(w_gate.shape, jnp.float32)
    up_total = jnp.zeros(w_up.shape, jnp.float32)
    down_total = jnp.zeros(w_down.shape, jnp.float32)
    spectral_mask = jnp.where(first, 1.0, 0.0).astype(jnp.float32)
    window_mask = 1.0 - spectral_mask
    results = []
    for batch_index in range(batches):
        mask_rows = (global_rows < lengths[batch_index]).astype(jnp.float32)[:, None]
        slab = io_pair[0, batch_index]
        spectral_hidden = slab.astype(jnp.float32) * mask_rows
        spectral_normed, spectral_factor = norm_forward(spectral_hidden, gains[0])
        spectral_u_real, spectral_u_imag, spectral_f_real, spectral_f_imag = spectral_inputs(
            spectral_normed.astype(jnp.bfloat16)
        )
        spectral_mixed = mix_rows(
            spectral_u_real, spectral_u_imag, spectral_f_real, spectral_f_imag
        )
        product = jnp.dot(spectral_mixed, maps_spectral, preferred_element_type=jnp.float32)
        convolved = to_time(
            product[: 2 * tok_rows].reshape(2, tok_rows, width),
            product[2 * tok_rows :].reshape(2, tok_rows, width),
        )
        spectral_middle = spectral_hidden + convolved
        spectral_branch, spectral_saved = mlp_forward(
            spectral_middle, gains[1], w_gate, w_up, w_down
        )
        sent = (mask_rows * (spectral_middle + spectral_branch)).astype(jnp.bfloat16)
        spectral_kept = (spectral_hidden, spectral_middle)
        sent, kept = (sent, spectral_kept)
        arrived = shifted(sent, "section", 1)
        window_hidden = arrived.astype(jnp.float32)
        window_normed, window_factor = norm_forward(window_hidden, gains[0])
        inputs = window_normed.astype(jnp.bfloat16)
        triple = jnp.einsum(
            "td,wde->wte", inputs, proj_blocks, preferred_element_type=jnp.float32
        ).astype(jnp.bfloat16)
        query_rows = triple[0]
        key_rows = triple[1]
        value_rows = triple[2]
        key_parts = []
        value_parts = []
        for distance in range(reach, 0, -1):
            far_key, far_value = shifted((key_rows, value_rows), "seq", distance)
            key_parts.append(far_key)
            value_parts.append(far_value)
        key_window = jnp.concatenate(key_parts + [key_rows], 0).reshape(-1, heads, HEAD_DIM)
        value_window = jnp.concatenate(value_parts + [value_rows], 0).reshape(-1, heads, HEAD_DIM)
        queries = query_rows.reshape(tok_rows, heads, HEAD_DIM)
        scores = (
            jnp.einsum("qhe,khe->hqk", queries, key_window, preferred_element_type=jnp.float32)
            * score_scale
        )
        key_place = (place - reach) * tok_rows + jnp.arange((reach + 1) * tok_rows, dtype=jnp.int32)
        distance_rows = global_rows[:, None] - key_place[None, :]
        allowed = (key_place[None, :] >= 0) & (distance_rows >= 0) & (distance_rows < WINDOW)
        scores = jnp.where(allowed[None], scores, BIG_NEGATIVE)
        highest = jnp.max(scores, axis=-1, keepdims=True)
        weights = jnp.exp(scores - highest)
        weights = weights / jnp.sum(weights, axis=-1, keepdims=True)
        weights_low = weights.astype(jnp.bfloat16)
        attended = jnp.einsum(
            "hqk,khe->qhe", weights_low, value_window, preferred_element_type=jnp.float32
        )
        attended = attended.reshape(tok_rows, width).astype(jnp.bfloat16)
        window_middle = window_hidden + jnp.dot(
            attended, maps_output, preferred_element_type=jnp.float32
        )
        window_branch, window_saved = mlp_forward(window_middle, gains[1], w_gate, w_up, w_down)
        block_out = (mask_rows * (window_middle + window_branch)).astype(jnp.bfloat16)
        window_upstream = slab.astype(jnp.float32) * mask_rows
        window_middle_grad, window_gain_two, window_gate_grad, window_up_grad, window_down_grad = (
            mlp_backward(
                window_middle, gains[1], w_gate, w_up, w_down, window_saved, window_upstream
            )
        )
        output_input = window_middle_grad.astype(jnp.bfloat16)
        output_grad = jnp.einsum(
            "td,te->de", attended, output_input, preferred_element_type=jnp.float32
        )
        attended_grad = jnp.einsum(
            "te,de->td", output_input, maps_output, preferred_element_type=jnp.float32
        )
        attended_grad = attended_grad.astype(jnp.bfloat16).reshape(tok_rows, heads, HEAD_DIM)
        value_grad = jnp.einsum(
            "hqk,qhe->khe", weights_low, attended_grad, preferred_element_type=jnp.float32
        )
        weight_grad = jnp.einsum(
            "qhe,khe->hqk", attended_grad, value_window, preferred_element_type=jnp.float32
        )
        row_total = jnp.sum(weights * weight_grad, axis=-1, keepdims=True)
        score_grad = (weights * (weight_grad - row_total)).astype(jnp.bfloat16)
        query_grad = (
            jnp.einsum("hqk,khe->qhe", score_grad, key_window, preferred_element_type=jnp.float32)
            * score_scale
        )
        key_grad = (
            jnp.einsum("hqk,qhe->khe", score_grad, queries, preferred_element_type=jnp.float32)
            * score_scale
        )
        key_grad = key_grad.reshape(-1, width)
        value_grad = value_grad.reshape(-1, width)
        own_key = key_grad[reach * tok_rows :]
        own_value = value_grad[reach * tok_rows :]
        for distance in range(reach, 0, -1):
            offset = (reach - distance) * tok_rows
            back_key, back_value = (
                shifted(
                    key_grad[offset : offset + tok_rows].astype(jnp.bfloat16), "seq", -distance
                ).astype(jnp.float32),
                shifted(
                    value_grad[offset : offset + tok_rows].astype(jnp.bfloat16), "seq", -distance
                ).astype(jnp.float32),
            )
            own_key = own_key + back_key
            own_value = own_value + back_value
        triple_grad = jnp.stack([query_grad.reshape(tok_rows, width), own_key, own_value]).astype(
            jnp.bfloat16
        )
        proj_grad = jnp.einsum(
            "td,wte->wde", inputs, triple_grad, preferred_element_type=jnp.float32
        ).reshape(3 * width, width)
        normed_grad = jnp.einsum(
            "wte,wde->td", triple_grad, proj_blocks, preferred_element_type=jnp.float32
        )
        window_hidden_grad, window_gain_one = norm_backward(
            window_hidden, window_factor, gains[0], normed_grad
        )
        slab_grad = (window_middle_grad + window_hidden_grad).astype(jnp.bfloat16)
        block_out, returned, window_grads = (
            block_out,
            slab_grad,
            (
                proj_grad,
                output_grad,
                jnp.stack([window_gain_one, window_gain_two]),
                window_gate_grad,
                window_up_grad,
                window_down_grad,
            ),
        )
        incoming = shifted(returned, "section", -1)
        inputs_grad, spectral_grads = spectral_backward(kept, incoming, mask_rows)
        results.append(jnp.where(first, inputs_grad, block_out))
        spectral_total = spectral_total + spectral_mask * spectral_grads[0]
        triple_total = triple_total + window_mask * window_grads[0]
        output_total = output_total + window_mask * window_grads[1]
        gain_total = gain_total + spectral_mask * spectral_grads[1] + window_mask * window_grads[2]
        gate_total = gate_total + spectral_mask * spectral_grads[2] + window_mask * window_grads[3]
        up_total = up_total + spectral_mask * spectral_grads[3] + window_mask * window_grads[4]
        down_total = down_total + spectral_mask * spectral_grads[4] + window_mask * window_grads[5]
    result_pair = jnp.stack(results)[None]
    spectral_out, triple_out, output_out = (
        lax.psum_scatter(spectral_total, ("section", "seq"), scatter_dimension=0, tiled=True),
        lax.psum_scatter(triple_total, ("section", "seq"), scatter_dimension=0, tiled=True),
        lax.psum_scatter(output_total, ("section", "seq"), scatter_dimension=0, tiled=True),
    )
    gain_out, gate_out, up_out, down_out = (
        lax.psum_scatter(gain_total[None], "seq", scatter_dimension=2, tiled=True),
        lax.psum_scatter(gate_total[None], "seq", scatter_dimension=1, tiled=True),
        lax.psum_scatter(up_total[None], "seq", scatter_dimension=1, tiled=True),
        lax.psum_scatter(down_total[None], "seq", scatter_dimension=1, tiled=True),
    )
    return (result_pair, spectral_out, triple_out, output_out, gain_out, gate_out, up_out, down_out)


def solution(mesh):
    placed = (
        P("section", None, "seq", None),
        P(),
        P("seq", None),
        P(("section", "seq"), None),
        P(("section", "seq"), None),
        P(("section", "seq"), None),
        P("section", None, "seq"),
        P("section", "seq", None),
        P("section", "seq", None),
        P("section", "seq", None),
    )
    return jax.shard_map(
        body,
        mesh=mesh,
        in_specs=placed,
        out_specs=(
            P("section", None, "seq", None),
            P(("section", "seq"), None),
            P(("section", "seq"), None),
            P(("section", "seq"), None),
            P("section", None, "seq"),
            P("section", "seq", None),
            P("section", "seq", None),
            P("section", "seq", None),
        ),
        check_vma=False,
    )
```

profile of v0, /device:TPU:0, one launch (start us, length us, event | category | flops | bytes accessed | tf_op | source)
XLA Modules:
  0.0 3214.8 jit_solution(12045496211126454633)
XLA Ops:
  12.3 8.3 all-to-all-start.1
  26.0 44.7 %all_gather.21 = bf16[1,2,512]{1,0,2:T(2,128)(2,1)S(1)} all-gather(bf16[1,2,32]{1,0,2:T(2,128)(2,1)S(1)} %copy.392), channel_id=1, replica_groups=mesh['section'=2,'seq'=16] {'seq'}, dimensions={2}, use_global_device_ids=true | all-gather | bytes 2176 | tf_op jit(solution)/shard_map/all_gather | solution.py:101
  82.1 7.1 all-to-all-done
  94.5 7.4 all-to-all-done.13
  111.8 12.6 all-to-all-done.14
  124.4 6.4 all-to-all-start.15
  133.3 12.0 all-to-all-done.15
  145.3 8.1 all-to-all-start.3
  155.5 12.2 all-to-all-done.3
  167.7 10.3 all-to-all-start.2
  180.0 12.3 all-to-all-done.2
  202.8 11.4 subtract_convert_fusion.1
  214.2 11.6 subtract_convert_fusion
  225.8 21.9 fusion.707
  247.8 32.3 %fusion.706 = f32[512,512]{1,0:T(8,128)S(1)} fusion(bf16[26112,512]{1,0:T(8,128)(2,1)} %all-gather.6.cloned.1.call-done, bf16[256,26112]{0,1:T(8,128)(2,1)} %bitcast.1072, bf16[256,26112]{0,1:T(8,128)(2,1)} %bitcast.1070), kind=kOutput, calls=%fused_computation.872 | convolution fusion | flops 13743685632 | bytes 54525952 | tf_op jit(solution)/shard_map/dot_general | solution.py:281
  290.4 7.4 all-to-all-start.5
  298.6 9.0 all-to-all-done.5
  313.5 7.2 all-to-all-done.4
  325.0 71.8 %all_gather.27 = bf16[512,512]{1,0:T(8,128)(2,1)S(1)} all-gather(bf16[16,512]{1,0:T(8,128)(2,1)S(1)} %copy-done.131), channel_id=1, replica_groups=mesh['section'=2,'seq'=16] {'section','seq'}, dimensions={0}, use_global_device_ids=true | all-gather | bytes 540672 | tf_op jit(solution)/shard_map/all_gather | solution.py:98
  406.4 6.8 all-to-all-done.17
  419.3 6.1 all-to-all-done.6
  669.7 7.3 collective-permute-done.13
  709.8 8.7 all-to-all-start.19
  720.8 5.8 all-to-all-done.19
  731.6 6.6 all-to-all-done.7
  744.7 18.4 pad_maximum_fusion
  763.9 6.9 all-to-all-start.21
  770.8 18.3 pad_maximum_fusion.1
  791.4 6.9 all-to-all-start.9
  800.4 6.5 all-to-all-done.9
  812.4 6.5 all-to-all-done.8
  820.9 17.3 broadcast.774.clone
  838.2 598.2 %while.30 = (s32[]{:T(128)}, f32[256,512]{1,0:T(8,128)}, f32[256,512]{1,0:T(8,128)}, f32[17,1536,512]{2,1,0:T(8,128)}, s32[17]{0:T(128)S(1)}, /*index=5*/f32[256...) while((s32[]{:T(128)}, f32[256,512]{1,0:T(8,128)}, ...), condition=%wide.region_11.12_spmd.clone, body=%wide.region_10.11_spmd.clone.sunk | while | flops 1630273536 | bytes 54563300 | solution.py:245
  1444.7 17.2 broadcast.774.clone.1
  1461.9 597.2 %while.31 = (s32[]{:T(128)}, f32[256,512]{1,0:T(8,128)S(1)}, f32[256,512]{1,0:T(8,128)S(1)}, f32[17,1536,512]{2,1,0:T(8,128)}, s32[17]{0:T(128)S(1)}, /*index=5*...) while((s32[]{:T(128)}, f32[256,512]{1,0:T(8,128)S(1)}, ...), condition=%wide.region_24.25_spmd.clone, body=%wide.region_23.24_spmd.clone.sunk | while | flops 1630273536 | bytes 46174580 | solution.py:245
  2002.0 5.7 fusion.923
  2070.4 7.6 all-to-all-done.11
  2082.4 7.7 all-to-all-done.10
  2095.2 7.1 all-to-all-done.22
  2122.4 5.9 all-to-all-done.12
  2132.3 7.4 all-to-all-done.24
  2168.3 52.5 %add_multiply_fusion = f32[17,1536,512]{2,1,0:T(8,128)} fusion(f32[17,1536,512]{2,1,0:T(8,128)} %get-tuple-element.120, f32[17,1536,512]{2,1,0:T(8,128)} %get-tuple-element.121, f32[]{:T(128)S(6)} %select_n.197), kind=kLoop, calls=%fused_computation.28 | loop fusion | flops 26738688 | bytes 160432128 | tf_op jit(solution)/shard_map/add | solution.py:407
  2233.4 119.2 %reduce-scatter.14.cloned.1.call-done = f32[16,512]{1,0:T(8,128)} async-done(((f32[512,512]{1,0:T(8,128)}), f32[16,512]{1,0:T(8,128)}) %reduce-scatter.14.cloned.1.call-update) | async-done | bytes 32784 | tf_op jit(solution)/shard_map/reduce_scatter | solution.py:418
  2352.7 104.2 %reduce-scatter.12.cloned.1.call-done = f32[48,512]{1,0:T(8,128)} async-done(((f32[1536,512]{1,0:T(8,128)}), f32[48,512]{1,0:T(8,128)}) %reduce-scatter.12.cloned.1.call-update) | async-done | bytes 98320 | tf_op jit(solution)/shard_map/reduce_scatter | solution.py:417
  2456.9 97.0 %reduce-scatter.16.cloned.1.call-done = f32[1,32,2048]{2,1,0:T(8,128)} async-done(((f32[1,512,2048]{2,1,0:T(8,128)}), f32[1,32,2048]{2,1,0:T(8,128)}) %reduce-scatter.16.cloned.1.call-update) | async-done | bytes 262160 | tf_op jit(solution)/shard_map/reduce_scatter | solution.py:422
  2553.8 97.5 %reduce-scatter.18.cloned.1.call-done = f32[1,32,2048]{2,1,0:T(8,128)} async-done(((f32[1,512,2048]{2,1,0:T(8,128)}), f32[1,32,2048]{2,1,0:T(8,128)}) %reduce-scatter.18.cloned.1.call-update) | async-done | bytes 262160 | tf_op jit(solution)/shard_map/reduce_scatter | solution.py:423
  2651.3 97.6 %reduce-scatter.20.cloned.1.call-done = f32[1,128,512]{2,1,0:T(8,128)} async-done(((f32[1,2048,512]{2,1,0:T(8,128)}), f32[1,128,512]{2,1,0:T(8,128)}) %reduce-scatter.20.cloned.1.call-update) | async-done | bytes 262160 | tf_op jit(solution)/shard_map/reduce_scatter | solution.py:424
  2749.0 458.6 %reduce-scatter.10.cloned.1.call-done = f32[816,512]{1,0:T(8,128)} async-done(((f32[26112,512]{1,0:T(8,128)}), f32[816,512]{1,0:T(8,128)}) %reduce-scatter.10.cloned.1.call-update) | async-done | bytes 1671184 | tf_op jit(solution)/shard_map/reduce_scatter | solution.py:416
  (1634 shorter events, 1626.5 us)
Async XLA Ops:
  7.2 218.6 %all-gather.6.cloned.1.call-start = ((), (), s32[]{:S(2)}) async-start(), calls=%async_computation.32 | async-start | bytes 27574272 | tf_op jit(solution)/shard_map/all_gather | solution.py:96
  7.9 421.0 %all-gather.12.cloned.1.call-start = ((), (), s32[]{:S(2)}) async-start(), calls=%async_computation.35 | async-start | bytes 2228224 | tf_op jit(solution)/shard_map/all_gather | solution.py:104
  12.3 64.0 %all-to-all-start.1 = ((bf16[16,2,192]{2,1,0:T(2,128)(2,1)}), bf16[16,2,192]{2,1,0:T(2,128)(2,1)S(1)}, u32[]{:S(2)}, u32[]{:S(2)}) async-start(bf16[16,2,192]{2,1,0:T(2,128)(2,1)} %reshape.1218), calls=%async_computation.1 | async-start | bytes 32768 | tf_op jit(solution)/shard_map/all_to_all | solution.py:178
  20.6 416.8 %all-gather.8.cloned.1.call-start = ((), (), s32[]{:S(2)}) async-start(), calls=%async_computation.33 | async-start | bytes 2228224 | tf_op jit(solution)/shard_map/all_gather | solution.py:102
  76.2 12.9 all-to-all-start
  89.2 12.7 all-to-all-start.13
  106.7 17.8 all-to-all-start.14
  110.2 329.2 %all-gather.10.cloned.1.call-start = ((), (), s32[]{:S(2)}) async-start(), calls=%async_computation.34 | async-start | bytes 2228224 | tf_op jit(solution)/shard_map/all_gather | solution.py:103
  124.4 20.9 all-to-all-start.15
  145.3 22.4 all-to-all-start.3
  167.7 24.6 all-to-all-start.2
  290.4 17.3 all-to-all-start.5
  307.6 13.1 all-to-all-start.4
  312.1 146.2 %all-gather.14.cloned.1.call-start = ((), (), s32[]{:S(2)}) async-start(), calls=%async_computation.36 | async-start | bytes 1622016 | tf_op jit(solution)/shard_map/all_gather | solution.py:97
  320.7 77.0 %all-to-all-start.16 = ((bf16[2,128,512]{2,0,1:T(2,128)(2,1)}), bf16[2,128,512]{2,0,1:T(2,128)(2,1)S(1)}, u32[]{:S(2)}, u32[]{:S(2)}) async-start(bf16[2,128,512]{2,0,1:T(2,128)(2,1)} %copy.492), calls=%async_computation.16 | async-start | bytes 524288 | tf_op jit(solution)/shard_map/all_to_all | solution.py:161
  397.7 15.5 all-to-all-start.17
  413.2 12.2 all-to-all-start.6
  461.1 31.7 collective-permute-start.19
  464.1 23.4 collective-permute-start.23
  468.1 104.0 %collective-permute-start.4 = (bf16[128,512]{1,0:T(8,128)(2,1)}, bf16[128,512]{1,0:T(8,128)(2,1)}, u32[]{:S(2)}, u32[]{:S(2)}) collective-permute-start(bf16[128,512]{1,0:T(8,128)(2,1)} %get-tuple-element.377), channel_id=1, source_target_pairs={{0,1},{1,2},{2,3},{3,4},{4,5},{5,6},{6,7},{7,8},{8,9},{9,10},{10,1... | collective-permute-start | bytes 393224 | tf_op jit(solution)/shard_map/ppermute | solution.py:24
  472.1 96.7 %collective-permute-start.3 = (bf16[128,512]{1,0:T(8,128)(2,1)}, bf16[128,512]{1,0:T(8,128)(2,1)}, u32[]{:S(2)}, u32[]{:S(2)}) collective-permute-start(bf16[128,512]{1,0:T(8,128)(2,1)} %get-tuple-element.377), channel_id=1, source_target_pairs={{0,2},{1,3},{2,4},{3,5},{4,6},{5,7},{6,8},{7,9},{8,10},{9,11},{10,... | collective-permute-start | bytes 393224 | tf_op jit(solution)/shard_map/ppermute | solution.py:24
  475.1 90.5 %collective-permute-start.2 = (bf16[128,512]{1,0:T(8,128)(2,1)}, bf16[128,512]{1,0:T(8,128)(2,1)}, u32[]{:S(2)}, u32[]{:S(2)}) collective-permute-start(bf16[128,512]{1,0:T(8,128)(2,1)} %get-tuple-element.377), channel_id=1, source_target_pairs={{0,3},{1,4},{2,5},{3,6},{4,7},{5,8},{6,9},{7,10},{8,11},{9,12},{10... | collective-permute-start | bytes 393224 | tf_op jit(solution)/shard_map/ppermute | solution.py:24
  492.7 12.4 collective-permute-start.25
  505.1 16.1 collective-permute-start.21
  521.2 23.7 collective-permute-start.1
  526.1 13.7 collective-permute-start.5
  544.9 12.6 collective-permute-start.7
  618.6 36.5 %collective-permute-start.32 = (bf16[128,512]{1,0:T(8,128)(2,1)}, bf16[128,512]{1,0:T(8,128)(2,1)}, u32[]{:S(2)}, u32[]{:S(2)}) collective-permute-start(bf16[128,512]{1,0:T(8,128)(2,1)} %copy.518), channel_id=1, source_target_pairs={{3,0},{4,1},{5,2},{6,3},{7,4},{8,5},{9,6},{10,7},{11,8},{12,9},{13... | collective-permute-start | bytes 393224 | tf_op jit(solution)/shard_map/ppermute | solution.py:24
  619.9 36.6 %collective-permute-start.33 = (bf16[128,512]{1,0:T(8,128)(2,1)}, bf16[128,512]{1,0:T(8,128)(2,1)}, u32[]{:S(2)}, u32[]{:S(2)}) collective-permute-start(bf16[128,512]{1,0:T(8,128)(2,1)} %copy.519), channel_id=1, source_target_pairs={{2,0},{3,1},{4,2},{5,3},{6,4},{7,5},{8,6},{9,7},{10,8},{11,9},{12,... | collective-permute-start | bytes 393224 | tf_op jit(solution)/shard_map/ppermute | solution.py:24
  621.2 36.7 %collective-permute-start.34 = (bf16[128,512]{1,0:T(8,128)(2,1)}, bf16[128,512]{1,0:T(8,128)(2,1)}, u32[]{:S(2)}, u32[]{:S(2)}) collective-permute-start(bf16[128,512]{1,0:T(8,128)(2,1)} %copy.520), channel_id=1, source_target_pairs={{1,0},{2,1},{3,2},{4,3},{5,4},{6,5},{7,6},{8,7},{9,8},{10,9},{11,1... | collective-permute-start | bytes 393224 | tf_op jit(solution)/shard_map/ppermute | solution.py:24
  622.5 36.7 %collective-permute-start.31 = (bf16[128,512]{1,0:T(8,128)(2,1)}, bf16[128,512]{1,0:T(8,128)(2,1)}, u32[]{:S(2)}, u32[]{:S(2)}) collective-permute-start(bf16[128,512]{1,0:T(8,128)(2,1)} %copy.516), channel_id=1, source_target_pairs={{4,0},{5,1},{6,2},{7,3},{8,4},{9,5},{10,6},{11,7},{12,8},{13,9},{1... | collective-permute-start | bytes 393224 | tf_op jit(solution)/shard_map/ppermute | solution.py:24
  633.2 57.4 %collective-permute-start.28 = (bf16[128,512]{1,0:T(8,128)(2,1)}, bf16[128,512]{1,0:T(8,128)(2,1)}, u32[]{:S(2)}, u32[]{:S(2)}) collective-permute-start(bf16[128,512]{1,0:T(8,128)(2,1)} %copy.513), channel_id=1, source_target_pairs={{3,0},{4,1},{5,2},{6,3},{7,4},{8,5},{9,6},{10,7},{11,8},{12,9},{13... | collective-permute-start | bytes 393224 | tf_op jit(solution)/shard_map/ppermute | solution.py:24
  659.1 17.9 collective-permute-start.13
  665.8 13.6 collective-permute-start.10
  667.1 13.6 collective-permute-start.11
  668.4 13.6 collective-permute-start.12
  709.8 16.8 all-to-all-start.19
  741.1 22.8 all-to-all-start.20
  763.9 27.5 all-to-all-start.21
  791.4 15.4 all-to-all-start.9
  2102.2 14.5 all-to-all-start.23
  2131.9 100.2 %reduce-scatter.22.cloned.1.call-start = ((), (), s32[]{:S(2)}) async-start(), calls=%async_computation.43 | async-start | bytes 278528
  2141.6 211.1 %reduce-scatter.14.cloned.1.call-start = ((), (), s32[]{:S(2)}) async-start(), calls=%async_computation.39 | async-start | bytes 1081344 | tf_op jit(solution)/shard_map/reduce_scatter | solution.py:418
  2143.1 313.7 %reduce-scatter.12.cloned.1.call-start = ((), (), s32[]{:S(2)}) async-start(), calls=%async_computation.38 | async-start | bytes 3244032 | tf_op jit(solution)/shard_map/reduce_scatter | solution.py:417
  2146.6 407.2 %reduce-scatter.16.cloned.1.call-start = ((), (), s32[]{:S(2)}) async-start(), calls=%async_computation.40 | async-start | bytes 4456448 | tf_op jit(solution)/shard_map/reduce_scatter | solution.py:422
  2153.9 497.5 %reduce-scatter.18.cloned.1.call-start = ((), (), s32[]{:S(2)}) async-start(), calls=%async_computation.41 | async-start | bytes 4456448 | tf_op jit(solution)/shard_map/reduce_scatter | solution.py:423
  2161.0 588.0 %reduce-scatter.20.cloned.1.call-start = ((), (), s32[]{:S(2)}) async-start(), calls=%async_computation.42 | async-start | bytes 4456448 | tf_op jit(solution)/shard_map/reduce_scatter | solution.py:424
  2168.3 1039.3 %reduce-scatter.10.cloned.1.call-start = ((), (), s32[]{:S(2)}) async-start(), calls=%async_computation.37 | async-start | bytes 55148544 | tf_op jit(solution)/shard_map/reduce_scatter | solution.py:416
  (351 other events, 6278.0 us)
Sparse Core Ops, SparseCore 0:
  10.9 195.9 all-gather.5
  209.6 59.7 all-gather.11
  272.2 65.2 all-gather.7
  340.1 59.9 all-gather.9
  402.8 55.3 all-gather.13
  2141.7 73.2 reduce-scatter.21
  2217.9 134.7 reduce-scatter.13
  2358.7 98.1 reduce-scatter.11
  2459.7 94.0 reduce-scatter.15
  2556.6 94.7 reduce-scatter.17
  2654.2 94.7 reduce-scatter.19
  2755.8 451.6 reduce-scatter.9
where the time goes:
time: 3240 us; the launch traced here: 3210 us
  waiting for transfers between devices  1170 us (36%)
  matrix products  975 us (30%)
  local copies, waits for them, and re-layouts  528 us (16%)
  starting transfers between devices  205 us (6%)
  other arithmetic  157 us (5%)
  blocking collectives  117 us (4%)
  loops' own time  49.1 us (2%)
    dot_general x184, matrix products, exact_dot(): jnp.einsum(formula, left, right, precision=lax.Precision.HIGHEST, preferr...  614 us
    reduce_scatter x1, waiting for transfers between devices, body(): lax.psum_scatter(spectral_total, ('section', 'seq'), scatter_dimension=0,...  459 us
    dot_general x34, matrix products, one_group(): jnp.einsum('rk,rd->kd', mixed_block, spectrum_grad, preferred_element_typ...  138 us
    reduce_scatter x1, waiting for transfers between devices, body(): lax.psum_scatter(output_total, ('section', 'seq'), scatter_dimension=0, t...  119 us
    reduce_scatter x1, waiting for transfers between devices, body(): lax.psum_scatter(triple_total, ('section', 'seq'), scatter_dimension=0, t...  104 us
    squeeze x34, local copies, waits for them, and re-layouts, one_group(): block_grad[0]  100 us
    reduce_scatter x1, waiting for transfers between devices, body(): lax.psum_scatter(down_total[None], 'seq', scatter_dimension=1, tiled=True)  97.6 us
    reduce_scatter x1, waiting for transfers between devices, body(): lax.psum_scatter(up_total[None], 'seq', scatter_dimension=1, tiled=True)  97.5 us
  transfers between devices with their start and end apart: 73, of which 33 were waited for; matrix products, arithmetic and copies ran while one was open for 12% of the time, Pallas kernels for 0%

commit v1 on v0

v1 whole, which is shorter than its diff:
```python
import functools
import math

import jax
import jax.numpy as jnp
from jax import lax
from jax.experimental import pallas as pl
from jax.experimental.pallas import tpu as pltpu
from jax.sharding import PartitionSpec as P

ORDER = 3
HEAD_DIM = 64
WINDOW = 512
EPSILON = 1e-05
BIG_NEGATIVE = -1e30
MESH = pl.DeviceIdType.MESH
BF = jnp.bfloat16
F32 = jnp.float32
LANES = 128
BLOCK = 256
PIECE = 16
VMEM_LIMIT = 60 * 1024 * 1024


class Plan:
    def __init__(self, chips, tok_rows, width, filter_count, map_rows):
        self.chips = chips
        self.rows = tok_rows
        self.half = tok_rows // 2
        self.width = width
        self.filters = filter_count
        self.cols_in = 4
        self.cols_out = max(1, math.isqrt(chips // 4))
        self.groups = chips // (self.cols_in * self.cols_out)
        self.local = filter_count // self.groups
        self.length = chips * self.half
        self.blocks = self.length // BLOCK
        self.jb = width // self.cols_in
        self.ia = width // self.cols_out
        self.map_rows = map_rows
        self.routed = map_rows % PIECE == 0
        self.pieces = map_rows // PIECE
        self.f_rows = -(-self.local // 16) * 16


def spot():
    return lax.axis_index("section"), lax.axis_index("seq")


def greet_everyone(chips):
    section, chip = spot()
    me = section * chips + chip
    barrier = pltpu.get_barrier_semaphore()

    def one(step, carry):
        peer = lax.rem(me + step, 2 * chips)
        pl.semaphore_signal(
            barrier, inc=1, device_id=(peer // chips, lax.rem(peer, chips)), device_id_type=MESH
        )
        return carry

    lax.fori_loop(1, 2 * chips, one, 0)
    pl.semaphore_wait(barrier, 2 * chips - 1)


def push(src, dst, send, recv, target):
    return pltpu.make_async_remote_copy(
        src_ref=src,
        dst_ref=dst,
        send_sem=send,
        recv_sem=recv,
        device_id=target,
        device_id_type=MESH,
    )


def bytes_of(ref, sem):
    pltpu.make_async_copy(ref, ref, sem).wait()


def entry_kernel(chips, count, *refs):
    given = refs[:count]
    gains = refs[count]
    taken = refs[count + 1 : 2 * count + 1]
    gains_all = refs[2 * count + 1]
    send, recv, gain_send, gain_recv = refs[2 * count + 2 :]
    section, chip = spot()
    me = section * chips + chip
    greet_everyone(chips)
    copies = [
        push(given[i], taken[i], send.at[i], recv.at[i], (1 - section, chip)) for i in range(count)
    ]
    for copy in copies[:1]:
        copy.start()

    def one(step, carry):
        peer = lax.rem(me + step, 2 * chips)
        push(
            gains,
            gains_all.at[section, chip],
            gain_send,
            gain_recv,
            (peer // chips, lax.rem(peer, chips)),
        ).start()
        return carry

    lax.fori_loop(1, 2 * chips, one, 0)
    pltpu.make_async_copy(gains, gains_all.at[section, chip], gain_recv).start()
    for copy in copies[1:]:
        copy.start()
    bytes_of(gains_all, gain_recv)

    def drain(step, carry):
        push(gains, gains_all.at[section, chip], gain_send, gain_recv, (section, chip)).wait_send()
        return carry

    lax.fori_loop(1, 2 * chips, drain, 0)
    for copy in copies:
        copy.wait()


def entry_call(chips, arrays, gains):
    count = len(arrays)
    any_spec = pl.BlockSpec(memory_space=pl.ANY)
    return pl.pallas_call(
        functools.partial(entry_kernel, chips, count),
        out_shape=[jax.ShapeDtypeStruct(a.shape, a.dtype) for a in arrays]
        + [jax.ShapeDtypeStruct((2, chips) + gains.shape, gains.dtype)],
        in_specs=[any_spec] * (count + 1),
        out_specs=[any_spec] * (count + 1),
        scratch_shapes=[
            pltpu.SemaphoreType.DMA((count,)),
            pltpu.SemaphoreType.DMA((count,)),
            pltpu.SemaphoreType.DMA,
            pltpu.SemaphoreType.DMA,
        ],
        compiler_params=pltpu.CompilerParams(collective_id=1, has_side_effects=True),
        name="entry",
    )(*arrays, gains)


def exit_kernel(chips, give, tiles, take, land, send, recv, gain_send, gain_recv):
    section, chip = spot()
    me = section * chips + chip
    greet_everyone(chips)
    swap = push(give, take, send, recv, (1 - section, chip))
    swap.start()

    def one(step, carry):
        peer = lax.rem(me + step, 2 * chips)
        push(
            tiles.at[peer],
            land.at[me],
            gain_send,
            gain_recv,
            (peer // chips, lax.rem(peer, chips)),
        ).start()
        return carry

    lax.fori_loop(1, 2 * chips, one, 0)
    pltpu.make_async_copy(tiles.at[me], land.at[me], gain_recv).start()
    bytes_of(land, gain_recv)
    bytes_of(land.at[pl.ds(0, 2 * chips - 1)], gain_send)
    swap.wait()


def exit_call(chips, give, tiles):
    any_spec = pl.BlockSpec(memory_space=pl.ANY)
    return pl.pallas_call(
        functools.partial(exit_kernel, chips),
        out_shape=[
            jax.ShapeDtypeStruct(give.shape, give.dtype),
            jax.ShapeDtypeStruct(tiles.shape, tiles.dtype),
        ],
        in_specs=[any_spec] * 2,
        out_specs=[any_spec] * 2,
        scratch_shapes=[
            pltpu.SemaphoreType.DMA,
            pltpu.SemaphoreType.DMA,
            pltpu.SemaphoreType.DMA,
            pltpu.SemaphoreType.DMA,
        ],
        compiler_params=pltpu.CompilerParams(collective_id=4, has_side_effects=True),
        name="leave",
    )(give, tiles)


def filter_rows(plan, land, table, first_row, backward):
    lane = lax.broadcasted_iota(jnp.int32, (plan.f_rows, LANES), 1)
    low = lane < plan.half
    total = plan.length // LANES
    for m in range(total):
        if backward:
            one, two = 2 * m, 2 * m + 1
        else:
            one, two = plan.chips - 1 - 2 * m, plan.chips - 2 - 2 * m
        left = land[one, first_row : first_row + plan.f_rows, :].astype(F32)
        right = land[two, first_row : first_row + plan.f_rows, :].astype(F32)
        even = jnp.where(low, left, pltpu.roll(right, plan.half, 1))
        odd = jnp.where(low, pltpu.roll(left, plan.half, 1), right)
        at = LANES * m + (BLOCK if backward else 0)
        table[0, :, at : at + LANES] = even
        table[1, :, at : at + LANES] = odd
    blank = jnp.zeros((plan.f_rows, BLOCK), F32)
    at = 0 if backward else plan.length
    for parity in range(2):
        table[parity, :, at : at + BLOCK] = blank


def build_strips(plan, table, strip, backward):
    span = plan.length + BLOCK
    shift = span - LANES if backward else span - (LANES - 1)
    part = 32

    def one(k, carry):
        for parity in range(2):
            row = table[parity, pl.ds(k, 1), :]
            for start in range(0, LANES, part):
                spread = jnp.broadcast_to(row, (part, span))
                rolled = pltpu.roll(
                    spread, (shift + start) % span, 1, stride=1, stride_axis=0
                ).astype(BF)
                strip[2 * k + parity, LANES + start : LANES + start + part, :] = rolled[
                    :, : plan.length
                ]
                strip[2 * k + parity, start : start + part, :] = rolled[
                    :, LANES : LANES + plan.length
                ]
        return carry

    lax.fori_loop(0, plan.local, one, 0)


def owner_pieces(plan, act):
    section, chip = spot()
    dev = section * plan.chips + chip
    per_map = plan.width // PIECE
    per_block = plan.jb // PIECE

    def unit(m, carry):
        g = plan.pieces * dev + m
        which = g // per_map
        inside = lax.rem(g, per_map)
        b = inside // per_block
        sub = lax.rem(inside, per_block)
        sign = which // plan.filters
        full = lax.rem(which, plan.filters)
        group = full // plan.local
        k = lax.rem(full, plan.local)

        @pl.when(sign < 2)
        def _():
            for a in range(plan.cols_out):
                target = a + plan.cols_out * (b + plan.cols_in * group)
                act(m, False, k, sub, a, sign, target)

        @pl.when(sign >= 2)
        def _():
            for a in range(plan.cols_out):
                for core in range(2):
                    act(m, True, full, sub, a, core, a + plan.cols_out * b)

        return carry

    lax.fori_loop(0, plan.pieces, unit, 0)


def forward_kernel(plan, *refs):
    if plan.routed:
        u_ref, f_ref, maps_ref = refs[:3]
        rest = refs[3:]
    else:
        u_ref, f_ref, mine_ref, other_ref, taps_ref = refs[:5]
        rest = refs[5:]
    (
        conv_ref,
        v_ref,
        pq_ref,
        tapw_ref,
        x_ref,
        xs_ref,
        filt_ref,
        x_buf,
        xo_buf,
        xs_buf,
        xf_buf,
        f_land,
        table,
        strip,
        mine,
        other,
        taps,
        pq,
        acc,
        y_buf,
        land,
        stage,
        u_send,
        x_recv,
        f_send,
        f_recv,
        m_send,
        m_recv,
        t_recv,
        o_send,
        o_recv,
        c_send,
        c_recv,
        v_sem,
        out_sem,
    ) = rest
    chips, half, jb, ia = plan.chips, plan.half, plan.jb, plan.ia
    section, chip = spot()
    dev = section * chips + chip
    my_group = chip // (plan.cols_out * plan.cols_in)
    greet_everyone(chips)

    def send_u(step, carry):
        peer = lax.rem(chip + step, chips)
        b = lax.rem(peer // plan.cols_out, plan.cols_in)
        group = peer // (plan.cols_out * plan.cols_in)
        push(
            u_ref.at[b],
            x_buf.at[pl.ds(half * chip, half), :],
            u_send,
            x_recv,
            (section, peer),
        ).start()
        push(f_ref.at[group], f_land.at[chip], f_send, f_recv, (section, peer)).start()
        return carry

    lax.fori_loop(1, chips, send_u, 0)
    pltpu.make_async_copy(
        u_ref.at[lax.rem(chip // plan.cols_out, plan.cols_in)],
        x_buf.at[pl.ds(half * chip, half), :],
        x_recv,
    ).start()
    pltpu.make_async_copy(f_ref.at[my_group], f_land.at[chip], f_recv).start()

    if plan.routed:

        def places(m, tap, k, sub, a):
            src = maps_ref.at[pl.ds(PIECE * m, PIECE), pl.ds(a * ia, ia)]
            if tap:
                return src, taps.at[pl.ds(jb * k + PIECE * sub, PIECE), :], t_recv
            return src, mine.at[k, pl.ds(PIECE * sub, PIECE), :], m_recv

        def start_piece(m, tap, k, sub, a, to_section, to_chip):
            src, dst, sem = places(m, tap, k, sub, a)
            here = to_section * chips + to_chip == dev

            @pl.when(here)
            def _():
                pltpu.make_async_copy(src, dst, sem).start()

            @pl.when(jnp.logical_not(here))
            def _():
                push(src, dst, m_send, sem, (to_section, to_chip)).start()

        def drain_piece(m, tap, k, sub, a, to_section, to_chip):
            src, dst, sem = places(m, tap, k, sub, a)

            @pl.when(to_section * chips + to_chip != dev)
            def _():
                push(src, dst, m_send, sem, (to_section, to_chip)).wait_send()

        owner_pieces(plan, start_piece)

    bytes_of(f_land, f_recv)
    filter_rows(plan, f_land, table, 0, False)
    build_strips(plan, table, strip, False)
    filt_out = pltpu.make_async_copy(f_land, filt_ref, out_sem.at[0])
    filt_out.start()

    if plan.routed:
        bytes_of(mine, m_recv)
        swap = push(mine, other, o_send, o_recv, (1 - section, chip))
        swap.start()

        @pl.when(my_group == 0)
        def _():
            bytes_of(taps, t_recv)

        @pl.when(my_group != 0)
        def _():
            taps[...] = jnp.zeros_like(taps)
    else:
        for src, dst in ((mine_ref, mine), (other_ref, other), (taps_ref, taps)):
            pltpu.sync_copy(src, dst)

    bytes_of(x_buf, x_recv)
    x_out = pltpu.make_async_copy(x_buf, x_ref, out_sem.at[1])
    x_out.start()
    xf_buf[0:8, :] = jnp.zeros((8, 2 * jb), F32)
    for i in range(plan.blocks):
        rows = slice(BLOCK * i, BLOCK * (i + 1))
        xf_buf[8 + BLOCK * i : 8 + BLOCK * (i + 1), :] = x_buf[rows, :].astype(F32)
    for i in range(plan.blocks):
        rows = slice(BLOCK * i, BLOCK * (i + 1))
        moved = xf_buf[7 + BLOCK * i : 7 + BLOCK * (i + 1), :].astype(BF)
        xs_buf[rows, :] = moved
        xo_buf[rows, :jb] = x_buf[rows, :jb]
        xo_buf[rows, jb:] = moved[:, jb:]
    xs_out = pltpu.make_async_copy(xs_buf, xs_ref, out_sem.at[2])
    xs_out.start()

    if plan.routed:
        swap.wait()
    turn = (1 - 2 * section).astype(F32)

    def mix(k, carry):
        first = mine[k].astype(F32)
        second = other[k].astype(F32)
        pq[k, :jb, :] = (first + second).astype(BF)
        pq[k, jb:, :] = ((first - second) * turn).astype(BF)
        return carry

    lax.fori_loop(0, plan.local, mix, 0)
    pq_out = pltpu.make_async_copy(pq, pq_ref, out_sem.at[3])
    pq_out.start()
    taps_out = pltpu.make_async_copy(taps, tapw_ref, out_sem.at[4])
    taps_out.start()

    for i in range(plan.blocks):
        rows = slice(BLOCK * i, BLOCK * (i + 1))
        depth = BLOCK * (i + 1)
        offset = plan.length - depth
        x_now = x_buf[rows, :]
        s_now = xs_buf[rows, :]
        acc[0] = jnp.dot(
            jnp.concatenate([x_now[:, :jb], s_now[:, jb:]], 1),
            taps[: 2 * jb, :],
            preferred_element_type=F32,
        ) + jnp.dot(s_now[:, :jb], taps[2 * jb :, :], preferred_element_type=F32)
        acc[1] = jnp.dot(
            jnp.concatenate([x_now[:, jb:], x_now[:, :jb]], 1),
            taps[: 2 * jb, :],
            preferred_element_type=F32,
        ) + jnp.dot(s_now[:, jb:], taps[2 * jb :, :], preferred_element_type=F32)

        def step(k, carry, i=i, depth=depth, offset=offset):
            slot = lax.rem(k, 2)
            v_copy = pltpu.make_async_copy(
                stage.at[slot], v_ref.at[k, :, pl.ds(BLOCK * i, BLOCK), :], v_sem.at[slot]
            )
            even = jnp.dot(
                strip[2 * k, :, offset:], x_buf[:depth, :], preferred_element_type=F32
            ).astype(BF)
            odd = jnp.dot(
                strip[2 * k + 1, :, offset:], xo_buf[:depth, :], preferred_element_type=F32
            ).astype(BF)
            first = jnp.concatenate([even[:, :jb], odd[:, jb:]], 1)
            second = jnp.concatenate([even[:, jb:], odd[:, :jb]], 1)
            if i == 0:
                pl.when(k >= 2)(v_copy.wait)
            else:
                v_copy.wait()
            stage[slot, 0] = first
            stage[slot, 1] = second
            v_copy.start()
            acc[0] += jnp.dot(first, pq[k], preferred_element_type=F32)
            acc[1] += jnp.dot(second, pq[k], preferred_element_type=F32)
            return carry

        lax.fori_loop(0, plan.local, step, 0)
        y_buf[0, rows, :] = acc[0].astype(BF)
        y_buf[1, rows, :] = acc[1].astype(BF)

        def give(r, carry, i=i):
            peer = BLOCK // half * i + r
            src = y_buf.at[:, pl.ds(half * peer, half), :]

            @pl.when(peer == chip)
            def _():
                pltpu.make_async_copy(src, land.at[chip], c_recv).start()

            @pl.when(peer != chip)
            def _():
                push(src, land.at[chip], c_send, c_recv, (section, peer)).start()

            return carry

        lax.fori_loop(0, BLOCK // half, give, 0)

    for slot in range(2):
        pltpu.make_async_copy(
            stage.at[slot], v_ref.at[slot, :, pl.ds(0, BLOCK), :], v_sem.at[slot]
        ).wait()
    bytes_of(x_buf.at[pl.ds(0, half * (chips - 1)), :], u_send)
    bytes_of(f_land.at[pl.ds(0, chips - 1)], f_send)
    if plan.routed:
        owner_pieces(plan, drain_piece)
    for copy in (filt_out, x_out, xs_out, pq_out, taps_out):
        copy.wait()
    bytes_of(land, c_recv)
    for a in range(plan.cols_out):
        total = None
        for other_part in range(plan.cols_in * plan.groups):
            term = land[a + plan.cols_out * other_part].astype(F32)
            total = term if total is None else total + term
        conv_ref[:, :, a * ia : (a + 1) * ia] = total
    bytes_of(land.at[pl.ds(0, chips - 1)], c_send)


def forward_call(plan, u, packed, maps):
    chips, half, jb, ia = plan.chips, plan.half, plan.jb, plan.ia
    any_spec = pl.BlockSpec(memory_space=pl.ANY)
    vmem_spec = pl.BlockSpec(memory_space=pltpu.VMEM)
    dma = pltpu.SemaphoreType.DMA
    shapes = [
        ((2, half, plan.width), F32),
        ((plan.local, 2, plan.length, 2 * jb), BF),
        ((plan.local, 2 * jb, ia), BF),
        ((ORDER * jb, ia), BF),
        ((plan.length, 2 * jb), BF),
        ((plan.length, 2 * jb), BF),
        ((chips, 2 * plan.f_rows, LANES), BF),
    ]
    return pl.pallas_call(
        functools.partial(forward_kernel, plan),
        out_shape=[jax.ShapeDtypeStruct(s, d) for s, d in shapes],
        in_specs=[vmem_spec] * 2 + [any_spec] * len(maps),
        out_specs=[vmem_spec] + [any_spec] * 6,
        scratch_shapes=[
            pltpu.VMEM((plan.length, 2 * jb), BF),
            pltpu.VMEM((plan.length, 2 * jb), BF),
            pltpu.VMEM((plan.length, 2 * jb), BF),
            pltpu.VMEM((plan.length + 8, 2 * jb), F32),
            pltpu.VMEM((chips, 2 * plan.f_rows, LANES), BF),
            pltpu.VMEM((2, plan.f_rows, plan.length + BLOCK), F32),
            pltpu.VMEM((2 * plan.local, BLOCK, plan.length), BF),
            pltpu.VMEM((plan.local, jb, ia), BF),
            pltpu.VMEM((plan.local, jb, ia), BF),
            pltpu.VMEM((ORDER * jb, ia), BF),
            pltpu.VMEM((plan.local, 2 * jb, ia), BF),
            pltpu.VMEM((2, BLOCK, ia), F32),
            pltpu.VMEM((2, plan.length, ia), BF),
            pltpu.VMEM((chips, 2, half, ia), BF),
            pltpu.VMEM((2, 2, BLOCK, 2 * jb), BF),
        ]
        + [dma] * 11
        + [dma((2,)), dma((5,))],
        compiler_params=pltpu.CompilerParams(
            collective_id=2, has_side_effects=True, vmem_limit_bytes=VMEM_LIMIT
        ),
        name="spectral_forward",
    )(u, packed, *maps)


def backward_kernel(plan, *refs):
    g_ref, filt_ref, v_ref, pq, tapw, x_buf, xs_buf, du_ref = refs[:8]
    if plan.routed:
        dmaps_ref = refs[8]
        rest = refs[9:]
    else:
        dmap_ref, dtap_ref = refs[8:10]
        rest = refs[10:]
    (
        g_buf,
        gt_buf,
        table,
        strip,
        v_buf,
        z_even,
        z_odd,
        acc_even,
        acc_odd,
        kept,
        give_m,
        take_m,
        total_m,
        kept_t,
        give_t,
        take_t,
        total_t,
        du_buf,
        land,
        g_send,
        g_recv,
        v_sem,
        m_send,
        m_recv,
        t_send,
        t_recv,
        w_send,
        w_recv,
        d_send,
        d_recv,
    ) = rest
    chips, half, jb, ia = plan.chips, plan.half, plan.jb, plan.ia
    section, chip = spot()
    dev = section * chips + chip
    my_a = lax.rem(chip, plan.cols_out)
    my_b = lax.rem(chip // plan.cols_out, plan.cols_in)
    my_group = chip // (plan.cols_out * plan.cols_in)
    greet_everyone(chips)

    def send_g(step, carry):
        peer = lax.rem(chip + step, chips)
        a = lax.rem(peer, plan.cols_out)
        push(
            g_ref.at[:, :, pl.ds(pl.multiple_of(a * ia, ia), ia)],
            g_buf.at[:, pl.ds(half * chip, half), :],
            g_send,
            g_recv,
            (section, peer),
        ).start()
        return carry

    lax.fori_loop(1, chips, send_g, 0)
    pltpu.make_async_copy(
        g_ref.at[:, :, pl.ds(pl.multiple_of(my_a * ia, ia), ia)],
        g_buf.at[:, pl.ds(half * chip, half), :],
        g_recv,
    ).start()
    v_copy = [pltpu.make_async_copy(v_ref.at[k], v_buf.at[k], v_sem.at[k]) for k in range(2)]
    for copy in v_copy:
        copy.start()
    filter_rows(plan, filt_ref, table, plan.f_rows, True)
    build_strips(plan, table, strip, True)
    acc_even[...] = jnp.zeros_like(acc_even)
    acc_odd[...] = jnp.zeros_like(acc_odd)
    bytes_of(g_buf, g_recv)
    for phase in range(2):
        for i in range(plan.blocks):
            rows = slice(BLOCK * i, BLOCK * (i + 1))
            gt_buf[phase, :, rows] = g_buf[phase, rows, :].astype(F32).T.astype(BF)
    turn = (1 - 2 * section).astype(F32)
    half_ways = (((1,), (1,)), ((), ()))

    def piece_of(k, tap, sub):
        per_map = plan.width // PIECE
        which = 2 * plan.filters + k if tap else section * plan.filters + my_group * plan.local + k
        g = which * per_map + my_b * (plan.jb // PIECE) + sub
        return g // plan.pieces, lax.rem(g, plan.pieces)

    def piece_copies(k, tap, begin):
        def one(sub, carry):
            owner, row = piece_of(k, tap, sub)
            src = (
                total_t.at[pl.ds(jb * k + PIECE * sub, PIECE), :]
                if tap
                else total_m.at[k, pl.ds(PIECE * sub, PIECE), :]
            )
            dst = dmaps_ref.at[
                pl.ds(PIECE * row, PIECE), pl.ds(pl.multiple_of(my_a * ia, ia), ia)
            ]
            if begin:

                @pl.when(owner == dev)
                def _():
                    pltpu.make_async_copy(src, dst, w_recv).start()

            @pl.when(owner != dev)
            def _():
                copy = push(src, dst, w_send, w_recv, (owner // chips, lax.rem(owner, chips)))
                if begin:
                    copy.start()
                else:
                    copy.wait_send()

            return carry

        lax.fori_loop(0, plan.jb // PIECE, one, 0)

    def exchange(k):
        return push(give_m.at[k], take_m.at[k], m_send.at[k], m_recv.at[k], (1 - section, chip))

    def finish(k):
        exchange(k).wait()
        total_m[k] = (kept[k] + take_m[k].astype(F32)).astype(BF)
        if plan.routed:
            piece_copies(k, False, True)

    x_even, x_odd = x_buf[:, :jb], x_buf[:, jb:]
    s_even, s_odd = xs_buf[:, :jb], xs_buf[:, jb:]
    for tap, (on_even, on_odd) in enumerate(((x_even, x_odd), (s_odd, x_even), (s_even, s_odd))):
        tap_grad = jnp.dot(gt_buf[0], on_even, preferred_element_type=F32) + jnp.dot(
            gt_buf[1], on_odd, preferred_element_type=F32
        )
        tap_grad = tap_grad.T
        kept_t[tap * jb : (tap + 1) * jb, :] = tap_grad
        give_t[tap * jb : (tap + 1) * jb, :] = tap_grad.astype(BF)
    tap_swap = push(give_t, take_t, t_send, t_recv, (1 - section, chip))
    tap_swap.start()
    for i in range(plan.blocks):
        rows = slice(BLOCK * i, BLOCK * (i + 1))
        from_even = lax.dot_general(
            g_buf[0, rows, :], tapw[...], half_ways, preferred_element_type=F32
        )
        from_odd = lax.dot_general(
            g_buf[1, rows, :], tapw[...], half_ways, preferred_element_type=F32
        )
        acc_even[rows, :jb] = from_even[:, :jb] + from_odd[:, jb : 2 * jb]
        acc_even[rows, jb : 2 * jb] = from_odd[:, :jb]
        acc_odd[rows, :jb] = from_even[:, 2 * jb :]
        acc_odd[rows, jb : 2 * jb] = from_even[:, jb : 2 * jb] + from_odd[:, 2 * jb :]

    def step(k, carry):
        slot = lax.rem(k, 2)
        for i in range(plan.blocks):
            rows = slice(BLOCK * i, BLOCK * (i + 1))
            from_even = lax.dot_general(
                g_buf[0, rows, :], pq[k], half_ways, preferred_element_type=F32
            ).astype(BF)
            from_odd = lax.dot_general(
                g_buf[1, rows, :], pq[k], half_ways, preferred_element_type=F32
            ).astype(BF)
            z_even[rows, :jb] = from_even[:, :jb]
            z_even[rows, jb:] = from_odd[:, :jb]
            z_odd[rows, :jb] = from_odd[:, jb:]
            z_odd[rows, jb:] = from_even[:, jb:]
        pltpu.make_async_copy(v_ref.at[k], v_buf.at[slot], v_sem.at[slot]).wait()
        grad = jnp.dot(gt_buf[0], v_buf[slot, 0], preferred_element_type=F32) + jnp.dot(
            gt_buf[1], v_buf[slot, 1], preferred_element_type=F32
        )
        grad = grad.T
        plus, minus = grad[:jb, :], grad[jb:, :] * turn
        kept[k] = plus + minus
        give_m[k] = (plus - minus).astype(BF)
        exchange(k).start()

        @pl.when(k + 2 < plan.local)
        def _():
            pltpu.make_async_copy(v_ref.at[k + 2], v_buf.at[slot], v_sem.at[slot]).start()

        for j in range(plan.blocks):
            rows = slice(BLOCK * j, BLOCK * (j + 1))
            depth = plan.length - BLOCK * j
            acc_even[rows, :] += jnp.dot(
                strip[2 * k, :, :depth], z_even[BLOCK * j :, :], preferred_element_type=F32
            )
            out = jnp.dot(
                strip[2 * k + 1, :, :depth], z_odd[BLOCK * j :, :], preferred_element_type=F32
            )
            acc_even[rows, :jb] += out[:, :jb]
            acc_odd[rows, jb:] += out[:, jb:]

        @pl.when(k >= 1)
        def _():
            finish(k - 1)

        return carry

    lax.fori_loop(0, plan.local, step, 0)
    for i in range(plan.blocks):
        rows = slice(BLOCK * i, BLOCK * (i + 1))
        moved = acc_odd[BLOCK * i + 1 : BLOCK * (i + 1) + 1, :]
        both = (acc_even[rows, :] + moved).astype(BF)
        du_buf[0, rows, :] = both[:, :jb]
        du_buf[1, rows, :] = both[:, jb:]

        def give(r, carry, i=i):
            peer = BLOCK // half * i + r
            src = du_buf.at[:, pl.ds(half * peer, half), :]

            @pl.when(peer == chip)
            def _():
                pltpu.make_async_copy(src, land.at[chip], d_recv).start()

            @pl.when(peer != chip)
            def _():
                push(src, land.at[chip], d_send, d_recv, (section, peer)).start()

            return carry

        lax.fori_loop(0, BLOCK // half, give, 0)
    finish(plan.local - 1)
    tap_swap.wait()
    total_t[...] = (kept_t[...] + take_t[...].astype(F32)).astype(BF)
    if plan.routed:

        @pl.when(jnp.logical_and(section == 0, my_group == 0))
        def _():
            for tap in range(ORDER):
                piece_copies(tap, True, True)
    else:
        pltpu.sync_copy(total_m, dmap_ref)
        pltpu.sync_copy(total_t, dtap_ref)
    bytes_of(g_buf.at[0, pl.ds(0, 2 * half * (chips - 1) // 2), :], g_send)
    bytes_of(g_buf.at[1, pl.ds(0, 2 * half * (chips - 1) // 2), :], g_send)
    bytes_of(land, d_recv)
    for b in range(plan.cols_in):
        total = None
        for c in range(plan.groups):
            for a in range(plan.cols_out):
                term = land[a + plan.cols_out * (b + plan.cols_in * c)].astype(F32)
                total = term if total is None else total + term
        du_ref[:, :, b * jb : (b + 1) * jb] = total
    bytes_of(land.at[pl.ds(0, chips - 1)], d_send)
    if plan.routed:

        def drain(k, carry):
            piece_copies(k, False, False)
            return carry

        lax.fori_loop(0, plan.local, drain, 0)

        @pl.when(jnp.logical_and(section == 0, my_group == 0))
        def _():
            for tap in range(ORDER):
                piece_copies(tap, True, False)

        bytes_of(dmaps_ref, w_recv)


def backward_call(plan, g, filt, v, pq, tapw, x, xs):
    chips, half, jb, ia = plan.chips, plan.half, plan.jb, plan.ia
    any_spec = pl.BlockSpec(memory_space=pl.ANY)
    vmem_spec = pl.BlockSpec(memory_space=pltpu.VMEM)
    dma = pltpu.SemaphoreType.DMA
    out_shape = [jax.ShapeDtypeStruct((2, half, plan.width), F32)]
    if plan.routed:
        out_shape.append(jax.ShapeDtypeStruct((plan.map_rows, plan.width), BF))
    else:
        out_shape.append(jax.ShapeDtypeStruct((plan.local, jb, ia), BF))
        out_shape.append(jax.ShapeDtypeStruct((ORDER * jb, ia), BF))
    return pl.pallas_call(
        functools.partial(backward_kernel, plan),
        out_shape=out_shape,
        in_specs=[vmem_spec, vmem_spec, any_spec] + [vmem_spec] * 4,
        out_specs=[vmem_spec] + [any_spec] * (len(out_shape) - 1),
        scratch_shapes=[
            pltpu.VMEM((2, plan.length, ia), BF),
            pltpu.VMEM((2, ia, plan.length), BF),
            pltpu.VMEM((2, plan.f_rows, plan.length + BLOCK), F32),
            pltpu.VMEM((2 * plan.local, BLOCK, plan.length), BF),
            pltpu.VMEM((2, 2, plan.length, 2 * jb), BF),
            pltpu.VMEM((plan.length, 2 * jb), BF),
            pltpu.VMEM((plan.length, 2 * jb), BF),
            pltpu.VMEM((plan.length, 2 * jb), F32),
            pltpu.VMEM((plan.length + 8, 2 * jb), F32),
            pltpu.VMEM((plan.local, jb, ia), F32),
            pltpu.VMEM((plan.local, jb, ia), BF),
            pltpu.VMEM((plan.local, jb, ia), BF),
            pltpu.VMEM((plan.local, jb, ia), BF),
            pltpu.VMEM((ORDER * jb, ia), F32),
            pltpu.VMEM((ORDER * jb, ia), BF),
            pltpu.VMEM((ORDER * jb, ia), BF),
            pltpu.VMEM((ORDER * jb, ia), BF),
            pltpu.VMEM((2, plan.length, jb), BF),
            pltpu.VMEM((chips, 2, half, jb), BF),
            dma,
            dma,
            dma((2,)),
            dma((plan.local,)),
            dma((plan.local,)),
            dma,
            dma,
            dma,
            dma,
            dma,
            dma,
        ],
        compiler_params=pltpu.CompilerParams(
            collective_id=3, has_side_effects=True, vmem_limit_bytes=VMEM_LIMIT
        ),
        name="spectral_backward",
    )(g, filt, v, pq, tapw, x, xs)


def swapped(block):
    return lax.ppermute(block, "section", [(0, 1), (1, 0)])


def shifted(block, axis, distance):
    devices = range(lax.axis_size(axis))
    route = [(i - distance, i) for i in devices if i - distance in devices]
    return lax.ppermute(block, axis, route)


def dot(formula, left, right):
    return jnp.einsum(formula, left, right, preferred_element_type=F32)


def norm_forward(values, weights):
    factor = lax.rsqrt(jnp.mean(values * values, axis=-1, keepdims=True) + EPSILON)
    return (values * factor * weights, factor)


def norm_backward(values, factor, weights, upstream):
    weighted = upstream * weights
    gain_grad = jnp.sum(upstream * values * factor, axis=0)
    correction = jnp.mean(weighted * values, axis=-1, keepdims=True)
    return (factor * weighted - values * factor * factor * factor * correction, gain_grad)


def mlp_forward(middle, gain, weights):
    w_gate, w_up, w_down = weights
    rows = middle.shape[0]
    normed, factor = norm_forward(middle, gain)
    own = normed.astype(BF)
    inputs = jnp.concatenate([own, swapped(own)], 0)
    gate_rows = dot("td,df->tf", inputs, w_gate)
    up_rows = dot("td,df->tf", inputs, w_up)
    active = (jax.nn.silu(gate_rows) * up_rows).astype(BF)
    part = dot("tf,fd->td", active, w_down)
    branch = part[:rows] + swapped(part[rows:].astype(BF)).astype(F32)
    return branch, (factor, inputs, gate_rows, up_rows, active)


def mlp_backward(middle, gain, weights, saved, upstream, branch_grad):
    w_gate, w_up, w_down = weights
    rows = middle.shape[0]
    factor, inputs, gate_rows, up_rows, active = saved
    down_grad = dot("tf,td->fd", active, branch_grad)
    active_grad = dot("td,fd->tf", branch_grad, w_down)
    sigmoid = jax.nn.sigmoid(gate_rows)
    slope = sigmoid * (1.0 + gate_rows * (1.0 - sigmoid))
    gate_grad = (active_grad * up_rows * slope).astype(BF)
    up_grad = (active_grad * gate_rows * sigmoid).astype(BF)
    gate_w_grad = dot("td,tf->df", inputs, gate_grad)
    up_w_grad = dot("td,tf->df", inputs, up_grad)
    part = dot("tf,df->td", gate_grad, w_gate) + dot("tf,df->td", up_grad, w_up)
    normed_grad = part[:rows] + swapped(part[rows:].astype(BF)).astype(F32)
    middle_grad, gain_grad = norm_backward(middle, factor, gain, normed_grad)
    return upstream + middle_grad, gain_grad, (gate_w_grad, up_w_grad, down_grad)


def body(
    io_pair, lengths, filters, stu_maps, attn_proj, attn_out, norm_gains, mlp_gate, mlp_up, mlp_down
):
    chips = lax.axis_size("seq")
    section, chip = spot()
    core_zero = section == 0
    tok_rows = io_pair.shape[2]
    width = io_pair.shape[3]
    half = tok_rows // 2
    heads = width // HEAD_DIM
    reach = WINDOW // tok_rows
    score_scale = HEAD_DIM ** (-0.5)
    plan = Plan(chips, tok_rows, width, filters.shape[1], stu_maps.shape[0])

    sib_io, sib_gate, sib_up, sib_down, sib_proj, sib_out, gains_all = entry_call(
        chips,
        [io_pair[0], mlp_gate[0], mlp_up[0], mlp_down[0], attn_proj, attn_out],
        norm_gains[0],
    )
    gains = jnp.transpose(gains_all, (0, 2, 1, 3)).reshape(2, 2, width).astype(F32)

    def split_phases(rows):
        return (
            rows.reshape(rows.shape[:-2] + (half, 2, width))
            .swapaxes(-3, -2)
            .reshape(rows.shape)
        )

    def join_phases(rows):
        return rows.reshape(2, half, width).swapaxes(0, 1).reshape(rows.shape)

    local = jnp.arange(tok_rows, dtype=jnp.int32)
    order = 2 * (local % half) + local // half
    places = chip * tok_rows + order
    own_length = jnp.where(core_zero, lengths[0], lengths[1])
    other_length = jnp.where(core_zero, lengths[1], lengths[0])
    mask_rows = (places < own_length).astype(F32)[:, None]
    other_mask = (places < other_length).astype(F32)[:, None]
    x = split_phases(jnp.where(core_zero, io_pair[0, 0], sib_io[1]))
    cot_pair = jnp.where(core_zero, sib_io, io_pair[0])
    cot = split_phases(jnp.where(core_zero, cot_pair[0], cot_pair[1]))
    cot_other = split_phases(jnp.where(core_zero, cot_pair[1], cot_pair[0]))
    hidden = x.astype(F32) * mask_rows
    normed, spectral_factor = norm_forward(hidden, gains[0, 0])
    u = normed.astype(BF)
    u_parts = jnp.transpose(
        u.reshape(2, half, plan.cols_in, plan.jb), (2, 1, 0, 3)
    ).reshape(plan.cols_in, half, 2 * plan.jb)

    lags = jnp.transpose(filters.reshape(half, 2, plan.filters), (2, 1, 0))
    lags = jnp.stack([lags[:, :, ::-1], lags], 0).reshape(
        2, plan.groups, plan.local, 2 * half
    )
    lags = jnp.pad(lags, ((0, 0), (0, 0), (0, plan.f_rows - plan.local), (0, LANES - 2 * half)))
    packed = jnp.transpose(lags, (1, 0, 2, 3)).reshape(plan.groups, 2 * plan.f_rows, LANES)

    my_a = chip % plan.cols_out
    my_b = (chip // plan.cols_out) % plan.cols_in
    my_group = chip // (plan.cols_out * plan.cols_in)
    if plan.routed:
        maps = [stu_maps]
    else:
        whole = lax.all_gather(stu_maps, ("section", "seq"), axis=0, tiled=True)
        whole = lax.dynamic_slice(
            whole.reshape(-1, width, width),
            (0, my_b * plan.jb, my_a * plan.ia),
            (whole.shape[0] // width, plan.jb, plan.ia),
        )
        pair = whole[: 2 * plan.filters].reshape(2, plan.filters, plan.jb, plan.ia)
        pair = lax.dynamic_slice_in_dim(pair, my_group * plan.local, plan.local, 1)
        taps = jnp.where(my_group == 0, whole[2 * plan.filters :], 0).astype(BF)
        maps = [
            jnp.where(core_zero, pair[0], pair[1]),
            jnp.where(core_zero, pair[1], pair[0]),
            taps.reshape(-1, plan.ia),
        ]
    conv, v, pq, tapw, x_all, xs_all, filt = forward_call(plan, u_parts, packed, maps)

    ff = mlp_gate.shape[2]
    ff_rows = mlp_down.shape[1]
    ff_half = ff_rows // 2

    def my_half(layer, gate, up, down):
        del layer
        def pick(w):
            w = w.reshape(w.shape[0], chips, 2, ff_half)
            return jnp.where(core_zero, w[:, :, 0], w[:, :, 1]).reshape(w.shape[0], -1)

        return (
            pick(gate),
            pick(up),
            jnp.where(core_zero, down[:ff_half], down[ff_half:]),
        )

    own_raw = (mlp_gate[0], mlp_up[0], mlp_down[0])
    sib_raw = (sib_gate, sib_up, sib_down)
    layers = []
    for layer in range(2):
        raw = tuple(
            jnp.where(core_zero == (layer == 0), mine, theirs)
            for mine, theirs in zip(own_raw, sib_raw)
        )
        shares = my_half(layer, *raw)
        layers.append(
            tuple(lax.all_gather(w, "seq", axis=0, tiled=True) for w in shares)
        )
    proj_rows = attn_proj.shape[0]
    out_rows = attn_out.shape[0]
    both_rows = jnp.concatenate(
        [
            jnp.where(core_zero, attn_proj, sib_proj),
            jnp.where(core_zero, sib_proj, attn_proj),
            jnp.where(core_zero, attn_out, sib_out),
            jnp.where(core_zero, sib_out, attn_out),
        ],
        0,
    )
    attn_all = lax.all_gather(both_rows, "seq", axis=0, tiled=False)
    w_proj = jnp.swapaxes(
        attn_all[:, : 2 * proj_rows].reshape(chips, 2, proj_rows, width), 0, 1
    ).reshape(3, width, width)
    w_out = jnp.swapaxes(
        attn_all[:, 2 * proj_rows :].reshape(chips, 2, out_rows, width), 0, 1
    ).reshape(width, width)

    middle0 = hidden + conv.reshape(tok_rows, width)
    branch0, saved0 = mlp_forward(middle0, gains[0, 1], layers[0])
    passed = (mask_rows * (middle0 + branch0)).astype(BF)

    window_hidden = passed.astype(F32)
    window_normed, window_factor = norm_forward(window_hidden, gains[1, 0])
    inputs = window_normed.astype(BF)
    triple = dot("td,wde->wte", inputs, w_proj).astype(BF)
    key_value = triple[1:]
    parts = [shifted(key_value, "seq", distance) for distance in range(reach, 0, -1)]
    windows = jnp.concatenate(parts + [key_value], 1)
    key_window = windows[0].reshape(-1, heads, HEAD_DIM)
    value_window = windows[1].reshape(-1, heads, HEAD_DIM)
    queries = triple[0].reshape(tok_rows, heads, HEAD_DIM)
    scores = dot("qhe,khe->hqk", queries, key_window) * score_scale
    key_place = (
        (chip - reach + jnp.arange(reach + 1, dtype=jnp.int32))[:, None] * tok_rows + order[None, :]
    ).reshape(-1)
    distance_rows = places[:, None] - key_place[None, :]
    allowed = (key_place[None, :] >= 0) & (distance_rows >= 0) & (distance_rows < WINDOW)
    scores = jnp.where(allowed[None], scores, BIG_NEGATIVE)
    highest = jnp.max(scores, axis=-1, keepdims=True)
    weights = jnp.exp(scores - highest)
    weights = weights / jnp.sum(weights, axis=-1, keepdims=True)
    weights_low = weights.astype(BF)
    attended = dot("hqk,khe->qhe", weights_low, value_window)
    attended = attended.reshape(tok_rows, width).astype(BF)
    middle1 = window_hidden + dot("td,de->te", attended, w_out)
    branch1, saved1 = mlp_forward(middle1, gains[1, 1], layers[1])
    block_out = (mask_rows * (middle1 + branch1)).astype(BF)

    upstream1 = cot.astype(F32) * mask_rows
    other_upstream = cot_other.astype(F32) * other_mask
    grad_pair = jnp.concatenate([upstream1, other_upstream], 0).astype(BF)
    middle1_grad, gain11, mlp1_grads = mlp_backward(
        middle1, gains[1, 1], layers[1], saved1, upstream1, grad_pair
    )
    output_input = middle1_grad.astype(BF)
    output_grad = dot("td,te->de", attended, output_input)
    attended_grad = dot("te,de->td", output_input, w_out)
    attended_grad = attended_grad.astype(BF).reshape(tok_rows, heads, HEAD_DIM)
    value_grad = dot("hqk,qhe->khe", weights_low, attended_grad)
    weight_grad = dot("qhe,khe->hqk", attended_grad, value_window)
    row_total = jnp.sum(weights * weight_grad, axis=-1, keepdims=True)
    score_grad = (weights * (weight_grad - row_total)).astype(BF)
    query_grad = dot("hqk,khe->qhe", score_grad, key_window) * score_scale
    key_grad = dot("hqk,qhe->khe", score_grad, queries) * score_scale
    pair_grad = jnp.stack([key_grad.reshape(-1, width), value_grad.reshape(-1, width)])
    own_pair = pair_grad[:, reach * tok_rows :]
    for distance in range(reach, 0, -1):
        offset = (reach - distance) * tok_rows
        back = shifted(pair_grad[:, offset : offset + tok_rows].astype(BF), "seq", -distance)
        own_pair = own_pair + back.astype(F32)
    triple_grad = jnp.concatenate([query_grad.reshape(1, tok_rows, width), own_pair], 0).astype(BF)
    proj_grad = dot("td,wte->wde", inputs, triple_grad).reshape(3 * width, width)
    normed_grad = dot("wte,wde->td", triple_grad, w_proj)
    hidden1_grad, gain10 = norm_backward(window_hidden, window_factor, gains[1, 0], normed_grad)
    passed_grad = (middle1_grad + hidden1_grad).astype(BF)

    upstream0 = passed_grad.astype(F32) * mask_rows
    own_branch = upstream0.astype(BF)
    branch_pair = jnp.concatenate([own_branch, swapped(own_branch)], 0)
    middle0_grad, gain01, mlp0_grads = mlp_backward(
        middle0, gains[0, 1], layers[0], saved0, upstream0, branch_pair
    )
    g = middle0_grad.astype(BF).reshape(2, half, width)
    results = backward_call(plan, g, filt, v, pq, tapw, x_all, xs_all)
    signal_grad = results[0].reshape(tok_rows, width)
    if plan.routed:
        maps_grad = results[1].astype(F32)
    else:
        piece, tap_piece = (r.astype(F32) for r in results[1:])
        full = jnp.zeros((2, plan.filters, width, width), F32)
        full = lax.dynamic_update_slice(
            full,
            piece[None],
            (section, my_group * plan.local, my_b * plan.jb, my_a * plan.ia),
        )
        tap_piece = jnp.where(core_zero & (my_group == 0), tap_piece, 0.0)
        tap_full = lax.dynamic_update_slice(
            jnp.zeros((ORDER, width, width), F32),
            tap_piece.reshape(ORDER, plan.jb, plan.ia),
            (0, my_b * plan.jb, my_a * plan.ia),
        )
        full = jnp.concatenate([full.reshape(-1, width), tap_full.reshape(-1, width)], 0)
        maps_grad = lax.psum_scatter(full, ("section", "seq"), scatter_dimension=0, tiled=True)
    hidden_grad, gain00 = norm_backward(hidden, spectral_factor, gains[0, 0], signal_grad)
    inputs_grad = (mask_rows * (middle0_grad + hidden_grad)).astype(BF)

    def scattered(grads):
        return [
            lax.psum_scatter(w.astype(BF), "seq", scatter_dimension=0, tiled=True) for w in grads
        ]

    halves = [scattered(mlp0_grads), scattered(mlp1_grads)]
    outs = []
    for index in range(3):
        keep = jnp.where(core_zero, halves[0][index], halves[1][index])
        give = jnp.where(core_zero, halves[1][index], halves[0][index])
        take = swapped(give)
        low = jnp.where(core_zero, keep, take).astype(F32)
        high = jnp.where(core_zero, take, keep).astype(F32)
        if index < 2:
            rows = low.shape[0]
            joined = jnp.stack(
                [low.reshape(rows, chips, ff_half), high.reshape(rows, chips, ff_half)], 2
            ).reshape(rows, ff)
        else:
            joined = jnp.concatenate([low, high], 0)
        outs.append(joined[None])
    proj_out = lax.psum_scatter(
        proj_grad.astype(BF), ("section", "seq"), scatter_dimension=0, tiled=True
    ).astype(F32)
    out_out = lax.psum_scatter(
        output_grad.astype(BF), ("section", "seq"), scatter_dimension=0, tiled=True
    ).astype(F32)

    gain_parts = jnp.stack([jnp.stack([gain00, gain01]), jnp.stack([gain10, gain11])])
    gain_cols = width // chips
    tiles = jnp.transpose(gain_parts.reshape(2, 2, chips, gain_cols), (0, 2, 1, 3))
    tiles = jnp.pad(
        tiles.reshape(2 * chips, 2, gain_cols), ((0, 0), (0, 6), (0, LANES - gain_cols))
    )
    done_in, done_out = join_phases(inputs_grad), join_phases(block_out)
    taken, landed = exit_call(chips, jnp.where(core_zero, done_out, done_in), tiles)
    first = jnp.where(core_zero, done_in, taken)
    second = jnp.where(core_zero, taken, done_out)
    result_pair = jnp.stack([first, second])[None]
    gain_out = jnp.sum(landed, axis=0)[None, :2, :gain_cols]
    return (result_pair, maps_grad, proj_out, out_out, gain_out, outs[0], outs[1], outs[2])


def solution(mesh):
    placed = (
        P("section", None, "seq", None),
        P(),
        P("seq", None),
        P(("section", "seq"), None),
        P(("section", "seq"), None),
        P(("section", "seq"), None),
        P("section", None, "seq"),
        P("section", "seq", None),
        P("section", "seq", None),
        P("section", "seq", None),
    )
    return jax.shard_map(
        body,
        mesh=mesh,
        in_specs=placed,
        out_specs=(
            P("section", None, "seq", None),
            P(("section", "seq"), None),
            P(("section", "seq"), None),
            P(("section", "seq"), None),
            P("section", None, "seq"),
            P("section", "seq", None),
            P("section", "seq", None),
            P("section", "seq", None),
        ),
        check_vma=False,
    )
```

time: 3240 us -> 1210 us (0.37)
  matrix products: 975 us -> 45.2 us
  local copies, waits for them, and re-layouts: 528 us -> 29.9 us
  waiting for transfers between devices: 1170 us -> 884 us
  starting transfers between devices: 205 us -> 20.3 us
  Pallas kernels: 0 us -> 182 us
  other arithmetic: 157 us -> 27.1 us
  blocking collectives: 117 us -> 0 us
  loops' own time: 49.1 us -> 0 us
    dot_general x312 -> x29, matrix products: 967 us -> 42.7 us  [dot(): return jnp.einsum(formula, left, right, preferred_element_type=F32)]
    reduce_scatter x6 -> x8, waiting for transfers between devices: 974 us -> 545 us  [the longest x6 458 us: scattered(): lax.psum_scatter(w.astype(BF), 'seq', scatter_dimension=0, tiled=True)]
    all_gather x5 -> x7, waiting for transfers between devices: 5.34 us -> 308 us  [the longest x6 248 us: body(): lax.all_gather(w, 'seq', axis=0, tiled=True)]
    pallas_call x0 -> x4, Pallas kernels: none -> 182 us  [the longest x1 80.3 us: forward_call(): pl.pallas_call(functools.partial(forward_kernel, plan), out_shape=[jax.Sh...]
    squeeze x68 -> x2, local copies, waits for them, and re-layouts: 173 us -> 0.12 us  [body(): x = split_phases(jnp.where(core_zero, io_pair[0, 0], sib_io[1]))]
    all_to_all x25 -> x0, waiting for transfers between devices: 164 us -> none  [the longest x4 31.4 us: finish_spectrum(): lax.all_to_all(twist_real.astype(jnp.bfloat16), 'seq', split_axis=0, conc...]
    all_to_all x25 -> x0, starting transfers between devices: 131 us -> none  [the longest x4 28.2 us: finish_spectrum(): lax.all_to_all(twist_imag.astype(jnp.bfloat16), 'seq', split_axis=0, conc...]
    all_gather x2 -> x0, blocking collectives: 117 us -> none  [the longest x1 71.8 us: body(): lax.all_gather(attn_out, ('section', 'seq'), axis=0, tiled=True)]
  transfers between devices with their start and end apart: 73 -> 33, of which waited for: 33 -> 20; matrix products, arithmetic and copies ran while one was open for 12% -> 6% of each run, Pallas kernels for 0% -> 14%
where the time goes in v1:
time: 1210 us
  waiting for transfers between devices  884 us (73%)
  Pallas kernels  182 us (15%)
  matrix products  45.2 us (4%)
  local copies, waits for them, and re-layouts  29.9 us (2%)
  other arithmetic  27.1 us (2%)
  starting transfers between devices  20.3 us (2%)
  between operations  18.4 us (2%)
    reduce_scatter x6, waiting for transfers between devices, scattered(): lax.psum_scatter(w.astype(BF), 'seq', scatter_dimension=0, tiled=True)  458 us
    all_gather x6, waiting for transfers between devices, body(): lax.all_gather(w, 'seq', axis=0, tiled=True)  248 us
    reduce_scatter x1, waiting for transfers between devices, body(): lax.psum_scatter(proj_grad.astype(BF), ('section', 'seq'), scatter_dimens...  86.9 us
    pallas_call x1, Pallas kernels, forward_call(): pl.pallas_call(functools.partial(forward_kernel, plan), out_shape=[jax.Sh...  80.3 us
    pallas_call x1, Pallas kernels, backward_call(): pl.pallas_call(functools.partial(backward_kernel, plan), out_shape=out_sh...  73.3 us
    all_gather x1, waiting for transfers between devices, body(): attn_all = lax.all_gather(both_rows, 'seq', axis=0, tiled=False)  59.4 us
    dot_general x29, matrix products, dot(): return jnp.einsum(formula, left, right, preferred_element_type=F32)  42.7 us
    ppermute x8, waiting for transfers between devices, shifted(): return lax.ppermute(block, axis, route)  28.4 us
  transfers between devices with their start and end apart: 33, of which 20 were waited for; matrix products, arithmetic and copies ran while one was open for 6% of the time, Pallas kernels for 14%

profile of v1, /device:TPU:0, one launch (start us, length us, event | category | flops | bytes accessed | tf_op | source)
XLA Modules:
  0.0 1206.5 jit_solution(3255369708867594267)
XLA Ops:
  7.2 11.0 entry.1
  31.2 80.3 %spectral_forward.1 = (f32[2,64,512]{2,1,0:T(8,128)}, bf16[12,2,1024,256]{3,2,1,0:T(8,128)(2,1)}, bf16[12,256,256]{2,1,0:T(8,128)(2,1)}, bf16[384,256]{1,0:T(8,1...) custom-call(bf16[4,64,256]{2,1,0:T(8,128)(2,1)} %reshape.413.refs_0_, ...), custom_call_target="tpu_custom_call" | custom-call | tf_op jit(solution)/shard_map/spectral_forward/pallas_call | solution.py:519
  116.7 1.7 fusion.75
  118.5 55.9 %all-gather.11.cloned.1.call-done = bf16[512,1024]{1,0:T(8,128)(2,1)} async-done(((bf16[32,1024]{1,0:T(8,128)(2,1)}), bf16[512,1024]{1,0:T(8,128)(2,1)}) %all-gather.11.cloned.1.call-update) | async-done | bytes 1048592 | tf_op jit(solution)/shard_map/all_gather | solution.py:1024
  174.4 2.7 multiply_convert_fusion.6
  177.1 54.7 %all-gather.13.cloned.1.call-done = bf16[1024,512]{1,0:T(8,128)(2,1)} async-done(((bf16[64,512]{1,0:T(8,128)(2,1)}), bf16[1024,512]{1,0:T(8,128)(2,1)}) %all-gather.13.cloned.1.call-update) | async-done | bytes 1048592 | tf_op jit(solution)/shard_map/all_gather | solution.py:1024
  231.8 1.7 fusion.88
  235.1 59.4 %all-gather.21.cloned.1.call-done = bf16[2048,512]{1,0:T(8,128)(2,1)} async-done(((bf16[128,512]{1,0:T(8,128)(2,1)}), bf16[2048,512]{1,0:T(8,128)(2,1)}) %all-gather.21.cloned.1.call-update) | async-done | bytes 2097168 | tf_op jit(solution)/shard_map/all_gather | solution.py:1037
  294.6 1.5 slice.196
  296.9 3.5 collective-permute-start.2
  300.4 3.4 collective-permute-start.3
  303.8 3.4 collective-permute-start.4
  307.3 2.9 collective-permute-start.5
  311.6 5.8 collective-permute-done.4
  317.7 2.5 fusion.87
  320.2 2.4 convolution_convert_fusion.10
  323.3 29.6 %all-gather.15.cloned.1.call-done = bf16[1024,512]{1,0:T(8,128)(2,1)} async-done(((bf16[64,512]{1,0:T(8,128)(2,1)}), bf16[1024,512]{1,0:T(8,128)(2,1)}) %all-gather.15.cloned.1.call-update) | async-done | bytes 1048592 | tf_op jit(solution)/shard_map/all_gather | solution.py:1024
  352.9 2.7 fusion.48
  355.5 54.0 %all-gather.17.cloned.1.call-done = bf16[512,1024]{1,0:T(8,128)(2,1)} async-done(((bf16[32,1024]{1,0:T(8,128)(2,1)}), bf16[512,1024]{1,0:T(8,128)(2,1)}) %all-gather.17.cloned.1.call-update) | async-done | bytes 1048592 | tf_op jit(solution)/shard_map/all_gather | solution.py:1024
  409.6 2.7 fusion.73
  412.3 54.1 %all-gather.19.cloned.1.call-done = bf16[512,1024]{1,0:T(8,128)(2,1)} async-done(((bf16[32,1024]{1,0:T(8,128)(2,1)}), bf16[512,1024]{1,0:T(8,128)(2,1)}) %all-gather.19.cloned.1.call-update) | async-done | bytes 1048592 | tf_op jit(solution)/shard_map/all_gather | solution.py:1024
  466.4 2.8 multiply_convert_fusion.4
  475.6 4.8 multiply_reduce_fusion
  480.4 1.5 fusion.8
  483.0 2.2 multiply_convert_fusion
  486.6 1.7 copy.85
  496.2 1.7 copy.86
  497.8 3.3 collective-permute-done.11
  501.1 8.3 collective-permute-done.10
  509.4 11.0 collective-permute-done.8
  522.5 1.8 convolution_convert_fusion
  524.5 1.4 convolution_convert_fusion.5
  526.3 2.1 fusion.30
  531.6 1.4 convolution_convert_fusion.6
  533.1 1.5 convolution_convert_fusion.3
  534.7 1.5 convolution_convert_fusion.4
  536.3 1.5 convolution_convert_fusion.1
  542.4 1.4 convolution_convert_fusion.2
  544.9 73.3 %spectral_backward.1 = (f32[2,64,512]{2,1,0:T(8,128)}, bf16[816,512]{1,0:T(8,128)(2,1)}) custom-call(bf16[2,64,512]{2,1,0:T(8,128)(2,1)} %bitcast.218, bf16[16,32,128]{2,1,0:T(8,128)(2,1)} %get-tuple-element.34.refs_1_, bf16[12,2,1024,256]{3,2,1,0:T(8,128)(2,1)} %get-tuple-element.35.refs_2_, bf16[12,256,256]{2,1,0:T(8,128)(2,1)} %get-tuple-element.36.refs_3_, ...), custom_call_target="tpu_custom_call" | custom-call | tf_op jit(solution)/shard_map/spectral_backward/pallas_call | solution.py:818
  623.9 17.1 %leave.1 = (bf16[128,512]{1,0:T(8,128)(2,1)}, f32[32,8,128]{2,1,0:T(8,128)}) custom-call(bf16[128,512]{1,0:T(8,128)(2,1)} %broadcast_select_fusion.6.give, f32[32,8,128]{2,1,0:T(8,128)} %pad.9.tiles), custom_call_target="tpu_custom_call" | custom-call | tf_op jit(solution)/shard_map/leave/pallas_call | solution.py:169
  645.4 86.9 %reduce-scatter.9.cloned.1.call-done = bf16[48,512]{1,0:T(8,128)(2,1)} async-done(((bf16[1536,512]{1,0:T(8,128)(2,1)}), bf16[48,512]{1,0:T(8,128)(2,1)}) %reduce-scatter.9.cloned.1.call-update) | async-done | bytes 49168 | tf_op jit(solution)/shard_map/reduce_scatter | solution.py:1155
  732.4 1.4 convert_element_type.299
  733.8 77.7 %reduce-scatter.15.cloned.1.call-done = bf16[32,1024]{1,0:T(8,128)(2,1)} async-done(((bf16[512,1024]{1,0:T(8,128)(2,1)}), bf16[32,1024]{1,0:T(8,128)(2,1)}) %reduce-scatter.15.cloned.1.call-update) | async-done | bytes 65552 | tf_op jit(solution)/shard_map/reduce_scatter | solution.py:1136
  811.5 76.3 %reduce-scatter.13.cloned.1.call-done = bf16[32,1024]{1,0:T(8,128)(2,1)} async-done(((bf16[512,1024]{1,0:T(8,128)(2,1)}), bf16[32,1024]{1,0:T(8,128)(2,1)}) %reduce-scatter.13.cloned.1.call-update) | async-done | bytes 65552 | tf_op jit(solution)/shard_map/reduce_scatter | solution.py:1136
  888.7 75.5 %reduce-scatter.19.cloned.1.call-done = bf16[32,1024]{1,0:T(8,128)(2,1)} async-done(((bf16[512,1024]{1,0:T(8,128)(2,1)}), bf16[32,1024]{1,0:T(8,128)(2,1)}) %reduce-scatter.19.cloned.1.call-update) | async-done | bytes 65552 | tf_op jit(solution)/shard_map/reduce_scatter | solution.py:1136
  964.2 76.3 %reduce-scatter.17.cloned.1.call-done = bf16[32,1024]{1,0:T(8,128)(2,1)} async-done(((bf16[512,1024]{1,0:T(8,128)(2,1)}), bf16[32,1024]{1,0:T(8,128)(2,1)}) %reduce-scatter.17.cloned.1.call-update) | async-done | bytes 65552 | tf_op jit(solution)/shard_map/reduce_scatter | solution.py:1136
  1041.4 75.5 %reduce-scatter.23.cloned.1.call-done = bf16[64,512]{1,0:T(8,128)(2,1)} async-done(((bf16[1024,512]{1,0:T(8,128)(2,1)}), bf16[64,512]{1,0:T(8,128)(2,1)}) %reduce-scatter.23.cloned.1.call-update) | async-done | bytes 65552 | tf_op jit(solution)/shard_map/reduce_scatter | solution.py:1136
  1117.0 76.4 %reduce-scatter.21.cloned.1.call-done = bf16[64,512]{1,0:T(8,128)(2,1)} async-done(((bf16[1024,512]{1,0:T(8,128)(2,1)}), bf16[64,512]{1,0:T(8,128)(2,1)}) %reduce-scatter.21.cloned.1.call-update) | async-done | bytes 65552 | tf_op jit(solution)/shard_map/reduce_scatter | solution.py:1136
  (375 shorter events, 65.9 us)
Async XLA Ops:
  7.2 109.6 %all-gather.9.cloned.1.call-start = ((), (), s32[]{:S(2)}) async-start(), calls=%async_computation.8 | async-start | bytes 1114112 | tf_op jit(solution)/shard_map/all_gather | solution.py:1024
  20.7 153.6 %all-gather.11.cloned.1.call-start = ((), (), s32[]{:S(2)}) async-start(), calls=%async_computation.9 | async-start | bytes 1114112 | tf_op jit(solution)/shard_map/all_gather | solution.py:1024
  22.4 209.5 %all-gather.13.cloned.1.call-start = ((), (), s32[]{:S(2)}) async-start(), calls=%async_computation.10 | async-start | bytes 1114112 | tf_op jit(solution)/shard_map/all_gather | solution.py:1024
  23.1 271.4 %all-gather.21.cloned.1.call-start = ((), (), s32[]{:S(2)}) async-start(), calls=%async_computation.22 | async-start | bytes 2228224 | tf_op jit(solution)/shard_map/all_gather | solution.py:1037
  24.0 328.9 %all-gather.15.cloned.1.call-start = ((), (), s32[]{:S(2)}) async-start(), calls=%async_computation.11 | async-start | bytes 1114112 | tf_op jit(solution)/shard_map/all_gather | solution.py:1024
  24.7 384.9 %all-gather.17.cloned.1.call-start = ((), (), s32[]{:S(2)}) async-start(), calls=%async_computation.12 | async-start | bytes 1114112 | tf_op jit(solution)/shard_map/all_gather | solution.py:1024
  26.2 440.3 %all-gather.19.cloned.1.call-start = ((), (), s32[]{:S(2)}) async-start(), calls=%async_computation.13 | async-start | bytes 1114112 | tf_op jit(solution)/shard_map/all_gather | solution.py:1024
  28.8 82.8 %copy-start.62 = (f32[2,64]{1,0:T(2,128)}, f32[2,64]{1,0:T(2,128)S(1)}, u32[]{:S(2)}) copy-start(f32[2,64]{1,0:T(2,128)S(1)} %compare_convert_fusion.1) | copy-start | bytes 1540
  113.2 121.7 %copy-start.64 = (f32[128]{0:T(128)}, f32[128]{0:T(128)S(1)}, u32[]{:S(2)}) copy-start(f32[128]{0:T(128)S(1)} %compare_convert_fusion.2) | copy-start | bytes 1540
  113.4 60.9 %copy-start.10 = (bf16[128,512]{1,0:T(8,128)(2,1)}, bf16[128,512]{1,0:T(8,128)(2,1)S(1)}, u32[]{:S(2)}) copy-start(bf16[128,512]{1,0:T(8,128)(2,1)S(1)} %get-tuple-element.58) | copy-start | bytes 393220
  113.4 239.4 %copy-start.27 = (bf16[128,512]{1,0:T(8,128)(2,1)}, bf16[128,512]{1,0:T(8,128)(2,1)S(1)}, u32[]{:S(2)}) copy-start(bf16[128,512]{1,0:T(8,128)(2,1)S(1)} %get-tuple-element.107) | copy-start | bytes 393220
  113.4 3.3 collective-permute-start
  114.9 529.2 %reduce-scatter.11.cloned.1.call-start = ((), (), s32[]{:S(2)}) async-start(), calls=%async_computation.15 | async-start | bytes 540672 | tf_op jit(solution)/shard_map/reduce_scatter | solution.py:1158
  116.6 236.2 %copy-start.25 = (bf16[128,512]{1,0:T(8,128)(2,1)}, bf16[128,512]{1,0:T(8,128)(2,1)S(1)}, u32[]{:S(2)}) copy-start(bf16[128,512]{1,0:T(8,128)(2,1)S(1)} %fusion.42) | copy-start | bytes 393220
  116.7 60.4 %copy-start.21 = (bf16[128,512]{1,0:T(8,128)(2,1)}, bf16[128,512]{1,0:T(8,128)(2,1)S(1)}, u32[]{:S(2)}) copy-start(bf16[128,512]{1,0:T(8,128)(2,1)S(1)} %collective-permute-done) | copy-start | bytes 393220
  118.4 58.7 %copy-start.31 = (f32[256,1024]{1,0:T(8,128)}, f32[256,1024]{1,0:T(8,128)S(1)}, u32[]{:S(2)}) copy-start(f32[256,1024]{1,0:T(8,128)S(1)} %fusion.75) | copy-start | bytes 3145732
  177.1 58.0 %copy-start.14 = (bf16[256,1024]{1,0:T(8,128)(2,1)}, bf16[256,1024]{1,0:T(8,128)(2,1)S(1)}, u32[]{:S(2)}) copy-start(bf16[256,1024]{1,0:T(8,128)(2,1)S(1)} %get-tuple-element.110) | copy-start | bytes 1572868
  233.5 1.4 collective-permute-start.1
  235.1 61.1 %copy-start.74 = (f32[128]{0:T(128)}, f32[128]{0:T(128)S(1)}, u32[]{:S(2)}) copy-start(f32[128]{0:T(128)S(1)} %add_rsqrt_fusion.3) | copy-start | bytes 1540
  296.9 14.5 %collective-permute-start.2 = (bf16[2,128,512]{1,2,0:T(8,128)(2,1)S(1)}, bf16[2,128,512]{1,2,0:T(8,128)(2,1)S(1)}, u32[]{:S(2)}, u32[]{:S(2)}) collective-permute-start(bf16[2,128,512]{1,2,0:T(8,128)(2,1)S(1)} %slice.198), channel_id=1, source_target_pairs={{0,4},{1,5},{2,6},{3,7},{4,8},{5,9},{6,10},{7,11},{8,12},{9,13},{1... | collective-permute-start | bytes 786440 | tf_op jit(solution)/shard_map/ppermute | solution.py:869
  300.4 11.1 collective-permute-start.3
  303.8 13.6 %collective-permute-start.4 = (bf16[2,128,512]{1,2,0:T(8,128)(2,1)S(1)}, bf16[2,128,512]{1,2,0:T(8,128)(2,1)S(1)}, u32[]{:S(2)}, u32[]{:S(2)}) collective-permute-start(bf16[2,128,512]{1,2,0:T(8,128)(2,1)S(1)} %slice.198), channel_id=1, source_target_pairs={{0,2},{1,3},{2,4},{3,5},{4,6},{5,7},{6,8},{7,9},{8,10},{9,11},{10,... | collective-permute-start | bytes 786440 | tf_op jit(solution)/shard_map/ppermute | solution.py:869
  307.3 10.1 collective-permute-start.5
  322.7 32.8 %copy-start.43 = (bf16[8,64,128]{2,1,0:T(8,128)(2,1)}, bf16[8,64,128]{2,1,0:T(8,128)(2,1)S(1)}, u32[]{:S(2)}) copy-start(bf16[8,64,128]{2,1,0:T(8,128)(2,1)S(1)} %convolution_convert_fusion.10) | copy-start | bytes 393220
  323.2 86.4 %collective-permute-start.6 = (bf16[128,512]{1,0:T(8,128)(2,1)S(1)}, bf16[128,512]{1,0:T(8,128)(2,1)S(1)}, u32[]{:S(2)}, u32[]{:S(2)}) collective-permute-start(bf16[128,512]{1,0:T(8,128)(2,1)S(1)} %multiply_convert_fusion.7), channel_id=1, source_target_pairs={{0,16},{16,0},{1,17},{17,1},{2,18},{18,2},{3,19},{19,3},{4,20},{20... | collective-permute-start | bytes 393224 | tf_op jit(solution)/shard_map/ppermute | solution.py:863
  409.6 59.6 %copy-start.23 = (bf16[128,512]{1,0:T(8,128)(2,1)}, bf16[128,512]{1,0:T(8,128)(2,1)S(1)}, u32[]{:S(2)}) copy-start(bf16[128,512]{1,0:T(8,128)(2,1)S(1)} %collective-permute-done.6) | copy-start | bytes 393220
  471.6 1.4 collective-permute-start.7
  472.2 1.5 collective-permute-start.14
  488.4 244.0 %reduce-scatter.9.cloned.1.call-start = ((), (), s32[]{:S(2)}) async-start(), calls=%async_computation.14 | async-start | bytes 1622016 | tf_op jit(solution)/shard_map/reduce_scatter | solution.py:1155
  489.7 11.5 collective-permute-start.11
  490.9 18.5 %collective-permute-start.10 = (bf16[2,128,512]{2,1,0:T(8,128)(2,1)}, bf16[2,128,512]{2,1,0:T(8,128)(2,1)}, u32[]{:S(2)}, u32[]{:S(2)}) collective-permute-start(bf16[2,128,512]{2,1,0:T(8,128)(2,1)} %get-tuple-element.69), channel_id=1, source_target_pairs={{2,0},{3,1},{4,2},{5,3},{6,4},{7,5},{8,6},{9,7},{10,8},{11,9},{12,... | collective-permute-start | bytes 786440 | tf_op jit(solution)/shard_map/ppermute | solution.py:869
  492.2 17.2 %collective-permute-start.9 = (bf16[2,128,512]{2,1,0:T(8,128)(2,1)}, bf16[2,128,512]{2,1,0:T(8,128)(2,1)}, u32[]{:S(2)}, u32[]{:S(2)}) collective-permute-start(bf16[2,128,512]{2,1,0:T(8,128)(2,1)} %get-tuple-element.70), channel_id=1, source_target_pairs={{3,0},{4,1},{5,2},{6,3},{7,4},{8,5},{9,6},{10,7},{11,8},{12,9},{13... | collective-permute-start | bytes 786440 | tf_op jit(solution)/shard_map/ppermute | solution.py:869
  493.5 26.9 %collective-permute-start.8 = (bf16[2,128,512]{2,1,0:T(8,128)(2,1)}, bf16[2,128,512]{2,1,0:T(8,128)(2,1)}, u32[]{:S(2)}, u32[]{:S(2)}) collective-permute-start(bf16[2,128,512]{2,1,0:T(8,128)(2,1)} %get-tuple-element.67), channel_id=1, source_target_pairs={{4,0},{5,1},{6,2},{7,3},{8,4},{9,5},{10,6},{11,7},{12,8},{13,9},{1... | collective-permute-start | bytes 786440 | tf_op jit(solution)/shard_map/ppermute | solution.py:869
  497.8 24.7 %copy-start.48 = (bf16[1,128,512]{2,1,0:T(8,128)(2,1)S(1)}, bf16[1,128,512]{2,1,0:T(8,128)(2,1)}, u32[]{:S(2)}) copy-start(bf16[1,128,512]{2,1,0:T(8,128)(2,1)} %copy.86) | copy-start | bytes 393220
  497.8 24.7 %copy-start.75 = (f32[128]{0:T(128)S(1)}, f32[128]{0:T(128)}, u32[]{:S(2)}) copy-start(f32[128]{0:T(128)} %copy-done.74) | copy-start | bytes 1540
  524.4 287.1 %reduce-scatter.15.cloned.1.call-start = ((), (), s32[]{:S(2)}) async-start(), calls=%async_computation.17 | async-start | bytes 1114112 | tf_op jit(solution)/shard_map/reduce_scatter | solution.py:1136
  525.9 361.8 %reduce-scatter.13.cloned.1.call-start = ((), (), s32[]{:S(2)}) async-start(), calls=%async_computation.16 | async-start | bytes 1114112 | tf_op jit(solution)/shard_map/reduce_scatter | solution.py:1136
  529.2 1.3 collective-permute-start.12
  533.0 431.1 %reduce-scatter.19.cloned.1.call-start = ((), (), s32[]{:S(2)}) async-start(), calls=%async_computation.19 | async-start | bytes 1114112 | tf_op jit(solution)/shard_map/reduce_scatter | solution.py:1136
  534.6 505.9 %reduce-scatter.17.cloned.1.call-start = ((), (), s32[]{:S(2)}) async-start(), calls=%async_computation.18 | async-start | bytes 1114112 | tf_op jit(solution)/shard_map/reduce_scatter | solution.py:1136
  536.2 580.8 %reduce-scatter.23.cloned.1.call-start = ((), (), s32[]{:S(2)}) async-start(), calls=%async_computation.21 | async-start | bytes 1114112 | tf_op jit(solution)/shard_map/reduce_scatter | solution.py:1136
  537.8 655.6 %reduce-scatter.21.cloned.1.call-start = ((), (), s32[]{:S(2)}) async-start(), calls=%async_computation.20 | async-start | bytes 1114112 | tf_op jit(solution)/shard_map/reduce_scatter | solution.py:1136
  541.9 2.0 collective-permute-start.13
  544.9 73.3 %copy-start.63 = (f32[2,64]{1,0:T(2,128)S(1)}, f32[2,64]{1,0:T(2,128)}, u32[]{:S(2)}) copy-start(f32[2,64]{1,0:T(2,128)} %copy-done.62) | copy-start | bytes 1540
  544.9 74.6 %copy-start.80 = (f32[128]{0:T(128)S(1)}, f32[128]{0:T(128)}, u32[]{:S(2)}) copy-start(f32[128]{0:T(128)} %rsqrt.44) | copy-start | bytes 1540
  888.6 305.7 %collective-permute-start.15 = (bf16[32,1024]{1,0:T(8,128)(2,1)S(1)}, bf16[32,1024]{1,0:T(8,128)(2,1)S(1)}, u32[]{:S(2)}, u32[]{:S(2)}) collective-permute-start(bf16[32,1024]{1,0:T(8,128)(2,1)S(1)} %broadcast_select_fusion.14), channel_id=1, source_target_pairs={{0,16},{16,0},{1,17},{17,1},{2,18},{18,2},{3,19},{19,3},{4,20},{20... | collective-permute-start | bytes 196616 | tf_op jit(solution)/shard_map/ppermute | solution.py:863
  1041.3 155.8 %collective-permute-start.16 = (bf16[32,1024]{1,0:T(8,128)(2,1)S(1)}, bf16[32,1024]{1,0:T(8,128)(2,1)S(1)}, u32[]{:S(2)}, u32[]{:S(2)}) collective-permute-start(bf16[32,1024]{1,0:T(8,128)(2,1)S(1)} %broadcast_select_fusion.10), channel_id=1, source_target_pairs={{0,16},{16,0},{1,17},{17,1},{2,18},{18,2},{3,19},{19,3},{4,20},{20... | collective-permute-start | bytes 196616 | tf_op jit(solution)/shard_map/ppermute | solution.py:863
  1194.2 5.0 collective-permute-start.17
  (67 other events, 178.9 us)
Sparse Core Ops, SparseCore 0:
  20.9 93.2 all-gather.8
  117.5 56.8 all-gather.10
  177.7 54.0 all-gather.12
  235.0 59.4 all-gather.20
  297.2 55.6 all-gather.14
  355.5 54.0 all-gather.16
  412.3 54.0 all-gather.18
  488.5 138.4 reduce-scatter.10
  633.1 99.1 reduce-scatter.8
  734.6 76.8 reduce-scatter.14
  813.7 73.9 reduce-scatter.12
  890.0 74.1 reduce-scatter.18
  966.4 74.0 reduce-scatter.16
  1042.7 74.2 reduce-scatter.22
  1119.1 74.2 reduce-scatter.20

commit v2 on v1

--- a/solution.py
+++ b/solution.py
@@ -19,7 +19,7 @@
 LANES = 128
 BLOCK = 256
 PIECE = 16
-VMEM_LIMIT = 60 * 1024 * 1024
+VMEM_LIMIT = 63 * 1024 * 1024
 
 
 class Plan:
@@ -41,6 +41,23 @@
         self.routed = map_rows % PIECE == 0
         self.pieces = map_rows // PIECE
         self.f_rows = -(-self.local // 16) * 16
+        self.side = max(1, math.isqrt(chips // 4))
+        self.depth = chips // (self.side * self.side)
+
+    def place(self, chip):
+        return (
+            chip // (self.side * self.side),
+            lax.rem(chip // self.side, self.side),
+            lax.rem(chip, self.side),
+        )
+
+    def chip_at(self, z, y, x):
+        return (z * self.side + y) * self.side + x
+
+    def routes(self, rows):
+        if rows % (2 * PIECE) == 0:
+            return [(0, rows // 2, True), (rows // 2, rows // 2, False)]
+        return [(0, rows, True)]
 
 
 def spot():
@@ -76,6 +93,193 @@
 
 def bytes_of(ref, sem):
     pltpu.make_async_copy(ref, ref, sem).wait()
+
+
+class Gather:
+    def __init__(self, plan, shards, outs, send, recv):
+        self.plan, self.shards, self.outs = plan, shards, outs
+        self.send, self.recv = send, recv
+        self.section, chip = spot()
+        self.z, self.y, self.x = plan.place(chip)
+
+    def to(self, z, y, x):
+        return self.section, self.plan.chip_at(z, y, x)
+
+    def parts(self, i):
+        for number, (start, rows, x_first) in enumerate(self.plan.routes(self.shards[i].shape[0])):
+            out = self.outs[i]
+            sl = pl.ds(start, rows)
+            yield number, x_first, out, sl
+
+    def begin(self):
+        plan = self.plan
+        for i, shard in enumerate(self.shards):
+            spot_ref = self.outs[i].at[self.z, self.y, self.x]
+            for step in range(1, plan.depth):
+                z = lax.rem(self.z + step, plan.depth)
+                push(
+                    shard, spot_ref, self.send.at[i, 0], self.recv.at[i, 0], self.to(z, self.y, self.x)
+                ).start()
+            pltpu.make_async_copy(shard, spot_ref, self.recv.at[i, 0]).start()
+
+    def second(self):
+        side = self.plan.side
+        for i in range(len(self.shards)):
+            bytes_of(self.outs[i].at[:, self.y, self.x], self.recv.at[i, 0])
+            for number, x_first, out, sl in self.parts(i):
+                src = out.at[:, self.y, self.x, sl]
+                for step in range(1, side):
+                    if x_first:
+                        peer = self.to(self.z, self.y, lax.rem(self.x + step, side))
+                    else:
+                        peer = self.to(self.z, lax.rem(self.y + step, side), self.x)
+                    push(
+                        src, src, self.send.at[i, 1 + number], self.recv.at[i, 1 + number], peer
+                    ).start()
+
+    def third(self):
+        side = self.plan.side
+        for i in range(len(self.shards)):
+            for number, x_first, out, sl in self.parts(i):
+                sem = self.recv.at[i, 1 + number]
+                if x_first:
+                    bytes_of(out.at[:, self.y, pl.ds(0, side - 1), sl], sem)
+                    src = out.at[:, self.y, :, sl]
+                else:
+                    bytes_of(out.at[:, pl.ds(0, side - 1), self.x, sl], sem)
+                    src = out.at[:, :, self.x, sl]
+                for step in range(1, side):
+                    if x_first:
+                        peer = self.to(self.z, lax.rem(self.y + step, side), self.x)
+                    else:
+                        peer = self.to(self.z, self.y, lax.rem(self.x + step, side))
+                    push(
+                        src, src, self.send.at[i, 3 + number], self.recv.at[i, 3 + number], peer
+                    ).start()
+
+    def end(self):
+        plan = self.plan
+        side = plan.side
+        for i in range(len(self.shards)):
+            bytes_of(self.outs[i].at[pl.ds(0, plan.depth - 1), 0, 0], self.send.at[i, 0])
+            for number, x_first, out, sl in self.parts(i):
+                bytes_of(out.at[:, 0, pl.ds(0, side - 1), sl], self.send.at[i, 1 + number])
+                last = out.at[:, :, pl.ds(0, side - 1), sl]
+                bytes_of(last, self.recv.at[i, 3 + number])
+                bytes_of(last, self.send.at[i, 3 + number])
+
+
+class Scatter:
+    @staticmethod
+    def scratch(plan, shapes):
+        refs = []
+        for rows, cols in shapes:
+            for _, part, _ in plan.routes(rows):
+                for lead in (
+                    (plan.side - 1, plan.depth, plan.side),
+                    (plan.depth, plan.side),
+                    (plan.side - 1, plan.depth),
+                    (plan.depth,),
+                    (plan.depth - 1,),
+                ):
+                    refs.append(pltpu.VMEM(lead + (part, cols), BF))
+        return refs
+
+    def __init__(self, plan, grads, outs, buffers, send, recv):
+        self.plan, self.grads, self.outs = plan, grads, outs
+        self.send, self.recv = send, recv
+        self.section, chip = spot()
+        self.z, self.y, self.x = plan.place(chip)
+        self.work = []
+        buffers = list(buffers)
+        for i, grad in enumerate(grads):
+            for number, (start, rows, x_first) in enumerate(plan.routes(grad.shape[3])):
+                self.work.append((i, number, start, rows, x_first, buffers[:5]))
+                buffers = buffers[5:]
+
+    def to(self, z, y, x):
+        return self.section, self.plan.chip_at(z, y, x)
+
+    def begin(self):
+        side = self.plan.side
+        for i, number, start, rows, x_first, (land, *_) in self.work:
+            grad, sl = self.grads[i], pl.ds(start, rows)
+            for step in range(1, side):
+                if x_first:
+                    y = lax.rem(self.y + step, side)
+                    src, peer = grad.at[:, y, :, sl], self.to(self.z, y, self.x)
+                else:
+                    x = lax.rem(self.x + step, side)
+                    src, peer = grad.at[:, :, x, sl], self.to(self.z, self.y, x)
+                push(
+                    src, land.at[step - 1], self.send.at[i, number], self.recv.at[i, number], peer
+                ).start()
+
+    def second(self):
+        plan, side = self.plan, self.plan.side
+        for i, number, start, rows, x_first, (land, part, land2, *_) in self.work:
+            grad = self.grads[i]
+            bytes_of(land, self.recv.at[i, number])
+
+            def one(index, carry, grad=grad, land=land, part=part, start=start, rows=rows, x_first=x_first):
+                z, j = index // side, lax.rem(index, side)
+                y, x = (self.y, j) if x_first else (j, self.x)
+                total = grad[z, y, x, start : start + rows, :].astype(F32)
+                for step in range(side - 1):
+                    total = total + land[step, z, j].astype(F32)
+                part[z, j] = total.astype(BF)
+                return carry
+
+            lax.fori_loop(0, plan.depth * side, one, 0)
+            for step in range(1, side):
+                if x_first:
+                    j = lax.rem(self.x + step, side)
+                    peer = self.to(self.z, self.y, j)
+                else:
+                    j = lax.rem(self.y + step, side)
+                    peer = self.to(self.z, j, self.x)
+                push(
+                    part.at[:, j],
+                    land2.at[step - 1],
+                    self.send.at[i, 2 + number],
+                    self.recv.at[i, 2 + number],
+                    peer,
+                ).start()
+
+    def third(self):
+        plan, side = self.plan, self.plan.side
+        for i, number, start, rows, x_first, (_, part, land2, line, land3) in self.work:
+            bytes_of(land2, self.recv.at[i, 2 + number])
+            mine = self.x if x_first else self.y
+
+            def one(z, carry, part=part, land2=land2, line=line, mine=mine):
+                total = part[z, mine].astype(F32)
+                for step in range(side - 1):
+                    total = total + land2[step, z].astype(F32)
+                line[z] = total.astype(BF)
+                return carry
+
+            lax.fori_loop(0, plan.depth, one, 0)
+            for step in range(1, plan.depth):
+                z = lax.rem(self.z + step, plan.depth)
+                push(
+                    line.at[z],
+                    land3.at[step - 1],
+                    self.send.at[i, 4 + number],
+                    self.recv.at[i, 4 + number],
+                    self.to(z, self.y, self.x),
+                ).start()
+
+    def end(self):
+        for i, number, start, rows, x_first, (land, part, land2, line, land3) in self.work:
+            bytes_of(land3, self.recv.at[i, 4 + number])
+            total = line[self.z].astype(F32)
+            for step in range(self.plan.depth - 1):
+                total = total + land3[step].astype(F32)
+            self.outs[i][start : start + rows, :] = total
+            bytes_of(land, self.send.at[i, number])
+            bytes_of(land2, self.send.at[i, 2 + number])
+            bytes_of(land3, self.send.at[i, 4 + number])
 
 
 def entry_kernel(chips, count, *refs):
@@ -266,12 +470,14 @@
 
 
 def forward_kernel(plan, *refs):
+    u_ref, f_ref, *shards = refs[:5]
     if plan.routed:
-        u_ref, f_ref, maps_ref = refs[:3]
-        rest = refs[3:]
+        maps_ref = refs[5]
+        rest = refs[6:]
     else:
-        u_ref, f_ref, mine_ref, other_ref, taps_ref = refs[:5]
-        rest = refs[5:]
+        mine_ref, other_ref, taps_ref = refs[5:8]
+        rest = refs[8:]
+    full_weights, rest = rest[:3], rest[3:]
     (
         conv_ref,
         v_ref,
@@ -308,6 +514,8 @@
         c_recv,
         v_sem,
         out_sem,
+        w_send,
+        w_recv,
     ) = rest
     chips, half, jb, ia = plan.chips, plan.half, plan.jb, plan.ia
     section, chip = spot()
@@ -366,6 +574,8 @@
 
         owner_pieces(plan, start_piece)
 
+    gather = Gather(plan, shards, full_weights, w_send, w_recv)
+    gather.begin()
     bytes_of(f_land, f_recv)
     filter_rows(plan, f_land, table, 0, False)
     build_strips(plan, table, strip, False)
@@ -421,7 +631,10 @@
     taps_out = pltpu.make_async_copy(taps, tapw_ref, out_sem.at[4])
     taps_out.start()
 
+    gather.second()
     for i in range(plan.blocks):
+        if i == plan.blocks // 2:
+            gather.third()
         rows = slice(BLOCK * i, BLOCK * (i + 1))
         depth = BLOCK * (i + 1)
         offset = plan.length - depth
@@ -500,14 +713,16 @@
             total = term if total is None else total + term
         conv_ref[:, :, a * ia : (a + 1) * ia] = total
     bytes_of(land.at[pl.ds(0, chips - 1)], c_send)
-
-
-def forward_call(plan, u, packed, maps):
+    gather.end()
+
+
+def forward_call(plan, u, packed, shards, maps):
     chips, half, jb, ia = plan.chips, plan.half, plan.jb, plan.ia
     any_spec = pl.BlockSpec(memory_space=pl.ANY)
     vmem_spec = pl.BlockSpec(memory_space=pltpu.VMEM)
     dma = pltpu.SemaphoreType.DMA
-    shapes = [
+    grid = (plan.depth, plan.side, plan.side)
+    shapes = [(grid + w.shape, BF) for w in shards] + [
         ((2, half, plan.width), F32),
         ((plan.local, 2, plan.length, 2 * jb), BF),
         ((plan.local, 2 * jb, ia), BF),
@@ -519,8 +734,8 @@
     return pl.pallas_call(
         functools.partial(forward_kernel, plan),
         out_shape=[jax.ShapeDtypeStruct(s, d) for s, d in shapes],
-        in_specs=[vmem_spec] * 2 + [any_spec] * len(maps),
-        out_specs=[vmem_spec] + [any_spec] * 6,
+        in_specs=[vmem_spec] * 2 + [any_spec] * (3 + len(maps)),
+        out_specs=[any_spec] * 3 + [vmem_spec] + [any_spec] * 6,
         scratch_shapes=[
             pltpu.VMEM((plan.length, 2 * jb), BF),
             pltpu.VMEM((plan.length, 2 * jb), BF),
@@ -539,22 +754,28 @@
             pltpu.VMEM((2, 2, BLOCK, 2 * jb), BF),
         ]
         + [dma] * 11
-        + [dma((2,)), dma((5,))],
+        + [dma((2,)), dma((5,)), dma((3, 5)), dma((3, 5))],
         compiler_params=pltpu.CompilerParams(
             collective_id=2, has_side_effects=True, vmem_limit_bytes=VMEM_LIMIT
         ),
         name="spectral_forward",
-    )(u, packed, *maps)
+    )(u, packed, *shards, *maps)
 
 
 def backward_kernel(plan, *refs):
-    g_ref, filt_ref, v_ref, pq, tapw, x_buf, xs_buf, du_ref = refs[:8]
+    g_ref, filt_ref, v_ref, pq, tapw, x_ref, xs_ref = refs[:7]
+    grads = refs[7:10]
+    sums = refs[10:13]
+    du_ref = refs[13]
     if plan.routed:
-        dmaps_ref = refs[8]
-        rest = refs[9:]
+        dmaps_ref = refs[14]
+        rest = refs[15:]
     else:
-        dmap_ref, dtap_ref = refs[8:10]
-        rest = refs[10:]
+        dmap_ref, dtap_ref = refs[14:16]
+        rest = refs[16:]
+    count = 5 * sum(len(plan.routes(grad.shape[3])) for grad in grads)
+    scatter = Scatter(plan, grads, sums, rest[:count], *rest[count : count + 2])
+    rest = rest[count + 2 :]
     (
         g_buf,
         gt_buf,
@@ -586,6 +807,7 @@
         w_recv,
         d_send,
         d_recv,
+        x_sem,
     ) = rest
     chips, half, jb, ia = plan.chips, plan.half, plan.jb, plan.ia
     section, chip = spot()
@@ -616,6 +838,13 @@
     v_copy = [pltpu.make_async_copy(v_ref.at[k], v_buf.at[k], v_sem.at[k]) for k in range(2)]
     for copy in v_copy:
         copy.start()
+    x_copy = [
+        pltpu.make_async_copy(src, dst, x_sem.at[i])
+        for i, (src, dst) in enumerate(((x_ref, z_even), (xs_ref, z_odd)))
+    ]
+    for copy in x_copy:
+        copy.start()
+    scatter.begin()
     filter_rows(plan, filt_ref, table, plan.f_rows, True)
     build_strips(plan, table, strip, True)
     acc_even[...] = jnp.zeros_like(acc_even)
@@ -672,8 +901,10 @@
         if plan.routed:
             piece_copies(k, False, True)
 
-    x_even, x_odd = x_buf[:, :jb], x_buf[:, jb:]
-    s_even, s_odd = xs_buf[:, :jb], xs_buf[:, jb:]
+    for copy in x_copy:
+        copy.wait()
+    x_even, x_odd = z_even[:, :jb], z_even[:, jb:]
+    s_even, s_odd = z_odd[:, :jb], z_odd[:, jb:]
     for tap, (on_even, on_odd) in enumerate(((x_even, x_odd), (s_odd, x_even), (s_even, s_odd))):
         tap_grad = jnp.dot(gt_buf[0], on_even, preferred_element_type=F32) + jnp.dot(
             gt_buf[1], on_odd, preferred_element_type=F32
@@ -740,6 +971,8 @@
         def _():
             finish(k - 1)
 
+        pl.when(k == plan.local // 4)(scatter.second)
+        pl.when(k == plan.local // 2 + 1)(scatter.third)
         return carry
 
     lax.fori_loop(0, plan.local, step, 0)
@@ -788,6 +1021,7 @@
                 total = term if total is None else total + term
         du_ref[:, :, b * jb : (b + 1) * jb] = total
     bytes_of(land.at[pl.ds(0, chips - 1)], d_send)
+    scatter.end()
     if plan.routed:
 
         def drain(k, carry):
@@ -804,12 +1038,14 @@
         bytes_of(dmaps_ref, w_recv)
 
 
-def backward_call(plan, g, filt, v, pq, tapw, x, xs):
+def backward_call(plan, g, filt, v, pq, tapw, x, xs, grads):
     chips, half, jb, ia = plan.chips, plan.half, plan.jb, plan.ia
     any_spec = pl.BlockSpec(memory_space=pl.ANY)
     vmem_spec = pl.BlockSpec(memory_space=pltpu.VMEM)
     dma = pltpu.SemaphoreType.DMA
-    out_shape = [jax.ShapeDtypeStruct((2, half, plan.width), F32)]
+    shapes = [g_part.shape[3:] for g_part in grads]
+    out_shape = [jax.ShapeDtypeStruct(shape, F32) for shape in shapes]
+    out_shape.append(jax.ShapeDtypeStruct((2, half, plan.width), F32))
     if plan.routed:
         out_shape.append(jax.ShapeDtypeStruct((plan.map_rows, plan.width), BF))
     else:
@@ -818,9 +1054,12 @@
     return pl.pallas_call(
         functools.partial(backward_kernel, plan),
         out_shape=out_shape,
-        in_specs=[vmem_spec, vmem_spec, any_spec] + [vmem_spec] * 4,
-        out_specs=[vmem_spec] + [any_spec] * (len(out_shape) - 1),
-        scratch_shapes=[
+        in_specs=[vmem_spec, vmem_spec, any_spec, vmem_spec, vmem_spec, any_spec, any_spec]
+        + [vmem_spec] * 3,
+        out_specs=[vmem_spec] * 4 + [any_spec] * (len(out_shape) - 4),
+        scratch_shapes=Scatter.scratch(plan, shapes)
+        + [dma((3, 6)), dma((3, 6))]
+        + [
             pltpu.VMEM((2, plan.length, ia), BF),
             pltpu.VMEM((2, ia, plan.length), BF),
             pltpu.VMEM((2, plan.f_rows, plan.length + BLOCK), F32),
@@ -851,12 +1090,13 @@
             dma,
             dma,
             dma,
+            dma((2,)),
         ],
         compiler_params=pltpu.CompilerParams(
             collective_id=3, has_side_effects=True, vmem_limit_bytes=VMEM_LIMIT
         ),
         name="spectral_backward",
-    )(g, filt, v, pq, tapw, x, xs)
+    )(g, filt, v, pq, tapw, x, xs, *grads)
 
 
 def swapped(block):
@@ -993,36 +1233,32 @@
             jnp.where(core_zero, pair[1], pair[0]),
             taps.reshape(-1, plan.ia),
         ]
-    conv, v, pq, tapw, x_all, xs_all, filt = forward_call(plan, u_parts, packed, maps)
 
     ff = mlp_gate.shape[2]
     ff_rows = mlp_down.shape[1]
     ff_half = ff_rows // 2
 
-    def my_half(layer, gate, up, down):
-        del layer
+    def my_half(layer):
+        mine = core_zero == (layer == 0)
+        gate, up, down = (
+            jnp.where(mine, own, theirs)
+            for own, theirs in (
+                (mlp_gate[0], sib_gate),
+                (mlp_up[0], sib_up),
+                (mlp_down[0], sib_down),
+            )
+        )
+
         def pick(w):
             w = w.reshape(w.shape[0], chips, 2, ff_half)
             return jnp.where(core_zero, w[:, :, 0], w[:, :, 1]).reshape(w.shape[0], -1)
 
-        return (
-            pick(gate),
-            pick(up),
-            jnp.where(core_zero, down[:ff_half], down[ff_half:]),
-        )
-
-    own_raw = (mlp_gate[0], mlp_up[0], mlp_down[0])
-    sib_raw = (sib_gate, sib_up, sib_down)
-    layers = []
-    for layer in range(2):
-        raw = tuple(
-            jnp.where(core_zero == (layer == 0), mine, theirs)
-            for mine, theirs in zip(own_raw, sib_raw)
-        )
-        shares = my_half(layer, *raw)
-        layers.append(
-            tuple(lax.all_gather(w, "seq", axis=0, tiled=True) for w in shares)
-        )
+        return pick(gate), pick(up), jnp.where(core_zero, down[:ff_half], down[ff_half:])
+
+    results = forward_call(plan, u_parts, packed, my_half(0), maps)
+    layer0 = tuple(w.reshape(-1, w.shape[-1]) for w in results[:3])
+    conv, v, pq, tapw, x_all, xs_all, filt = results[3:]
+    gate1, up1, down1 = my_half(1)
     proj_rows = attn_proj.shape[0]
     out_rows = attn_out.shape[0]
     both_rows = jnp.concatenate(
@@ -1031,19 +1267,32 @@
             jnp.where(core_zero, sib_proj, attn_proj),
             jnp.where(core_zero, attn_out, sib_out),
             jnp.where(core_zero, sib_out, attn_out),
+            down1,
         ],
         0,
     )
-    attn_all = lax.all_gather(both_rows, "seq", axis=0, tiled=False)
+    gate_rows = gate1.shape[0]
+    pieces = [both_rows]
+    for w in (gate1, up1):
+        pieces += [w[:, :width], w[:, width:]]
+    attn_all = lax.all_gather(jnp.concatenate(pieces, 0), "seq", axis=0, tiled=False)
+    at = both_rows.shape[0]
+    columns = [attn_all[:, at + gate_rows * i : at + gate_rows * (i + 1)] for i in range(4)]
+    columns = [c.reshape(-1, width) for c in columns]
+    layer1 = (
+        jnp.concatenate(columns[:2], 1),
+        jnp.concatenate(columns[2:], 1),
+        attn_all[:, at - ff_half : at].reshape(-1, width),
+    )
     w_proj = jnp.swapaxes(
         attn_all[:, : 2 * proj_rows].reshape(chips, 2, proj_rows, width), 0, 1
     ).reshape(3, width, width)
     w_out = jnp.swapaxes(
-        attn_all[:, 2 * proj_rows :].reshape(chips, 2, out_rows, width), 0, 1
+        attn_all[:, 2 * proj_rows : 2 * (proj_rows + out_rows)].reshape(chips, 2, out_rows, width), 0, 1
     ).reshape(width, width)
 
     middle0 = hidden + conv.reshape(tok_rows, width)
-    branch0, saved0 = mlp_forward(middle0, gains[0, 1], layers[0])
+    branch0, saved0 = mlp_forward(middle0, gains[0, 1], layer0)
     passed = (mask_rows * (middle0 + branch0)).astype(BF)
 
     window_hidden = passed.astype(F32)
@@ -1070,14 +1319,14 @@
     attended = dot("hqk,khe->qhe", weights_low, value_window)
     attended = attended.reshape(tok_rows, width).astype(BF)
     middle1 = window_hidden + dot("td,de->te", attended, w_out)
-    branch1, saved1 = mlp_forward(middle1, gains[1, 1], layers[1])
+    branch1, saved1 = mlp_forward(middle1, gains[1, 1], layer1)
     block_out = (mask_rows * (middle1 + branch1)).astype(BF)
 
     upstream1 = cot.astype(F32) * mask_rows
     other_upstream = cot_other.astype(F32) * other_mask
     grad_pair = jnp.concatenate([upstream1, other_upstream], 0).astype(BF)
     middle1_grad, gain11, mlp1_grads = mlp_backward(
-        middle1, gains[1, 1], layers[1], saved1, upstream1, grad_pair
+        middle1, gains[1, 1], layer1, saved1, upstream1, grad_pair
     )
     output_input = middle1_grad.astype(BF)
     output_grad = dot("td,te->de", attended, output_input)
@@ -1105,10 +1354,15 @@
     own_branch = upstream0.astype(BF)
     branch_pair = jnp.concatenate([own_branch, swapped(own_branch)], 0)
     middle0_grad, gain01, mlp0_grads = mlp_backward(
-        middle0, gains[0, 1], layers[0], saved0, upstream0, branch_pair
+        middle0, gains[0, 1], layer0, saved0, upstream0, branch_pair
     )
     g = middle0_grad.astype(BF).reshape(2, half, width)
-    results = backward_call(plan, g, filt, v, pq, tapw, x_all, xs_all)
+    grid = (plan.depth, plan.side, plan.side)
+    blocks0 = [
+        w.astype(BF).reshape(grid + (w.shape[0] // chips, w.shape[1])) for w in mlp0_grads
+    ]
+    results = backward_call(plan, g, filt, v, pq, tapw, x_all, xs_all, blocks0)
+    half0, results = results[:3], results[3:]
     signal_grad = results[0].reshape(tok_rows, width)
     if plan.routed:
         maps_grad = results[1].astype(F32)
@@ -1131,17 +1385,40 @@
     hidden_grad, gain00 = norm_backward(hidden, spectral_factor, gains[0, 0], signal_grad)
     inputs_grad = (mask_rows * (middle0_grad + hidden_grad)).astype(BF)
 
-    def scattered(grads):
-        return [
-            lax.psum_scatter(w.astype(BF), "seq", scatter_dimension=0, tiled=True) for w in grads
-        ]
-
-    halves = [scattered(mlp0_grads), scattered(mlp1_grads)]
+    proj_blocks = jnp.swapaxes(proj_grad.reshape(2, chips, proj_rows, width), 0, 1)
+    out_blocks = jnp.swapaxes(output_grad.reshape(2, chips, out_rows, width), 0, 1)
+    pieces = [
+        proj_blocks.reshape(chips, 2 * proj_rows, width),
+        out_blocks.reshape(chips, 2 * out_rows, width),
+        mlp1_grads[2].reshape(chips, ff_half, width),
+    ]
+    for w in mlp1_grads[:2]:
+        w = w.reshape(chips, gate_rows, 2 * width)
+        pieces += [w[:, :, :width], w[:, :, width:]]
+    packed_grads = jnp.concatenate([p.astype(BF) for p in pieces], 1)
+    summed = lax.psum_scatter(packed_grads, "seq", scatter_dimension=0, tiled=False)
+    columns = [summed[at + gate_rows * i : at + gate_rows * (i + 1)] for i in range(4)]
+    half1 = [
+        jnp.concatenate(columns[:2], 1),
+        jnp.concatenate(columns[2:], 1),
+        summed[at - ff_half : at],
+    ]
+    attn_parts = summed[: 2 * (proj_rows + out_rows)]
+    low_part = jnp.concatenate(
+        [attn_parts[:proj_rows], attn_parts[2 * proj_rows : 2 * proj_rows + out_rows]], 0
+    )
+    high_part = jnp.concatenate(
+        [attn_parts[proj_rows : 2 * proj_rows], attn_parts[2 * proj_rows + out_rows :]], 0
+    )
+    attn_keep = jnp.where(core_zero, low_part, high_part).astype(F32)
+    attn_take = swapped(jnp.where(core_zero, high_part, low_part)).astype(F32)
+    attn_sum = attn_keep + attn_take
+    proj_out, out_out = attn_sum[:proj_rows], attn_sum[proj_rows:]
     outs = []
     for index in range(3):
-        keep = jnp.where(core_zero, halves[0][index], halves[1][index])
-        give = jnp.where(core_zero, halves[1][index], halves[0][index])
-        take = swapped(give)
+        zero, one = half0[index].astype(BF), half1[index]
+        keep = jnp.where(core_zero, zero, one)
+        take = swapped(jnp.where(core_zero, one, zero))
         low = jnp.where(core_zero, keep, take).astype(F32)
         high = jnp.where(core_zero, take, keep).astype(F32)
         if index < 2:
@@ -1152,12 +1429,6 @@
         else:
             joined = jnp.concatenate([low, high], 0)
         outs.append(joined[None])
-    proj_out = lax.psum_scatter(
-        proj_grad.astype(BF), ("section", "seq"), scatter_dimension=0, tiled=True
-    ).astype(F32)
-    out_out = lax.psum_scatter(
-        output_grad.astype(BF), ("section", "seq"), scatter_dimension=0, tiled=True
-    ).astype(F32)
 
     gain_parts = jnp.stack([jnp.stack([gain00, gain01]), jnp.stack([gain10, gain11])])
     gain_cols = width // chips

time: 1210 us -> 507 us (0.42)
  waiting for transfers between devices: 884 us -> 27.3 us
  Pallas kernels: 182 us -> 310 us
  starting transfers between devices: 20.3 us -> 41.2 us
    reduce_scatter x8 -> x1, waiting for transfers between devices: 545 us -> 0.01 us  [body(): lax.psum_scatter(packed_grads, 'seq', scatter_dimension=0, tiled=False)]
    all_gather x7 -> x1, waiting for transfers between devices: 308 us -> 7.18 us  [body(): lax.all_gather(jnp.concatenate(pieces, 0), 'seq', axis=0, tiled=False)]
    pallas_call x1, Pallas kernels: 73.3 us -> 160 us  [backward_call(): pl.pallas_call(functools.partial(backward_kernel, plan), out_shape=out_sh...]
    pallas_call x1, Pallas kernels: 80.3 us -> 124 us  [forward_call(): pl.pallas_call(functools.partial(forward_kernel, plan), out_shape=[jax.Sh...]
    ppermute x8, starting transfers between devices: 18.2 us -> 38.1 us  [shifted(): return lax.ppermute(block, axis, route)]
  transfers between devices with their start and end apart: 33 -> 21, of which waited for: 20 -> 8; matrix products, arithmetic and copies ran while one was open for 6% -> 10% of each run, Pallas kernels for 14% -> 60%
where the time goes in v2:
time: 507 us; the launch traced here: 498 us
  Pallas kernels  310 us (61%)
  local copies, waits for them, and re-layouts  41.6 us (8%)
  starting transfers between devices  41.2 us (8%)
  matrix products  33.8 us (7%)
  waiting for transfers between devices  27.3 us (5%)
  other arithmetic  25.4 us (5%)
  between operations  18.7 us (4%)
    pallas_call x1, Pallas kernels, backward_call(): pl.pallas_call(functools.partial(backward_kernel, plan), out_shape=out_sh...  160 us
    pallas_call x1, Pallas kernels, forward_call(): pl.pallas_call(functools.partial(forward_kernel, plan), out_shape=[jax.Sh...  124 us
    ppermute x8, starting transfers between devices, shifted(): return lax.ppermute(block, axis, route)  38.1 us
    dot_general x29, matrix products, dot(): return jnp.einsum(formula, left, right, preferred_element_type=F32)  31.3 us
    ppermute x8, waiting for transfers between devices, shifted(): return lax.ppermute(block, axis, route)  18.2 us
    pallas_call x1, Pallas kernels, exit_call(): pl.pallas_call(functools.partial(exit_kernel, chips), out_shape=[jax.Shap...  15.5 us
    unnamed x174, local copies, waits for them, and re-layouts  11.5 us
    pallas_call x1, Pallas kernels, entry_call(): pl.pallas_call(functools.partial(entry_kernel, chips, count), out_shape=[...  10.9 us
  transfers between devices with their start and end apart: 21, of which 8 were waited for; matrix products, arithmetic and copies ran while one was open for 10% of the time, Pallas kernels for 60%

profile of v2, /device:TPU:0, one launch (start us, length us, event | category | flops | bytes accessed | tf_op | source)
XLA Modules:
  0.0 498.2 jit_solution(11528407625725509854)
XLA Ops:
  7.2 10.9 %entry.1 = (bf16[2,128,512]{2,1,0:T(8,128)(2,1)}, bf16[32,2048]{1,0:T(8,128)(2,1)}, bf16[32,2048]{1,0:T(8,128)(2,1)}, bf16[128,512]{1,0:T(8,128)(2,1)}, bf16[48,...) custom-call(bf16[2,128,512]{2,1,0:T(8,128)(2,1)} %bitcast.278, ...), custom_call_target="tpu_custom_call" | custom-call | tf_op jit(solution)/shard_map/entry/pallas_call | solution.py:329
  19.2 1.1 broadcast_select_fusion.4
  32.5 123.9 %spectral_forward.1 = (bf16[4,2,2,32,1024]{4,3,2,1,0:T(8,128)(2,1)}, bf16[4,2,2,32,1024]{4,3,2,1,0:T(8,128)(2,1)}, bf16[4,2,2,64,512]{4,3,2,1,0:T(8,128)(2,1)}, ...) custom-call(bf16[4,64,256]{2,1,0:T(8,128)(2,1)} %reshape.469.refs_0_, ...), custom_call_target="tpu_custom_call" | custom-call | tf_op jit(solution)/shard_map/spectral_forward/pallas_call | solution.py:734
  156.4 1.2 multiply_reduce_fusion.8
  157.7 1.7 multiply_convert_fusion.8
  162.7 1.5 multiply_convert_fusion.6
  166.9 7.2 %all-gather.3.cloned.1.call-done = bf16[5120,512]{1,0:T(8,128)(2,1)} async-done(((bf16[320,512]{1,0:T(8,128)(2,1)}), bf16[5120,512]{1,0:T(8,128)(2,1)}) %all-gather.3.cloned.1.call-update) | async-done | bytes 5242896 | tf_op jit(solution)/shard_map/all_gather | solution.py:1278
  174.0 1.5 slice.348
  175.7 1.1 copy-done.2
  177.5 15.3 %collective-permute-start.4 = (bf16[2,128,512]{1,2,0:T(8,128)(2,1)S(1)}, bf16[2,128,512]{1,2,0:T(8,128)(2,1)S(1)}, u32[]{:S(2)}, u32[]{:S(2)}) collective-permute-start(bf16[2,128,512]{1,2,0:T(8,128)(2,1)S(1)} %slice.350), channel_id=1, source_target_pairs={{0,2},{1,3},{2,4},{3,5},{4,6},{5,7},{6,8},{7,9},{8,10},{9,11},{10,... | collective-permute-start | bytes 786440 | tf_op jit(solution)/shard_map/ppermute | solution.py:1109
  192.8 7.8 %collective-permute-start.3 = (bf16[2,128,512]{1,2,0:T(8,128)(2,1)S(1)}, bf16[2,128,512]{1,2,0:T(8,128)(2,1)S(1)}, u32[]{:S(2)}, u32[]{:S(2)}) collective-permute-start(bf16[2,128,512]{1,2,0:T(8,128)(2,1)S(1)} %slice.350), channel_id=1, source_target_pairs={{0,3},{1,4},{2,5},{3,6},{4,7},{5,8},{6,9},{7,10},{8,11},{9,12},{10... | collective-permute-start | bytes 786440 | tf_op jit(solution)/shard_map/ppermute | solution.py:1109
  200.6 7.2 %collective-permute-start.2 = (bf16[2,128,512]{1,2,0:T(8,128)(2,1)S(1)}, bf16[2,128,512]{1,2,0:T(8,128)(2,1)S(1)}, u32[]{:S(2)}, u32[]{:S(2)}) collective-permute-start(bf16[2,128,512]{1,2,0:T(8,128)(2,1)S(1)} %slice.350), channel_id=1, source_target_pairs={{0,4},{1,5},{2,6},{3,7},{4,8},{5,9},{6,10},{7,11},{8,12},{9,13},{1... | collective-permute-start | bytes 786440 | tf_op jit(solution)/shard_map/ppermute | solution.py:1109
  207.8 1.4 fusion.87
  209.3 2.5 collective-permute-start.5
  211.9 1.5 collective-permute-done.2
  213.6 3.7 collective-permute-done.5
  218.4 2.5 fusion.96
  221.0 2.7 convolution_convert_fusion.10
  227.6 1.4 convolution_convert_fusion.3
  230.6 1.5 convolution_convert_fusion.1
  232.1 1.5 convolution_convert_fusion.2
  235.5 2.3 fusion.12
  238.1 2.7 multiply_reduce_fusion
  242.4 3.0 multiply_convert_fusion
  245.5 1.5 convolution_multiply_fusion
  246.9 1.7 copy.96
  249.9 1.3 collective-permute-start.8
  251.2 1.3 collective-permute-start.11
  252.5 1.3 collective-permute-start.10
  253.8 1.5 collective-permute-start.9
  255.3 1.3 fusion.8
  256.6 1.7 copy.98
  258.2 7.1 %collective-permute-done.8 = bf16[2,128,512]{2,1,0:T(8,128)(2,1)} collective-permute-done((bf16[2,128,512]{2,1,0:T(8,128)(2,1)}, bf16[2,128,512]{2,1,0:T(8,128)(2,1)}, u32[]{:S(2)}, u32[]{:S(2)}) %collective-permute-start.8) | collective-permute-done | bytes 262176 | tf_op jit(solution)/shard_map/ppermute | solution.py:1109
  265.3 5.8 %collective-permute-done.10 = bf16[2,128,512]{2,1,0:T(8,128)(2,1)} collective-permute-done((bf16[2,128,512]{2,1,0:T(8,128)(2,1)}, bf16[2,128,512]{2,1,0:T(8,128)(2,1)}, u32[]{:S(2)}, u32[]{:S(2)}) %collective-permute-start.10) | collective-permute-done | bytes 262176 | tf_op jit(solution)/shard_map/ppermute | solution.py:1109
  271.2 1.4 fusion.20
  273.4 1.3 constant_dynamic-update-slice_fusion.13
  280.2 1.4 copy-done.3
  284.8 2.6 multiply_convert_fusion.2
  289.8 1.5 convolution_convert_fusion.4
  291.2 1.5 convolution_convert_fusion.5
  292.7 1.4 convolution_convert_fusion.6
  295.2 159.8 %spectral_backward.1 = (f32[32,1024]{1,0:T(8,128)}, f32[32,1024]{1,0:T(8,128)}, f32[64,512]{1,0:T(8,128)}, f32[2,64,512]{2,1,0:T(8,128)}, bf16[816,512]{1,0:T(8,128)(2,1)}) custom-call(bf16[2,64,512]{2,1,0:T(8,128)(2,1)} %bitcast.288, bf16[16,32,128]{2,1,0:T(8,128)(2,1)} %get-tuple-element.43.refs_1_, bf16[12,2,1024,256]{3,2,1,0:T(8,128)(2,1)} %get-tuple-element.44.refs_2_, ...), custom_call_target="tpu_custom_call" | custom-call | tf_op jit(solution)/shard_map/spectral_backward/pallas_call | solution.py:1054
  455.1 1.3 multiply_reduce_fusion.3
  456.4 1.1 fusion.45
  459.3 15.5 %leave.1 = (bf16[128,512]{1,0:T(8,128)(2,1)}, f32[32,8,128]{2,1,0:T(8,128)}) custom-call(bf16[128,512]{1,0:T(8,128)(2,1)} %broadcast_select_fusion.6.give, f32[32,8,128]{2,1,0:T(8,128)} %pad.9.tiles), custom_call_target="tpu_custom_call" | custom-call | tf_op jit(solution)/shard_map/leave/pallas_call | solution.py:373
  475.8 1.4 convert_element_type.320
  486.4 1.2 reshape.510
  488.1 1.2 reshape.511
  (352 shorter events, 55.4 us)
Async XLA Ops:
  7.2 166.9 %all-gather.3.cloned.1.call-start = ((), (), s32[]{:S(2)}) async-start(), calls=%async_computation.2 | async-start | bytes 5570560 | tf_op jit(solution)/shard_map/all_gather | solution.py:1278
  21.4 3.5 copy-start.64
  21.4 3.6 copy-start.30
  23.6 454.9 %reduce-scatter.2.cloned.1.call-start = ((), (), s32[]{:S(2)}) async-start(), calls=%async_computation.1 | async-start | bytes 5570560 | tf_op jit(solution)/shard_map/reduce_scatter | solution.py:1399
  27.0 129.4 %copy-start.58 = (f32[2,64]{1,0:T(2,128)}, f32[2,64]{1,0:T(2,128)S(1)}, u32[]{:S(2)}) copy-start(f32[2,64]{1,0:T(2,128)S(1)} %compare_convert_fusion.1) | copy-start | bytes 1540
  29.6 128.2 %copy-start.13 = (f32[2,64,512]{2,1,0:T(8,128)}, f32[2,64,512]{2,1,0:T(8,128)S(1)}, u32[]{:S(2)}) copy-start(f32[2,64,512]{2,1,0:T(8,128)S(1)} %copy.74) | copy-start | bytes 786436
  156.4 5.9 %copy-start.8 = (bf16[4,2,2,32,1024]{4,3,2,1,0:T(8,128)(2,1)S(1)}, bf16[4,2,2,32,1024]{4,3,2,1,0:T(8,128)(2,1)}, u32[]{:S(2)}) copy-start(bf16[4,2,2,32,1024]{4,3,2,1,0:T(8,128)(2,1)} %get-tuple-element.38) | copy-start | bytes 3145732
  157.7 4.2 copy-start.70
  157.7 8.9 %copy-start.60 = (f32[128]{0:T(128)}, f32[128]{0:T(128)S(1)}, u32[]{:S(2)}) copy-start(f32[128]{0:T(128)S(1)} %compare_convert_fusion.2) | copy-start | bytes 1540
  159.4 2.8 collective-permute-start
  165.2 1.5 collective-permute-start.1
  166.8 8.9 %copy-start.72 = (f32[128]{0:T(128)}, f32[128]{0:T(128)S(1)}, u32[]{:S(2)}) copy-start(f32[128]{0:T(128)S(1)} %add_rsqrt_fusion.3) | copy-start | bytes 1540
  175.6 32.3 %copy-start.4 = (bf16[5120,512]{1,0:T(8,128)(2,1)S(1)}, bf16[5120,512]{1,0:T(8,128)(2,1)}, u32[]{:S(2)}) copy-start(bf16[5120,512]{1,0:T(8,128)(2,1)} %all-gather.3.cloned.1.call-done) | copy-start | bytes 15728644
  177.5 36.0 %collective-permute-start.4 = (bf16[2,128,512]{1,2,0:T(8,128)(2,1)S(1)}, bf16[2,128,512]{1,2,0:T(8,128)(2,1)S(1)}, u32[]{:S(2)}, u32[]{:S(2)}) collective-permute-start(bf16[2,128,512]{1,2,0:T(8,128)(2,1)S(1)} %slice.350), channel_id=1, source_target_pairs={{0,2},{1,3},{2,4},{3,5},{4,6},{5,7},{6,8},{7,9},{8,10},{9,11},{10,... | collective-permute-start | bytes 786440 | tf_op jit(solution)/shard_map/ppermute | solution.py:1109
  192.8 20.7 %collective-permute-start.3 = (bf16[2,128,512]{1,2,0:T(8,128)(2,1)S(1)}, bf16[2,128,512]{1,2,0:T(8,128)(2,1)S(1)}, u32[]{:S(2)}, u32[]{:S(2)}) collective-permute-start(bf16[2,128,512]{1,2,0:T(8,128)(2,1)S(1)} %slice.350), channel_id=1, source_target_pairs={{0,3},{1,4},{2,5},{3,6},{4,7},{5,8},{6,9},{7,10},{8,11},{9,12},{10... | collective-permute-start | bytes 786440 | tf_op jit(solution)/shard_map/ppermute | solution.py:1109
  200.6 12.8 %collective-permute-start.2 = (bf16[2,128,512]{1,2,0:T(8,128)(2,1)S(1)}, bf16[2,128,512]{1,2,0:T(8,128)(2,1)S(1)}, u32[]{:S(2)}, u32[]{:S(2)}) collective-permute-start(bf16[2,128,512]{1,2,0:T(8,128)(2,1)S(1)} %slice.350), channel_id=1, source_target_pairs={{0,4},{1,5},{2,6},{3,7},{4,8},{5,9},{6,10},{7,11},{8,12},{9,13},{1... | collective-permute-start | bytes 786440 | tf_op jit(solution)/shard_map/ppermute | solution.py:1109
  209.3 9.1 %copy-start.44 = (bf16[1,128,512]{1,2,0:T(8,128)(2,1)}, bf16[1,128,512]{1,2,0:T(8,128)(2,1)S(1)}, u32[]{:S(2)}) copy-start(bf16[1,128,512]{1,2,0:T(8,128)(2,1)S(1)} %slice.352) | copy-start | bytes 393220
  209.3 8.0 %collective-permute-start.5 = (bf16[2,128,512]{1,2,0:T(8,128)(2,1)S(1)}, bf16[2,128,512]{1,2,0:T(8,128)(2,1)S(1)}, u32[]{:S(2)}, u32[]{:S(2)}) collective-permute-start(bf16[2,128,512]{1,2,0:T(8,128)(2,1)S(1)} %slice.350), channel_id=1, source_target_pairs={{0,1},{1,2},{2,3},{3,4},{4,5},{5,6},{6,7},{7,8},{8,9},{9,10},{10,1... | collective-permute-start | bytes 786440 | tf_op jit(solution)/shard_map/ppermute | solution.py:1109
  213.5 4.9 copy-start.55
  221.0 3.6 copy-start.21
  224.4 1.4 collective-permute-start.6
  230.1 4.2 copy-start.14
  230.1 4.2 copy-start.61
  230.1 4.1 collective-permute-start.14
  230.3 3.3 collective-permute-start.7
  248.7 6.6 %copy-start.1 = (bf16[8,128,640]{2,1,0:T(8,128)(2,1)S(1)}, bf16[8,128,640]{2,1,0:T(8,128)(2,1)}, u32[]{:S(2)}) copy-start(bf16[8,128,640]{2,1,0:T(8,128)(2,1)} %copy-done) | copy-start | bytes 3932164
  248.7 6.6 %copy-start.12 = (bf16[1,640,512]{1,2,0:T(8,128)(2,1)S(1)}, bf16[1,640,512]{1,2,0:T(8,128)(2,1)}, u32[]{:S(2)}) copy-start(bf16[1,640,512]{1,2,0:T(8,128)(2,1)} %copy-done.11) | copy-start | bytes 1966084
  249.9 15.5 %collective-permute-start.8 = (bf16[2,128,512]{2,1,0:T(8,128)(2,1)}, bf16[2,128,512]{2,1,0:T(8,128)(2,1)}, u32[]{:S(2)}, u32[]{:S(2)}) collective-permute-start(bf16[2,128,512]{2,1,0:T(8,128)(2,1)} %get-tuple-element.84), channel_id=1, source_target_pairs={{4,0},{5,1},{6,2},{7,3},{8,4},{9,5},{10,6},{11,7},{12,8},{13,9},{1... | collective-permute-start | bytes 786440 | tf_op jit(solution)/shard_map/ppermute | solution.py:1109
  251.2 14.2 %collective-permute-start.11 = (bf16[2,128,512]{2,1,0:T(8,128)(2,1)}, bf16[2,128,512]{2,1,0:T(8,128)(2,1)}, u32[]{:S(2)}, u32[]{:S(2)}) collective-permute-start(bf16[2,128,512]{2,1,0:T(8,128)(2,1)} %get-tuple-element.85), channel_id=1, source_target_pairs={{1,0},{2,1},{3,2},{4,3},{5,4},{6,5},{7,6},{8,7},{9,8},{10,9},{11,1... | collective-permute-start | bytes 786440 | tf_op jit(solution)/shard_map/ppermute | solution.py:1109
  252.5 18.7 %collective-permute-start.10 = (bf16[2,128,512]{2,1,0:T(8,128)(2,1)}, bf16[2,128,512]{2,1,0:T(8,128)(2,1)}, u32[]{:S(2)}, u32[]{:S(2)}) collective-permute-start(bf16[2,128,512]{2,1,0:T(8,128)(2,1)} %get-tuple-element.86), channel_id=1, source_target_pairs={{2,0},{3,1},{4,2},{5,3},{6,4},{7,5},{8,6},{9,7},{10,8},{11,9},{12,... | collective-permute-start | bytes 786440 | tf_op jit(solution)/shard_map/ppermute | solution.py:1109
  253.8 17.4 %collective-permute-start.9 = (bf16[2,128,512]{2,1,0:T(8,128)(2,1)}, bf16[2,128,512]{2,1,0:T(8,128)(2,1)}, u32[]{:S(2)}, u32[]{:S(2)}) collective-permute-start(bf16[2,128,512]{2,1,0:T(8,128)(2,1)} %get-tuple-element.87), channel_id=1, source_target_pairs={{3,0},{4,1},{5,2},{6,3},{7,4},{8,5},{9,6},{10,7},{11,8},{12,9},{13... | collective-permute-start | bytes 786440 | tf_op jit(solution)/shard_map/ppermute | solution.py:1109
  256.6 16.0 %copy-start.73 = (f32[128]{0:T(128)S(1)}, f32[128]{0:T(128)}, u32[]{:S(2)}) copy-start(f32[128]{0:T(128)} %copy-done.72) | copy-start | bytes 1540
  258.2 14.3 %copy-start.46 = (bf16[1,128,512]{2,1,0:T(8,128)(2,1)S(1)}, bf16[1,128,512]{2,1,0:T(8,128)(2,1)}, u32[]{:S(2)}) copy-start(bf16[1,128,512]{2,1,0:T(8,128)(2,1)} %copy.98) | copy-start | bytes 393220
  283.2 4.2 copy-start.31
  283.2 1.6 collective-permute-start.12
  289.2 4.9 collective-permute-start.13
  295.2 159.9 %copy-start.59 = (f32[2,64]{1,0:T(2,128)S(1)}, f32[2,64]{1,0:T(2,128)}, u32[]{:S(2)}) copy-start(f32[2,64]{1,0:T(2,128)} %copy-done.58) | copy-start | bytes 1540
  295.2 159.9 %copy-start.67 = (f32[2,64]{1,0:T(2,128)S(1)}, f32[2,64]{1,0:T(2,128)}, u32[]{:S(2)}) copy-start(f32[2,64]{1,0:T(2,128)} %copy-done.65) | copy-start | bytes 1540
  295.2 161.2 %copy-start.79 = (f32[128]{0:T(128)S(1)}, f32[128]{0:T(128)}, u32[]{:S(2)}) copy-start(f32[128]{0:T(128)} %rsqrt.44) | copy-start | bytes 1540
  295.2 162.6 %copy-start.57 = (f32[1,1,16,32]{3,1,2,0:T(1,128)S(1)}, f32[1,1,16,32]{3,1,2,0:T(1,128)}, u32[]{:S(2)}) copy-start(f32[1,1,16,32]{3,1,2,0:T(1,128)} %stack.59) | copy-start | bytes 6148
  455.1 20.7 %copy-start.28 = (bf16[816,512]{1,0:T(8,128)(2,1)S(1)}, bf16[816,512]{1,0:T(8,128)(2,1)}, u32[]{:S(2)}) copy-start(bf16[816,512]{1,0:T(8,128)(2,1)} %get-tuple-element.51) | copy-start | bytes 2506756
  459.3 19.2 %copy-start.37 = (f32[64,512]{1,0:T(8,128)S(1)}, f32[64,512]{1,0:T(8,128)}, u32[]{:S(2)}) copy-start(f32[64,512]{1,0:T(8,128)} %get-tuple-element.55) | copy-start | bytes 393220
  475.7 4.5 copy-start.39
  475.8 5.1 %copy-start.38 = (f32[32,1024]{1,0:T(8,128)S(1)}, f32[32,1024]{1,0:T(8,128)}, u32[]{:S(2)}) copy-start(f32[32,1024]{1,0:T(8,128)} %get-tuple-element.54) | copy-start | bytes 393220
  479.3 9.9 %collective-permute-start.18 = (bf16[64,512]{1,0:T(8,128)(2,1)S(1)}, bf16[64,512]{1,0:T(8,128)(2,1)S(1)}, u32[]{:S(2)}, u32[]{:S(2)}) collective-permute-start(bf16[64,512]{1,0:T(8,128)(2,1)S(1)} %broadcast_select_fusion.18), channel_id=1, source_target_pairs={{0,16},{16,0},{1,17},{17,1},{2,18},{18,2},{3,19},{19,3},{4,20},{20... | collective-permute-start | bytes 196616 | tf_op jit(solution)/shard_map/ppermute | solution.py:1103
  480.3 2.8 collective-permute-start.16
  480.9 4.6 collective-permute-start.17
  482.5 1.5 collective-permute-start.15
  (53 other events, 108.7 us)
Sparse Core Ops, SparseCore 0:
  23.7 150.2 all-gather.2
  280.3 196.0 reduce-scatter.1

commit v3 on v2

--- a/solution.py
+++ b/solution.py
@@ -23,7 +23,7 @@
 
 
 class Plan:
-    def __init__(self, chips, tok_rows, width, filter_count, map_rows):
+    def __init__(self, chips, tok_rows, width, filter_count, map_rows, ff):
         self.chips = chips
         self.rows = tok_rows
         self.half = tok_rows // 2
@@ -41,6 +41,8 @@
         self.routed = map_rows % PIECE == 0
         self.pieces = map_rows // PIECE
         self.f_rows = -(-self.local // 16) * 16
+        self.ff = ff
+        self.pick_here = ff // chips == LANES
         self.side = max(1, math.isqrt(chips // 4))
         self.depth = chips // (self.side * self.side)
 
@@ -54,10 +56,10 @@
     def chip_at(self, z, y, x):
         return (z * self.side + y) * self.side + x
 
-    def routes(self, rows):
+    def routes(self, rows, index=0):
         if rows % (2 * PIECE) == 0:
             return [(0, rows // 2, True), (rows // 2, rows // 2, False)]
-        return [(0, rows, True)]
+        return [(0, rows, index % 2 == 0)]
 
 
 def spot():
@@ -77,7 +79,11 @@
         return carry
 
     lax.fori_loop(1, 2 * chips, one, 0)
-    pl.semaphore_wait(barrier, 2 * chips - 1)
+
+    def wait():
+        pl.semaphore_wait(barrier, 2 * chips - 1)
+
+    return wait
 
 
 def push(src, dst, send, recv, target):
@@ -95,6 +101,18 @@
     pltpu.make_async_copy(ref, ref, sem).wait()
 
 
+def rows_dot(left, right):
+    return lax.dot_general(left, right, (((1,), (1,)), ((), ())), preferred_element_type=F32)
+
+
+def cols_dot(left, right):
+    return lax.dot_general(left, right, (((0,), (0,)), ((), ())), preferred_element_type=F32)
+
+
+def flat_dot(left, right):
+    return jnp.dot(left, right, preferred_element_type=F32)
+
+
 class Gather:
     def __init__(self, plan, shards, outs, send, recv):
         self.plan, self.shards, self.outs = plan, shards, outs
@@ -106,7 +124,7 @@
         return self.section, self.plan.chip_at(z, y, x)
 
     def parts(self, i):
-        for number, (start, rows, x_first) in enumerate(self.plan.routes(self.shards[i].shape[0])):
+        for number, (start, rows, x_first) in enumerate(self.plan.routes(self.shards[i].shape[0], i)):
             out = self.outs[i]
             sl = pl.ds(start, rows)
             yield number, x_first, out, sl
@@ -173,8 +191,8 @@
     @staticmethod
     def scratch(plan, shapes):
         refs = []
-        for rows, cols in shapes:
-            for _, part, _ in plan.routes(rows):
+        for index, (rows, cols) in enumerate(shapes):
+            for _, part, _ in plan.routes(rows, index):
                 for lead in (
                     (plan.side - 1, plan.depth, plan.side),
                     (plan.depth, plan.side),
@@ -193,7 +211,7 @@
         self.work = []
         buffers = list(buffers)
         for i, grad in enumerate(grads):
-            for number, (start, rows, x_first) in enumerate(plan.routes(grad.shape[3])):
+            for number, (start, rows, x_first) in enumerate(plan.routes(grad.shape[3], i)):
                 self.work.append((i, number, start, rows, x_first, buffers[:5]))
                 buffers = buffers[5:]
 
@@ -282,71 +300,10 @@
             bytes_of(land3, self.send.at[i, 4 + number])
 
 
-def entry_kernel(chips, count, *refs):
-    given = refs[:count]
-    gains = refs[count]
-    taken = refs[count + 1 : 2 * count + 1]
-    gains_all = refs[2 * count + 1]
-    send, recv, gain_send, gain_recv = refs[2 * count + 2 :]
-    section, chip = spot()
-    me = section * chips + chip
-    greet_everyone(chips)
-    copies = [
-        push(given[i], taken[i], send.at[i], recv.at[i], (1 - section, chip)) for i in range(count)
-    ]
-    for copy in copies[:1]:
-        copy.start()
-
-    def one(step, carry):
-        peer = lax.rem(me + step, 2 * chips)
-        push(
-            gains,
-            gains_all.at[section, chip],
-            gain_send,
-            gain_recv,
-            (peer // chips, lax.rem(peer, chips)),
-        ).start()
-        return carry
-
-    lax.fori_loop(1, 2 * chips, one, 0)
-    pltpu.make_async_copy(gains, gains_all.at[section, chip], gain_recv).start()
-    for copy in copies[1:]:
-        copy.start()
-    bytes_of(gains_all, gain_recv)
-
-    def drain(step, carry):
-        push(gains, gains_all.at[section, chip], gain_send, gain_recv, (section, chip)).wait_send()
-        return carry
-
-    lax.fori_loop(1, 2 * chips, drain, 0)
-    for copy in copies:
-        copy.wait()
-
-
-def entry_call(chips, arrays, gains):
-    count = len(arrays)
-    any_spec = pl.BlockSpec(memory_space=pl.ANY)
-    return pl.pallas_call(
-        functools.partial(entry_kernel, chips, count),
-        out_shape=[jax.ShapeDtypeStruct(a.shape, a.dtype) for a in arrays]
-        + [jax.ShapeDtypeStruct((2, chips) + gains.shape, gains.dtype)],
-        in_specs=[any_spec] * (count + 1),
-        out_specs=[any_spec] * (count + 1),
-        scratch_shapes=[
-            pltpu.SemaphoreType.DMA((count,)),
-            pltpu.SemaphoreType.DMA((count,)),
-            pltpu.SemaphoreType.DMA,
-            pltpu.SemaphoreType.DMA,
-        ],
-        compiler_params=pltpu.CompilerParams(collective_id=1, has_side_effects=True),
-        name="entry",
-    )(*arrays, gains)
-
-
 def exit_kernel(chips, give, tiles, take, land, send, recv, gain_send, gain_recv):
     section, chip = spot()
     me = section * chips + chip
-    greet_everyone(chips)
+    greet_everyone(chips)()
     swap = push(give, take, send, recv, (1 - section, chip))
     swap.start()
 
@@ -435,7 +392,7 @@
     lax.fori_loop(0, plan.local, one, 0)
 
 
-def owner_pieces(plan, act):
+def owner_pieces(plan, act, first=0, last=None):
     section, chip = spot()
     dev = section * plan.chips + chip
     per_map = plan.width // PIECE
@@ -466,26 +423,45 @@
 
         return carry
 
-    lax.fori_loop(0, plan.pieces, unit, 0)
+    lax.fori_loop(first, plan.pieces if last is None else last, unit, 0)
 
 
 def forward_kernel(plan, *refs):
-    u_ref, f_ref, *shards = refs[:5]
+    io_ref, gain_ref, filters_ref, lengths_ref = refs[:4]
+    gate_raw, up_raw, down_raw, proj_raw, attn_raw = refs[4:9]
     if plan.routed:
-        maps_ref = refs[5]
-        rest = refs[6:]
+        maps_ref = refs[9]
+        rest = refs[10:]
     else:
-        mine_ref, other_ref, taps_ref = refs[5:8]
-        rest = refs[8:]
-    full_weights, rest = rest[:3], rest[3:]
+        mine_ref, other_ref, taps_ref = refs[9:12]
+        rest = refs[12:]
+    full_weights, rest = rest[:10], rest[10:]
     (
         conv_ref,
+        hidden_ref,
+        upstream_ref,
+        pair_ref,
+        gains_ref,
+        mask_ref,
         v_ref,
         pq_ref,
         tapw_ref,
         x_ref,
         xs_ref,
         filt_ref,
+        io_own,
+        io_sib,
+        gain_tile,
+        gain_land,
+        gate_half,
+        gate_shard,
+        up_half,
+        up_shard,
+        down_shard,
+        proj_shard,
+        attn_shard,
+        u_ref,
+        f_ref,
         x_buf,
         xo_buf,
         xs_buf,
@@ -501,6 +477,11 @@
         y_buf,
         land,
         stage,
+        io_sem,
+        gain_send,
+        gain_recv,
+        s_send,
+        s_recv,
         u_send,
         x_recv,
         f_send,
@@ -517,11 +498,149 @@
         w_send,
         w_recv,
     ) = rest
-    chips, half, jb, ia = plan.chips, plan.half, plan.jb, plan.ia
+    chips, half, jb, ia, rows_here = plan.chips, plan.half, plan.jb, plan.ia, plan.rows
     section, chip = spot()
     dev = section * chips + chip
+    sibling = (1 - section, chip)
     my_group = chip // (plan.cols_out * plan.cols_in)
-    greet_everyone(chips)
+    greeted = greet_everyone(chips)
+
+    row = lax.broadcasted_iota(jnp.int32, (rows_here, rows_here), 0)
+    col = lax.broadcasted_iota(jnp.int32, (rows_here, rows_here), 1)
+    order = jnp.where(col == 2 * lax.rem(row, half) + row // half, 1.0, 0.0).astype(BF)
+    for i in range(2):
+        io_own[i] = flat_dot(order, io_ref[i]).astype(BF)
+    cols = gain_ref.shape[1]
+    gain_tile[...] = jnp.zeros_like(gain_tile)
+    gain_tile[0:2, 0:cols] = gain_ref[...].astype(F32)
+    if plan.pick_here:
+        lane = lax.broadcasted_iota(jnp.int32, (gate_raw.shape[0], LANES), 1)
+        low = lane < half
+        for raw, halves, shard in ((gate_raw, gate_half, gate_shard), (up_raw, up_half, up_shard)):
+            for j in range(raw.shape[1] // (2 * LANES)):
+                one = raw[:, 2 * LANES * j : 2 * LANES * j + LANES].astype(F32)
+                two = raw[:, 2 * LANES * j + LANES : 2 * LANES * (j + 1)].astype(F32)
+                zero_half = jnp.where(low, one, pltpu.roll(two, half, 1)).astype(BF)
+                one_half = jnp.where(low, pltpu.roll(one, half, 1), two).astype(BF)
+                at = slice(LANES * j, LANES * (j + 1))
+                shard[section, :, at] = jnp.where(section == 0, zero_half, one_half)
+                halves[:, at] = jnp.where(section == 0, one_half, zero_half)
+    else:
+        for raw, halves, shard in ((gate_raw, gate_half, gate_shard), (up_raw, up_half, up_shard)):
+            shard[section] = raw[section]
+            halves[...] = raw[1 - section]
+    part = down_shard.shape[1]
+    down_shard[section] = down_raw[pl.ds(pl.multiple_of(part * section, 16), part), :]
+    proj_shard[section] = proj_raw[...]
+    attn_shard[section] = attn_raw[...]
+    greeted()
+    io_swap = push(io_own, io_sib, io_sem.at[0], io_sem.at[1], sibling)
+    io_swap.start()
+
+    def send_gain(step, carry):
+        peer = lax.rem(dev + step, 2 * chips)
+        push(
+            gain_tile,
+            gain_land.at[section, chip],
+            gain_send,
+            gain_recv,
+            (peer // chips, lax.rem(peer, chips)),
+        ).start()
+        return carry
+
+    lax.fori_loop(1, 2 * chips, send_gain, 0)
+    pltpu.make_async_copy(gain_tile, gain_land.at[section, chip], gain_recv).start()
+    shares = [
+        push(src, dst, s_send.at[i], s_recv.at[i], sibling)
+        for i, (src, dst) in enumerate(
+            (
+                (gate_half, gate_shard.at[section]),
+                (up_half, up_shard.at[section]),
+                (
+                    down_raw.at[pl.ds(pl.multiple_of(part * (1 - section), 16), part), :],
+                    down_shard.at[section],
+                ),
+                (proj_shard.at[section], proj_shard.at[section]),
+                (attn_shard.at[section], attn_shard.at[section]),
+            )
+        )
+    ]
+    for share in shares:
+        share.start()
+
+    if plan.routed:
+
+        def places(m, tap, k, sub, a):
+            src = maps_ref.at[pl.ds(PIECE * m, PIECE), pl.ds(a * ia, ia)]
+            if tap:
+                return src, taps.at[pl.ds(jb * k + PIECE * sub, PIECE), :], t_recv
+            return src, mine.at[k, pl.ds(PIECE * sub, PIECE), :], m_recv
+
+        def start_piece(m, tap, k, sub, a, to_section, to_chip):
+            src, dst, sem = places(m, tap, k, sub, a)
+            here = to_section * chips + to_chip == dev
+
+            @pl.when(here)
+            def _():
+                pltpu.make_async_copy(src, dst, sem).start()
+
+            @pl.when(jnp.logical_not(here))
+            def _():
+                push(src, dst, m_send, sem, (to_section, to_chip)).start()
+
+        def drain_piece(m, tap, k, sub, a, to_section, to_chip):
+            src, dst, sem = places(m, tap, k, sub, a)
+
+            @pl.when(to_section * chips + to_chip != dev)
+            def _():
+                push(src, dst, m_send, sem, (to_section, to_chip)).wait_send()
+
+        owner_pieces(plan, start_piece, 0, plan.pieces // 3)
+
+    lag = lax.broadcasted_iota(jnp.int32, (rows_here, LANES), 0)
+    lane = lax.broadcasted_iota(jnp.int32, (rows_here, LANES), 1)
+    stretch = lax.rem(lane, half)
+    backwards = jnp.where(lag == 2 * (half - 1 - stretch) + lane // half, 1.0, 0.0).astype(BF)
+    plain = jnp.where(lag == 2 * stretch + lane // half, 1.0, 0.0).astype(BF)
+    for group in range(plan.groups):
+        source = lax.broadcasted_iota(jnp.int32, (plan.filters, plan.f_rows), 0)
+        target = lax.broadcasted_iota(jnp.int32, (plan.filters, plan.f_rows), 1)
+        chosen = jnp.where(
+            (source == group * plan.local + target) & (target < plan.local), 1.0, 0.0
+        ).astype(BF)
+        some = flat_dot(filters_ref[...], chosen).astype(BF)
+        f_ref[group, : plan.f_rows, :] = cols_dot(some, backwards).astype(BF)
+        f_ref[group, plan.f_rows :, :] = cols_dot(some, plain).astype(BF)
+
+    bytes_of(gain_land, gain_recv)
+    pick_row = lax.broadcasted_iota(jnp.int32, (LANES, plan.width), 0)
+    pick_col = lax.broadcasted_iota(jnp.int32, (LANES, plan.width), 1)
+    repeat = jnp.where(pick_row == lax.rem(pick_col, cols), 1.0, 0.0).astype(BF)
+    tile_row = lax.broadcasted_iota(jnp.int32, (chips * 8, plan.width), 0)
+    tile_col = lax.broadcasted_iota(jnp.int32, (chips * 8, plan.width), 1)
+    for layer in range(2):
+        spread = flat_dot(gain_land[layer].reshape(chips * 8, LANES).astype(BF), repeat)
+        for number in range(2):
+            here = (tile_row // 8 == tile_col // cols) & (lax.rem(tile_row, 8) == number)
+            gains_ref[2 * layer + number : 2 * layer + number + 1, :] = jnp.sum(
+                jnp.where(here, spread, 0.0), axis=0, keepdims=True
+            )
+    position = lax.broadcasted_iota(jnp.int32, (rows_here, 1), 0)
+    position = chip * rows_here + 2 * lax.rem(position, half) + position // half
+    length_own = jnp.where(section == 0, lengths_ref[0], lengths_ref[1])
+    length_other = jnp.where(section == 0, lengths_ref[1], lengths_ref[0])
+    mask = jnp.where(position < length_own, 1.0, 0.0)
+    mask_other = jnp.where(position < length_other, 1.0, 0.0)
+    mask_ref[...] = mask
+    io_swap.wait()
+    core_zero = section == 0
+    hidden = jnp.where(core_zero, io_own[0], io_sib[1]).astype(F32) * mask
+    hidden_ref[...] = hidden
+    factor = lax.rsqrt(jnp.mean(hidden * hidden, axis=-1, keepdims=True) + EPSILON)
+    u = (hidden * factor * gains_ref[0:1, :]).astype(BF)
+    for b in range(plan.cols_in):
+        u_ref[b, :, :jb] = u[:half, b * jb : (b + 1) * jb]
+        u_ref[b, :, jb:] = u[half:, b * jb : (b + 1) * jb]
 
     def send_u(step, carry):
         peer = lax.rem(chip + step, chips)
@@ -544,38 +663,35 @@
         x_recv,
     ).start()
     pltpu.make_async_copy(f_ref.at[my_group], f_land.at[chip], f_recv).start()
-
     if plan.routed:
-
-        def places(m, tap, k, sub, a):
-            src = maps_ref.at[pl.ds(PIECE * m, PIECE), pl.ds(a * ia, ia)]
-            if tap:
-                return src, taps.at[pl.ds(jb * k + PIECE * sub, PIECE), :], t_recv
-            return src, mine.at[k, pl.ds(PIECE * sub, PIECE), :], m_recv
-
-        def start_piece(m, tap, k, sub, a, to_section, to_chip):
-            src, dst, sem = places(m, tap, k, sub, a)
-            here = to_section * chips + to_chip == dev
-
-            @pl.when(here)
-            def _():
-                pltpu.make_async_copy(src, dst, sem).start()
-
-            @pl.when(jnp.logical_not(here))
-            def _():
-                push(src, dst, m_send, sem, (to_section, to_chip)).start()
-
-        def drain_piece(m, tap, k, sub, a, to_section, to_chip):
-            src, dst, sem = places(m, tap, k, sub, a)
-
-            @pl.when(to_section * chips + to_chip != dev)
-            def _():
-                push(src, dst, m_send, sem, (to_section, to_chip)).wait_send()
-
-        owner_pieces(plan, start_piece)
-
-    gather = Gather(plan, shards, full_weights, w_send, w_recv)
-    gather.begin()
+        owner_pieces(plan, start_piece, plan.pieces // 3)
+
+    for share in shares:
+        share.wait_recv()
+    groups = []
+    for first, arrays in (
+        (0, (gate_shard.at[0], up_shard.at[0], down_shard.at[0])),
+        (3, (proj_shard.at[0], proj_shard.at[1], attn_shard.at[0], attn_shard.at[1])),
+        (7, (gate_shard.at[1], up_shard.at[1], down_shard.at[1])),
+    ):
+        last = first + len(arrays)
+        groups.append(
+            Gather(
+                plan,
+                arrays,
+                full_weights[first:last],
+                w_send.at[pl.ds(first, len(arrays))],
+                w_recv.at[pl.ds(first, len(arrays))],
+            )
+        )
+    layer0, attention, layer1 = groups
+    for group in groups:
+        group.begin()
+    cot_own = jnp.where(core_zero, io_sib[0], io_own[1]).astype(F32) * mask
+    cot_other = jnp.where(core_zero, io_sib[1], io_own[0]).astype(F32) * mask_other
+    upstream_ref[...] = cot_own
+    pair_ref[:rows_here, :] = cot_own.astype(BF)
+    pair_ref[rows_here:, :] = cot_other.astype(BF)
     bytes_of(f_land, f_recv)
     filter_rows(plan, f_land, table, 0, False)
     build_strips(plan, table, strip, False)
@@ -631,10 +747,15 @@
     taps_out = pltpu.make_async_copy(taps, tapw_ref, out_sem.at[4])
     taps_out.start()
 
-    gather.second()
+    layer0.second()
     for i in range(plan.blocks):
+        if i == 1:
+            attention.second()
         if i == plan.blocks // 2:
-            gather.third()
+            layer0.third()
+        if i == plan.blocks - 1:
+            layer1.second()
+            attention.third()
         rows = slice(BLOCK * i, BLOCK * (i + 1))
         depth = BLOCK * (i + 1)
         offset = plan.length - depth
@@ -695,6 +816,7 @@
 
         lax.fori_loop(0, BLOCK // half, give, 0)
 
+    layer1.third()
     for slot in range(2):
         pltpu.make_async_copy(
             stage.at[slot], v_ref.at[slot, :, pl.ds(0, BLOCK), :], v_sem.at[slot]
@@ -713,17 +835,39 @@
             total = term if total is None else total + term
         conv_ref[:, :, a * ia : (a + 1) * ia] = total
     bytes_of(land.at[pl.ds(0, chips - 1)], c_send)
-    gather.end()
-
-
-def forward_call(plan, u, packed, shards, maps):
-    chips, half, jb, ia = plan.chips, plan.half, plan.jb, plan.ia
+    for group in groups:
+        group.end()
+    def drain_gain(step, carry):
+        push(
+            gain_tile, gain_land.at[section, chip], gain_send, gain_recv, sibling
+        ).wait_send()
+        return carry
+
+    lax.fori_loop(1, 2 * chips, drain_gain, 0)
+    for share in shares:
+        share.wait_send()
+
+
+def forward_call(plan, io, gain, filters, lengths, raw, maps):
+    chips, half, jb, ia, rows = plan.chips, plan.half, plan.jb, plan.ia, plan.rows
+    width = plan.width
     any_spec = pl.BlockSpec(memory_space=pl.ANY)
     vmem_spec = pl.BlockSpec(memory_space=pltpu.VMEM)
+    smem_spec = pl.BlockSpec(memory_space=pltpu.SMEM)
     dma = pltpu.SemaphoreType.DMA
+    down, proj, attn = raw[2].shape, raw[3].shape, raw[4].shape
+    share = (raw[0].shape[-2], plan.ff // 2)
+    down_share = (down[0] // 2, width)
     grid = (plan.depth, plan.side, plan.side)
-    shapes = [(grid + w.shape, BF) for w in shards] + [
-        ((2, half, plan.width), F32),
+    layer = [share, share, down_share]
+    gathered = layer + [proj, proj, attn, attn] + layer
+    shapes = [(grid + w, BF) for w in gathered] + [
+        ((2, half, width), F32),
+        ((rows, width), F32),
+        ((rows, width), F32),
+        ((2 * rows, width), BF),
+        ((8, width), F32),
+        ((rows, 1), F32),
         ((plan.local, 2, plan.length, 2 * jb), BF),
         ((plan.local, 2 * jb, ia), BF),
         ((ORDER * jb, ia), BF),
@@ -734,9 +878,25 @@
     return pl.pallas_call(
         functools.partial(forward_kernel, plan),
         out_shape=[jax.ShapeDtypeStruct(s, d) for s, d in shapes],
-        in_specs=[vmem_spec] * 2 + [any_spec] * (3 + len(maps)),
-        out_specs=[any_spec] * 3 + [vmem_spec] + [any_spec] * 6,
+        in_specs=[vmem_spec] * 3
+        + [smem_spec]
+        + [vmem_spec] * 5
+        + [any_spec] * len(maps),
+        out_specs=[any_spec] * 10 + [vmem_spec] * 6 + [any_spec] * 6,
         scratch_shapes=[
+            pltpu.VMEM((2, rows, width), BF),
+            pltpu.VMEM((2, rows, width), BF),
+            pltpu.VMEM((8, LANES), F32),
+            pltpu.VMEM((2, chips, 8, LANES), F32),
+            pltpu.VMEM(share, BF),
+            pltpu.VMEM((2,) + share, BF),
+            pltpu.VMEM(share, BF),
+            pltpu.VMEM((2,) + share, BF),
+            pltpu.VMEM((2,) + down_share, BF),
+            pltpu.VMEM((2,) + proj, BF),
+            pltpu.VMEM((2,) + attn, BF),
+            pltpu.VMEM((plan.cols_in, half, 2 * jb), BF),
+            pltpu.VMEM((plan.groups, 2 * plan.f_rows, LANES), BF),
             pltpu.VMEM((plan.length, 2 * jb), BF),
             pltpu.VMEM((plan.length, 2 * jb), BF),
             pltpu.VMEM((plan.length, 2 * jb), BF),
@@ -752,27 +912,32 @@
             pltpu.VMEM((2, plan.length, ia), BF),
             pltpu.VMEM((chips, 2, half, ia), BF),
             pltpu.VMEM((2, 2, BLOCK, 2 * jb), BF),
+            dma((2,)),
+            dma,
+            dma,
+            dma((5,)),
+            dma((5,)),
         ]
         + [dma] * 11
-        + [dma((2,)), dma((5,)), dma((3, 5)), dma((3, 5))],
+        + [dma((2,)), dma((5,)), dma((10, 5)), dma((10, 5))],
         compiler_params=pltpu.CompilerParams(
             collective_id=2, has_side_effects=True, vmem_limit_bytes=VMEM_LIMIT
         ),
         name="spectral_forward",
-    )(u, packed, *shards, *maps)
-
-
-def backward_kernel(plan, *refs):
+    )(io, gain, filters, lengths, *raw, *maps)
+
+
+def backward_kernel(plan, number, *refs):
     g_ref, filt_ref, v_ref, pq, tapw, x_ref, xs_ref = refs[:7]
-    grads = refs[7:10]
-    sums = refs[10:13]
-    du_ref = refs[13]
+    grads, rest = refs[7 : 7 + number], refs[7 + number :]
+    sums, rest = rest[:number], rest[number:]
+    du_ref = rest[0]
     if plan.routed:
-        dmaps_ref = refs[14]
-        rest = refs[15:]
+        dmaps_ref = rest[1]
+        rest = rest[2:]
     else:
-        dmap_ref, dtap_ref = refs[14:16]
-        rest = refs[16:]
+        dmap_ref, dtap_ref = rest[1:3]
+        rest = rest[3:]
     count = 5 * sum(len(plan.routes(grad.shape[3])) for grad in grads)
     scatter = Scatter(plan, grads, sums, rest[:count], *rest[count : count + 2])
     rest = rest[count + 2 :]
@@ -815,7 +980,7 @@
     my_a = lax.rem(chip, plan.cols_out)
     my_b = lax.rem(chip // plan.cols_out, plan.cols_in)
     my_group = chip // (plan.cols_out * plan.cols_in)
-    greet_everyone(chips)
+    greet_everyone(chips)()
 
     def send_g(step, carry):
         peer = lax.rem(chip + step, chips)
@@ -1052,13 +1217,13 @@
         out_shape.append(jax.ShapeDtypeStruct((plan.local, jb, ia), BF))
         out_shape.append(jax.ShapeDtypeStruct((ORDER * jb, ia), BF))
     return pl.pallas_call(
-        functools.partial(backward_kernel, plan),
+        functools.partial(backward_kernel, plan, len(grads)),
         out_shape=out_shape,
         in_specs=[vmem_spec, vmem_spec, any_spec, vmem_spec, vmem_spec, any_spec, any_spec]
-        + [vmem_spec] * 3,
-        out_specs=[vmem_spec] * 4 + [any_spec] * (len(out_shape) - 4),
+        + [vmem_spec] * len(grads),
+        out_specs=[vmem_spec] * (len(grads) + 1) + [any_spec] * (len(out_shape) - len(grads) - 1),
         scratch_shapes=Scatter.scratch(plan, shapes)
-        + [dma((3, 6)), dma((3, 6))]
+        + [dma((len(grads), 6)), dma((len(grads), 6))]
         + [
             pltpu.VMEM((2, plan.length, ia), BF),
             pltpu.VMEM((2, ia, plan.length), BF),
@@ -1098,24 +1263,394 @@
         name="spectral_backward",
     )(g, filt, v, pq, tapw, x, xs, *grads)
 
+SWAPS = 7
+
+
+def middle_kernel(plan, *refs):
+    (
+        conv_ref,
+        hidden_ref,
+        gains_ref,
+        mask_ref,
+        up_ref,
+        up_pair,
+        *stored,
+    ) = refs[:16]
+    (
+        out_ref,
+        g_ref,
+        dmid_ref,
+        gain_ref,
+        gate0_g,
+        up0_g,
+        down0_g,
+        gate1_g,
+        up1_g,
+        down1_g,
+        proj_g,
+        attn_g,
+    ) = refs[16:28]
+    held = refs[28:36]
+    (
+        pair0,
+        pair1,
+        give,
+        take,
+        gates,
+        ups,
+        acts,
+        dgate,
+        dup,
+        kv,
+        q_buf,
+        probs,
+        dkv,
+        back,
+        back_land,
+        att,
+        dq_buf,
+        load_sem,
+        send,
+        recv,
+        kv_send,
+        kv_recv,
+        bk_send,
+        bk_recv,
+    ) = refs[36:]
+    chips, rows, width = plan.chips, plan.rows, plan.width
+    section, chip = spot()
+    sibling = (1 - section, chip)
+    reach = WINDOW // rows
+    span = (reach + 1) * rows
+    layer0, (w_proj, w_out), layer1 = held[:3], held[3:5], held[5:]
+    split = 3 * plan.width // 2
+    homes = [
+        *layer0,
+        w_proj.at[:split],
+        w_proj.at[split:],
+        w_out.at[: plan.width // 2],
+        w_out.at[plan.width // 2 :],
+        *layer1,
+    ]
+    loads = [
+        pltpu.make_async_copy(a, b, load_sem.at[i]) for i, (a, b) in enumerate(zip(stored, homes))
+    ]
+    for load in loads:
+        load.start()
+    greet_everyone(chips)()
+    ff = layer0[0].shape[1]
+    own = slice(0, rows)
+    second = slice(rows, 2 * rows)
+    mask = mask_ref[...]
+
+    def swap(number, src, dst):
+        copy = push(src, dst, send.at[number], recv.at[number], sibling)
+        copy.start()
+        copy.wait()
+
+    def norm(values, gain):
+        factor = lax.rsqrt(jnp.mean(values * values, axis=-1, keepdims=True) + EPSILON)
+        return values * factor * gain, factor
+
+    def norm_back(values, factor, gain, upstream):
+        weighted = upstream * gain
+        gain_grad = jnp.sum(upstream * values * factor, axis=0, keepdims=True)
+        correction = jnp.mean(weighted * values, axis=-1, keepdims=True)
+        return factor * weighted - values * factor * factor * factor * correction, gain_grad
+
+    def feed(layer, pair, weights, number):
+        w_gate, w_up, w_down = weights
+        swap(number, pair.at[own], pair.at[second])
+        for start in range(0, ff, BLOCK):
+            cols = slice(start, start + BLOCK)
+            gate_rows = flat_dot(pair[...], w_gate[:, cols])
+            up_rows = flat_dot(pair[...], w_up[:, cols])
+            gates[layer, :, cols] = gate_rows
+            ups[layer, :, cols] = up_rows
+            acts[layer, :, cols] = (gate_rows * jax.nn.sigmoid(gate_rows) * up_rows).astype(BF)
+        part = flat_dot(acts[layer], w_down[...])
+        give[number] = part[second].astype(BF)
+        swap(number + 1, give.at[number], take.at[number])
+        return part[own] + take[number].astype(F32)
+
+    def feed_back(layer, pair, weights, grads, upstream_pair, number):
+        w_gate, w_up, w_down = weights
+        gate_g, up_g, down_g = grads
+        turned = pair[...].astype(F32).T.astype(BF)
+        for start in range(0, ff, BLOCK):
+            cols = slice(start, start + BLOCK)
+            active_grad = rows_dot(upstream_pair, w_down[cols, :])
+            gate_rows, up_rows = gates[layer, :, cols], ups[layer, :, cols]
+            sigmoid = jax.nn.sigmoid(gate_rows)
+            slope = sigmoid * (1.0 + gate_rows * (1.0 - sigmoid))
+            gate_grad = (active_grad * up_rows * slope).astype(BF)
+            up_grad = (active_grad * gate_rows * sigmoid).astype(BF)
+            dgate[:, cols] = gate_grad
+            dup[:, cols] = up_grad
+        for start in range(0, width, BLOCK):
+            cols = slice(start, start + BLOCK)
+            part = rows_dot(dgate[...], w_gate[cols, :]) + rows_dot(dup[...], w_up[cols, :])
+            give[number, :, cols] = part[second].astype(BF)
+            att[:, cols] = part[own]
+        copy = push(
+            give.at[number], take.at[number], send.at[number], recv.at[number], sibling
+        )
+        copy.start()
+        for start in range(0, ff, BLOCK):
+            cols = slice(start, start + BLOCK)
+            gate_g[:, cols] = flat_dot(turned, dgate[:, cols]).astype(BF)
+            up_g[:, cols] = flat_dot(turned, dup[:, cols]).astype(BF)
+            down_g[cols, :] = flat_dot(
+                acts[layer, :, cols].astype(F32).T.astype(BF), upstream_pair
+            ).astype(BF)
+        copy.wait()
+        return att[...] + take[number].astype(F32)
+
+    middle0 = hidden_ref[...] + conv_ref[...]
+    normed, factor0 = norm(middle0, gains_ref[1:2, :])
+    pair0[own] = normed.astype(BF)
+    dmid_ref[...] = middle0
+    for load in loads[:3]:
+        load.wait()
+    branch = feed(0, pair0, layer0, 0)
+    passed = (mask * (dmid_ref[...] + branch)).astype(BF).astype(F32)
+
+    normed, factor10 = norm(passed, gains_ref[2:3, :])
+    inputs = normed.astype(BF)
+    for load in loads[3:7]:
+        load.wait()
+    mine = slice(reach * rows, span)
+    q_buf[...] = flat_dot(inputs, w_proj[:width]).astype(BF)
+    kv[mine, :width] = flat_dot(inputs, w_proj[width : 2 * width]).astype(BF)
+    kv[mine, width:] = flat_dot(inputs, w_proj[2 * width :]).astype(BF)
+
+    def ahead(distance):
+        return push(
+            kv.at[mine],
+            kv.at[pl.ds((reach - distance) * rows, rows)],
+            kv_send.at[distance - 1],
+            kv_recv.at[distance - 1],
+            (section, chip + distance),
+        )
+
+    for distance in range(1, reach + 1):
+
+        @pl.when(chip + distance < chips)
+        def _():
+            ahead(distance).start()
+
+        @pl.when(chip < distance)
+        def _():
+            kv[(reach - distance) * rows : (reach - distance + 1) * rows, :] = jnp.zeros(
+                (rows, 2 * width), BF
+            )
+
+    half = plan.half
+    row = lax.broadcasted_iota(jnp.int32, (rows, span), 0)
+    col = lax.broadcasted_iota(jnp.int32, (rows, span), 1)
+    inner = lax.rem(col, rows)
+    q_place = 2 * lax.rem(row, half) + row // half
+    k_place = (col // rows - reach) * rows + 2 * lax.rem(inner, half) + inner // half
+    distance_rows = q_place - k_place
+    allowed = (
+        (k_place + chip * rows >= 0) & (distance_rows >= 0) & (distance_rows < WINDOW)
+    )
+    lane = lax.broadcasted_iota(jnp.int32, (rows, LANES), 1)
+    low = lane < HEAD_DIM
+    scale = HEAD_DIM ** (-0.5)
+    zero = jnp.zeros((rows, LANES), BF)
+    for distance in range(1, reach + 1):
+
+        @pl.when(chip >= distance)
+        def _():
+            push(
+                kv.at[mine],
+                kv.at[pl.ds((reach - distance) * rows, rows)],
+                kv_send.at[distance - 1],
+                kv_recv.at[distance - 1],
+                sibling,
+            ).wait_recv()
+
+    for pair in range(width // LANES):
+        lanes = slice(LANES * pair, LANES * (pair + 1))
+        keys, values = kv[:, lanes], kv[:, width + LANES * pair : width + LANES * (pair + 1)]
+        parts = []
+        for side in range(2):
+            here = low if side == 0 else jnp.logical_not(low)
+            queries = jnp.where(here, q_buf[:, lanes], zero)
+            scores = rows_dot(queries, keys) * scale
+            scores = jnp.where(allowed, scores, BIG_NEGATIVE)
+            weights = jnp.exp(scores - jnp.max(scores, axis=-1, keepdims=True))
+            weights = weights / jnp.sum(weights, axis=-1, keepdims=True)
+            probs[2 * pair + side] = weights
+            parts.append(flat_dot(weights.astype(BF), values))
+        att[:, lanes] = jnp.where(low, parts[0], parts[1])
+    attended = att[...].astype(BF)
+    middle1 = passed + flat_dot(attended, w_out[...])
+
+    for load in loads[7:]:
+        load.wait()
+    normed, factor11 = norm(middle1, gains_ref[3:4, :])
+    pair1[own] = normed.astype(BF)
+    branch = feed(1, pair1, layer1, 2)
+    out_ref[...] = (mask * (middle1 + branch)).astype(BF)
+    dnormed = feed_back(1, pair1, layer1, (gate1_g, up1_g, down1_g), up_pair[...], 4)
+    dmiddle, gain11 = norm_back(middle1, factor11, gains_ref[3:4, :], dnormed)
+    dmiddle = up_ref[...] + dmiddle
+    gain_ref[3:4, :] = gain11
+
+    dy = dmiddle.astype(BF)
+    attn_g[...] = flat_dot(attended.astype(F32).T.astype(BF), dy).astype(BF)
+    datt = rows_dot(dy, w_out[...]).astype(BF)
+    for pair in range(width // LANES):
+        lanes = slice(LANES * pair, LANES * (pair + 1))
+        value_lanes = slice(width + LANES * pair, width + LANES * (pair + 1))
+        keys, values = kv[:, lanes], kv[:, value_lanes]
+        dq_parts, key_grad, value_grad = [], None, None
+        for side in range(2):
+            here = low if side == 0 else jnp.logical_not(low)
+            queries = jnp.where(here, q_buf[:, lanes], zero)
+            upstream = jnp.where(here, datt[:, lanes], zero)
+            weights = probs[2 * pair + side]
+            grad = rows_dot(upstream, values)
+            total = jnp.sum(weights * grad, axis=-1, keepdims=True)
+            dscores = weights * (grad - total)
+            dq_parts.append(flat_dot(dscores.astype(BF), keys))
+            one = flat_dot(dscores.T.astype(BF), queries)
+            two = flat_dot(weights.T.astype(BF), upstream)
+            key_grad = one if key_grad is None else key_grad + one
+            value_grad = two if value_grad is None else value_grad + two
+        dq_buf[0, :, lanes] = (jnp.where(low, dq_parts[0], dq_parts[1]) * scale).astype(BF)
+        key_grad = key_grad * scale
+        back[:, lanes] = key_grad[: reach * rows].astype(BF)
+        back[:, value_lanes] = value_grad[: reach * rows].astype(BF)
+        dkv[:, lanes] = key_grad[reach * rows :]
+        dkv[:, value_lanes] = value_grad[reach * rows :]
+
+    def behind(distance, peer):
+        return push(
+            back.at[pl.ds((reach - distance) * rows, rows)],
+            back_land.at[distance - 1],
+            bk_send.at[distance - 1],
+            bk_recv.at[distance - 1],
+            (section, peer),
+        )
+
+    for distance in range(1, reach + 1):
+
+        @pl.when(chip >= distance)
+        def _():
+            behind(distance, chip - distance).start()
+
+    for distance in range(1, reach + 1):
+
+        @pl.when(chip + distance < chips)
+        def _():
+            behind(distance, chip).wait_recv()
+            dkv[...] += back_land[distance - 1].astype(F32)
+
+    dq_buf[1] = dkv[:, :width].astype(BF)
+    dq_buf[2] = dkv[:, width:].astype(BF)
+    turned = inputs.astype(F32).T.astype(BF)
+    dnormed = None
+    for part in range(3):
+        term = rows_dot(dq_buf[part], w_proj[part * width : (part + 1) * width])
+        dnormed = term if dnormed is None else dnormed + term
+    dpassed, gain10 = norm_back(passed, factor10, gains_ref[2:3, :], dnormed)
+    gain_ref[2:3, :] = gain10
+    dpassed = (dmiddle + dpassed).astype(BF).astype(F32)
+
+    upstream0 = mask * dpassed
+    give[5] = upstream0.astype(BF)
+    copy = push(give.at[5], take.at[5], send.at[5], recv.at[5], sibling)
+    copy.start()
+    for part in range(3):
+        proj_g[part * width : (part + 1) * width, :] = flat_dot(turned, dq_buf[part]).astype(BF)
+    copy.wait()
+    both = jnp.concatenate([give[5], take[5]], 0)
+    dnormed = feed_back(0, pair0, layer0, (gate0_g, up0_g, down0_g), both, 6)
+    middle0 = dmid_ref[...]
+    dmiddle, gain01 = norm_back(middle0, factor0, gains_ref[1:2, :], dnormed)
+    gain_ref[1:2, :] = gain01
+    dmiddle = upstream0 + dmiddle
+    dmid_ref[...] = dmiddle
+    g_ref[...] = dmiddle.astype(BF)
+
+    for distance in range(1, reach + 1):
+
+        @pl.when(chip + distance < chips)
+        def _():
+            ahead(distance).wait_send()
+
+        @pl.when(chip >= distance)
+        def _():
+            behind(distance, chip).wait_send()
+
+
+def middle_call(plan, conv, hidden, gains, mask, upstream, pair, stored):
+    rows, width = plan.rows, plan.width
+    reach = WINDOW // rows
+    ff = plan.ff // 2
+    any_spec = pl.BlockSpec(memory_space=pl.ANY)
+    vmem_spec = pl.BlockSpec(memory_space=pltpu.VMEM)
+    dma = pltpu.SemaphoreType.DMA
+    layer = [(width, ff), (width, ff), (ff, width)]
+    held = layer + [(3 * width, width), (width, width)] + layer
+    shapes = [
+        ((rows, width), BF),
+        ((rows, width), BF),
+        ((rows, width), F32),
+        ((8, width), F32),
+        ((width, ff), BF),
+        ((width, ff), BF),
+        ((ff, width), BF),
+        ((width, ff), BF),
+        ((width, ff), BF),
+        ((ff, width), BF),
+        ((3 * width, width), BF),
+        ((width, width), BF),
+    ]
+    return pl.pallas_call(
+        functools.partial(middle_kernel, plan),
+        out_shape=[jax.ShapeDtypeStruct(s, d) for s, d in shapes],
+        in_specs=[vmem_spec] * 6 + [any_spec] * 10,
+        out_specs=[vmem_spec] * len(shapes),
+        scratch_shapes=[pltpu.VMEM(w, BF) for w in held]
+        + [
+            pltpu.VMEM((2 * rows, width), BF),
+            pltpu.VMEM((2 * rows, width), BF),
+            pltpu.VMEM((SWAPS, rows, width), BF),
+            pltpu.VMEM((SWAPS, rows, width), BF),
+            pltpu.VMEM((2, 2 * rows, ff), F32),
+            pltpu.VMEM((2, 2 * rows, ff), F32),
+            pltpu.VMEM((2, 2 * rows, ff), BF),
+            pltpu.VMEM((2 * rows, ff), BF),
+            pltpu.VMEM((2 * rows, ff), BF),
+            pltpu.VMEM(((reach + 1) * rows, 2 * width), BF),
+            pltpu.VMEM((rows, width), BF),
+            pltpu.VMEM((width // HEAD_DIM, rows, (reach + 1) * rows), F32),
+            pltpu.VMEM((rows, 2 * width), F32),
+            pltpu.VMEM((reach * rows, 2 * width), BF),
+            pltpu.VMEM((reach, rows, 2 * width), BF),
+            pltpu.VMEM((rows, width), F32),
+            pltpu.VMEM((3, rows, width), BF),
+            dma((10,)),
+            dma((SWAPS,)),
+            dma((SWAPS,)),
+            dma((reach,)),
+            dma((reach,)),
+            dma((reach,)),
+            dma((reach,)),
+        ],
+        compiler_params=pltpu.CompilerParams(
+            collective_id=5, has_side_effects=True, vmem_limit_bytes=VMEM_LIMIT
+        ),
+        name="middle",
+    )(conv, hidden, gains, mask, upstream, pair, *stored)
+
 
 def swapped(block):
     return lax.ppermute(block, "section", [(0, 1), (1, 0)])
-
-
-def shifted(block, axis, distance):
-    devices = range(lax.axis_size(axis))
-    route = [(i - distance, i) for i in devices if i - distance in devices]
-    return lax.ppermute(block, axis, route)
-
-
-def dot(formula, left, right):
-    return jnp.einsum(formula, left, right, preferred_element_type=F32)
-
-
-def norm_forward(values, weights):
-    factor = lax.rsqrt(jnp.mean(values * values, axis=-1, keepdims=True) + EPSILON)
-    return (values * factor * weights, factor)
 
 
 def norm_backward(values, factor, weights, upstream):
@@ -1123,38 +1658,6 @@
     gain_grad = jnp.sum(upstream * values * factor, axis=0)
     correction = jnp.mean(weighted * values, axis=-1, keepdims=True)
     return (factor * weighted - values * factor * factor * factor * correction, gain_grad)
-
-
-def mlp_forward(middle, gain, weights):
-    w_gate, w_up, w_down = weights
-    rows = middle.shape[0]
-    normed, factor = norm_forward(middle, gain)
-    own = normed.astype(BF)
-    inputs = jnp.concatenate([own, swapped(own)], 0)
-    gate_rows = dot("td,df->tf", inputs, w_gate)
-    up_rows = dot("td,df->tf", inputs, w_up)
-    active = (jax.nn.silu(gate_rows) * up_rows).astype(BF)
-    part = dot("tf,fd->td", active, w_down)
-    branch = part[:rows] + swapped(part[rows:].astype(BF)).astype(F32)
-    return branch, (factor, inputs, gate_rows, up_rows, active)
-
-
-def mlp_backward(middle, gain, weights, saved, upstream, branch_grad):
-    w_gate, w_up, w_down = weights
-    rows = middle.shape[0]
-    factor, inputs, gate_rows, up_rows, active = saved
-    down_grad = dot("tf,td->fd", active, branch_grad)
-    active_grad = dot("td,fd->tf", branch_grad, w_down)
-    sigmoid = jax.nn.sigmoid(gate_rows)
-    slope = sigmoid * (1.0 + gate_rows * (1.0 - sigmoid))
-    gate_grad = (active_grad * up_rows * slope).astype(BF)
-    up_grad = (active_grad * gate_rows * sigmoid).astype(BF)
-    gate_w_grad = dot("td,tf->df", inputs, gate_grad)
-    up_w_grad = dot("td,tf->df", inputs, up_grad)
-    part = dot("tf,df->td", gate_grad, w_gate) + dot("tf,df->td", up_grad, w_up)
-    normed_grad = part[:rows] + swapped(part[rows:].astype(BF)).astype(F32)
-    middle_grad, gain_grad = norm_backward(middle, factor, gain, normed_grad)
-    return upstream + middle_grad, gain_grad, (gate_w_grad, up_w_grad, down_grad)
 
 
 def body(
@@ -1166,52 +1669,12 @@
     tok_rows = io_pair.shape[2]
     width = io_pair.shape[3]
     half = tok_rows // 2
-    heads = width // HEAD_DIM
-    reach = WINDOW // tok_rows
-    score_scale = HEAD_DIM ** (-0.5)
-    plan = Plan(chips, tok_rows, width, filters.shape[1], stu_maps.shape[0])
-
-    sib_io, sib_gate, sib_up, sib_down, sib_proj, sib_out, gains_all = entry_call(
-        chips,
-        [io_pair[0], mlp_gate[0], mlp_up[0], mlp_down[0], attn_proj, attn_out],
-        norm_gains[0],
-    )
-    gains = jnp.transpose(gains_all, (0, 2, 1, 3)).reshape(2, 2, width).astype(F32)
-
-    def split_phases(rows):
-        return (
-            rows.reshape(rows.shape[:-2] + (half, 2, width))
-            .swapaxes(-3, -2)
-            .reshape(rows.shape)
-        )
+    ff = mlp_gate.shape[2]
+    ff_half = mlp_down.shape[1] // 2
+    plan = Plan(chips, tok_rows, width, filters.shape[1], stu_maps.shape[0], ff)
 
     def join_phases(rows):
         return rows.reshape(2, half, width).swapaxes(0, 1).reshape(rows.shape)
-
-    local = jnp.arange(tok_rows, dtype=jnp.int32)
-    order = 2 * (local % half) + local // half
-    places = chip * tok_rows + order
-    own_length = jnp.where(core_zero, lengths[0], lengths[1])
-    other_length = jnp.where(core_zero, lengths[1], lengths[0])
-    mask_rows = (places < own_length).astype(F32)[:, None]
-    other_mask = (places < other_length).astype(F32)[:, None]
-    x = split_phases(jnp.where(core_zero, io_pair[0, 0], sib_io[1]))
-    cot_pair = jnp.where(core_zero, sib_io, io_pair[0])
-    cot = split_phases(jnp.where(core_zero, cot_pair[0], cot_pair[1]))
-    cot_other = split_phases(jnp.where(core_zero, cot_pair[1], cot_pair[0]))
-    hidden = x.astype(F32) * mask_rows
-    normed, spectral_factor = norm_forward(hidden, gains[0, 0])
-    u = normed.astype(BF)
-    u_parts = jnp.transpose(
-        u.reshape(2, half, plan.cols_in, plan.jb), (2, 1, 0, 3)
-    ).reshape(plan.cols_in, half, 2 * plan.jb)
-
-    lags = jnp.transpose(filters.reshape(half, 2, plan.filters), (2, 1, 0))
-    lags = jnp.stack([lags[:, :, ::-1], lags], 0).reshape(
-        2, plan.groups, plan.local, 2 * half
-    )
-    lags = jnp.pad(lags, ((0, 0), (0, 0), (0, plan.f_rows - plan.local), (0, LANES - 2 * half)))
-    packed = jnp.transpose(lags, (1, 0, 2, 3)).reshape(plan.groups, 2 * plan.f_rows, LANES)
 
     my_a = chip % plan.cols_out
     my_b = (chip // plan.cols_out) % plan.cols_in
@@ -1234,135 +1697,69 @@
             taps.reshape(-1, plan.ia),
         ]
 
-    ff = mlp_gate.shape[2]
-    ff_rows = mlp_down.shape[1]
-    ff_half = ff_rows // 2
-
-    def my_half(layer):
-        mine = core_zero == (layer == 0)
-        gate, up, down = (
-            jnp.where(mine, own, theirs)
-            for own, theirs in (
-                (mlp_gate[0], sib_gate),
-                (mlp_up[0], sib_up),
-                (mlp_down[0], sib_down),
+    gate, up = mlp_gate[0], mlp_up[0]
+    if not plan.pick_here:
+        gate, up = (
+            jnp.transpose(w.reshape(w.shape[0], chips, 2, ff_half), (2, 0, 1, 3)).reshape(
+                2, w.shape[0], ff // 2
             )
+            for w in (gate, up)
         )
-
-        def pick(w):
-            w = w.reshape(w.shape[0], chips, 2, ff_half)
-            return jnp.where(core_zero, w[:, :, 0], w[:, :, 1]).reshape(w.shape[0], -1)
-
-        return pick(gate), pick(up), jnp.where(core_zero, down[:ff_half], down[ff_half:])
-
-    results = forward_call(plan, u_parts, packed, my_half(0), maps)
-    layer0 = tuple(w.reshape(-1, w.shape[-1]) for w in results[:3])
-    conv, v, pq, tapw, x_all, xs_all, filt = results[3:]
-    gate1, up1, down1 = my_half(1)
+    results = forward_call(
+        plan,
+        io_pair[0],
+        norm_gains[0],
+        filters,
+        lengths,
+        [gate, up, mlp_down[0], attn_proj, attn_out],
+        maps,
+    )
+    weights = [w.reshape(-1, w.shape[-1]) for w in results[:10]]
+    conv, hidden, upstream1, grad_pair, gains, mask_rows = results[10:16]
+    v, pq, tapw, x_all, xs_all, filt = results[16:]
     proj_rows = attn_proj.shape[0]
-    out_rows = attn_out.shape[0]
-    both_rows = jnp.concatenate(
-        [
-            jnp.where(core_zero, attn_proj, sib_proj),
-            jnp.where(core_zero, sib_proj, attn_proj),
-            jnp.where(core_zero, attn_out, sib_out),
-            jnp.where(core_zero, sib_out, attn_out),
-            down1,
-        ],
-        0,
+    block_out, g, middle0_grad, gain_sums, *grads = middle_call(
+        plan,
+        conv.reshape(tok_rows, width),
+        hidden,
+        gains,
+        mask_rows,
+        upstream1,
+        grad_pair,
+        weights,
     )
-    gate_rows = gate1.shape[0]
-    pieces = [both_rows]
-    for w in (gate1, up1):
-        pieces += [w[:, :width], w[:, width:]]
-    attn_all = lax.all_gather(jnp.concatenate(pieces, 0), "seq", axis=0, tiled=False)
-    at = both_rows.shape[0]
-    columns = [attn_all[:, at + gate_rows * i : at + gate_rows * (i + 1)] for i in range(4)]
-    columns = [c.reshape(-1, width) for c in columns]
-    layer1 = (
-        jnp.concatenate(columns[:2], 1),
-        jnp.concatenate(columns[2:], 1),
-        attn_all[:, at - ff_half : at].reshape(-1, width),
-    )
-    w_proj = jnp.swapaxes(
-        attn_all[:, : 2 * proj_rows].reshape(chips, 2, proj_rows, width), 0, 1
-    ).reshape(3, width, width)
-    w_out = jnp.swapaxes(
-        attn_all[:, 2 * proj_rows : 2 * (proj_rows + out_rows)].reshape(chips, 2, out_rows, width), 0, 1
-    ).reshape(width, width)
-
-    middle0 = hidden + conv.reshape(tok_rows, width)
-    branch0, saved0 = mlp_forward(middle0, gains[0, 1], layer0)
-    passed = (mask_rows * (middle0 + branch0)).astype(BF)
-
-    window_hidden = passed.astype(F32)
-    window_normed, window_factor = norm_forward(window_hidden, gains[1, 0])
-    inputs = window_normed.astype(BF)
-    triple = dot("td,wde->wte", inputs, w_proj).astype(BF)
-    key_value = triple[1:]
-    parts = [shifted(key_value, "seq", distance) for distance in range(reach, 0, -1)]
-    windows = jnp.concatenate(parts + [key_value], 1)
-    key_window = windows[0].reshape(-1, heads, HEAD_DIM)
-    value_window = windows[1].reshape(-1, heads, HEAD_DIM)
-    queries = triple[0].reshape(tok_rows, heads, HEAD_DIM)
-    scores = dot("qhe,khe->hqk", queries, key_window) * score_scale
-    key_place = (
-        (chip - reach + jnp.arange(reach + 1, dtype=jnp.int32))[:, None] * tok_rows + order[None, :]
-    ).reshape(-1)
-    distance_rows = places[:, None] - key_place[None, :]
-    allowed = (key_place[None, :] >= 0) & (distance_rows >= 0) & (distance_rows < WINDOW)
-    scores = jnp.where(allowed[None], scores, BIG_NEGATIVE)
-    highest = jnp.max(scores, axis=-1, keepdims=True)
-    weights = jnp.exp(scores - highest)
-    weights = weights / jnp.sum(weights, axis=-1, keepdims=True)
-    weights_low = weights.astype(BF)
-    attended = dot("hqk,khe->qhe", weights_low, value_window)
-    attended = attended.reshape(tok_rows, width).astype(BF)
-    middle1 = window_hidden + dot("td,de->te", attended, w_out)
-    branch1, saved1 = mlp_forward(middle1, gains[1, 1], layer1)
-    block_out = (mask_rows * (middle1 + branch1)).astype(BF)
-
-    upstream1 = cot.astype(F32) * mask_rows
-    other_upstream = cot_other.astype(F32) * other_mask
-    grad_pair = jnp.concatenate([upstream1, other_upstream], 0).astype(BF)
-    middle1_grad, gain11, mlp1_grads = mlp_backward(
-        middle1, gains[1, 1], layer1, saved1, upstream1, grad_pair
-    )
-    output_input = middle1_grad.astype(BF)
-    output_grad = dot("td,te->de", attended, output_input)
-    attended_grad = dot("te,de->td", output_input, w_out)
-    attended_grad = attended_grad.astype(BF).reshape(tok_rows, heads, HEAD_DIM)
-    value_grad = dot("hqk,qhe->khe", weights_low, attended_grad)
-    weight_grad = dot("qhe,khe->hqk", attended_grad, value_window)
-    row_total = jnp.sum(weights * weight_grad, axis=-1, keepdims=True)
-    score_grad = (weights * (weight_grad - row_total)).astype(BF)
-    query_grad = dot("hqk,khe->qhe", score_grad, key_window) * score_scale
-    key_grad = dot("hqk,qhe->khe", score_grad, queries) * score_scale
-    pair_grad = jnp.stack([key_grad.reshape(-1, width), value_grad.reshape(-1, width)])
-    own_pair = pair_grad[:, reach * tok_rows :]
-    for distance in range(reach, 0, -1):
-        offset = (reach - distance) * tok_rows
-        back = shifted(pair_grad[:, offset : offset + tok_rows].astype(BF), "seq", -distance)
-        own_pair = own_pair + back.astype(F32)
-    triple_grad = jnp.concatenate([query_grad.reshape(1, tok_rows, width), own_pair], 0).astype(BF)
-    proj_grad = dot("td,wte->wde", inputs, triple_grad).reshape(3 * width, width)
-    normed_grad = dot("wte,wde->td", triple_grad, w_proj)
-    hidden1_grad, gain10 = norm_backward(window_hidden, window_factor, gains[1, 0], normed_grad)
-    passed_grad = (middle1_grad + hidden1_grad).astype(BF)
-
-    upstream0 = passed_grad.astype(F32) * mask_rows
-    own_branch = upstream0.astype(BF)
-    branch_pair = jnp.concatenate([own_branch, swapped(own_branch)], 0)
-    middle0_grad, gain01, mlp0_grads = mlp_backward(
-        middle0, gains[0, 1], layer0, saved0, upstream0, branch_pair
-    )
-    g = middle0_grad.astype(BF).reshape(2, half, width)
+    mlp0_grads, mlp1_grads = tuple(grads[:3]), tuple(grads[3:6])
+    proj_grad, output_grad = grads[6:]
+    gain01, gain10, gain11 = gain_sums[1], gain_sums[2], gain_sums[3]
+    g = g.reshape(2, half, width)
     grid = (plan.depth, plan.side, plan.side)
+    half_width = width // 2
     blocks0 = [
         w.astype(BF).reshape(grid + (w.shape[0] // chips, w.shape[1])) for w in mlp0_grads
     ]
-    results = backward_call(plan, g, filt, v, pq, tapw, x_all, xs_all, blocks0)
-    half0, results = results[:3], results[3:]
+    blocks1 = [
+        w.astype(BF).reshape(grid + (w.shape[0] // chips, w.shape[1]))
+        for w in mlp1_grads
+        + (
+            proj_grad[: width + half_width],
+            proj_grad[width + half_width :],
+            output_grad[:half_width],
+            output_grad[half_width:],
+        )
+    ]
+    if plan.routed:
+        results = backward_call(plan, g, filt, v, pq, tapw, x_all, xs_all, blocks0 + blocks1)
+        half0, half1, attn_sums, results = results[:3], results[3:6], results[6:10], results[10:]
+    else:
+        results = backward_call(plan, g, filt, v, pq, tapw, x_all, xs_all, blocks0)
+        half0, results = results[:3], results[3:]
+        summed = [
+            lax.psum_scatter(
+                w.reshape((chips,) + w.shape[3:]), "seq", scatter_dimension=0, tiled=False
+            )
+            for w in blocks1
+        ]
+        half1, attn_sums = summed[:3], summed[3:]
     signal_grad = results[0].reshape(tok_rows, width)
     if plan.routed:
         maps_grad = results[1].astype(F32)
@@ -1382,41 +1779,19 @@
         )
         full = jnp.concatenate([full.reshape(-1, width), tap_full.reshape(-1, width)], 0)
         maps_grad = lax.psum_scatter(full, ("section", "seq"), scatter_dimension=0, tiled=True)
-    hidden_grad, gain00 = norm_backward(hidden, spectral_factor, gains[0, 0], signal_grad)
+    spectral_factor = lax.rsqrt(jnp.mean(hidden * hidden, axis=-1, keepdims=True) + EPSILON)
+    hidden_grad, gain00 = norm_backward(hidden, spectral_factor, gains[0], signal_grad)
     inputs_grad = (mask_rows * (middle0_grad + hidden_grad)).astype(BF)
 
-    proj_blocks = jnp.swapaxes(proj_grad.reshape(2, chips, proj_rows, width), 0, 1)
-    out_blocks = jnp.swapaxes(output_grad.reshape(2, chips, out_rows, width), 0, 1)
-    pieces = [
-        proj_blocks.reshape(chips, 2 * proj_rows, width),
-        out_blocks.reshape(chips, 2 * out_rows, width),
-        mlp1_grads[2].reshape(chips, ff_half, width),
-    ]
-    for w in mlp1_grads[:2]:
-        w = w.reshape(chips, gate_rows, 2 * width)
-        pieces += [w[:, :, :width], w[:, :, width:]]
-    packed_grads = jnp.concatenate([p.astype(BF) for p in pieces], 1)
-    summed = lax.psum_scatter(packed_grads, "seq", scatter_dimension=0, tiled=False)
-    columns = [summed[at + gate_rows * i : at + gate_rows * (i + 1)] for i in range(4)]
-    half1 = [
-        jnp.concatenate(columns[:2], 1),
-        jnp.concatenate(columns[2:], 1),
-        summed[at - ff_half : at],
-    ]
-    attn_parts = summed[: 2 * (proj_rows + out_rows)]
-    low_part = jnp.concatenate(
-        [attn_parts[:proj_rows], attn_parts[2 * proj_rows : 2 * proj_rows + out_rows]], 0
-    )
-    high_part = jnp.concatenate(
-        [attn_parts[proj_rows : 2 * proj_rows], attn_parts[2 * proj_rows + out_rows :]], 0
-    )
+    low_part = jnp.concatenate([attn_sums[0], attn_sums[2]], 0)
+    high_part = jnp.concatenate([attn_sums[1], attn_sums[3]], 0)
     attn_keep = jnp.where(core_zero, low_part, high_part).astype(F32)
-    attn_take = swapped(jnp.where(core_zero, high_part, low_part)).astype(F32)
+    attn_take = swapped(jnp.where(core_zero, high_part, low_part).astype(BF)).astype(F32)
     attn_sum = attn_keep + attn_take
     proj_out, out_out = attn_sum[:proj_rows], attn_sum[proj_rows:]
     outs = []
     for index in range(3):
-        zero, one = half0[index].astype(BF), half1[index]
+        zero, one = half0[index].astype(BF), half1[index].astype(BF)
         keep = jnp.where(core_zero, zero, one)
         take = swapped(jnp.where(core_zero, one, zero))
         low = jnp.where(core_zero, keep, take).astype(F32)

time: 507 us -> 416 us (0.82); the launches traced: 498 us -> 415 us
  Pallas kernels: 310 us -> 388 us
  starting transfers between devices: 41.2 us -> 1.27 us
  matrix products: 33.8 us -> 0 us
  waiting for transfers between devices: 27.3 us -> 0.01 us
  local copies, waits for them, and re-layouts: 41.6 us -> 16.7 us
  between operations: 18.7 us -> 1.02 us
  other arithmetic: 25.4 us -> 8.39 us
    pallas_call x2, Pallas kernels: 171 us -> 221 us  [the longest x1 141 us: backward_call(): pl.pallas_call(functools.partial(backward_kernel, plan, len(grads)), out_...]
    ppermute x8 -> x0, starting transfers between devices: 38.1 us -> none  [shifted(): return lax.ppermute(block, axis, route)]
    dot_general x29 -> x0, matrix products: 31.3 us -> none  [dot(): return jnp.einsum(formula, left, right, preferred_element_type=F32)]
    pallas_call x1, Pallas kernels: 124 us -> 153 us  [forward_call(): pl.pallas_call(functools.partial(forward_kernel, plan), out_shape=[jax.Sh...]
    ppermute x8 -> x0, waiting for transfers between devices: 18.2 us -> none  [shifted(): return lax.ppermute(block, axis, route)]
    unnamed x174 -> x31, local copies, waits for them, and re-layouts: 11.5 us -> 3.3 us
    convert_element_type x11 -> x1, other arithmetic: 7.25 us -> 0.02 us  [body(): jnp.where(core_zero, high_part, low_part).astype(BF)]
    all_gather x1 -> x0, waiting for transfers between devices: 7.18 us -> none  [body(): lax.all_gather(jnp.concatenate(pieces, 0), 'seq', axis=0, tiled=False)]
  transfers between devices with their start and end apart: 21 -> 4, of which waited for: 8 -> 0; matrix products, arithmetic and copies ran while one was open for 10% -> 4% of each run, Pallas kernels for 60% -> 3%
where the time goes in v3:
time: 416 us; the launch traced here: 415 us
  Pallas kernels  388 us (93%)
  local copies, waits for them, and re-layouts  16.7 us (4%)
  other arithmetic  8.39 us (2%)
    pallas_call x1, Pallas kernels, forward_call(): pl.pallas_call(functools.partial(forward_kernel, plan), out_shape=[jax.Sh...  153 us
    pallas_call x1, Pallas kernels, backward_call(): pl.pallas_call(functools.partial(backward_kernel, plan, len(grads)), out_...  141 us
    pallas_call x1, Pallas kernels, middle_call(): pl.pallas_call(functools.partial(middle_kernel, plan), out_shape=[jax.Sha...  79.9 us
    pallas_call x1, Pallas kernels, exit_call(): pl.pallas_call(functools.partial(exit_kernel, chips), out_shape=[jax.Shap...  13.8 us
  transfers between devices with their start and end apart: 4, of which 0 were waited for; matrix products, arithmetic and copies ran while one was open for 4% of the time, Pallas kernels for 3%

profile of v3, /device:TPU:0, one launch (start us, length us, event | category | flops | bytes accessed | tf_op | source)
XLA Modules:
  0.0 415.4 jit_solution(10622344490156855282)
XLA Ops:
  0.6 1.4 copy.25.refs_2_
  2.0 152.9 %spectral_forward.1 = (bf16[4,2,2,32,1024]{4,3,2,1,0:T(8,128)(2,1)}, bf16[4,2,2,32,1024]{4,3,2,1,0:T(8,128)(2,1)}, bf16[4,2,2,64,512]{4,3,2,1,0:T(8,128)(2,1)}, ...) custom-call(bf16[2,128,512]{2,1,0:T(8,128)(2,1)} %bitcast.88, ...), custom_call_target="tpu_custom_call" | custom-call | tf_op jit(solution)/shard_map/spectral_forward/pallas_call | solution.py:878
  154.9 79.9 %middle.1 = (bf16[128,512]{1,0:T(8,128)(2,1)}, bf16[128,512]{1,0:T(8,128)(2,1)}, f32[128,512]{1,0:T(8,128)}, f32[8,512]{1,0:T(8,128)}, bf16[512,1024]{1,0:T(8,12...) custom-call(f32[128,512]{1,0:T(8,128)} %bitcast.87, ...), custom_call_target="tpu_custom_call" | custom-call | tf_op jit(solution)/shard_map/middle/pallas_call | solution.py:1613
  234.9 2.7 fusion.3
  237.6 0.8 fusion.4
  238.4 141.4 %spectral_backward.1 = (f32[32,1024]{1,0:T(8,128)}, f32[32,1024]{1,0:T(8,128)}, f32[64,512]{1,0:T(8,128)}, f32[32,1024]{1,0:T(8,128)}, f32[32,1024]{1,0:T(8,128)...) custom-call(bf16[2,64,512]{2,1,0:T(8,128)(2,1)} %bitcast.89, ...), custom_call_target="tpu_custom_call" | custom-call | tf_op jit(solution)/shard_map/spectral_backward/pallas_call | solution.py:1219
  379.9 1.1 broadcast_select_fusion.11
  380.9 0.1 collective-permute-start.3
  381.0 1.0 broadcast_select_fusion.3
  382.0 0.6 collective-permute-start.2
  382.6 1.0 broadcast_select_fusion.7
  383.6 0.1 collective-permute-start.1
  383.6 0.9 constant_dynamic-update-slice_fusion.1
  384.5 0.9 constant_dynamic-update-slice_fusion.3
  385.5 0.8 constant_dynamic-update-slice_fusion
  386.3 0.6 collective-permute-start
  386.8 0.1 multiply_reduce_fusion.1
  386.9 0.7 slice.34
  387.7 0.7 stack.38
  388.4 0.7 slice_reduce_fusion
  389.2 0.1 fusion.1
  389.3 0.1 stack.35
  389.4 0.1 stack.39
  389.5 0.1 stack.36
  389.6 0.1 reduce
  389.7 0.1 multiply_convert_fusion
  389.8 0.1 copy.35
  390.1 0.1 copy.34
  390.3 0.7 pad.4.tiles
  391.0 0.7 broadcast_select_fusion.give
  391.7 13.8 %leave.1 = (bf16[128,512]{1,0:T(8,128)(2,1)}, f32[32,8,128]{2,1,0:T(8,128)}) custom-call(bf16[128,512]{1,0:T(8,128)(2,1)} %broadcast_select_fusion.give, f32[32,8,128]{2,1,0:T(8,128)} %pad.4.tiles), custom_call_target="tpu_custom_call" | custom-call | tf_op jit(solution)/shard_map/leave/pallas_call | solution.py:330
  405.5 1.0 select_bitcast_fusion.1
  406.5 1.4 convert_element_type.39
  407.9 0.6 slice_bitcast_fusion
  408.5 0.7 maximum_bitcast_fusion
  409.2 0.6 slice.39
  409.9 0.6 slice.40
  410.6 0.1 stack_reshape.19
  410.7 0.1 stack_reshape.18
  410.9 0.1 maximum_convert_fusion.1
  411.0 0.4 copy.31
  411.4 1.2 reshape.149
  412.6 0.1 stack_reshape.17
  412.8 0.1 stack_reshape.16
  412.9 0.1 maximum_convert_fusion
  413.0 0.4 copy.30
  413.4 1.2 reshape.148
  414.7 0.7 fusion.2
  (47 shorter events, 0.4 us)
Async XLA Ops:
  234.9 2.7 copy-start.3
  379.8 7.0 %copy-start = (f32[128,512]{1,0:T(8,128)S(1)}, f32[128,512]{1,0:T(8,128)}, u32[]{:S(2)}) copy-start(f32[128,512]{1,0:T(8,128)} %get-tuple-element.58.refs_1_) | copy-start | bytes 786436
  379.8 9.3 %copy-start.1 = (f32[2,64,512]{2,1,0:T(8,128)S(1)}, f32[2,64,512]{2,1,0:T(8,128)}, u32[]{:S(2)}) copy-start(f32[2,64,512]{2,1,0:T(8,128)} %get-tuple-element.88) | copy-start | bytes 786436
  379.9 9.7 %copy-start.10 = (f32[128,1]{1,0:T(8,128)S(1)}, f32[128,1]{1,0:T(8,128)}, u32[]{:S(2)}) copy-start(f32[128,1]{1,0:T(8,128)} %get-tuple-element.56.refs_3_) | copy-start | bytes 1540
  379.9 9.8 %copy-start.11 = (f32[128,512]{1,0:T(8,128)S(1)}, f32[128,512]{1,0:T(8,128)}, u32[]{:S(2)}) copy-start(f32[128,512]{1,0:T(8,128)} %get-tuple-element.72) | copy-start | bytes 786436
  380.9 33.7 %collective-permute-start.3 = (bf16[64,512]{1,0:T(8,128)(2,1)S(1)}, bf16[64,512]{1,0:T(8,128)(2,1)S(1)}, u32[]{:S(2)}, u32[]{:S(2)}) collective-permute-start(bf16[64,512]{1,0:T(8,128)(2,1)S(1)} %broadcast_select_fusion.11), channel_id=1, source_target_pairs={{0,16},{16,0},{1,17},{17,1},{2,18},{18,2},{3,19},{19,3},{4,20},{20... | collective-permute-start | bytes 196616 | tf_op jit(solution)/shard_map/ppermute | solution.py:1653
  382.0 28.5 %collective-permute-start.2 = (bf16[32,1024]{1,0:T(8,128)(2,1)S(1)}, bf16[32,1024]{1,0:T(8,128)(2,1)S(1)}, u32[]{:S(2)}, u32[]{:S(2)}) collective-permute-start(bf16[32,1024]{1,0:T(8,128)(2,1)S(1)} %broadcast_select_fusion.3), channel_id=1, source_target_pairs={{0,16},{16,0},{1,17},{17,1},{2,18},{18,2},{3,19},{19,3},{4,20},{20... | collective-permute-start | bytes 196616 | tf_op jit(solution)/shard_map/ppermute | solution.py:1653
  383.6 29.0 %collective-permute-start.1 = (bf16[32,1024]{1,0:T(8,128)(2,1)S(1)}, bf16[32,1024]{1,0:T(8,128)(2,1)S(1)}, u32[]{:S(2)}, u32[]{:S(2)}) collective-permute-start(bf16[32,1024]{1,0:T(8,128)(2,1)S(1)} %broadcast_select_fusion.7), channel_id=1, source_target_pairs={{0,16},{16,0},{1,17},{17,1},{2,18},{18,2},{3,19},{19,3},{4,20},{20... | collective-permute-start | bytes 196616 | tf_op jit(solution)/shard_map/ppermute | solution.py:1653
  384.5 5.5 %copy-start.12 = (bf16[128,512]{1,0:T(8,128)(2,1)S(1)}, bf16[128,512]{1,0:T(8,128)(2,1)}, u32[]{:S(2)}) copy-start(bf16[128,512]{1,0:T(8,128)(2,1)} %get-tuple-element.89) | copy-start | bytes 393220
  386.3 22.9 %collective-permute-start = (bf16[64,512]{1,0:T(8,128)(2,1)S(1)}, bf16[64,512]{1,0:T(8,128)(2,1)S(1)}, u32[]{:S(2)}, u32[]{:S(2)}) collective-permute-start(bf16[64,512]{1,0:T(8,128)(2,1)S(1)} %select_convert_fusion), channel_id=1, source_target_pairs={{0,16},{16,0},{1,17},{17,1},{2,18},{18,2},{3,19},{19,3},{4,20},{20... | collective-permute-start | bytes 196616 | tf_op jit(solution)/shard_map/ppermute | solution.py:1653
  389.7 16.8 %copy-start.2 = (bf16[816,512]{1,0:T(8,128)(2,1)S(1)}, bf16[816,512]{1,0:T(8,128)(2,1)}, u32[]{:S(2)}) copy-start(bf16[816,512]{1,0:T(8,128)(2,1)} %get-tuple-element.92) | copy-start | bytes 2506756
  405.5 2.4 copy-start.13
  406.5 4.1 copy-start.8
  406.5 4.1 copy-start.9
  410.5 2.0 copy-start.6
  410.6 2.0 copy-start.7
  412.6 2.0 copy-start.4
  412.6 2.0 copy-start.5

commit v4 on v3

--- a/solution.py
+++ b/solution.py
@@ -41,8 +41,11 @@
         self.routed = map_rows % PIECE == 0
         self.pieces = map_rows // PIECE
         self.f_rows = -(-self.local // 16) * 16
+        self.batch = 4 if self.local % 4 == 0 else 2
         self.ff = ff
         self.pick_here = ff // chips == LANES
+        self.late = self.pick_here and self.routed
+        self.routed = self.late
         self.side = max(1, math.isqrt(chips // 4))
         self.depth = chips // (self.side * self.side)
 
@@ -113,6 +116,46 @@
     return jnp.dot(left, right, preferred_element_type=F32)
 
 
+class Flat:
+    def __init__(self, ref):
+        self.ref = ref
+        self.split = len(ref.shape) == 5
+        if self.split:
+            depth, side, _, rows, _ = ref.shape
+            self.plane = side * side * rows
+
+    def columns(self, start, count):
+        sl = slice(start, start + count)
+        if self.split:
+            return self.ref[:, :, :, :, sl].reshape(-1, count)
+        return self.ref[:, sl]
+
+    def rows(self, start, count):
+        if self.split:
+            sl = slice(start // self.plane, (start + count) // self.plane)
+            return self.ref[sl].reshape(count, self.ref.shape[4])
+        return self.ref[start : start + count, :]
+
+    def all(self):
+        return self.ref[...].reshape(-1, self.ref.shape[-1])
+
+    def put_columns(self, start, value):
+        sl = slice(start, start + value.shape[1])
+        if self.split:
+            shape = self.ref.shape[:4] + (value.shape[1],)
+            self.ref[:, :, :, :, sl] = value.reshape(shape)
+        else:
+            self.ref[:, sl] = value
+
+    def put_rows(self, start, value):
+        count = value.shape[0]
+        if self.split:
+            sl = slice(start // self.plane, (start + count) // self.plane)
+            self.ref[sl] = value.reshape((count // self.plane,) + self.ref.shape[1:])
+        else:
+            self.ref[start : start + count, :] = value
+
+
 class Gather:
     def __init__(self, plan, shards, outs, send, recv):
         self.plan, self.shards, self.outs = plan, shards, outs
@@ -120,71 +163,102 @@
         self.section, chip = spot()
         self.z, self.y, self.x = plan.place(chip)
 
+    @staticmethod
+    def semaphores(plan, count):
+        return [
+            pltpu.SemaphoreType.DMA((count, 5)),
+            pltpu.SemaphoreType.DMA((count, 5 * plan.depth)),
+        ]
+
     def to(self, z, y, x):
         return self.section, self.plan.chip_at(z, y, x)
 
-    def parts(self, i):
+    def across(self, step, along_x):
+        side = self.plan.side
+        if along_x:
+            return self.to(self.z, self.y, lax.rem(self.x + step, side))
+        return self.to(self.z, lax.rem(self.y + step, side), self.x)
+
+    def routes(self, i):
         for number, (start, rows, x_first) in enumerate(self.plan.routes(self.shards[i].shape[0], i)):
-            out = self.outs[i]
-            sl = pl.ds(start, rows)
-            yield number, x_first, out, sl
+            yield number, x_first, self.outs[i], pl.ds(start, rows)
+
+    def level(self, t):
+        return lax.rem(self.z - t + self.plan.depth, self.plan.depth)
 
     def begin(self):
         plan = self.plan
         for i, shard in enumerate(self.shards):
-            spot_ref = self.outs[i].at[self.z, self.y, self.x]
+            home = self.outs[i].at[self.z, self.y, self.x]
             for step in range(1, plan.depth):
                 z = lax.rem(self.z + step, plan.depth)
                 push(
-                    shard, spot_ref, self.send.at[i, 0], self.recv.at[i, 0], self.to(z, self.y, self.x)
+                    shard, home, self.send.at[i, 0], self.recv.at[i, step], self.to(z, self.y, self.x)
                 ).start()
-            pltpu.make_async_copy(shard, spot_ref, self.recv.at[i, 0]).start()
-
-    def second(self):
-        side = self.plan.side
-        for i in range(len(self.shards)):
-            bytes_of(self.outs[i].at[:, self.y, self.x], self.recv.at[i, 0])
-            for number, x_first, out, sl in self.parts(i):
-                src = out.at[:, self.y, self.x, sl]
+            pltpu.make_async_copy(shard, home, self.recv.at[i, 0]).start()
+        self.second(0)
+
+    def second(self, t):
+        plan = self.plan
+        for i, shard in enumerate(self.shards):
+            z = self.level(t)
+            if t > 0:
+                bytes_of(self.outs[i].at[z, self.y, self.x], self.recv.at[i, t])
+            for number, x_first, out, sl in self.routes(i):
+                dst = out.at[z, self.y, self.x, sl]
+                src = shard.at[sl] if t == 0 else dst
+                for step in range(1, plan.side):
+                    push(
+                        src,
+                        dst,
+                        self.send.at[i, 1 + number],
+                        self.recv.at[i, (1 + number) * plan.depth + t],
+                        self.across(step, x_first),
+                    ).start()
+
+    def third(self, t):
+        plan, side = self.plan, self.plan.side
+        for i, shard in enumerate(self.shards):
+            z = self.level(t)
+            if t == 0:
+                pltpu.make_async_copy(
+                    shard, self.outs[i].at[z, self.y, self.x], self.recv.at[i, 0]
+                ).wait()
+            for number, x_first, out, sl in self.routes(i):
+                sem = self.recv.at[i, (1 + number) * plan.depth + t]
+                if x_first:
+                    bytes_of(out.at[z, self.y, pl.ds(0, side - 1), sl], sem)
+                    src = out.at[z, self.y, :, sl]
+                else:
+                    bytes_of(out.at[z, pl.ds(0, side - 1), self.x, sl], sem)
+                    src = out.at[z, :, self.x, sl]
                 for step in range(1, side):
-                    if x_first:
-                        peer = self.to(self.z, self.y, lax.rem(self.x + step, side))
-                    else:
-                        peer = self.to(self.z, lax.rem(self.y + step, side), self.x)
                     push(
-                        src, src, self.send.at[i, 1 + number], self.recv.at[i, 1 + number], peer
+                        src,
+                        src,
+                        self.send.at[i, 3 + number],
+                        self.recv.at[i, (3 + number) * plan.depth + t],
+                        self.across(step, not x_first),
                     ).start()
 
-    def third(self):
-        side = self.plan.side
-        for i in range(len(self.shards)):
-            for number, x_first, out, sl in self.parts(i):
-                sem = self.recv.at[i, 1 + number]
-                if x_first:
-                    bytes_of(out.at[:, self.y, pl.ds(0, side - 1), sl], sem)
-                    src = out.at[:, self.y, :, sl]
-                else:
-                    bytes_of(out.at[:, pl.ds(0, side - 1), self.x, sl], sem)
-                    src = out.at[:, :, self.x, sl]
-                for step in range(1, side):
-                    if x_first:
-                        peer = self.to(self.z, lax.rem(self.y + step, side), self.x)
-                    else:
-                        peer = self.to(self.z, self.y, lax.rem(self.x + step, side))
-                    push(
-                        src, src, self.send.at[i, 3 + number], self.recv.at[i, 3 + number], peer
-                    ).start()
-
     def end(self):
-        plan = self.plan
-        side = plan.side
+        plan, side = self.plan, self.plan.side
         for i in range(len(self.shards)):
             bytes_of(self.outs[i].at[pl.ds(0, plan.depth - 1), 0, 0], self.send.at[i, 0])
-            for number, x_first, out, sl in self.parts(i):
+            for number, x_first, out, sl in self.routes(i):
                 bytes_of(out.at[:, 0, pl.ds(0, side - 1), sl], self.send.at[i, 1 + number])
-                last = out.at[:, :, pl.ds(0, side - 1), sl]
-                bytes_of(last, self.recv.at[i, 3 + number])
-                bytes_of(last, self.send.at[i, 3 + number])
+                for t in range(plan.depth):
+                    bytes_of(
+                        out.at[0, :, pl.ds(0, side - 1), sl],
+                        self.recv.at[i, (3 + number) * plan.depth + t],
+                    )
+                bytes_of(out.at[:, :, pl.ds(0, side - 1), sl], self.send.at[i, 3 + number])
+
+    def stage(self, number):
+        if number > 0:
+            self.third(number - 1)
+        if 0 <= number < self.plan.depth - 1:
+            self.second(number + 1)
 
 
 class Scatter:
@@ -194,14 +268,21 @@
         for index, (rows, cols) in enumerate(shapes):
             for _, part, _ in plan.routes(rows, index):
                 for lead in (
-                    (plan.side - 1, plan.depth, plan.side),
+                    (plan.depth, plan.side - 1, plan.side),
                     (plan.depth, plan.side),
-                    (plan.side - 1, plan.depth),
+                    (plan.depth, plan.side - 1),
                     (plan.depth,),
                     (plan.depth - 1,),
                 ):
                     refs.append(pltpu.VMEM(lead + (part, cols), BF))
         return refs
+
+    @staticmethod
+    def semaphores(plan, count):
+        return [
+            pltpu.SemaphoreType.DMA((count, 6)),
+            pltpu.SemaphoreType.DMA((count, 4 * plan.depth + 2)),
+        ]
 
     def __init__(self, plan, grads, outs, buffers, send, recv):
         self.plan, self.grads, self.outs = plan, grads, outs
@@ -218,37 +299,42 @@
     def to(self, z, y, x):
         return self.section, self.plan.chip_at(z, y, x)
 
+    def level(self, t):
+        return lax.rem(self.z + 1 + t, self.plan.depth)
+
     def begin(self):
-        side = self.plan.side
-        for i, number, start, rows, x_first, (land, *_) in self.work:
-            grad, sl = self.grads[i], pl.ds(start, rows)
-            for step in range(1, side):
-                if x_first:
-                    y = lax.rem(self.y + step, side)
-                    src, peer = grad.at[:, y, :, sl], self.to(self.z, y, self.x)
-                else:
-                    x = lax.rem(self.x + step, side)
-                    src, peer = grad.at[:, :, x, sl], self.to(self.z, self.y, x)
-                push(
-                    src, land.at[step - 1], self.send.at[i, number], self.recv.at[i, number], peer
-                ).start()
-
-    def second(self):
         plan, side = self.plan, self.plan.side
+        for t in range(plan.depth):
+            z = self.level(t)
+            for i, number, start, rows, x_first, (land, *_) in self.work:
+                grad, sl = self.grads[i], pl.ds(start, rows)
+                for step in range(1, side):
+                    if x_first:
+                        y = lax.rem(self.y + step, side)
+                        src, peer = grad.at[z, y, :, sl], self.to(self.z, y, self.x)
+                    else:
+                        x = lax.rem(self.x + step, side)
+                        src, peer = grad.at[z, :, x, sl], self.to(self.z, self.y, x)
+                    push(
+                        src,
+                        land.at[t, step - 1],
+                        self.send.at[i, number],
+                        self.recv.at[i, number * plan.depth + t],
+                        peer,
+                    ).start()
+
+    def second(self, t):
+        plan, side = self.plan, self.plan.side
+        z = self.level(t)
         for i, number, start, rows, x_first, (land, part, land2, *_) in self.work:
             grad = self.grads[i]
-            bytes_of(land, self.recv.at[i, number])
-
-            def one(index, carry, grad=grad, land=land, part=part, start=start, rows=rows, x_first=x_first):
-                z, j = index // side, lax.rem(index, side)
+            bytes_of(land.at[t], self.recv.at[i, number * plan.depth + t])
+            for j in range(side):
                 y, x = (self.y, j) if x_first else (j, self.x)
                 total = grad[z, y, x, start : start + rows, :].astype(F32)
                 for step in range(side - 1):
-                    total = total + land[step, z, j].astype(F32)
-                part[z, j] = total.astype(BF)
-                return carry
-
-            lax.fori_loop(0, plan.depth * side, one, 0)
+                    total = total + land[t, step, j].astype(F32)
+                part[t, j] = total.astype(BF)
             for step in range(1, side):
                 if x_first:
                     j = lax.rem(self.x + step, side)
@@ -257,47 +343,48 @@
                     j = lax.rem(self.y + step, side)
                     peer = self.to(self.z, j, self.x)
                 push(
-                    part.at[:, j],
-                    land2.at[step - 1],
+                    part.at[t, j],
+                    land2.at[t, step - 1],
                     self.send.at[i, 2 + number],
-                    self.recv.at[i, 2 + number],
+                    self.recv.at[i, (2 + number) * plan.depth + t],
                     peer,
                 ).start()
 
-    def third(self):
+    def third(self, t):
         plan, side = self.plan, self.plan.side
         for i, number, start, rows, x_first, (_, part, land2, line, land3) in self.work:
-            bytes_of(land2, self.recv.at[i, 2 + number])
+            bytes_of(land2.at[t], self.recv.at[i, (2 + number) * plan.depth + t])
             mine = self.x if x_first else self.y
-
-            def one(z, carry, part=part, land2=land2, line=line, mine=mine):
-                total = part[z, mine].astype(F32)
-                for step in range(side - 1):
-                    total = total + land2[step, z].astype(F32)
-                line[z] = total.astype(BF)
-                return carry
-
-            lax.fori_loop(0, plan.depth, one, 0)
-            for step in range(1, plan.depth):
-                z = lax.rem(self.z + step, plan.depth)
+            total = part[t, mine].astype(F32)
+            for step in range(side - 1):
+                total = total + land2[t, step].astype(F32)
+            line[t] = total.astype(BF)
+            if t < plan.depth - 1:
                 push(
-                    line.at[z],
-                    land3.at[step - 1],
+                    line.at[t],
+                    land3.at[t],
                     self.send.at[i, 4 + number],
-                    self.recv.at[i, 4 + number],
-                    self.to(z, self.y, self.x),
+                    self.recv.at[i, 4 * plan.depth + number],
+                    self.to(self.level(t), self.y, self.x),
                 ).start()
 
     def end(self):
+        plan = self.plan
         for i, number, start, rows, x_first, (land, part, land2, line, land3) in self.work:
-            bytes_of(land3, self.recv.at[i, 4 + number])
-            total = line[self.z].astype(F32)
-            for step in range(self.plan.depth - 1):
+            bytes_of(land3, self.recv.at[i, 4 * plan.depth + number])
+            total = line[plan.depth - 1].astype(F32)
+            for step in range(plan.depth - 1):
                 total = total + land3[step].astype(F32)
             self.outs[i][start : start + rows, :] = total
             bytes_of(land, self.send.at[i, number])
             bytes_of(land2, self.send.at[i, 2 + number])
             bytes_of(land3, self.send.at[i, 4 + number])
+
+    def stage(self, number):
+        if number < self.plan.depth:
+            self.second(number)
+        if number > 0:
+            self.third(number - 1)
 
 
 def exit_kernel(chips, give, tiles, take, land, send, recv, gain_send, gain_recv):
@@ -381,10 +468,10 @@
                 rolled = pltpu.roll(
                     spread, (shift + start) % span, 1, stride=1, stride_axis=0
                 ).astype(BF)
-                strip[2 * k + parity, LANES + start : LANES + start + part, :] = rolled[
+                strip[parity, k, LANES + start : LANES + start + part, :] = rolled[
                     :, : plan.length
                 ]
-                strip[2 * k + parity, start : start + part, :] = rolled[
+                strip[parity, k, start : start + part, :] = rolled[
                     :, LANES : LANES + plan.length
                 ]
         return carry
@@ -392,38 +479,52 @@
     lax.fori_loop(0, plan.local, one, 0)
 
 
-def owner_pieces(plan, act, first=0, last=None):
+def sizes(plan):
+    size = plan.jb // PIECE
+    while size:
+        yield size
+        size //= 2
+
+
+def owner_pieces(plan, act):
     section, chip = spot()
-    dev = section * plan.chips + chip
-    per_map = plan.width // PIECE
+    start = plan.pieces * (section * plan.chips + chip)
     per_block = plan.jb // PIECE
 
-    def unit(m, carry):
-        g = plan.pieces * dev + m
-        which = g // per_map
-        inside = lax.rem(g, per_map)
-        b = inside // per_block
-        sub = lax.rem(inside, per_block)
+    def block(j, carry):
+        number = start // per_block + j
+        base = number * per_block
+        low = jnp.maximum(start - base, 0)
+        high = jnp.minimum(start + plan.pieces - base, per_block)
+        count = jnp.maximum(high - low, 0)
+        which = number // plan.cols_in
+        b = lax.rem(number, plan.cols_in)
         sign = which // plan.filters
         full = lax.rem(which, plan.filters)
         group = full // plan.local
         k = lax.rem(full, plan.local)
-
-        @pl.when(sign < 2)
-        def _():
-            for a in range(plan.cols_out):
-                target = a + plan.cols_out * (b + plan.cols_in * group)
-                act(m, False, k, sub, a, sign, target)
-
-        @pl.when(sign >= 2)
-        def _():
-            for a in range(plan.cols_out):
-                for core in range(2):
-                    act(m, True, full, sub, a, core, a + plan.cols_out * b)
+        for size in sizes(plan):
+            done = count // (2 * size) * (2 * size)
+            here = lax.rem(count // size, 2) == 1
+            source = base + low - start + done
+            target = low + done
+
+            @pl.when(jnp.logical_and(here, sign < 2))
+            def _():
+                for a in range(plan.cols_out):
+                    to_chip = a + plan.cols_out * (b + plan.cols_in * group)
+                    act(source, size, False, k, target, a, sign, to_chip)
+
+            @pl.when(jnp.logical_and(here, sign >= 2))
+            def _():
+                for a in range(plan.cols_out):
+                    for core in range(2):
+                        to_chip = a + plan.cols_out * (b + plan.cols_in * (plan.groups - 1))
+                        act(source, size, True, full, target, a, core, to_chip)
 
         return carry
 
-    lax.fori_loop(first, plan.pieces if last is None else last, unit, 0)
+    lax.fori_loop(0, plan.pieces // per_block + 2, block, 0)
 
 
 def forward_kernel(plan, *refs):
@@ -435,7 +536,7 @@
     else:
         mine_ref, other_ref, taps_ref = refs[9:12]
         rest = refs[12:]
-    full_weights, rest = rest[:10], rest[10:]
+    full_weights, rest = rest[:8], rest[8:]
     (
         conv_ref,
         hidden_ref,
@@ -452,14 +553,11 @@
         io_own,
         io_sib,
         gain_tile,
-        gain_land,
         gate_half,
         gate_shard,
         up_half,
         up_shard,
         down_shard,
-        proj_shard,
-        attn_shard,
         u_ref,
         f_ref,
         x_buf,
@@ -474,6 +572,7 @@
         taps,
         pq,
         acc,
+        joined,
         y_buf,
         land,
         stage,
@@ -511,8 +610,8 @@
     for i in range(2):
         io_own[i] = flat_dot(order, io_ref[i]).astype(BF)
     cols = gain_ref.shape[1]
-    gain_tile[...] = jnp.zeros_like(gain_tile)
-    gain_tile[0:2, 0:cols] = gain_ref[...].astype(F32)
+    gain_tile[0] = jnp.zeros((8, LANES), F32)
+    gain_tile[0, 0:2, 0:cols] = gain_ref[...].astype(F32)
     if plan.pick_here:
         lane = lax.broadcasted_iota(jnp.int32, (gate_raw.shape[0], LANES), 1)
         low = lane < half
@@ -531,25 +630,12 @@
             halves[...] = raw[1 - section]
     part = down_shard.shape[1]
     down_shard[section] = down_raw[pl.ds(pl.multiple_of(part * section, 16), part), :]
-    proj_shard[section] = proj_raw[...]
-    attn_shard[section] = attn_raw[...]
     greeted()
     io_swap = push(io_own, io_sib, io_sem.at[0], io_sem.at[1], sibling)
     io_swap.start()
 
-    def send_gain(step, carry):
-        peer = lax.rem(dev + step, 2 * chips)
-        push(
-            gain_tile,
-            gain_land.at[section, chip],
-            gain_send,
-            gain_recv,
-            (peer // chips, lax.rem(peer, chips)),
-        ).start()
-        return carry
-
-    lax.fori_loop(1, 2 * chips, send_gain, 0)
-    pltpu.make_async_copy(gain_tile, gain_land.at[section, chip], gain_recv).start()
+    gain_swap = push(gain_tile.at[0], gain_tile.at[1], gain_send, gain_recv, sibling)
+    gain_swap.start()
     shares = [
         push(src, dst, s_send.at[i], s_recv.at[i], sibling)
         for i, (src, dst) in enumerate(
@@ -560,8 +646,6 @@
                     down_raw.at[pl.ds(pl.multiple_of(part * (1 - section), 16), part), :],
                     down_shard.at[section],
                 ),
-                (proj_shard.at[section], proj_shard.at[section]),
-                (attn_shard.at[section], attn_shard.at[section]),
             )
         )
     ]
@@ -570,14 +654,15 @@
 
     if plan.routed:
 
-        def places(m, tap, k, sub, a):
-            src = maps_ref.at[pl.ds(PIECE * m, PIECE), pl.ds(a * ia, ia)]
+        def places(source, size, tap, k, target, a):
+            rows = size * PIECE
+            src = maps_ref.at[pl.ds(PIECE * source, rows), pl.ds(a * ia, ia)]
             if tap:
-                return src, taps.at[pl.ds(jb * k + PIECE * sub, PIECE), :], t_recv
-            return src, mine.at[k, pl.ds(PIECE * sub, PIECE), :], m_recv
-
-        def start_piece(m, tap, k, sub, a, to_section, to_chip):
-            src, dst, sem = places(m, tap, k, sub, a)
+                return src, taps.at[pl.ds(jb * k + PIECE * target, rows), :], t_recv
+            return src, mine.at[k, pl.ds(PIECE * target, rows), :], m_recv
+
+        def start_piece(source, size, tap, k, target, a, to_section, to_chip):
+            src, dst, sem = places(source, size, tap, k, target, a)
             here = to_section * chips + to_chip == dev
 
             @pl.when(here)
@@ -588,20 +673,26 @@
             def _():
                 push(src, dst, m_send, sem, (to_section, to_chip)).start()
 
-        def drain_piece(m, tap, k, sub, a, to_section, to_chip):
-            src, dst, sem = places(m, tap, k, sub, a)
+        def drain_piece(source, size, tap, k, target, a, to_section, to_chip):
+            src, dst, sem = places(source, size, tap, k, target, a)
 
             @pl.when(to_section * chips + to_chip != dev)
             def _():
                 push(src, dst, m_send, sem, (to_section, to_chip)).wait_send()
 
-        owner_pieces(plan, start_piece, 0, plan.pieces // 3)
+        owner_pieces(plan, start_piece)
 
     lag = lax.broadcasted_iota(jnp.int32, (rows_here, LANES), 0)
     lane = lax.broadcasted_iota(jnp.int32, (rows_here, LANES), 1)
     stretch = lax.rem(lane, half)
     backwards = jnp.where(lag == 2 * (half - 1 - stretch) + lane // half, 1.0, 0.0).astype(BF)
     plain = jnp.where(lag == 2 * stretch + lane // half, 1.0, 0.0).astype(BF)
+    gain_swap.wait_recv()
+    core_zero = section == 0
+    own_gain, sib_gain = gain_tile[0], gain_tile[1]
+    gain_rows = jnp.concatenate(
+        [jnp.where(core_zero, own_gain, sib_gain), jnp.where(core_zero, sib_gain, own_gain)], 0
+    ).astype(BF)
     for group in range(plan.groups):
         source = lax.broadcasted_iota(jnp.int32, (plan.filters, plan.f_rows), 0)
         target = lax.broadcasted_iota(jnp.int32, (plan.filters, plan.f_rows), 1)
@@ -610,70 +701,28 @@
         ).astype(BF)
         some = flat_dot(filters_ref[...], chosen).astype(BF)
         f_ref[group, : plan.f_rows, :] = cols_dot(some, backwards).astype(BF)
-        f_ref[group, plan.f_rows :, :] = cols_dot(some, plain).astype(BF)
-
-    bytes_of(gain_land, gain_recv)
-    pick_row = lax.broadcasted_iota(jnp.int32, (LANES, plan.width), 0)
-    pick_col = lax.broadcasted_iota(jnp.int32, (LANES, plan.width), 1)
-    repeat = jnp.where(pick_row == lax.rem(pick_col, cols), 1.0, 0.0).astype(BF)
-    tile_row = lax.broadcasted_iota(jnp.int32, (chips * 8, plan.width), 0)
-    tile_col = lax.broadcasted_iota(jnp.int32, (chips * 8, plan.width), 1)
-    for layer in range(2):
-        spread = flat_dot(gain_land[layer].reshape(chips * 8, LANES).astype(BF), repeat)
-        for number in range(2):
-            here = (tile_row // 8 == tile_col // cols) & (lax.rem(tile_row, 8) == number)
-            gains_ref[2 * layer + number : 2 * layer + number + 1, :] = jnp.sum(
-                jnp.where(here, spread, 0.0), axis=0, keepdims=True
-            )
-    position = lax.broadcasted_iota(jnp.int32, (rows_here, 1), 0)
-    position = chip * rows_here + 2 * lax.rem(position, half) + position // half
-    length_own = jnp.where(section == 0, lengths_ref[0], lengths_ref[1])
-    length_other = jnp.where(section == 0, lengths_ref[1], lengths_ref[0])
-    mask = jnp.where(position < length_own, 1.0, 0.0)
-    mask_other = jnp.where(position < length_other, 1.0, 0.0)
-    mask_ref[...] = mask
-    io_swap.wait()
-    core_zero = section == 0
-    hidden = jnp.where(core_zero, io_own[0], io_sib[1]).astype(F32) * mask
-    hidden_ref[...] = hidden
-    factor = lax.rsqrt(jnp.mean(hidden * hidden, axis=-1, keepdims=True) + EPSILON)
-    u = (hidden * factor * gains_ref[0:1, :]).astype(BF)
-    for b in range(plan.cols_in):
-        u_ref[b, :, :jb] = u[:half, b * jb : (b + 1) * jb]
-        u_ref[b, :, jb:] = u[half:, b * jb : (b + 1) * jb]
-
-    def send_u(step, carry):
+        f_ref[group, plan.f_rows : 2 * plan.f_rows, :] = cols_dot(some, plain).astype(BF)
+        f_ref[group, 2 * plan.f_rows :, :] = gain_rows
+
+    def send_f(step, carry):
         peer = lax.rem(chip + step, chips)
-        b = lax.rem(peer // plan.cols_out, plan.cols_in)
         group = peer // (plan.cols_out * plan.cols_in)
-        push(
-            u_ref.at[b],
-            x_buf.at[pl.ds(half * chip, half), :],
-            u_send,
-            x_recv,
-            (section, peer),
-        ).start()
         push(f_ref.at[group], f_land.at[chip], f_send, f_recv, (section, peer)).start()
         return carry
 
-    lax.fori_loop(1, chips, send_u, 0)
-    pltpu.make_async_copy(
-        u_ref.at[lax.rem(chip // plan.cols_out, plan.cols_in)],
-        x_buf.at[pl.ds(half * chip, half), :],
-        x_recv,
-    ).start()
+    lax.fori_loop(1, chips, send_f, 0)
     pltpu.make_async_copy(f_ref.at[my_group], f_land.at[chip], f_recv).start()
-    if plan.routed:
-        owner_pieces(plan, start_piece, plan.pieces // 3)
-
     for share in shares:
         share.wait_recv()
+    second_layer = (gate_shard.at[1], up_shard.at[1], down_shard.at[1])
+    parts = [
+        (0, (gate_shard.at[0], up_shard.at[0], down_shard.at[0])),
+        (3, (proj_raw, attn_raw)),
+    ]
+    if not plan.late:
+        parts.append((5, second_layer))
     groups = []
-    for first, arrays in (
-        (0, (gate_shard.at[0], up_shard.at[0], down_shard.at[0])),
-        (3, (proj_shard.at[0], proj_shard.at[1], attn_shard.at[0], attn_shard.at[1])),
-        (7, (gate_shard.at[1], up_shard.at[1], down_shard.at[1])),
-    ):
+    for first, arrays in parts:
         last = first + len(arrays)
         groups.append(
             Gather(
@@ -684,15 +733,72 @@
                 w_recv.at[pl.ds(first, len(arrays))],
             )
         )
-    layer0, attention, layer1 = groups
-    for group in groups:
+    layer0, attention = groups[:2]
+    layer0.begin()
+    position = lax.broadcasted_iota(jnp.int32, (rows_here, 1), 0)
+    position = chip * rows_here + 2 * lax.rem(position, half) + position // half
+    length_own = jnp.where(section == 0, lengths_ref[0], lengths_ref[1])
+    length_other = jnp.where(section == 0, lengths_ref[1], lengths_ref[0])
+    mask = jnp.where(position < length_own, 1.0, 0.0)
+    mask_other = jnp.where(position < length_other, 1.0, 0.0)
+    mask_ref[...] = mask
+    io_swap.wait()
+    bytes_of(f_land, f_recv)
+    pick_row = lax.broadcasted_iota(jnp.int32, (LANES, plan.width), 0)
+    pick_col = lax.broadcasted_iota(jnp.int32, (LANES, plan.width), 1)
+    repeat = jnp.where(pick_row == lax.rem(pick_col, cols), 1.0, 0.0).astype(BF)
+    tile_row = lax.broadcasted_iota(jnp.int32, (chips * 16, plan.width), 0)
+    tile_col = lax.broadcasted_iota(jnp.int32, (chips * 16, plan.width), 1)
+    rows_all = f_land[:, 2 * plan.f_rows :, :].reshape(chips * 16, LANES)
+    spread = jnp.where(
+        tile_row // 16 == tile_col // cols, flat_dot(rows_all, repeat), 0.0
+    ).astype(BF)
+    gain_row = lax.broadcasted_iota(jnp.int32, (16, chips * 16), 0)
+    gain_col = lax.broadcasted_iota(jnp.int32, (16, chips * 16), 1)
+    gather_rows = jnp.where(lax.rem(gain_col, 16) == gain_row, 1.0, 0.0).astype(BF)
+    gathered = flat_dot(gather_rows, spread)
+    gains_ref[0:2, :] = gathered[0:2, :]
+    gains_ref[2:4, :] = gathered[8:10, :]
+    gains_ref[4:8, :] = jnp.zeros((4, plan.width), F32)
+    hidden = jnp.where(core_zero, io_own[0], io_sib[1]).astype(F32) * mask
+    hidden_ref[...] = hidden
+    factor = lax.rsqrt(jnp.mean(hidden * hidden, axis=-1, keepdims=True) + EPSILON)
+    u = (hidden * factor * gains_ref[0:1, :]).astype(BF)
+    for b in range(plan.cols_in):
+        u_ref[b, :, :jb] = u[:half, b * jb : (b + 1) * jb]
+        u_ref[b, :, jb:] = u[half:, b * jb : (b + 1) * jb]
+
+    def send_u(step, carry):
+        peer = lax.rem(chip + step, chips)
+        b = lax.rem(peer // plan.cols_out, plan.cols_in)
+        push(
+            u_ref.at[b],
+            x_buf.at[pl.ds(half * chip, half), :],
+            u_send,
+            x_recv,
+            (section, peer),
+        ).start()
+        return carry
+
+    lax.fori_loop(1, chips, send_u, 0)
+    pltpu.make_async_copy(
+        u_ref.at[lax.rem(chip // plan.cols_out, plan.cols_in)],
+        x_buf.at[pl.ds(half * chip, half), :],
+        x_recv,
+    ).start()
+    for group in groups[1:]:
         group.begin()
+    kept_copies = []
+    if plan.late:
+        for i, (src, dst) in enumerate(zip(second_layer, full_weights[5:])):
+            kept_copies.append(pltpu.make_async_copy(src, dst, w_recv.at[5 + i, 0]))
+            kept_copies[-1].start()
     cot_own = jnp.where(core_zero, io_sib[0], io_own[1]).astype(F32) * mask
     cot_other = jnp.where(core_zero, io_sib[1], io_own[0]).astype(F32) * mask_other
     upstream_ref[...] = cot_own
     pair_ref[:rows_here, :] = cot_own.astype(BF)
     pair_ref[rows_here:, :] = cot_other.astype(BF)
-    bytes_of(f_land, f_recv)
+    layer0.stage(0)
     filter_rows(plan, f_land, table, 0, False)
     build_strips(plan, table, strip, False)
     filt_out = pltpu.make_async_copy(f_land, filt_ref, out_sem.at[0])
@@ -703,17 +809,18 @@
         swap = push(mine, other, o_send, o_recv, (1 - section, chip))
         swap.start()
 
-        @pl.when(my_group == 0)
+        @pl.when(my_group == plan.groups - 1)
         def _():
             bytes_of(taps, t_recv)
 
-        @pl.when(my_group != 0)
+        @pl.when(my_group != plan.groups - 1)
         def _():
             taps[...] = jnp.zeros_like(taps)
     else:
         for src, dst in ((mine_ref, mine), (other_ref, other), (taps_ref, taps)):
             pltpu.sync_copy(src, dst)
 
+    layer0.stage(1)
     bytes_of(x_buf, x_recv)
     x_out = pltpu.make_async_copy(x_buf, x_ref, out_sem.at[1])
     x_out.start()
@@ -747,58 +854,64 @@
     taps_out = pltpu.make_async_copy(taps, tapw_ref, out_sem.at[4])
     taps_out.start()
 
-    layer0.second()
+    layer0.stage(2)
+    attention.stage(0)
+    batch = plan.batch
     for i in range(plan.blocks):
         if i == 1:
-            attention.second()
-        if i == plan.blocks // 2:
-            layer0.third()
-        if i == plan.blocks - 1:
-            layer1.second()
-            attention.third()
+            layer0.stage(3)
+            attention.stage(1)
+        if i == 2:
+            layer0.stage(4)
+            attention.stage(2)
+        if i == 3:
+            attention.stage(3)
+            attention.stage(4)
         rows = slice(BLOCK * i, BLOCK * (i + 1))
         depth = BLOCK * (i + 1)
         offset = plan.length - depth
         x_now = x_buf[rows, :]
         s_now = xs_buf[rows, :]
-        acc[0] = jnp.dot(
-            jnp.concatenate([x_now[:, :jb], s_now[:, jb:]], 1),
-            taps[: 2 * jb, :],
-            preferred_element_type=F32,
-        ) + jnp.dot(s_now[:, :jb], taps[2 * jb :, :], preferred_element_type=F32)
-        acc[1] = jnp.dot(
-            jnp.concatenate([x_now[:, jb:], x_now[:, :jb]], 1),
-            taps[: 2 * jb, :],
-            preferred_element_type=F32,
-        ) + jnp.dot(s_now[:, jb:], taps[2 * jb :, :], preferred_element_type=F32)
-
-        def step(k, carry, i=i, depth=depth, offset=offset):
-            slot = lax.rem(k, 2)
+        acc[:BLOCK] = flat_dot(
+            jnp.concatenate([x_now[:, :jb], s_now[:, jb:]], 1), taps[: 2 * jb, :]
+        ) + flat_dot(s_now[:, :jb], taps[2 * jb :, :])
+        acc[BLOCK:] = flat_dot(
+            jnp.concatenate([x_now[:, jb:], x_now[:, :jb]], 1), taps[: 2 * jb, :]
+        ) + flat_dot(s_now[:, jb:], taps[2 * jb :, :])
+
+        def step(t, carry, i=i, depth=depth, offset=offset):
+            count = plan.local // batch * i + t
+            slot = lax.rem(count, 2)
+            some = pl.ds(batch * t, batch)
             v_copy = pltpu.make_async_copy(
-                stage.at[slot], v_ref.at[k, :, pl.ds(BLOCK * i, BLOCK), :], v_sem.at[slot]
+                stage.at[slot], v_ref.at[some, :, pl.ds(BLOCK * i, BLOCK), :], v_sem.at[slot]
             )
-            even = jnp.dot(
-                strip[2 * k, :, offset:], x_buf[:depth, :], preferred_element_type=F32
+            even = flat_dot(
+                strip[0, some, :, offset:].reshape(batch * BLOCK, depth), x_buf[:depth, :]
             ).astype(BF)
-            odd = jnp.dot(
-                strip[2 * k + 1, :, offset:], xo_buf[:depth, :], preferred_element_type=F32
+            odd = flat_dot(
+                strip[1, some, :, offset:].reshape(batch * BLOCK, depth), xo_buf[:depth, :]
             ).astype(BF)
-            first = jnp.concatenate([even[:, :jb], odd[:, jb:]], 1)
-            second = jnp.concatenate([even[:, jb:], odd[:, :jb]], 1)
             if i == 0:
-                pl.when(k >= 2)(v_copy.wait)
+                pl.when(t >= 2)(v_copy.wait)
             else:
                 v_copy.wait()
-            stage[slot, 0] = first
-            stage[slot, 1] = second
+            for k in range(batch):
+                here = slice(BLOCK * k, BLOCK * (k + 1))
+                first = jnp.concatenate([even[here, :jb], odd[here, jb:]], 1)
+                second = jnp.concatenate([even[here, jb:], odd[here, :jb]], 1)
+                stage[slot, k, 0] = first
+                stage[slot, k, 1] = second
+                lanes = slice(2 * jb * k, 2 * jb * (k + 1))
+                joined[:BLOCK, lanes] = first
+                joined[BLOCK:, lanes] = second
             v_copy.start()
-            acc[0] += jnp.dot(first, pq[k], preferred_element_type=F32)
-            acc[1] += jnp.dot(second, pq[k], preferred_element_type=F32)
+            acc[...] += flat_dot(joined[...], pq[some].reshape(batch * 2 * jb, ia))
             return carry
 
-        lax.fori_loop(0, plan.local, step, 0)
-        y_buf[0, rows, :] = acc[0].astype(BF)
-        y_buf[1, rows, :] = acc[1].astype(BF)
+        lax.fori_loop(0, plan.local // batch, step, 0)
+        y_buf[0, rows, :] = acc[:BLOCK].astype(BF)
+        y_buf[1, rows, :] = acc[BLOCK:].astype(BF)
 
         def give(r, carry, i=i):
             peer = BLOCK // half * i + r
@@ -816,10 +929,12 @@
 
         lax.fori_loop(0, BLOCK // half, give, 0)
 
-    layer1.third()
+    if not plan.late:
+        for turn_number in range(plan.depth + 1):
+            groups[2].stage(turn_number)
     for slot in range(2):
         pltpu.make_async_copy(
-            stage.at[slot], v_ref.at[slot, :, pl.ds(0, BLOCK), :], v_sem.at[slot]
+            stage.at[slot], v_ref.at[pl.ds(0, batch), :, pl.ds(0, BLOCK), :], v_sem.at[slot]
         ).wait()
     bytes_of(x_buf.at[pl.ds(0, half * (chips - 1)), :], u_send)
     bytes_of(f_land.at[pl.ds(0, chips - 1)], f_send)
@@ -837,13 +952,9 @@
     bytes_of(land.at[pl.ds(0, chips - 1)], c_send)
     for group in groups:
         group.end()
-    def drain_gain(step, carry):
-        push(
-            gain_tile, gain_land.at[section, chip], gain_send, gain_recv, sibling
-        ).wait_send()
-        return carry
-
-    lax.fori_loop(1, 2 * chips, drain_gain, 0)
+    for copy in kept_copies:
+        copy.wait()
+    gain_swap.wait_send()
     for share in shares:
         share.wait_send()
 
@@ -860,8 +971,9 @@
     down_share = (down[0] // 2, width)
     grid = (plan.depth, plan.side, plan.side)
     layer = [share, share, down_share]
-    gathered = layer + [proj, proj, attn, attn] + layer
-    shapes = [(grid + w, BF) for w in gathered] + [
+    gathered = [grid + w for w in layer + [proj, attn]]
+    gathered += layer if plan.late else [grid + w for w in layer]
+    shapes = [(w, BF) for w in gathered] + [
         ((2, half, width), F32),
         ((rows, width), F32),
         ((rows, width), F32),
@@ -873,53 +985,52 @@
         ((ORDER * jb, ia), BF),
         ((plan.length, 2 * jb), BF),
         ((plan.length, 2 * jb), BF),
-        ((chips, 2 * plan.f_rows, LANES), BF),
+        ((chips, 2 * plan.f_rows + 16, LANES), BF),
     ]
     return pl.pallas_call(
         functools.partial(forward_kernel, plan),
         out_shape=[jax.ShapeDtypeStruct(s, d) for s, d in shapes],
         in_specs=[vmem_spec] * 3
         + [smem_spec]
-        + [vmem_spec] * 5
-        + [any_spec] * len(maps),
-        out_specs=[any_spec] * 10 + [vmem_spec] * 6 + [any_spec] * 6,
+        + [vmem_spec] * 3
+        + [any_spec] * 2
+        + [vmem_spec if plan.routed else any_spec] * len(maps),
+        out_specs=[any_spec] * 8 + [vmem_spec] * 6 + [any_spec] * 6,
         scratch_shapes=[
             pltpu.VMEM((2, rows, width), BF),
             pltpu.VMEM((2, rows, width), BF),
-            pltpu.VMEM((8, LANES), F32),
-            pltpu.VMEM((2, chips, 8, LANES), F32),
+            pltpu.VMEM((2, 8, LANES), F32),
             pltpu.VMEM(share, BF),
             pltpu.VMEM((2,) + share, BF),
             pltpu.VMEM(share, BF),
             pltpu.VMEM((2,) + share, BF),
             pltpu.VMEM((2,) + down_share, BF),
-            pltpu.VMEM((2,) + proj, BF),
-            pltpu.VMEM((2,) + attn, BF),
             pltpu.VMEM((plan.cols_in, half, 2 * jb), BF),
-            pltpu.VMEM((plan.groups, 2 * plan.f_rows, LANES), BF),
+            pltpu.VMEM((plan.groups, 2 * plan.f_rows + 16, LANES), BF),
             pltpu.VMEM((plan.length, 2 * jb), BF),
             pltpu.VMEM((plan.length, 2 * jb), BF),
             pltpu.VMEM((plan.length, 2 * jb), BF),
             pltpu.VMEM((plan.length + 8, 2 * jb), F32),
-            pltpu.VMEM((chips, 2 * plan.f_rows, LANES), BF),
+            pltpu.VMEM((chips, 2 * plan.f_rows + 16, LANES), BF),
             pltpu.VMEM((2, plan.f_rows, plan.length + BLOCK), F32),
-            pltpu.VMEM((2 * plan.local, BLOCK, plan.length), BF),
+            pltpu.VMEM((2, plan.local, BLOCK, plan.length), BF),
             pltpu.VMEM((plan.local, jb, ia), BF),
             pltpu.VMEM((plan.local, jb, ia), BF),
             pltpu.VMEM((ORDER * jb, ia), BF),
             pltpu.VMEM((plan.local, 2 * jb, ia), BF),
-            pltpu.VMEM((2, BLOCK, ia), F32),
+            pltpu.VMEM((2 * BLOCK, ia), F32),
+            pltpu.VMEM((2 * BLOCK, plan.batch * 2 * jb), BF),
             pltpu.VMEM((2, plan.length, ia), BF),
             pltpu.VMEM((chips, 2, half, ia), BF),
-            pltpu.VMEM((2, 2, BLOCK, 2 * jb), BF),
+            pltpu.VMEM((2, plan.batch, 2, BLOCK, 2 * jb), BF),
             dma((2,)),
             dma,
             dma,
-            dma((5,)),
-            dma((5,)),
+            dma((3,)),
+            dma((3,)),
         ]
         + [dma] * 11
-        + [dma((2,)), dma((5,)), dma((10, 5)), dma((10, 5))],
+        + [dma((2,)), dma((5,)), *Gather.semaphores(plan, 8)],
         compiler_params=pltpu.CompilerParams(
             collective_id=2, has_side_effects=True, vmem_limit_bytes=VMEM_LIMIT
         ),
@@ -930,13 +1041,17 @@
 def backward_kernel(plan, number, *refs):
     g_ref, filt_ref, v_ref, pq, tapw, x_ref, xs_ref = refs[:7]
     grads, rest = refs[7 : 7 + number], refs[7 + number :]
-    sums, rest = rest[:number], rest[number:]
-    du_ref = rest[0]
-    if plan.routed:
-        dmaps_ref = rest[1]
-        rest = rest[2:]
+    if plan.late:
+        hidden_ref, gains_ref, mask_ref, dmid_ref, out_ref, gain_sums_ref, *half1 = rest[:9]
+        res_ref, gate_ref, up_ref, down_ref, proj_ref, attn_ref, gain_out, dmaps_ref = rest[9:17]
+        du_ref, gain_buf, gain_land, give_res, *half_parts = rest[17:30]
+        half0, crossing, arrived = half_parts[:3], half_parts[3:6], half_parts[6:9]
+        e_send, e_recv, n_send, n_recv = rest[30:34]
+        rest = rest[34:]
+        sums = [*half0, proj_ref, attn_ref]
     else:
-        dmap_ref, dtap_ref = rest[1:3]
+        sums, rest = rest[:number], rest[number:]
+        du_ref, dmap_ref, dtap_ref = rest[:3]
         rest = rest[3:]
     count = 5 * sum(len(plan.routes(grad.shape[3])) for grad in grads)
     scatter = Scatter(plan, grads, sums, rest[:count], *rest[count : count + 2])
@@ -980,6 +1095,7 @@
     my_a = lax.rem(chip, plan.cols_out)
     my_b = lax.rem(chip // plan.cols_out, plan.cols_in)
     my_group = chip // (plan.cols_out * plan.cols_in)
+    sibling = (1 - section, chip)
     greet_everyone(chips)()
 
     def send_g(step, carry):
@@ -1022,40 +1138,39 @@
     turn = (1 - 2 * section).astype(F32)
     half_ways = (((1,), (1,)), ((), ()))
 
-    def piece_of(k, tap, sub):
-        per_map = plan.width // PIECE
+    def piece_copies(k, tap, begin):
+        per_block = jb // PIECE
         which = 2 * plan.filters + k if tap else section * plan.filters + my_group * plan.local + k
-        g = which * per_map + my_b * (plan.jb // PIECE) + sub
-        return g // plan.pieces, lax.rem(g, plan.pieces)
-
-    def piece_copies(k, tap, begin):
-        def one(sub, carry):
-            owner, row = piece_of(k, tap, sub)
-            src = (
-                total_t.at[pl.ds(jb * k + PIECE * sub, PIECE), :]
-                if tap
-                else total_m.at[k, pl.ds(PIECE * sub, PIECE), :]
-            )
-            dst = dmaps_ref.at[
-                pl.ds(PIECE * row, PIECE), pl.ds(pl.multiple_of(my_a * ia, ia), ia)
-            ]
-            if begin:
-
-                @pl.when(owner == dev)
+        start = (which * plan.cols_in + my_b) * per_block
+        owner, row = start // plan.pieces, lax.rem(start, plan.pieces)
+        first = jnp.minimum(plan.pieces - row, per_block)
+        for to, at, base, count in ((owner, row, 0, first), (owner + 1, 0, first, per_block - first)):
+            for size in sizes(plan):
+                done = count // (2 * size) * (2 * size)
+                rows = size * PIECE
+                here = lax.rem(count // size, 2) == 1
+                source = PIECE * (base + done)
+                src = (
+                    total_t.at[pl.ds(jb * k + source, rows), :]
+                    if tap
+                    else total_m.at[k, pl.ds(source, rows), :]
+                )
+                dst = dmaps_ref.at[
+                    pl.ds(PIECE * (at + done), rows), pl.ds(pl.multiple_of(my_a * ia, ia), ia)
+                ]
+                if begin:
+
+                    @pl.when(jnp.logical_and(here, to == dev))
+                    def _():
+                        pltpu.make_async_copy(src, dst, w_recv).start()
+
+                @pl.when(jnp.logical_and(here, to != dev))
                 def _():
-                    pltpu.make_async_copy(src, dst, w_recv).start()
-
-            @pl.when(owner != dev)
-            def _():
-                copy = push(src, dst, w_send, w_recv, (owner // chips, lax.rem(owner, chips)))
-                if begin:
-                    copy.start()
-                else:
-                    copy.wait_send()
-
-            return carry
-
-        lax.fori_loop(0, plan.jb // PIECE, one, 0)
+                    copy = push(src, dst, w_send, w_recv, (to // chips, lax.rem(to, chips)))
+                    if begin:
+                        copy.start()
+                    else:
+                        copy.wait_send()
 
     def exchange(k):
         return push(give_m.at[k], take_m.at[k], m_send.at[k], m_recv.at[k], (1 - section, chip))
@@ -1094,18 +1209,12 @@
 
     def step(k, carry):
         slot = lax.rem(k, 2)
-        for i in range(plan.blocks):
-            rows = slice(BLOCK * i, BLOCK * (i + 1))
-            from_even = lax.dot_general(
-                g_buf[0, rows, :], pq[k], half_ways, preferred_element_type=F32
-            ).astype(BF)
-            from_odd = lax.dot_general(
-                g_buf[1, rows, :], pq[k], half_ways, preferred_element_type=F32
-            ).astype(BF)
-            z_even[rows, :jb] = from_even[:, :jb]
-            z_even[rows, jb:] = from_odd[:, :jb]
-            z_odd[rows, :jb] = from_odd[:, jb:]
-            z_odd[rows, jb:] = from_even[:, jb:]
+        from_even = rows_dot(g_buf[0], pq[k]).astype(BF)
+        from_odd = rows_dot(g_buf[1], pq[k]).astype(BF)
+        z_even[:, :jb] = from_even[:, :jb]
+        z_even[:, jb:] = from_odd[:, :jb]
+        z_odd[:, :jb] = from_odd[:, jb:]
+        z_odd[:, jb:] = from_even[:, jb:]
         pltpu.make_async_copy(v_ref.at[k], v_buf.at[slot], v_sem.at[slot]).wait()
         grad = jnp.dot(gt_buf[0], v_buf[slot, 0], preferred_element_type=F32) + jnp.dot(
             gt_buf[1], v_buf[slot, 1], preferred_element_type=F32
@@ -1124,10 +1233,10 @@
             rows = slice(BLOCK * j, BLOCK * (j + 1))
             depth = plan.length - BLOCK * j
             acc_even[rows, :] += jnp.dot(
-                strip[2 * k, :, :depth], z_even[BLOCK * j :, :], preferred_element_type=F32
+                strip[0, k, :, :depth], z_even[BLOCK * j :, :], preferred_element_type=F32
             )
             out = jnp.dot(
-                strip[2 * k + 1, :, :depth], z_odd[BLOCK * j :, :], preferred_element_type=F32
+                strip[1, k, :, :depth], z_odd[BLOCK * j :, :], preferred_element_type=F32
             )
             acc_even[rows, :jb] += out[:, :jb]
             acc_odd[rows, jb:] += out[:, jb:]
@@ -1136,8 +1245,9 @@
         def _():
             finish(k - 1)
 
-        pl.when(k == plan.local // 4)(scatter.second)
-        pl.when(k == plan.local // 2 + 1)(scatter.third)
+        for turn_number in range(plan.depth + 1):
+            at = 1 + (turn_number * (plan.local - 2)) // plan.depth
+            pl.when(k == at)(functools.partial(scatter.stage, turn_number))
         return carry
 
     lax.fori_loop(0, plan.local, step, 0)
@@ -1168,7 +1278,7 @@
     total_t[...] = (kept_t[...] + take_t[...].astype(F32)).astype(BF)
     if plan.routed:
 
-        @pl.when(jnp.logical_and(section == 0, my_group == 0))
+        @pl.when(jnp.logical_and(section == 0, my_group == plan.groups - 1))
         def _():
             for tap in range(ORDER):
                 piece_copies(tap, True, True)
@@ -1187,6 +1297,73 @@
         du_ref[:, :, b * jb : (b + 1) * jb] = total
     bytes_of(land.at[pl.ds(0, chips - 1)], d_send)
     scatter.end()
+    if plan.late:
+        core_zero = section == 0
+        for i in range(3):
+            crossing[i][...] = jnp.where(core_zero, half1[i][...], half0[i][...])
+            push(crossing[i], arrived[i], e_send.at[i], e_recv.at[i], sibling).start()
+        hidden = hidden_ref[...]
+        factor = lax.rsqrt(jnp.mean(hidden * hidden, axis=-1, keepdims=True) + EPSILON)
+        signal_grad = du_ref[...].reshape(plan.rows, plan.width)
+        weighted = signal_grad * gains_ref[0:1, :]
+        correction = jnp.mean(weighted * hidden, axis=-1, keepdims=True)
+        hidden_grad = factor * weighted - hidden * factor * factor * factor * correction
+        gain_buf[...] = gain_sums_ref[...]
+        gain_buf[0:1, :] = jnp.sum(signal_grad * hidden * factor, axis=0, keepdims=True)
+        per_tile = LANES * chips // plan.width
+
+        def send_gain(step, carry):
+            peer = lax.rem(dev + step, 2 * chips)
+            tile = lax.rem(peer, chips) // per_tile
+            push(
+                gain_buf.at[:, pl.ds(pl.multiple_of(LANES * tile, LANES), LANES)],
+                gain_land.at[dev],
+                n_send,
+                n_recv,
+                (peer // chips, lax.rem(peer, chips)),
+            ).start()
+            return carry
+
+        lax.fori_loop(1, 2 * chips, send_gain, 0)
+        pltpu.make_async_copy(
+            gain_buf.at[:, pl.ds(pl.multiple_of(LANES * (chip // per_tile), LANES), LANES)],
+            gain_land.at[dev],
+            n_recv,
+        ).start()
+        done_in = (mask_ref[...] * (dmid_ref[...] + hidden_grad)).astype(BF)
+        row = lax.broadcasted_iota(jnp.int32, (plan.rows, plan.rows), 0)
+        col = lax.broadcasted_iota(jnp.int32, (plan.rows, plan.rows), 1)
+        order = jnp.where(col == 2 * lax.rem(row, half) + row // half, 1.0, 0.0).astype(BF)
+        done_in = cols_dot(order, done_in).astype(BF)
+        done_out = cols_dot(order, out_ref[...]).astype(BF)
+        give_res[...] = jnp.where(core_zero, done_out, done_in)
+        swap_res = push(give_res, res_ref.at[section], e_send.at[3], e_recv.at[3], sibling)
+        swap_res.start()
+        res_ref[section] = jnp.where(core_zero, done_in, done_out)
+        for i in range(3):
+            push(crossing[i], arrived[i], e_send.at[i], e_recv.at[i], sibling).wait()
+        lane = lax.broadcasted_iota(jnp.int32, (gate_ref.shape[0], LANES), 1)
+        low = lane < half
+        kept_half = [jnp.where(core_zero, half0[i][...], half1[i][...]) for i in range(3)]
+        for i, out in ((0, gate_ref), (1, up_ref)):
+            came = arrived[i][...]
+            first = jnp.where(core_zero, kept_half[i], came)
+            second = jnp.where(core_zero, came, kept_half[i])
+            for j in range(out.shape[1] // (2 * LANES)):
+                one, two = (w[:, LANES * j : LANES * (j + 1)] for w in (first, second))
+                at = 2 * LANES * j
+                out[:, at : at + LANES] = jnp.where(low, one, pltpu.roll(two, half, 1))
+                out[:, at + LANES : at + 2 * LANES] = jnp.where(
+                    low, pltpu.roll(one, half, 1), two
+                )
+        part = half0[2].shape[0]
+        came = arrived[2][...]
+        down_ref[:part, :] = jnp.where(core_zero, kept_half[2], came)
+        down_ref[part:, :] = jnp.where(core_zero, came, kept_half[2])
+        swap_res.wait()
+        bytes_of(gain_land, n_recv)
+        gain_out[...] = jnp.sum(gain_land[...], axis=0)
+        bytes_of(gain_land.at[pl.ds(0, 2 * chips - 1)], n_send)
     if plan.routed:
 
         def drain(k, carry):
@@ -1195,7 +1372,7 @@
 
         lax.fori_loop(0, plan.local, drain, 0)
 
-        @pl.when(jnp.logical_and(section == 0, my_group == 0))
+        @pl.when(jnp.logical_and(section == 0, my_group == plan.groups - 1))
         def _():
             for tap in range(ORDER):
                 piece_copies(tap, True, False)
@@ -1203,32 +1380,56 @@
         bytes_of(dmaps_ref, w_recv)
 
 
-def backward_call(plan, g, filt, v, pq, tapw, x, xs, grads):
+def backward_call(plan, g, filt, v, pq, tapw, x, xs, grads, rest=()):
     chips, half, jb, ia = plan.chips, plan.half, plan.jb, plan.ia
     any_spec = pl.BlockSpec(memory_space=pl.ANY)
     vmem_spec = pl.BlockSpec(memory_space=pltpu.VMEM)
     dma = pltpu.SemaphoreType.DMA
     shapes = [g_part.shape[3:] for g_part in grads]
-    out_shape = [jax.ShapeDtypeStruct(shape, F32) for shape in shapes]
-    out_shape.append(jax.ShapeDtypeStruct((2, half, plan.width), F32))
-    if plan.routed:
-        out_shape.append(jax.ShapeDtypeStruct((plan.map_rows, plan.width), BF))
+    rows, width = plan.rows, plan.width
+    finish = []
+    if plan.late:
+        out_shape = [jax.ShapeDtypeStruct((2, rows, width), BF)]
+        out_shape += [
+            jax.ShapeDtypeStruct(shape, F32)
+            for shape in (
+                (shapes[0][0], plan.ff),
+                (shapes[1][0], plan.ff),
+                (2 * shapes[2][0], width),
+                *shapes[3:],
+                (8, LANES),
+            )
+        ]
+        in_vmem = len(out_shape)
+        out_shape.append(jax.ShapeDtypeStruct((plan.map_rows, width), BF))
+        finish = [
+            pltpu.VMEM((2, half, width), F32),
+            pltpu.VMEM((8, width), F32),
+            pltpu.VMEM((2 * chips, 8, LANES), F32),
+            pltpu.VMEM((rows, width), BF),
+        ]
+        finish += [pltpu.VMEM(shape, F32) for shape in shapes[:3]] * 3
+        finish += [dma((4,)), dma((4,)), dma, dma]
     else:
+        out_shape = [jax.ShapeDtypeStruct(shape, F32) for shape in shapes]
+        out_shape.append(jax.ShapeDtypeStruct((2, half, width), F32))
+        in_vmem = len(out_shape)
         out_shape.append(jax.ShapeDtypeStruct((plan.local, jb, ia), BF))
         out_shape.append(jax.ShapeDtypeStruct((ORDER * jb, ia), BF))
     return pl.pallas_call(
         functools.partial(backward_kernel, plan, len(grads)),
         out_shape=out_shape,
         in_specs=[vmem_spec, vmem_spec, any_spec, vmem_spec, vmem_spec, any_spec, any_spec]
-        + [vmem_spec] * len(grads),
-        out_specs=[vmem_spec] * (len(grads) + 1) + [any_spec] * (len(out_shape) - len(grads) - 1),
-        scratch_shapes=Scatter.scratch(plan, shapes)
-        + [dma((len(grads), 6)), dma((len(grads), 6))]
+        + [vmem_spec] * (len(grads) + len(rest)),
+        out_specs=[vmem_spec] * in_vmem + [any_spec] * (len(out_shape) - in_vmem),
+        scratch_shapes=finish
+        + Scatter.scratch(plan, shapes)
+        + Scatter.semaphores(plan, len(grads))
         + [
             pltpu.VMEM((2, plan.length, ia), BF),
             pltpu.VMEM((2, ia, plan.length), BF),
             pltpu.VMEM((2, plan.f_rows, plan.length + BLOCK), F32),
-            pltpu.VMEM((2 * plan.local, BLOCK, plan.length), BF),
+            pltpu.VMEM((2, plan.local, BLOCK, plan.length), BF),
             pltpu.VMEM((2, 2, plan.length, 2 * jb), BF),
             pltpu.VMEM((plan.length, 2 * jb), BF),
             pltpu.VMEM((plan.length, 2 * jb), BF),
@@ -1261,7 +1462,7 @@
             collective_id=3, has_side_effects=True, vmem_limit_bytes=VMEM_LIMIT
         ),
         name="spectral_backward",
-    )(g, filt, v, pq, tapw, x, xs, *grads)
+    )(g, filt, v, pq, tapw, x, xs, *grads, *rest)
 
 SWAPS = 7
 
@@ -1275,7 +1476,7 @@
         up_ref,
         up_pair,
         *stored,
-    ) = refs[:16]
+    ) = refs[:14]
     (
         out_ref,
         g_ref,
@@ -1289,8 +1490,8 @@
         down1_g,
         proj_g,
         attn_g,
-    ) = refs[16:28]
-    held = refs[28:36]
+    ) = refs[14:26]
+    held = refs[26:34]
     (
         pair0,
         pair1,
@@ -1309,36 +1510,52 @@
         back_land,
         att,
         dq_buf,
+        proj_all,
+        attn_all,
+        proj_take,
+        attn_take,
         load_sem,
+        a_send,
+        a_recv,
         send,
         recv,
         kv_send,
         kv_recv,
         bk_send,
         bk_recv,
-    ) = refs[36:]
+        *extra,
+    ) = refs[34:]
     chips, rows, width = plan.chips, plan.rows, plan.width
     section, chip = spot()
     sibling = (1 - section, chip)
     reach = WINDOW // rows
     span = (reach + 1) * rows
     layer0, (w_proj, w_out), layer1 = held[:3], held[3:5], held[5:]
-    split = 3 * plan.width // 2
-    homes = [
-        *layer0,
-        w_proj.at[:split],
-        w_proj.at[split:],
-        w_out.at[: plan.width // 2],
-        w_out.at[plan.width // 2 :],
-        *layer1,
+    split, cut = 3 * plan.width // 2, plan.width // 2
+    own_rows = [
+        w_proj.at[pl.ds(pl.multiple_of(split * section, 16), split), :],
+        w_out.at[pl.ds(pl.multiple_of(cut * section, 16), cut), :],
     ]
+    homes = list(layer0) + own_rows + ([] if plan.late else list(layer1))
     loads = [
         pltpu.make_async_copy(a, b, load_sem.at[i]) for i, (a, b) in enumerate(zip(stored, homes))
     ]
     for load in loads:
         load.start()
     greet_everyone(chips)()
-    ff = layer0[0].shape[1]
+    passes = [
+        push(stored[3 + i], own_rows[i], a_send.at[i], a_recv.at[i], sibling) for i in range(2)
+    ]
+    for copy in passes:
+        copy.start()
+    if plan.late:
+        grads1, gather_send, gather_recv, scatter_send, scatter_recv = extra[:3], *extra[3:7]
+        gather = Gather(plan, stored[5:], layer1, gather_send, gather_recv)
+        scatter = Scatter(
+            plan, grads1, (gate1_g, up1_g, down1_g), extra[7:], scatter_send, scatter_recv
+        )
+        gather.begin()
+    ff = plan.ff // 2
     own = slice(0, rows)
     second = slice(rows, 2 * rows)
     mask = mask_ref[...]
@@ -1359,27 +1576,27 @@
         return factor * weighted - values * factor * factor * factor * correction, gain_grad
 
     def feed(layer, pair, weights, number):
-        w_gate, w_up, w_down = weights
+        w_gate, w_up, w_down = (Flat(w) for w in weights)
         swap(number, pair.at[own], pair.at[second])
         for start in range(0, ff, BLOCK):
             cols = slice(start, start + BLOCK)
-            gate_rows = flat_dot(pair[...], w_gate[:, cols])
-            up_rows = flat_dot(pair[...], w_up[:, cols])
+            gate_rows = flat_dot(pair[...], w_gate.columns(start, BLOCK))
+            up_rows = flat_dot(pair[...], w_up.columns(start, BLOCK))
             gates[layer, :, cols] = gate_rows
             ups[layer, :, cols] = up_rows
             acts[layer, :, cols] = (gate_rows * jax.nn.sigmoid(gate_rows) * up_rows).astype(BF)
-        part = flat_dot(acts[layer], w_down[...])
+        part = flat_dot(acts[layer], w_down.all())
         give[number] = part[second].astype(BF)
         swap(number + 1, give.at[number], take.at[number])
         return part[own] + take[number].astype(F32)
 
     def feed_back(layer, pair, weights, grads, upstream_pair, number):
-        w_gate, w_up, w_down = weights
-        gate_g, up_g, down_g = grads
+        w_gate, w_up, w_down = (Flat(w) for w in weights)
+        gate_g, up_g, down_g = (Flat(w) for w in grads)
         turned = pair[...].astype(F32).T.astype(BF)
         for start in range(0, ff, BLOCK):
             cols = slice(start, start + BLOCK)
-            active_grad = rows_dot(upstream_pair, w_down[cols, :])
+            active_grad = rows_dot(upstream_pair, w_down.rows(start, BLOCK))
             gate_rows, up_rows = gates[layer, :, cols], ups[layer, :, cols]
             sigmoid = jax.nn.sigmoid(gate_rows)
             slope = sigmoid * (1.0 + gate_rows * (1.0 - sigmoid))
@@ -1389,7 +1606,9 @@
             dup[:, cols] = up_grad
         for start in range(0, width, BLOCK):
             cols = slice(start, start + BLOCK)
-            part = rows_dot(dgate[...], w_gate[cols, :]) + rows_dot(dup[...], w_up[cols, :])
+            part = rows_dot(dgate[...], w_gate.rows(start, BLOCK)) + rows_dot(
+                dup[...], w_up.rows(start, BLOCK)
+            )
             give[number, :, cols] = part[second].astype(BF)
             att[:, cols] = part[own]
         copy = push(
@@ -1398,11 +1617,12 @@
         copy.start()
         for start in range(0, ff, BLOCK):
             cols = slice(start, start + BLOCK)
-            gate_g[:, cols] = flat_dot(turned, dgate[:, cols]).astype(BF)
-            up_g[:, cols] = flat_dot(turned, dup[:, cols]).astype(BF)
-            down_g[cols, :] = flat_dot(
-                acts[layer, :, cols].astype(F32).T.astype(BF), upstream_pair
-            ).astype(BF)
+            gate_g.put_columns(start, flat_dot(turned, dgate[:, cols]).astype(BF))
+            up_g.put_columns(start, flat_dot(turned, dup[:, cols]).astype(BF))
+            down_g.put_rows(
+                start,
+                flat_dot(acts[layer, :, cols].astype(F32).T.astype(BF), upstream_pair).astype(BF),
+            )
         copy.wait()
         return att[...] + take[number].astype(F32)
 
@@ -1414,11 +1634,16 @@
         load.wait()
     branch = feed(0, pair0, layer0, 0)
     passed = (mask * (dmid_ref[...] + branch)).astype(BF).astype(F32)
+    if plan.late:
+        gather.stage(0)
+        gather.stage(1)
 
     normed, factor10 = norm(passed, gains_ref[2:3, :])
     inputs = normed.astype(BF)
-    for load in loads[3:7]:
+    for load in loads[3:5]:
         load.wait()
+    for copy in passes:
+        copy.wait()
     mine = slice(reach * rows, span)
     q_buf[...] = flat_dot(inputs, w_proj[:width]).astype(BF)
     kv[mine, :width] = flat_dot(inputs, w_proj[width : 2 * width]).astype(BF)
@@ -1445,6 +1670,8 @@
                 (rows, 2 * width), BF
             )
 
+    if plan.late:
+        gather.stage(2)
     half = plan.half
     row = lax.broadcasted_iota(jnp.int32, (rows, span), 0)
     col = lax.broadcasted_iota(jnp.int32, (rows, span), 1)
@@ -1471,7 +1698,11 @@
                 sibling,
             ).wait_recv()
 
+    if plan.late:
+        gather.stage(3)
     for pair in range(width // LANES):
+        if plan.late and pair == 1:
+            gather.stage(4)
         lanes = slice(LANES * pair, LANES * (pair + 1))
         keys, values = kv[:, lanes], kv[:, width + LANES * pair : width + LANES * (pair + 1)]
         parts = []
@@ -1488,21 +1719,29 @@
     attended = att[...].astype(BF)
     middle1 = passed + flat_dot(attended, w_out[...])
 
-    for load in loads[7:]:
+    if plan.late:
+        gather.end()
+    for load in loads[5:]:
         load.wait()
     normed, factor11 = norm(middle1, gains_ref[3:4, :])
     pair1[own] = normed.astype(BF)
     branch = feed(1, pair1, layer1, 2)
     out_ref[...] = (mask * (middle1 + branch)).astype(BF)
-    dnormed = feed_back(1, pair1, layer1, (gate1_g, up1_g, down1_g), up_pair[...], 4)
+    if not plan.late:
+        grads1 = (gate1_g, up1_g, down1_g)
+    dnormed = feed_back(1, pair1, layer1, grads1, up_pair[...], 4)
+    if plan.late:
+        scatter.begin()
     dmiddle, gain11 = norm_back(middle1, factor11, gains_ref[3:4, :], dnormed)
     dmiddle = up_ref[...] + dmiddle
     gain_ref[3:4, :] = gain11
 
     dy = dmiddle.astype(BF)
-    attn_g[...] = flat_dot(attended.astype(F32).T.astype(BF), dy).astype(BF)
+    attn_all[...] = flat_dot(attended.astype(F32).T.astype(BF), dy).astype(BF)
     datt = rows_dot(dy, w_out[...]).astype(BF)
     for pair in range(width // LANES):
+        if plan.late and 1 <= pair <= 3:
+            scatter.stage(pair - 1)
         lanes = slice(LANES * pair, LANES * (pair + 1))
         value_lanes = slice(width + LANES * pair, width + LANES * (pair + 1))
         keys, values = kv[:, lanes], kv[:, value_lanes]
@@ -1542,6 +1781,8 @@
         def _():
             behind(distance, chip - distance).start()
 
+    if plan.late:
+        scatter.stage(3)
     for distance in range(1, reach + 1):
 
         @pl.when(chip + distance < chips)
@@ -1560,13 +1801,29 @@
     gain_ref[2:3, :] = gain10
     dpassed = (dmiddle + dpassed).astype(BF).astype(F32)
 
+    if plan.late:
+        scatter.stage(4)
     upstream0 = mask * dpassed
     give[5] = upstream0.astype(BF)
     copy = push(give.at[5], take.at[5], send.at[5], recv.at[5], sibling)
     copy.start()
     for part in range(3):
-        proj_g[part * width : (part + 1) * width, :] = flat_dot(turned, dq_buf[part]).astype(BF)
+        proj_all[part * width : (part + 1) * width, :] = flat_dot(turned, dq_buf[part]).astype(BF)
     copy.wait()
+    crossing = [
+        push(
+            whole.at[pl.ds(pl.multiple_of(size * (1 - section), 16), size), :],
+            land,
+            a_send.at[2 + i],
+            a_recv.at[2 + i],
+            sibling,
+        )
+        for i, (whole, land, size) in enumerate(
+            ((proj_all, proj_take, split), (attn_all, attn_take, cut))
+        )
+    ]
+    for cross in crossing:
+        cross.start()
     both = jnp.concatenate([give[5], take[5]], 0)
     dnormed = feed_back(0, pair0, layer0, (gate0_g, up0_g, down0_g), both, 6)
     middle0 = dmid_ref[...]
@@ -1575,6 +1832,16 @@
     dmiddle = upstream0 + dmiddle
     dmid_ref[...] = dmiddle
     g_ref[...] = dmiddle.astype(BF)
+    for cross in crossing:
+        cross.wait()
+    for whole, land, size, out in (
+        (proj_all, proj_take, split, proj_g),
+        (attn_all, attn_take, cut, attn_g),
+    ):
+        own_part = whole[pl.ds(pl.multiple_of(size * section, 16), size), :]
+        out[...] = (own_part.astype(F32) + land[...].astype(F32)).astype(BF)
+    if plan.late:
+        scatter.end()
 
     for distance in range(1, reach + 1):
 
@@ -1595,25 +1862,29 @@
     vmem_spec = pl.BlockSpec(memory_space=pltpu.VMEM)
     dma = pltpu.SemaphoreType.DMA
     layer = [(width, ff), (width, ff), (ff, width)]
-    held = layer + [(3 * width, width), (width, width)] + layer
+    grid = (plan.depth, plan.side, plan.side)
+    chips = plan.chips
+    spread = [grid + (a // chips, b) for a, b in layer]
+    held = layer + [(3 * width, width), (width, width)] + (spread if plan.late else layer)
+    split, cut = 3 * width // 2, width // 2
+    extra = []
+    if plan.late:
+        extra = [pltpu.VMEM(w, BF) for w in spread]
+        extra += Gather.semaphores(plan, 3) + Scatter.semaphores(plan, 3)
+        extra += Scatter.scratch(plan, [w[3:] for w in spread])
     shapes = [
         ((rows, width), BF),
         ((rows, width), BF),
         ((rows, width), F32),
         ((8, width), F32),
-        ((width, ff), BF),
-        ((width, ff), BF),
-        ((ff, width), BF),
-        ((width, ff), BF),
-        ((width, ff), BF),
-        ((ff, width), BF),
-        ((3 * width, width), BF),
-        ((width, width), BF),
     ]
+    shapes += [(w, BF) for w in layer]
+    shapes += [(w[3:], F32) for w in spread] if plan.late else [(w, BF) for w in layer]
+    shapes += [((split, width), BF), ((cut, width), BF)]
     return pl.pallas_call(
         functools.partial(middle_kernel, plan),
         out_shape=[jax.ShapeDtypeStruct(s, d) for s, d in shapes],
-        in_specs=[vmem_spec] * 6 + [any_spec] * 10,
+        in_specs=[vmem_spec] * 6 + [any_spec] * 8,
         out_specs=[vmem_spec] * len(shapes),
         scratch_shapes=[pltpu.VMEM(w, BF) for w in held]
         + [
@@ -1634,14 +1905,21 @@
             pltpu.VMEM((reach, rows, 2 * width), BF),
             pltpu.VMEM((rows, width), F32),
             pltpu.VMEM((3, rows, width), BF),
-            dma((10,)),
+            pltpu.VMEM((3 * width, width), BF),
+            pltpu.VMEM((width, width), BF),
+            pltpu.VMEM((split, width), BF),
+            pltpu.VMEM((cut, width), BF),
+            dma((8,)),
+            dma((4,)),
+            dma((4,)),
             dma((SWAPS,)),
             dma((SWAPS,)),
             dma((reach,)),
             dma((reach,)),
             dma((reach,)),
             dma((reach,)),
-        ],
+        ]
+        + extra,
         compiler_params=pltpu.CompilerParams(
             collective_id=5, has_side_effects=True, vmem_limit_bytes=VMEM_LIMIT
         ),
@@ -1714,10 +1992,9 @@
         [gate, up, mlp_down[0], attn_proj, attn_out],
         maps,
     )
-    weights = [w.reshape(-1, w.shape[-1]) for w in results[:10]]
-    conv, hidden, upstream1, grad_pair, gains, mask_rows = results[10:16]
-    v, pq, tapw, x_all, xs_all, filt = results[16:]
-    proj_rows = attn_proj.shape[0]
+    weights = [w.reshape(-1, w.shape[-1]) for w in results[:8]]
+    conv, hidden, upstream1, grad_pair, gains, mask_rows = results[8:14]
+    v, pq, tapw, x_all, xs_all, filt = results[14:]
     block_out, g, middle0_grad, gain_sums, *grads = middle_call(
         plan,
         conv.reshape(tok_rows, width),
@@ -1728,67 +2005,74 @@
         grad_pair,
         weights,
     )
-    mlp0_grads, mlp1_grads = tuple(grads[:3]), tuple(grads[3:6])
-    proj_grad, output_grad = grads[6:]
+    mlp0_grads, half1, attn_grads = grads[:3], grads[3:6], grads[6:]
     gain01, gain10, gain11 = gain_sums[1], gain_sums[2], gain_sums[3]
     g = g.reshape(2, half, width)
     grid = (plan.depth, plan.side, plan.side)
-    half_width = width // 2
-    blocks0 = [
-        w.astype(BF).reshape(grid + (w.shape[0] // chips, w.shape[1])) for w in mlp0_grads
+    blocks0 = [w.reshape(grid + (w.shape[0] // chips, w.shape[1])) for w in mlp0_grads]
+    blocks1 = [w.reshape(grid + (w.shape[0] // chips, w.shape[1])) for w in attn_grads]
+    if plan.late:
+        result, gate_out, up_out, down_out, proj_out, out_out, gain_tile, maps_out = backward_call(
+            plan,
+            g,
+            filt,
+            v,
+            pq,
+            tapw,
+            x_all,
+            xs_all,
+            blocks0 + blocks1,
+            [hidden, gains, mask_rows, middle0_grad, block_out, gain_sums, *half1],
+        )
+        cols = width // chips
+        gain_out = lax.dynamic_slice(
+            gain_tile, (2 * section, (chip % (LANES // cols)) * cols), (2, cols)
+        )
+        return (
+            result[None],
+            maps_out.astype(F32),
+            proj_out,
+            out_out,
+            gain_out[None],
+            gate_out[None],
+            up_out[None],
+            down_out[None],
+        )
+    results = backward_call(plan, g, filt, v, pq, tapw, x_all, xs_all, blocks0)
+    half0, results = results[:3], results[3:]
+    attn_sums = [
+        lax.psum_scatter(
+            w.reshape((chips,) + w.shape[3:]), "seq", scatter_dimension=0, tiled=False
+        )
+        for w in blocks1
     ]
-    blocks1 = [
-        w.astype(BF).reshape(grid + (w.shape[0] // chips, w.shape[1]))
-        for w in mlp1_grads
-        + (
-            proj_grad[: width + half_width],
-            proj_grad[width + half_width :],
-            output_grad[:half_width],
-            output_grad[half_width:],
+    half1 = [
+        lax.psum_scatter(
+            w.reshape(chips, -1, w.shape[-1]), "seq", scatter_dimension=0, tiled=False
         )
+        for w in half1
     ]
-    if plan.routed:
-        results = backward_call(plan, g, filt, v, pq, tapw, x_all, xs_all, blocks0 + blocks1)
-        half0, half1, attn_sums, results = results[:3], results[3:6], results[6:10], results[10:]
-    else:
-        results = backward_call(plan, g, filt, v, pq, tapw, x_all, xs_all, blocks0)
-        half0, results = results[:3], results[3:]
-        summed = [
-            lax.psum_scatter(
-                w.reshape((chips,) + w.shape[3:]), "seq", scatter_dimension=0, tiled=False
-            )
-            for w in blocks1
-        ]
-        half1, attn_sums = summed[:3], summed[3:]
     signal_grad = results[0].reshape(tok_rows, width)
-    if plan.routed:
-        maps_grad = results[1].astype(F32)
-    else:
-        piece, tap_piece = (r.astype(F32) for r in results[1:])
-        full = jnp.zeros((2, plan.filters, width, width), F32)
-        full = lax.dynamic_update_slice(
-            full,
-            piece[None],
-            (section, my_group * plan.local, my_b * plan.jb, my_a * plan.ia),
-        )
-        tap_piece = jnp.where(core_zero & (my_group == 0), tap_piece, 0.0)
-        tap_full = lax.dynamic_update_slice(
-            jnp.zeros((ORDER, width, width), F32),
-            tap_piece.reshape(ORDER, plan.jb, plan.ia),
-            (0, my_b * plan.jb, my_a * plan.ia),
-        )
-        full = jnp.concatenate([full.reshape(-1, width), tap_full.reshape(-1, width)], 0)
-        maps_grad = lax.psum_scatter(full, ("section", "seq"), scatter_dimension=0, tiled=True)
+    piece, tap_piece = (r.astype(F32) for r in results[1:])
+    full = jnp.zeros((2, plan.filters, width, width), F32)
+    full = lax.dynamic_update_slice(
+        full,
+        piece[None],
+        (section, my_group * plan.local, my_b * plan.jb, my_a * plan.ia),
+    )
+    tap_piece = jnp.where(core_zero & (my_group == 0), tap_piece, 0.0)
+    tap_full = lax.dynamic_update_slice(
+        jnp.zeros((ORDER, width, width), F32),
+        tap_piece.reshape(ORDER, plan.jb, plan.ia),
+        (0, my_b * plan.jb, my_a * plan.ia),
+    )
+    full = jnp.concatenate([full.reshape(-1, width), tap_full.reshape(-1, width)], 0)
+    maps_grad = lax.psum_scatter(full, ("section", "seq"), scatter_dimension=0, tiled=True)
     spectral_factor = lax.rsqrt(jnp.mean(hidden * hidden, axis=-1, keepdims=True) + EPSILON)
     hidden_grad, gain00 = norm_backward(hidden, spectral_factor, gains[0], signal_grad)
     inputs_grad = (mask_rows * (middle0_grad + hidden_grad)).astype(BF)
 
-    low_part = jnp.concatenate([attn_sums[0], attn_sums[2]], 0)
-    high_part = jnp.concatenate([attn_sums[1], attn_sums[3]], 0)
-    attn_keep = jnp.where(core_zero, low_part, high_part).astype(F32)
-    attn_take = swapped(jnp.where(core_zero, high_part, low_part).astype(BF)).astype(F32)
-    attn_sum = attn_keep + attn_take
-    proj_out, out_out = attn_sum[:proj_rows], attn_sum[proj_rows:]
+    proj_out, out_out = (w.astype(F32) for w in attn_sums)
     outs = []
     for index in range(3):
         zero, one = half0[index].astype(BF), half1[index].astype(BF)

time: 416 us -> 353 us (0.85)
  Pallas kernels: 388 us -> 343 us
  local copies, waits for them, and re-layouts: 16.7 us -> 6.81 us
  other arithmetic: 8.39 us -> 2.64 us
    pallas_call x1, Pallas kernels: 79.9 us -> 150 us  [middle_call(): pl.pallas_call(functools.partial(middle_kernel, plan), out_shape=[jax.Sha...]
    pallas_call x1, Pallas kernels: 153 us -> 94.5 us  [forward_call(): pl.pallas_call(functools.partial(forward_kernel, plan), out_shape=[jax.Sh...]
    pallas_call x1, Pallas kernels: 141 us -> 98.5 us  [backward_call(): pl.pallas_call(functools.partial(backward_kernel, plan, len(grads)), out_...]
    pallas_call x1 -> x0, Pallas kernels: 13.8 us -> none  [exit_call(): pl.pallas_call(functools.partial(exit_kernel, chips), out_shape=[jax.Shap...]
    slice x6 -> x0, local copies, waits for them, and re-layouts: 6.27 us -> none  [the longest x1 2.72 us: body(): proj_grad[width + half_width:]]
    another operation x13 -> x0, local copies, waits for them, and re-layouts: 4.72 us -> none  [the longest x4 3.17 us: body(): outs.append(joined[None])]
  transfers between devices with their start and end apart: 4 -> 0, of which waited for: 0 -> 0; matrix products, arithmetic and copies ran while one was open for 4% -> 0% of each run, Pallas kernels for 3% -> 0%
where the time goes in v4:
time: 353 us
  Pallas kernels  343 us (97%)
  local copies, waits for them, and re-layouts  6.81 us (2%)
    pallas_call x1, Pallas kernels, middle_call(): pl.pallas_call(functools.partial(middle_kernel, plan), out_shape=[jax.Sha...  150 us
    pallas_call x1, Pallas kernels, backward_call(): pl.pallas_call(functools.partial(backward_kernel, plan, len(grads)), out_...  98.5 us
    pallas_call x1, Pallas kernels, forward_call(): pl.pallas_call(functools.partial(forward_kernel, plan), out_shape=[jax.Sh...  94.5 us

profile of v4, /device:TPU:0, one launch (start us, length us, event | category | flops | bytes accessed | tf_op | source)
XLA Modules:
  0.0 353.0 jit_solution(11997671814231140850)
XLA Ops:
  0.6 1.4 copy.18.refs_2_
  2.0 94.5 %spectral_forward.1 = (bf16[4,2,2,32,1024]{4,3,2,1,0:T(8,128)(2,1)}, bf16[4,2,2,32,1024]{4,3,2,1,0:T(8,128)(2,1)}, bf16[4,2,2,64,512]{4,3,2,1,0:T(8,128)(2,1)}, ...) custom-call(bf16[2,128,512]{2,1,0:T(8,128)(2,1)} %bitcast.36, ...), custom_call_target="tpu_custom_call" | custom-call | tf_op jit(solution)/shard_map/spectral_forward/pallas_call | solution.py:990
  96.6 149.8 %middle.1 = (bf16[128,512]{1,0:T(8,128)(2,1)}, bf16[128,512]{1,0:T(8,128)(2,1)}, f32[128,512]{1,0:T(8,128)}, f32[8,512]{1,0:T(8,128)}, bf16[512,1024]{1,0:T(8,12...) custom-call(f32[128,512]{1,0:T(8,128)} %bitcast.38, ...), custom_call_target="tpu_custom_call" | custom-call | tf_op jit(solution)/shard_map/middle/pallas_call | solution.py:1884
  246.4 98.5 %spectral_backward.1 = (bf16[2,128,512]{2,1,0:T(8,128)(2,1)}, f32[32,2048]{1,0:T(8,128)}, f32[32,2048]{1,0:T(8,128)}, f32[128,512]{1,0:T(8,128)}, f32[48,512]{1,...) custom-call(bf16[2,64,512]{2,1,0:T(8,128)(2,1)} %bitcast.39, ...), custom_call_target="tpu_custom_call" | custom-call | tf_op jit(solution)/shard_map/spectral_backward/pallas_call | solution.py:1419
  344.9 0.0 copy-start.3
  344.9 0.0 copy-start.4
  344.9 0.0 copy-start.5
  344.9 0.0 copy-start.2
  344.9 0.0 copy-start.1
  344.9 0.0 copy-start
  345.0 2.6 convert_element_type.3
  347.6 1.3 dynamic-slice_bitcast_fusion
  348.9 0.0 copy-done.3
  348.9 0.7 copy.25
  349.6 0.0 copy-done.4
  349.6 0.6 copy.26
  350.3 0.0 copy-done.5
  350.3 0.6 copy.27
  350.9 0.0 copy-done.2
  350.9 0.7 copy.28
  351.6 0.0 copy-done.1
  351.6 0.7 copy.29
  352.3 0.0 copy-done
  352.3 0.7 copy.30
Async XLA Ops:
  344.9 4.0 %copy-start.3 = (bf16[2,128,512]{2,1,0:T(8,128)(2,1)S(1)}, bf16[2,128,512]{2,1,0:T(8,128)(2,1)}, u32[]{:S(2)}) copy-start(bf16[2,128,512]{2,1,0:T(8,128)(2,1)} %get-tuple-element.80) | copy-start | bytes 786436
  344.9 4.7 %copy-start.4 = (f32[48,512]{1,0:T(8,128)S(1)}, f32[48,512]{1,0:T(8,128)}, u32[]{:S(2)}) copy-start(f32[48,512]{1,0:T(8,128)} %get-tuple-element.98) | copy-start | bytes 294916
  344.9 5.3 %copy-start.5 = (f32[16,512]{1,0:T(8,128)S(1)}, f32[16,512]{1,0:T(8,128)}, u32[]{:S(2)}) copy-start(f32[16,512]{1,0:T(8,128)} %get-tuple-element.99) | copy-start | bytes 98308
  344.9 6.0 %copy-start.2 = (f32[32,2048]{1,0:T(8,128)S(1)}, f32[32,2048]{1,0:T(8,128)}, u32[]{:S(2)}) copy-start(f32[32,2048]{1,0:T(8,128)} %get-tuple-element.85) | copy-start | bytes 786436
  344.9 6.6 %copy-start.1 = (f32[32,2048]{1,0:T(8,128)S(1)}, f32[32,2048]{1,0:T(8,128)}, u32[]{:S(2)}) copy-start(f32[32,2048]{1,0:T(8,128)} %get-tuple-element.86) | copy-start | bytes 786436
  344.9 7.3 %copy-start = (f32[128,512]{1,0:T(8,128)S(1)}, f32[128,512]{1,0:T(8,128)}, u32[]{:S(2)}) copy-start(f32[128,512]{1,0:T(8,128)} %get-tuple-element.87) | copy-start | bytes 786436

commit v5 on v4

--- a/solution.py
+++ b/solution.py
@@ -48,6 +48,8 @@
         self.routed = self.late
         self.side = max(1, math.isqrt(chips // 4))
         self.depth = chips // (self.side * self.side)
+        self.layer = self.side * self.side
+        self.layered = self.layer * tok_rows == WINDOW
 
     def place(self, chip):
         return (
@@ -55,6 +57,15 @@
             lax.rem(chip // self.side, self.side),
             lax.rem(chip, self.side),
         )
+
+    def a_of(self, chip):
+        return lax.rem(chip // self.cols_in, self.cols_out)
+
+    def b_of(self, chip):
+        return lax.rem(chip, self.cols_in)
+
+    def part_at(self, a, b, c):
+        return b + self.cols_in * (a + self.cols_out * c)
 
     def chip_at(self, z, y, x):
         return (z * self.side + y) * self.side + x
@@ -180,7 +191,7 @@
         return self.to(self.z, lax.rem(self.y + step, side), self.x)
 
     def routes(self, i):
-        for number, (start, rows, x_first) in enumerate(self.plan.routes(self.shards[i].shape[0], i)):
+        for number, (start, rows, x_first) in enumerate(self.plan.routes(self.outs[i].shape[3], i)):
             yield number, x_first, self.outs[i], pl.ds(start, rows)
 
     def level(self, t):
@@ -215,6 +226,45 @@
                         self.recv.at[i, (1 + number) * plan.depth + t],
                         self.across(step, x_first),
                     ).start()
+
+    def hand_over(self):
+        plan, side = self.plan, self.plan.side
+        for i, shard in enumerate(self.shards):
+            pltpu.make_async_copy(
+                shard, self.outs[i].at[self.z, self.y, self.x], self.recv.at[i, 0]
+            ).wait()
+            bytes_of(self.outs[i].at[pl.ds(0, plan.depth - 1), 0, 0], self.send.at[i, 0])
+            for number, x_first, out, sl in self.routes(i):
+                for t in range(plan.depth):
+                    bytes_of(
+                        out.at[0, 0, pl.ds(0, side - 1), sl],
+                        self.recv.at[i, (1 + number) * plan.depth + t],
+                    )
+                bytes_of(out.at[:, 0, pl.ds(0, side - 1), sl], self.send.at[i, 1 + number])
+
+    def held_parts(self, whole):
+        for i, source in enumerate(whole):
+            for number, x_first, out, sl in self.routes(i):
+                if x_first:
+                    yield source.at[:, self.y, :, sl], out.at[:, self.y, :, sl]
+                else:
+                    yield source.at[:, :, self.x, sl], out.at[:, :, self.x, sl]
+
+    def last_only(self):
+        plan, side = self.plan, self.plan.side
+        for t in range(plan.depth):
+            z = self.level(t)
+            for i in range(len(self.shards)):
+                for number, x_first, out, sl in self.routes(i):
+                    src = out.at[z, self.y, :, sl] if x_first else out.at[z, :, self.x, sl]
+                    for step in range(1, side):
+                        push(
+                            src,
+                            src,
+                            self.send.at[i, 3 + number],
+                            self.recv.at[i, (3 + number) * plan.depth + t],
+                            self.across(step, not x_first),
+                        ).start()
 
     def third(self, t):
         plan, side = self.plan, self.plan.side
@@ -241,12 +291,14 @@
                         self.across(step, not x_first),
                     ).start()
 
-    def end(self):
+    def end(self, last_only=False):
         plan, side = self.plan, self.plan.side
         for i in range(len(self.shards)):
-            bytes_of(self.outs[i].at[pl.ds(0, plan.depth - 1), 0, 0], self.send.at[i, 0])
+            if not last_only:
+                bytes_of(self.outs[i].at[pl.ds(0, plan.depth - 1), 0, 0], self.send.at[i, 0])
             for number, x_first, out, sl in self.routes(i):
-                bytes_of(out.at[:, 0, pl.ds(0, side - 1), sl], self.send.at[i, 1 + number])
+                if not last_only:
+                    bytes_of(out.at[:, 0, pl.ds(0, side - 1), sl], self.send.at[i, 1 + number])
                 for t in range(plan.depth):
                     bytes_of(
                         out.at[0, :, pl.ds(0, side - 1), sl],
@@ -284,8 +336,9 @@
             pltpu.SemaphoreType.DMA((count, 4 * plan.depth + 2)),
         ]
 
-    def __init__(self, plan, grads, outs, buffers, send, recv):
+    def __init__(self, plan, grads, outs, buffers, send, recv, lines_only=False):
         self.plan, self.grads, self.outs = plan, grads, outs
+        self.lines_only = lines_only
         self.send, self.recv = send, recv
         self.section, chip = spot()
         self.z, self.y, self.x = plan.place(chip)
@@ -359,7 +412,7 @@
             for step in range(side - 1):
                 total = total + land2[t, step].astype(F32)
             line[t] = total.astype(BF)
-            if t < plan.depth - 1:
+            if t < plan.depth - 1 and not self.lines_only:
                 push(
                     line.at[t],
                     land3.at[t],
@@ -371,6 +424,11 @@
     def end(self):
         plan = self.plan
         for i, number, start, rows, x_first, (land, part, land2, line, land3) in self.work:
+            if self.lines_only:
+                self.outs[i][:, start : start + rows, :] = line[...]
+                bytes_of(land, self.send.at[i, number])
+                bytes_of(land2, self.send.at[i, 2 + number])
+                continue
             bytes_of(land3, self.recv.at[i, 4 * plan.depth + number])
             total = line[plan.depth - 1].astype(F32)
             for step in range(plan.depth - 1):
@@ -512,14 +570,14 @@
             @pl.when(jnp.logical_and(here, sign < 2))
             def _():
                 for a in range(plan.cols_out):
-                    to_chip = a + plan.cols_out * (b + plan.cols_in * group)
+                    to_chip = plan.part_at(a, b, group)
                     act(source, size, False, k, target, a, sign, to_chip)
 
             @pl.when(jnp.logical_and(here, sign >= 2))
             def _():
                 for a in range(plan.cols_out):
                     for core in range(2):
-                        to_chip = a + plan.cols_out * (b + plan.cols_in * (plan.groups - 1))
+                        to_chip = plan.part_at(a, b, plan.groups - 1)
                         act(source, size, True, full, target, a, core, to_chip)
 
         return carry
@@ -575,6 +633,8 @@
         joined,
         y_buf,
         land,
+        reduced,
+        final,
         stage,
         io_sem,
         gain_send,
@@ -592,6 +652,8 @@
         o_recv,
         c_send,
         c_recv,
+        d_send,
+        r_recv,
         v_sem,
         out_sem,
         w_send,
@@ -719,8 +781,7 @@
         (0, (gate_shard.at[0], up_shard.at[0], down_shard.at[0])),
         (3, (proj_raw, attn_raw)),
     ]
-    if not plan.late:
-        parts.append((5, second_layer))
+    parts.append((5, second_layer))
     groups = []
     for first, arrays in parts:
         last = first + len(arrays)
@@ -733,7 +794,7 @@
                 w_recv.at[pl.ds(first, len(arrays))],
             )
         )
-    layer0, attention = groups[:2]
+    layer0, attention, layer1 = groups
     layer0.begin()
     position = lax.broadcasted_iota(jnp.int32, (rows_here, 1), 0)
     position = chip * rows_here + 2 * lax.rem(position, half) + position // half
@@ -770,7 +831,7 @@
 
     def send_u(step, carry):
         peer = lax.rem(chip + step, chips)
-        b = lax.rem(peer // plan.cols_out, plan.cols_in)
+        b = plan.b_of(peer)
         push(
             u_ref.at[b],
             x_buf.at[pl.ds(half * chip, half), :],
@@ -782,17 +843,12 @@
 
     lax.fori_loop(1, chips, send_u, 0)
     pltpu.make_async_copy(
-        u_ref.at[lax.rem(chip // plan.cols_out, plan.cols_in)],
+        u_ref.at[plan.b_of(chip)],
         x_buf.at[pl.ds(half * chip, half), :],
         x_recv,
     ).start()
     for group in groups[1:]:
         group.begin()
-    kept_copies = []
-    if plan.late:
-        for i, (src, dst) in enumerate(zip(second_layer, full_weights[5:])):
-            kept_copies.append(pltpu.make_async_copy(src, dst, w_recv.at[5 + i, 0]))
-            kept_copies[-1].start()
     cot_own = jnp.where(core_zero, io_sib[0], io_own[1]).astype(F32) * mask
     cot_other = jnp.where(core_zero, io_sib[1], io_own[0]).astype(F32) * mask_other
     upstream_ref[...] = cot_own
@@ -857,6 +913,29 @@
     layer0.stage(2)
     attention.stage(0)
     batch = plan.batch
+    my_b, level = plan.b_of(chip), chip // plan.cols_in
+
+    def reduce_level(i):
+        bytes_of(land.at[i], r_recv.at[i])
+        total = y_buf[:, pl.ds(pl.multiple_of(BLOCK * i + half * my_b, half), half), :].astype(F32)
+        for step_number in range(plan.cols_in - 1):
+            total = total + land[i, step_number].astype(F32)
+        reduced[i] = total.astype(BF)
+
+        @pl.when(level == i)
+        def _():
+            final[i] = reduced[i]
+
+        @pl.when(level != i)
+        def _():
+            push(
+                reduced.at[i],
+                final.at[level],
+                d_send,
+                c_recv,
+                (section, i * plan.cols_in + my_b),
+            ).start()
+
     for i in range(plan.blocks):
         if i == 1:
             layer0.stage(3)
@@ -864,9 +943,11 @@
         if i == 2:
             layer0.stage(4)
             attention.stage(2)
+            layer1.second(1)
         if i == 3:
             attention.stage(3)
             attention.stage(4)
+            layer1.second(2)
         rows = slice(BLOCK * i, BLOCK * (i + 1))
         depth = BLOCK * (i + 1)
         offset = plan.length - depth
@@ -913,6 +994,20 @@
         y_buf[0, rows, :] = acc[:BLOCK].astype(BF)
         y_buf[1, rows, :] = acc[BLOCK:].astype(BF)
 
+        if plan.layered:
+            for step_number in range(1, plan.cols_in):
+                peer = lax.rem(my_b + step_number, plan.cols_in)
+                push(
+                    y_buf.at[:, pl.ds(BLOCK * i + half * peer, half), :],
+                    land.at[i, step_number - 1],
+                    c_send,
+                    r_recv.at[i],
+                    (section, level * plan.cols_in + peer),
+                ).start()
+            if i > 0:
+                reduce_level(i - 1)
+            continue
+
         def give(r, carry, i=i):
             peer = BLOCK // half * i + r
             src = y_buf.at[:, pl.ds(half * peer, half), :]
@@ -929,9 +1024,10 @@
 
         lax.fori_loop(0, BLOCK // half, give, 0)
 
+    layer1.second(3)
     if not plan.late:
-        for turn_number in range(plan.depth + 1):
-            groups[2].stage(turn_number)
+        for number in range(plan.depth):
+            layer1.third(number)
     for slot in range(2):
         pltpu.make_async_copy(
             stage.at[slot], v_ref.at[pl.ds(0, batch), :, pl.ds(0, BLOCK), :], v_sem.at[slot]
@@ -942,18 +1038,33 @@
         owner_pieces(plan, drain_piece)
     for copy in (filt_out, x_out, xs_out, pq_out, taps_out):
         copy.wait()
-    bytes_of(land, c_recv)
+    if plan.layered:
+        reduce_level(plan.blocks - 1)
+        bytes_of(final.at[pl.ds(0, plan.blocks - 1)], c_recv)
+    else:
+        bytes_of(land, c_recv)
     for a in range(plan.cols_out):
         total = None
-        for other_part in range(plan.cols_in * plan.groups):
-            term = land[a + plan.cols_out * other_part].astype(F32)
-            total = term if total is None else total + term
+        for c in range(plan.groups):
+            if plan.layered:
+                terms = [final[a + plan.cols_out * c]]
+            else:
+                terms = [land[plan.part_at(a, b, c)] for b in range(plan.cols_in)]
+            for term in terms:
+                term = term.astype(F32)
+                total = term if total is None else total + term
         conv_ref[:, :, a * ia : (a + 1) * ia] = total
-    bytes_of(land.at[pl.ds(0, chips - 1)], c_send)
-    for group in groups:
+    if plan.layered:
+        bytes_of(land, c_send)
+        bytes_of(final.at[pl.ds(0, plan.blocks - 1)], d_send)
+    else:
+        bytes_of(land.at[pl.ds(0, chips - 1)], c_send)
+    for group in groups[:2]:
         group.end()
-    for copy in kept_copies:
-        copy.wait()
+    if plan.late:
+        layer1.hand_over()
+    else:
+        layer1.end()
     gain_swap.wait_send()
     for share in shares:
         share.wait_send()
@@ -971,8 +1082,12 @@
     down_share = (down[0] // 2, width)
     grid = (plan.depth, plan.side, plan.side)
     layer = [share, share, down_share]
+    levels = plan.blocks if plan.layered else 1
+    land_shape = (
+        (levels, plan.cols_in - 1, 2, half, ia) if plan.layered else (chips, 2, half, ia)
+    )
     gathered = [grid + w for w in layer + [proj, attn]]
-    gathered += layer if plan.late else [grid + w for w in layer]
+    gathered += [grid + w for w in layer]
     shapes = [(w, BF) for w in gathered] + [
         ((2, half, width), F32),
         ((rows, width), F32),
@@ -1021,7 +1136,9 @@
             pltpu.VMEM((2 * BLOCK, ia), F32),
             pltpu.VMEM((2 * BLOCK, plan.batch * 2 * jb), BF),
             pltpu.VMEM((2, plan.length, ia), BF),
-            pltpu.VMEM((chips, 2, half, ia), BF),
+            pltpu.VMEM(land_shape, BF),
+            pltpu.VMEM((levels, 2, half, ia), BF),
+            pltpu.VMEM((levels, 2, half, ia), BF),
             pltpu.VMEM((2, plan.batch, 2, BLOCK, 2 * jb), BF),
             dma((2,)),
             dma,
@@ -1029,8 +1146,8 @@
             dma((3,)),
             dma((3,)),
         ]
-        + [dma] * 11
-        + [dma((2,)), dma((5,)), *Gather.semaphores(plan, 8)],
+        + [dma] * 12
+        + [dma((levels,)), dma((2,)), dma((5,)), *Gather.semaphores(plan, 8)],
         compiler_params=pltpu.CompilerParams(
             collective_id=2, has_side_effects=True, vmem_limit_bytes=VMEM_LIMIT
         ),
@@ -1042,12 +1159,13 @@
     g_ref, filt_ref, v_ref, pq, tapw, x_ref, xs_ref = refs[:7]
     grads, rest = refs[7 : 7 + number], refs[7 + number :]
     if plan.late:
-        hidden_ref, gains_ref, mask_ref, dmid_ref, out_ref, gain_sums_ref, *half1 = rest[:9]
+        hidden_ref, gains_ref, mask_ref, dmid_ref, out_ref, gain_sums_ref, *lines = rest[:9]
         res_ref, gate_ref, up_ref, down_ref, proj_ref, attn_ref, gain_out, dmaps_ref = rest[9:17]
         du_ref, gain_buf, gain_land, give_res, *half_parts = rest[17:30]
         half0, crossing, arrived = half_parts[:3], half_parts[3:6], half_parts[6:9]
         e_send, e_recv, n_send, n_recv = rest[30:34]
-        rest = rest[34:]
+        half1, line_land, (l_send, l_recv) = rest[34:37], rest[37:40], rest[40:42]
+        rest = rest[42:]
         sums = [*half0, proj_ref, attn_ref]
     else:
         sums, rest = rest[:number], rest[number:]
@@ -1088,19 +1206,20 @@
         d_send,
         d_recv,
         x_sem,
+        z_send,
+        z_recv,
     ) = rest
     chips, half, jb, ia = plan.chips, plan.half, plan.jb, plan.ia
     section, chip = spot()
     dev = section * chips + chip
-    my_a = lax.rem(chip, plan.cols_out)
-    my_b = lax.rem(chip // plan.cols_out, plan.cols_in)
+    my_a, my_b = plan.a_of(chip), plan.b_of(chip)
     my_group = chip // (plan.cols_out * plan.cols_in)
     sibling = (1 - section, chip)
     greet_everyone(chips)()
 
     def send_g(step, carry):
         peer = lax.rem(chip + step, chips)
-        a = lax.rem(peer, plan.cols_out)
+        a = plan.a_of(peer)
         push(
             g_ref.at[:, :, pl.ds(pl.multiple_of(a * ia, ia), ia)],
             g_buf.at[:, pl.ds(half * chip, half), :],
@@ -1110,12 +1229,44 @@
         ).start()
         return carry
 
-    lax.fori_loop(1, chips, send_g, 0)
-    pltpu.make_async_copy(
-        g_ref.at[:, :, pl.ds(pl.multiple_of(my_a * ia, ia), ia)],
-        g_buf.at[:, pl.ds(half * chip, half), :],
-        g_recv,
-    ).start()
+    own_g = g_ref.at[:, :, pl.ds(pl.multiple_of(my_a * ia, ia), ia)]
+    level, levels = chip // plan.cols_in, chips // plan.cols_in
+
+    def g_rows(t):
+        source = lax.rem(level - t + levels, levels) * plan.cols_in + my_b
+        return g_buf.at[:, pl.ds(pl.multiple_of(half * source, half), half), :]
+
+    def spread_g(t):
+        if t > 0:
+            bytes_of(g_rows(t), z_recv.at[t])
+        for step_number in range(1, plan.cols_in):
+            peer = lax.rem(my_b + step_number, plan.cols_in)
+            push(
+                own_g if t == 0 else g_rows(t),
+                g_rows(t),
+                g_send,
+                g_recv,
+                (section, level * plan.cols_in + peer),
+            ).start()
+
+    if plan.layered:
+        for t in range(1, levels):
+            to_level = lax.rem(level + t, levels)
+            to_a = lax.rem(to_level, plan.cols_out)
+            push(
+                g_ref.at[:, :, pl.ds(pl.multiple_of(to_a * ia, ia), ia)],
+                g_rows(0),
+                z_send,
+                z_recv.at[t],
+                (section, to_level * plan.cols_in + my_b),
+            ).start()
+        spread_g(0)
+        pltpu.make_async_copy(own_g, g_rows(0), z_recv.at[0]).start()
+    else:
+        lax.fori_loop(1, chips, send_g, 0)
+        pltpu.make_async_copy(
+            own_g, g_buf.at[:, pl.ds(half * chip, half), :], g_recv
+        ).start()
     v_copy = [pltpu.make_async_copy(v_ref.at[k], v_buf.at[k], v_sem.at[k]) for k in range(2)]
     for copy in v_copy:
         copy.start()
@@ -1125,12 +1276,27 @@
     ]
     for copy in x_copy:
         copy.start()
-    scatter.begin()
     filter_rows(plan, filt_ref, table, plan.f_rows, True)
     build_strips(plan, table, strip, True)
+    if plan.layered:
+        for t in range(1, levels):
+            spread_g(t)
     acc_even[...] = jnp.zeros_like(acc_even)
     acc_odd[...] = jnp.zeros_like(acc_odd)
-    bytes_of(g_buf, g_recv)
+    if plan.layered:
+        pltpu.make_async_copy(own_g, g_rows(0), z_recv.at[0]).wait()
+        bytes_of(g_buf.at[:, pl.ds(0, half * levels * (plan.cols_in - 1)), :], g_recv)
+    else:
+        bytes_of(g_buf, g_recv)
+    scatter.begin()
+    if plan.late:
+        z, y, x = plan.place(chip)
+        for i in range(3):
+            for t in range(plan.depth - 1):
+                to = (section, plan.chip_at(lax.rem(z + 1 + t, plan.depth), y, x))
+                push(
+                    lines[i].at[t], line_land[i].at[t], l_send.at[i], l_recv.at[i], to
+                ).start()
     for phase in range(2):
         for i in range(plan.blocks):
             rows = slice(BLOCK * i, BLOCK * (i + 1))
@@ -1285,14 +1451,17 @@
     else:
         pltpu.sync_copy(total_m, dmap_ref)
         pltpu.sync_copy(total_t, dtap_ref)
-    bytes_of(g_buf.at[0, pl.ds(0, 2 * half * (chips - 1) // 2), :], g_send)
-    bytes_of(g_buf.at[1, pl.ds(0, 2 * half * (chips - 1) // 2), :], g_send)
+    if plan.layered:
+        bytes_of(g_buf.at[:, pl.ds(0, half * levels * (plan.cols_in - 1)), :], g_send)
+        bytes_of(g_buf.at[:, pl.ds(0, half * (levels - 1)), :], z_send)
+    else:
+        bytes_of(g_buf.at[:, pl.ds(0, half * (chips - 1)), :], g_send)
     bytes_of(land, d_recv)
     for b in range(plan.cols_in):
         total = None
         for c in range(plan.groups):
             for a in range(plan.cols_out):
-                term = land[a + plan.cols_out * (b + plan.cols_in * c)].astype(F32)
+                term = land[plan.part_at(a, b, c)].astype(F32)
                 total = term if total is None else total + term
         du_ref[:, :, b * jb : (b + 1) * jb] = total
     bytes_of(land.at[pl.ds(0, chips - 1)], d_send)
@@ -1300,6 +1469,12 @@
     if plan.late:
         core_zero = section == 0
         for i in range(3):
+            bytes_of(line_land[i], l_recv.at[i])
+            total = lines[i][plan.depth - 1].astype(F32)
+            for t in range(plan.depth - 1):
+                total = total + line_land[i][t].astype(F32)
+            half1[i][...] = total
+            bytes_of(line_land[i], l_send.at[i])
             crossing[i][...] = jnp.where(core_zero, half1[i][...], half0[i][...])
             push(crossing[i], arrived[i], e_send.at[i], e_recv.at[i], sibling).start()
         hidden = hidden_ref[...]
@@ -1410,6 +1585,9 @@
         ]
         finish += [pltpu.VMEM(shape, F32) for shape in shapes[:3]] * 3
         finish += [dma((4,)), dma((4,)), dma, dma]
+        finish += [pltpu.VMEM(shape, F32) for shape in shapes[:3]]
+        finish += [pltpu.VMEM((plan.depth - 1,) + shape, BF) for shape in shapes[:3]]
+        finish += [dma((3,)), dma((3,))]
     else:
         out_shape = [jax.ShapeDtypeStruct(shape, F32) for shape in shapes]
         out_shape.append(jax.ShapeDtypeStruct((2, half, width), F32))
@@ -1457,6 +1635,8 @@
             dma,
             dma,
             dma((2,)),
+            dma,
+            dma((plan.depth,)),
         ],
         compiler_params=pltpu.CompilerParams(
             collective_id=3, has_side_effects=True, vmem_limit_bytes=VMEM_LIMIT
@@ -1508,6 +1688,7 @@
         dkv,
         back,
         back_land,
+        down_land,
         att,
         dq_buf,
         proj_all,
@@ -1540,6 +1721,15 @@
     loads = [
         pltpu.make_async_copy(a, b, load_sem.at[i]) for i, (a, b) in enumerate(zip(stored, homes))
     ]
+    if plan.late:
+        grads1, gather_send, gather_recv, scatter_send, scatter_recv = extra[:3], *extra[3:7]
+        gather = Gather(plan, layer1, layer1, gather_send, gather_recv)
+        held_loads = [
+            pltpu.make_async_copy(src, dst, gather_recv.at[i // 2, i % 2])
+            for i, (src, dst) in enumerate(gather.held_parts(stored[5:]))
+        ]
+        for load in held_loads:
+            load.start()
     for load in loads:
         load.start()
     greet_everyone(chips)()
@@ -1549,12 +1739,12 @@
     for copy in passes:
         copy.start()
     if plan.late:
-        grads1, gather_send, gather_recv, scatter_send, scatter_recv = extra[:3], *extra[3:7]
-        gather = Gather(plan, stored[5:], layer1, gather_send, gather_recv)
         scatter = Scatter(
-            plan, grads1, (gate1_g, up1_g, down1_g), extra[7:], scatter_send, scatter_recv
+            plan, grads1, (gate1_g, up1_g, down1_g), extra[7:], scatter_send, scatter_recv, True
         )
-        gather.begin()
+        for load in held_loads:
+            load.wait()
+        gather.last_only()
     ff = plan.ff // 2
     own = slice(0, rows)
     second = slice(rows, 2 * rows)
@@ -1634,9 +1824,6 @@
         load.wait()
     branch = feed(0, pair0, layer0, 0)
     passed = (mask * (dmid_ref[...] + branch)).astype(BF).astype(F32)
-    if plan.late:
-        gather.stage(0)
-        gather.stage(1)
 
     normed, factor10 = norm(passed, gains_ref[2:3, :])
     inputs = normed.astype(BF)
@@ -1649,18 +1836,42 @@
     kv[mine, :width] = flat_dot(inputs, w_proj[width : 2 * width]).astype(BF)
     kv[mine, width:] = flat_dot(inputs, w_proj[2 * width :]).astype(BF)
 
+    layer, level = plan.layer, chip // plan.layer
+    within = lax.rem(chip, layer)
+
+    def slot(distance):
+        return kv.at[pl.ds((reach - distance) * rows, rows)]
+
     def ahead(distance):
         return push(
             kv.at[mine],
-            kv.at[pl.ds((reach - distance) * rows, rows)],
+            slot(distance),
             kv_send.at[distance - 1],
             kv_recv.at[distance - 1],
             (section, chip + distance),
         )
 
-    for distance in range(1, reach + 1):
-
-        @pl.when(chip + distance < chips)
+    def pass_on(place):
+        distance = reach - (within - place)
+        return push(
+            slot(reach),
+            slot(distance),
+            kv_send.at[reach + place],
+            kv_recv.at[distance - 1],
+            (section, level * layer + place),
+        )
+
+    def goes_ahead(distance):
+        if plan.layered and distance < reach:
+            return within + distance < layer
+        return chip + distance < chips
+
+    def comes(distance):
+        return chip >= distance
+
+    for distance in range(reach, 0, -1):
+
+        @pl.when(goes_ahead(distance))
         def _():
             ahead(distance).start()
 
@@ -1670,8 +1881,6 @@
                 (rows, 2 * width), BF
             )
 
-    if plan.late:
-        gather.stage(2)
     half = plan.half
     row = lax.broadcasted_iota(jnp.int32, (rows, span), 0)
     col = lax.broadcasted_iota(jnp.int32, (rows, span), 1)
@@ -1686,23 +1895,27 @@
     low = lane < HEAD_DIM
     scale = HEAD_DIM ** (-0.5)
     zero = jnp.zeros((rows, LANES), BF)
-    for distance in range(1, reach + 1):
-
-        @pl.when(chip >= distance)
-        def _():
-            push(
-                kv.at[mine],
-                kv.at[pl.ds((reach - distance) * rows, rows)],
-                kv_send.at[distance - 1],
-                kv_recv.at[distance - 1],
-                sibling,
-            ).wait_recv()
-
-    if plan.late:
-        gather.stage(3)
+    def arrived(distance):
+        push(
+            kv.at[mine],
+            slot(distance),
+            kv_send.at[distance - 1],
+            kv_recv.at[distance - 1],
+            sibling,
+        ).wait_recv()
+
+    pl.when(comes(reach))(functools.partial(arrived, reach))
+    if plan.layered:
+        for place in range(layer - 1):
+
+            @pl.when(jnp.logical_and(level > 0, place < within))
+            def _():
+                pass_on(place).start()
+
+    for distance in range(1, reach):
+        pl.when(comes(distance))(functools.partial(arrived, distance))
+
     for pair in range(width // LANES):
-        if plan.late and pair == 1:
-            gather.stage(4)
         lanes = slice(LANES * pair, LANES * (pair + 1))
         keys, values = kv[:, lanes], kv[:, width + LANES * pair : width + LANES * (pair + 1)]
         parts = []
@@ -1720,7 +1933,7 @@
     middle1 = passed + flat_dot(attended, w_out[...])
 
     if plan.late:
-        gather.end()
+        gather.end(True)
     for load in loads[5:]:
         load.wait()
     normed, factor11 = norm(middle1, gains_ref[3:4, :])
@@ -1730,8 +1943,6 @@
     if not plan.late:
         grads1 = (gate1_g, up1_g, down1_g)
     dnormed = feed_back(1, pair1, layer1, grads1, up_pair[...], 4)
-    if plan.late:
-        scatter.begin()
     dmiddle, gain11 = norm_back(middle1, factor11, gains_ref[3:4, :], dnormed)
     dmiddle = up_ref[...] + dmiddle
     gain_ref[3:4, :] = gain11
@@ -1740,8 +1951,6 @@
     attn_all[...] = flat_dot(attended.astype(F32).T.astype(BF), dy).astype(BF)
     datt = rows_dot(dy, w_out[...]).astype(BF)
     for pair in range(width // LANES):
-        if plan.late and 1 <= pair <= 3:
-            scatter.stage(pair - 1)
         lanes = slice(LANES * pair, LANES * (pair + 1))
         value_lanes = slice(width + LANES * pair, width + LANES * (pair + 1))
         keys, values = kv[:, lanes], kv[:, value_lanes]
@@ -1775,20 +1984,88 @@
             (section, peer),
         )
 
-    for distance in range(1, reach + 1):
-
-        @pl.when(chip >= distance)
+    def to_place(place):
+        distance = lax.rem(within - place + layer, layer)
+        return push(
+            back.at[pl.ds((reach - distance) * rows, rows)],
+            back_land.at[within],
+            bk_send.at[place],
+            bk_recv.at[within],
+            (section, level * layer + place),
+        )
+
+    def came_from(place):
+        push(
+            back_land.at[place],
+            back_land.at[place],
+            bk_send.at[place],
+            bk_recv.at[place],
+            sibling,
+        ).wait_recv()
+
+    def down():
+        return push(
+            back.at[pl.ds(0, rows)],
+            down_land,
+            bk_send.at[reach],
+            bk_recv.at[reach],
+            (section, chip - layer),
+        )
+
+    if plan.layered:
+        for place in range(layer - 1, -1, -1):
+
+            @pl.when(jnp.logical_and(place > within, level > 0))
+            def _():
+                to_place(place).start()
+
+        for place in range(layer):
+
+            @pl.when(place < within)
+            def _():
+                to_place(place).start()
+
+    else:
+        for distance in range(1, reach + 1):
+
+            @pl.when(chip >= distance)
+            def _():
+                behind(distance, chip - distance).start()
+
+    if plan.late:
+        scatter.begin()
+    if plan.layered:
+        for place in range(layer - 1):
+
+            @pl.when(jnp.logical_and(place < within, level > 0))
+            def _():
+                came_from(place)
+                below = back[:rows, :].astype(F32) + back_land[place].astype(F32)
+                back[:rows, :] = below.astype(BF)
+
+        @pl.when(level > 0)
         def _():
-            behind(distance, chip - distance).start()
-
-    if plan.late:
-        scatter.stage(3)
-    for distance in range(1, reach + 1):
-
-        @pl.when(chip + distance < chips)
+            down().start()
+
+        for place in range(1, layer):
+
+            @pl.when(place > within)
+            def _():
+                came_from(place)
+                dkv[...] += back_land[place].astype(F32)
+
+        @pl.when(level < plan.depth - 1)
         def _():
-            behind(distance, chip).wait_recv()
-            dkv[...] += back_land[distance - 1].astype(F32)
+            down().wait_recv()
+            dkv[...] += down_land[...].astype(F32)
+
+    else:
+        for distance in range(1, reach + 1):
+
+            @pl.when(chip + distance < chips)
+            def _():
+                behind(distance, chip).wait_recv()
+                dkv[...] += back_land[distance - 1].astype(F32)
 
     dq_buf[1] = dkv[:, :width].astype(BF)
     dq_buf[2] = dkv[:, width:].astype(BF)
@@ -1802,7 +2079,7 @@
     dpassed = (dmiddle + dpassed).astype(BF).astype(F32)
 
     if plan.late:
-        scatter.stage(4)
+        scatter.stage(0)
     upstream0 = mask * dpassed
     give[5] = upstream0.astype(BF)
     copy = push(give.at[5], take.at[5], send.at[5], recv.at[5], sibling)
@@ -1824,8 +2101,13 @@
     ]
     for cross in crossing:
         cross.start()
+    if plan.late:
+        scatter.stage(1)
     both = jnp.concatenate([give[5], take[5]], 0)
     dnormed = feed_back(0, pair0, layer0, (gate0_g, up0_g, down0_g), both, 6)
+    if plan.late:
+        for number in range(2, plan.depth + 1):
+            scatter.stage(number)
     middle0 = dmid_ref[...]
     dmiddle, gain01 = norm_back(middle0, factor0, gains_ref[1:2, :], dnormed)
     gain_ref[1:2, :] = gain01
@@ -1845,13 +2127,31 @@
 
     for distance in range(1, reach + 1):
 
-        @pl.when(chip + distance < chips)
+        @pl.when(goes_ahead(distance))
         def _():
             ahead(distance).wait_send()
 
-        @pl.when(chip >= distance)
+    if plan.layered:
+        for place in range(layer):
+
+            @pl.when(jnp.logical_and(level > 0, place < within))
+            def _():
+                pass_on(place).wait_send()
+
+            @pl.when((place < within) | ((place > within) & (level > 0)))
+            def _():
+                to_place(place).wait_send()
+
+        @pl.when(level > 0)
         def _():
-            behind(distance, chip).wait_send()
+            down().wait_send()
+
+    else:
+        for distance in range(1, reach + 1):
+
+            @pl.when(chip >= distance)
+            def _():
+                behind(distance, chip).wait_send()
 
 
 def middle_call(plan, conv, hidden, gains, mask, upstream, pair, stored):
@@ -1879,7 +2179,7 @@
         ((8, width), F32),
     ]
     shapes += [(w, BF) for w in layer]
-    shapes += [(w[3:], F32) for w in spread] if plan.late else [(w, BF) for w in layer]
+    shapes += [((plan.depth,) + w[3:] if plan.late else v, BF) for v, w in zip(layer, spread)]
     shapes += [((split, width), BF), ((cut, width), BF)]
     return pl.pallas_call(
         functools.partial(middle_kernel, plan),
@@ -1903,6 +2203,7 @@
             pltpu.VMEM((rows, 2 * width), F32),
             pltpu.VMEM((reach * rows, 2 * width), BF),
             pltpu.VMEM((reach, rows, 2 * width), BF),
+            pltpu.VMEM((rows, 2 * width), BF),
             pltpu.VMEM((rows, width), F32),
             pltpu.VMEM((3, rows, width), BF),
             pltpu.VMEM((3 * width, width), BF),
@@ -1914,10 +2215,10 @@
             dma((4,)),
             dma((SWAPS,)),
             dma((SWAPS,)),
+            dma((2 * reach,)),
             dma((reach,)),
-            dma((reach,)),
-            dma((reach,)),
-            dma((reach,)),
+            dma((reach + 1,)),
+            dma((reach + 1,)),
         ]
         + extra,
         compiler_params=pltpu.CompilerParams(
@@ -1954,8 +2255,7 @@
     def join_phases(rows):
         return rows.reshape(2, half, width).swapaxes(0, 1).reshape(rows.shape)
 
-    my_a = chip % plan.cols_out
-    my_b = (chip // plan.cols_out) % plan.cols_in
+    my_a, my_b = plan.a_of(chip), plan.b_of(chip)
     my_group = chip // (plan.cols_out * plan.cols_in)
     if plan.routed:
         maps = [stu_maps]
@@ -1992,7 +2292,8 @@
         [gate, up, mlp_down[0], attn_proj, attn_out],
         maps,
     )
-    weights = [w.reshape(-1, w.shape[-1]) for w in results[:8]]
+    flat = 5 if plan.late else 8
+    weights = [w.reshape(-1, w.shape[-1]) for w in results[:flat]] + list(results[flat:8])
     conv, hidden, upstream1, grad_pair, gains, mask_rows = results[8:14]
     v, pq, tapw, x_all, xs_all, filt = results[14:]
     block_out, g, middle0_grad, gain_sums, *grads = middle_call(

time: 353 us -> 321 us (0.909)
  Pallas kernels: 343 us -> 311 us
    pallas_call x1, Pallas kernels: 150 us -> 120 us  [middle_call(): pl.pallas_call(functools.partial(middle_kernel, plan), out_shape=[jax.Sha...]
    pallas_call x1, Pallas kernels: 94.5 us -> 89.8 us  [forward_call(): pl.pallas_call(functools.partial(forward_kernel, plan), out_shape=[jax.Sh...]
where the time goes in v5:
time: 321 us
  Pallas kernels  311 us (97%)
  local copies, waits for them, and re-layouts  6.81 us (2%)
    pallas_call x1, Pallas kernels, middle_call(): pl.pallas_call(functools.partial(middle_kernel, plan), out_shape=[jax.Sha...  120 us
    pallas_call x1, Pallas kernels, backward_call(): pl.pallas_call(functools.partial(backward_kernel, plan, len(grads)), out_...  101 us
    pallas_call x1, Pallas kernels, forward_call(): pl.pallas_call(functools.partial(forward_kernel, plan), out_shape=[jax.Sh...  89.8 us

profile of v5, /device:TPU:0, one launch (start us, length us, event | category | flops | bytes accessed | tf_op | source)
XLA Modules:
  0.0 321.0 jit_solution(4439420973478618052)
XLA Ops:
  0.6 1.4 copy.18.refs_2_
  2.0 89.8 %spectral_forward.1 = (bf16[4,2,2,32,1024]{4,3,2,1,0:T(8,128)(2,1)}, bf16[4,2,2,32,1024]{4,3,2,1,0:T(8,128)(2,1)}, bf16[4,2,2,64,512]{4,3,2,1,0:T(8,128)(2,1)}, ...) custom-call(bf16[2,128,512]{2,1,0:T(8,128)(2,1)} %bitcast.38, ...), custom_call_target="tpu_custom_call" | custom-call | tf_op jit(solution)/shard_map/spectral_forward/pallas_call | solution.py:1105
  91.8 119.6 %middle.1 = (bf16[128,512]{1,0:T(8,128)(2,1)}, bf16[128,512]{1,0:T(8,128)(2,1)}, f32[128,512]{1,0:T(8,128)}, f32[8,512]{1,0:T(8,128)}, bf16[512,1024]{1,0:T(8,12...) custom-call(f32[128,512]{1,0:T(8,128)} %bitcast.33, ...), custom_call_target="tpu_custom_call" | custom-call | tf_op jit(solution)/shard_map/middle/pallas_call | solution.py:2184
  211.4 101.4 %spectral_backward.1 = (bf16[2,128,512]{2,1,0:T(8,128)(2,1)}, f32[32,2048]{1,0:T(8,128)}, f32[32,2048]{1,0:T(8,128)}, f32[128,512]{1,0:T(8,128)}, f32[48,512]{1,...) custom-call(bf16[2,64,512]{2,1,0:T(8,128)(2,1)} %bitcast.39, ...), custom_call_target="tpu_custom_call" | custom-call | tf_op jit(solution)/shard_map/spectral_backward/pallas_call | solution.py:1597
  312.9 0.0 copy-start.3
  312.9 0.0 copy-start.4
  312.9 0.0 copy-start.5
  312.9 0.0 copy-start.2
  312.9 0.0 copy-start.1
  312.9 0.0 copy-start
  312.9 2.6 convert_element_type.3
  315.6 1.3 dynamic-slice_bitcast_fusion
  316.9 0.0 copy-done.3
  316.9 0.7 copy.25
  317.6 0.0 copy-done.4
  317.6 0.6 copy.26
  318.2 0.0 copy-done.5
  318.2 0.6 copy.27
  318.8 0.0 copy-done.2
  318.8 0.7 copy.28
  319.5 0.0 copy-done.1
  319.5 0.7 copy.29
  320.2 0.0 copy-done
  320.3 0.7 copy.30
Async XLA Ops:
  312.9 4.0 %copy-start.3 = (bf16[2,128,512]{2,1,0:T(8,128)(2,1)S(1)}, bf16[2,128,512]{2,1,0:T(8,128)(2,1)}, u32[]{:S(2)}) copy-start(bf16[2,128,512]{2,1,0:T(8,128)(2,1)} %get-tuple-element.80) | copy-start | bytes 786436
  312.9 4.7 %copy-start.4 = (f32[48,512]{1,0:T(8,128)S(1)}, f32[48,512]{1,0:T(8,128)}, u32[]{:S(2)}) copy-start(f32[48,512]{1,0:T(8,128)} %get-tuple-element.98) | copy-start | bytes 294916
  312.9 5.3 %copy-start.5 = (f32[16,512]{1,0:T(8,128)S(1)}, f32[16,512]{1,0:T(8,128)}, u32[]{:S(2)}) copy-start(f32[16,512]{1,0:T(8,128)} %get-tuple-element.99) | copy-start | bytes 98308
  312.9 5.9 %copy-start.2 = (f32[32,2048]{1,0:T(8,128)S(1)}, f32[32,2048]{1,0:T(8,128)}, u32[]{:S(2)}) copy-start(f32[32,2048]{1,0:T(8,128)} %get-tuple-element.85) | copy-start | bytes 786436
  312.9 6.6 %copy-start.1 = (f32[32,2048]{1,0:T(8,128)S(1)}, f32[32,2048]{1,0:T(8,128)}, u32[]{:S(2)}) copy-start(f32[32,2048]{1,0:T(8,128)} %get-tuple-element.86) | copy-start | bytes 786436
  312.9 7.3 %copy-start = (f32[128,512]{1,0:T(8,128)S(1)}, f32[128,512]{1,0:T(8,128)}, u32[]{:S(2)}) copy-start(f32[128,512]{1,0:T(8,128)} %get-tuple-element.87) | copy-start | bytes 786436

commit v6 on v5

--- a/solution.py
+++ b/solution.py
@@ -355,9 +355,9 @@
     def level(self, t):
         return lax.rem(self.z + 1 + t, self.plan.depth)
 
-    def begin(self):
+    def begin(self, first=0, last=None):
         plan, side = self.plan, self.plan.side
-        for t in range(plan.depth):
+        for t in range(first, plan.depth if last is None else last):
             z = self.level(t)
             for i, number, start, rows, x_first, (land, *_) in self.work:
                 grad, sl = self.grads[i], pl.ds(start, rows)
@@ -1276,6 +1276,15 @@
     ]
     for copy in x_copy:
         copy.start()
+    if plan.late:
+        z, y, x = plan.place(chip)
+        for i in range(3):
+            for t in range(plan.depth - 1):
+                to = (section, plan.chip_at(lax.rem(z + 1 + t, plan.depth), y, x))
+                push(
+                    lines[i].at[t], line_land[i].at[t], l_send.at[i], l_recv.at[i], to
+                ).start()
+    scatter.begin(0, EARLY)
     filter_rows(plan, filt_ref, table, plan.f_rows, True)
     build_strips(plan, table, strip, True)
     if plan.layered:
@@ -1288,15 +1297,7 @@
         bytes_of(g_buf.at[:, pl.ds(0, half * levels * (plan.cols_in - 1)), :], g_recv)
     else:
         bytes_of(g_buf, g_recv)
-    scatter.begin()
-    if plan.late:
-        z, y, x = plan.place(chip)
-        for i in range(3):
-            for t in range(plan.depth - 1):
-                to = (section, plan.chip_at(lax.rem(z + 1 + t, plan.depth), y, x))
-                push(
-                    lines[i].at[t], line_land[i].at[t], l_send.at[i], l_recv.at[i], to
-                ).start()
+    scatter.begin(EARLY)
     for phase in range(2):
         for i in range(plan.blocks):
             rows = slice(BLOCK * i, BLOCK * (i + 1))
@@ -1645,6 +1646,7 @@
     )(g, filt, v, pq, tapw, x, xs, *grads, *rest)
 
 SWAPS = 7
+EARLY = 1
 
 
 def middle_kernel(plan, *refs):
@@ -1682,10 +1684,12 @@
         acts,
         dgate,
         dup,
+        window,
         kv,
         q_buf,
         probs,
         dkv,
+        dn,
         back,
         back_land,
         down_land,
@@ -1827,24 +1831,18 @@
 
     normed, factor10 = norm(passed, gains_ref[2:3, :])
     inputs = normed.astype(BF)
-    for load in loads[3:5]:
-        load.wait()
-    for copy in passes:
-        copy.wait()
     mine = slice(reach * rows, span)
-    q_buf[...] = flat_dot(inputs, w_proj[:width]).astype(BF)
-    kv[mine, :width] = flat_dot(inputs, w_proj[width : 2 * width]).astype(BF)
-    kv[mine, width:] = flat_dot(inputs, w_proj[2 * width :]).astype(BF)
+    window[mine, :] = inputs
 
     layer, level = plan.layer, chip // plan.layer
     within = lax.rem(chip, layer)
 
     def slot(distance):
-        return kv.at[pl.ds((reach - distance) * rows, rows)]
+        return window.at[pl.ds((reach - distance) * rows, rows)]
 
     def ahead(distance):
         return push(
-            kv.at[mine],
+            window.at[mine],
             slot(distance),
             kv_send.at[distance - 1],
             kv_recv.at[distance - 1],
@@ -1877,8 +1875,8 @@
 
         @pl.when(chip < distance)
         def _():
-            kv[(reach - distance) * rows : (reach - distance + 1) * rows, :] = jnp.zeros(
-                (rows, 2 * width), BF
+            window[(reach - distance) * rows : (reach - distance + 1) * rows, :] = jnp.zeros(
+                (rows, width), BF
             )
 
     half = plan.half
@@ -1895,9 +1893,18 @@
     low = lane < HEAD_DIM
     scale = HEAD_DIM ** (-0.5)
     zero = jnp.zeros((rows, LANES), BF)
+    for load in loads[3:5]:
+        load.wait()
+    for copy in passes:
+        copy.wait()
+    w_query, w_key, w_value = (w_proj.at[pl.ds(part * width, width)] for part in range(3))
+    q_buf[...] = flat_dot(inputs, w_query[...]).astype(BF)
+    kv[mine, :width] = flat_dot(inputs, w_key[...]).astype(BF)
+    kv[mine, width:] = flat_dot(inputs, w_value[...]).astype(BF)
+
     def arrived(distance):
         push(
-            kv.at[mine],
+            window.at[mine],
             slot(distance),
             kv_send.at[distance - 1],
             kv_recv.at[distance - 1],
@@ -1914,6 +1921,9 @@
 
     for distance in range(1, reach):
         pl.when(comes(distance))(functools.partial(arrived, distance))
+    earlier = slice(0, reach * rows)
+    kv[earlier, :width] = flat_dot(window[earlier, :], w_key[...]).astype(BF)
+    kv[earlier, width:] = flat_dot(window[earlier, :], w_value[...]).astype(BF)
 
     for pair in range(width // LANES):
         lanes = slice(LANES * pair, LANES * (pair + 1))
@@ -1968,12 +1978,12 @@
             two = flat_dot(weights.T.astype(BF), upstream)
             key_grad = one if key_grad is None else key_grad + one
             value_grad = two if value_grad is None else value_grad + two
-        dq_buf[0, :, lanes] = (jnp.where(low, dq_parts[0], dq_parts[1]) * scale).astype(BF)
-        key_grad = key_grad * scale
-        back[:, lanes] = key_grad[: reach * rows].astype(BF)
-        back[:, value_lanes] = value_grad[: reach * rows].astype(BF)
-        dkv[:, lanes] = key_grad[reach * rows :]
-        dkv[:, value_lanes] = value_grad[reach * rows :]
+        dq_buf[:, lanes] = (jnp.where(low, dq_parts[0], dq_parts[1]) * scale).astype(BF)
+        dkv[:, lanes] = (key_grad * scale).astype(BF)
+        dkv[:, value_lanes] = value_grad.astype(BF)
+    back[...] = (
+        rows_dot(dkv[earlier, :width], w_key[...]) + rows_dot(dkv[earlier, width:], w_value[...])
+    ).astype(BF)
 
     def behind(distance, peer):
         return push(
@@ -2034,6 +2044,11 @@
 
     if plan.late:
         scatter.begin()
+    dn[...] = (
+        rows_dot(dq_buf[...], w_query[...])
+        + rows_dot(dkv[mine, :width], w_key[...])
+        + rows_dot(dkv[mine, width:], w_value[...])
+    )
     if plan.layered:
         for place in range(layer - 1):
 
@@ -2052,12 +2067,12 @@
             @pl.when(place > within)
             def _():
                 came_from(place)
-                dkv[...] += back_land[place].astype(F32)
+                dn[...] += back_land[place].astype(F32)
 
         @pl.when(level < plan.depth - 1)
         def _():
             down().wait_recv()
-            dkv[...] += down_land[...].astype(F32)
+            dn[...] += down_land[...].astype(F32)
 
     else:
         for distance in range(1, reach + 1):
@@ -2065,15 +2080,9 @@
             @pl.when(chip + distance < chips)
             def _():
                 behind(distance, chip).wait_recv()
-                dkv[...] += back_land[distance - 1].astype(F32)
-
-    dq_buf[1] = dkv[:, :width].astype(BF)
-    dq_buf[2] = dkv[:, width:].astype(BF)
-    turned = inputs.astype(F32).T.astype(BF)
-    dnormed = None
-    for part in range(3):
-        term = rows_dot(dq_buf[part], w_proj[part * width : (part + 1) * width])
-        dnormed = term if dnormed is None else dnormed + term
+                dn[...] += back_land[distance - 1].astype(F32)
+
+    dnormed = dn[...]
     dpassed, gain10 = norm_back(passed, factor10, gains_ref[2:3, :], dnormed)
     gain_ref[2:3, :] = gain10
     dpassed = (dmiddle + dpassed).astype(BF).astype(F32)
@@ -2084,8 +2093,10 @@
     give[5] = upstream0.astype(BF)
     copy = push(give.at[5], take.at[5], send.at[5], recv.at[5], sibling)
     copy.start()
-    for part in range(3):
-        proj_all[part * width : (part + 1) * width, :] = flat_dot(turned, dq_buf[part]).astype(BF)
+    turned = window[...].astype(F32).T.astype(BF)
+    proj_all[:width, :] = flat_dot(turned[:, reach * rows :], dq_buf[...]).astype(BF)
+    proj_all[width : 2 * width, :] = flat_dot(turned, dkv[:, :width]).astype(BF)
+    proj_all[2 * width :, :] = flat_dot(turned, dkv[:, width:]).astype(BF)
     copy.wait()
     crossing = [
         push(
@@ -2197,15 +2208,17 @@
             pltpu.VMEM((2, 2 * rows, ff), BF),
             pltpu.VMEM((2 * rows, ff), BF),
             pltpu.VMEM((2 * rows, ff), BF),
+            pltpu.VMEM(((reach + 1) * rows, width), BF),
             pltpu.VMEM(((reach + 1) * rows, 2 * width), BF),
             pltpu.VMEM((rows, width), BF),
             pltpu.VMEM((width // HEAD_DIM, rows, (reach + 1) * rows), F32),
-            pltpu.VMEM((rows, 2 * width), F32),
-            pltpu.VMEM((reach * rows, 2 * width), BF),
-            pltpu.VMEM((reach, rows, 2 * width), BF),
-            pltpu.VMEM((rows, 2 * width), BF),
+            pltpu.VMEM(((reach + 1) * rows, 2 * width), BF),
             pltpu.VMEM((rows, width), F32),
-            pltpu.VMEM((3, rows, width), BF),
+            pltpu.VMEM((reach * rows, width), BF),
+            pltpu.VMEM((reach, rows, width), BF),
+            pltpu.VMEM((rows, width), BF),
+            pltpu.VMEM((rows, width), F32),
+            pltpu.VMEM((rows, width), BF),
             pltpu.VMEM((3 * width, width), BF),
             pltpu.VMEM((width, width), BF),
             pltpu.VMEM((split, width), BF),

time: 321 us -> 310 us (0.966)
  Pallas kernels: 311 us -> 300 us
    pallas_call x1, Pallas kernels: 120 us -> 109 us  [middle_call(): pl.pallas_call(functools.partial(middle_kernel, plan), out_shape=[jax.Sha...]
where the time goes in v6:
time: 310 us
  Pallas kernels  300 us (97%)
  local copies, waits for them, and re-layouts  6.81 us (2%)
    pallas_call x1, Pallas kernels, middle_call(): pl.pallas_call(functools.partial(middle_kernel, plan), out_shape=[jax.Sha...  109 us
    pallas_call x1, Pallas kernels, backward_call(): pl.pallas_call(functools.partial(backward_kernel, plan, len(grads)), out_...  100 us
    pallas_call x1, Pallas kernels, forward_call(): pl.pallas_call(functools.partial(forward_kernel, plan), out_shape=[jax.Sh...  89.8 us

profile of v6, /device:TPU:0, one launch (start us, length us, event | category | flops | bytes accessed | tf_op | source)
XLA Modules:
  0.0 309.8 jit_solution(12809760612617626883)
XLA Ops:
  0.6 1.4 copy.18.refs_2_
  2.0 89.8 %spectral_forward.1 = (bf16[4,2,2,32,1024]{4,3,2,1,0:T(8,128)(2,1)}, bf16[4,2,2,32,1024]{4,3,2,1,0:T(8,128)(2,1)}, bf16[4,2,2,64,512]{4,3,2,1,0:T(8,128)(2,1)}, ...) custom-call(bf16[2,128,512]{2,1,0:T(8,128)(2,1)} %bitcast.38, ...), custom_call_target="tpu_custom_call" | custom-call | tf_op jit(solution)/shard_map/spectral_forward/pallas_call | solution.py:1105
  91.8 109.5 %middle.1 = (bf16[128,512]{1,0:T(8,128)(2,1)}, bf16[128,512]{1,0:T(8,128)(2,1)}, f32[128,512]{1,0:T(8,128)}, f32[8,512]{1,0:T(8,128)}, bf16[512,1024]{1,0:T(8,12...) custom-call(f32[128,512]{1,0:T(8,128)} %bitcast.33, ...), custom_call_target="tpu_custom_call" | custom-call | tf_op jit(solution)/shard_map/middle/pallas_call | solution.py:2195
  201.3 100.4 %spectral_backward.1 = (bf16[2,128,512]{2,1,0:T(8,128)(2,1)}, f32[32,2048]{1,0:T(8,128)}, f32[32,2048]{1,0:T(8,128)}, f32[128,512]{1,0:T(8,128)}, f32[48,512]{1,...) custom-call(bf16[2,64,512]{2,1,0:T(8,128)(2,1)} %bitcast.39, ...), custom_call_target="tpu_custom_call" | custom-call | tf_op jit(solution)/shard_map/spectral_backward/pallas_call | solution.py:1598
  301.7 0.0 copy-start.3
  301.8 0.0 copy-start.4
  301.8 0.0 copy-start.5
  301.8 0.0 copy-start.2
  301.8 0.0 copy-start.1
  301.8 0.0 copy-start
  301.8 2.6 convert_element_type.3
  304.4 1.3 dynamic-slice_bitcast_fusion
  305.7 0.0 copy-done.3
  305.8 0.7 copy.25
  306.5 0.0 copy-done.4
  306.5 0.6 copy.26
  307.1 0.0 copy-done.5
  307.1 0.6 copy.27
  307.7 0.0 copy-done.2
  307.7 0.7 copy.28
  308.4 0.0 copy-done.1
  308.4 0.7 copy.29
  309.1 0.0 copy-done
  309.1 0.7 copy.30
Async XLA Ops:
  301.7 4.0 %copy-start.3 = (bf16[2,128,512]{2,1,0:T(8,128)(2,1)S(1)}, bf16[2,128,512]{2,1,0:T(8,128)(2,1)}, u32[]{:S(2)}) copy-start(bf16[2,128,512]{2,1,0:T(8,128)(2,1)} %get-tuple-element.80) | copy-start | bytes 786436
  301.8 4.7 %copy-start.4 = (f32[48,512]{1,0:T(8,128)S(1)}, f32[48,512]{1,0:T(8,128)}, u32[]{:S(2)}) copy-start(f32[48,512]{1,0:T(8,128)} %get-tuple-element.98) | copy-start | bytes 294916
  301.8 5.3 %copy-start.5 = (f32[16,512]{1,0:T(8,128)S(1)}, f32[16,512]{1,0:T(8,128)}, u32[]{:S(2)}) copy-start(f32[16,512]{1,0:T(8,128)} %get-tuple-element.99) | copy-start | bytes 98308
  301.8 5.9 %copy-start.2 = (f32[32,2048]{1,0:T(8,128)S(1)}, f32[32,2048]{1,0:T(8,128)}, u32[]{:S(2)}) copy-start(f32[32,2048]{1,0:T(8,128)} %get-tuple-element.85) | copy-start | bytes 786436
  301.8 6.6 %copy-start.1 = (f32[32,2048]{1,0:T(8,128)S(1)}, f32[32,2048]{1,0:T(8,128)}, u32[]{:S(2)}) copy-start(f32[32,2048]{1,0:T(8,128)} %get-tuple-element.86) | copy-start | bytes 786436
  301.8 7.3 %copy-start = (f32[128,512]{1,0:T(8,128)S(1)}, f32[128,512]{1,0:T(8,128)}, u32[]{:S(2)}) copy-start(f32[128,512]{1,0:T(8,128)} %get-tuple-element.87) | copy-start | bytes 786436

commit v7 on v6

--- a/solution.py
+++ b/solution.py
@@ -1413,8 +1413,9 @@
             finish(k - 1)
 
         for turn_number in range(plan.depth + 1):
-            at = 1 + (turn_number * (plan.local - 2)) // plan.depth
-            pl.when(k == at)(functools.partial(scatter.stage, turn_number))
+            at = plan.local // 2 - 1 + 3 * turn_number
+            if at < plan.local:
+                pl.when(k == at)(functools.partial(scatter.stage, turn_number))
         return carry
 
     lax.fori_loop(0, plan.local, step, 0)
@@ -1440,6 +1441,9 @@
             return carry
 
         lax.fori_loop(0, BLOCK // half, give, 0)
+    for turn_number in range(plan.depth + 1):
+        if plan.local // 2 - 1 + 3 * turn_number >= plan.local:
+            scatter.stage(turn_number)
     finish(plan.local - 1)
     tap_swap.wait()
     total_t[...] = (kept_t[...] + take_t[...].astype(F32)).astype(BF)
@@ -1953,6 +1957,8 @@
     if not plan.late:
         grads1 = (gate1_g, up1_g, down1_g)
     dnormed = feed_back(1, pair1, layer1, grads1, up_pair[...], 4)
+    if plan.late:
+        scatter.begin(0, plan.depth // 2)
     dmiddle, gain11 = norm_back(middle1, factor11, gains_ref[3:4, :], dnormed)
     dmiddle = up_ref[...] + dmiddle
     gain_ref[3:4, :] = gain11
@@ -2043,7 +2049,7 @@
                 behind(distance, chip - distance).start()
 
     if plan.late:
-        scatter.begin()
+        scatter.begin(plan.depth // 2)
     dn[...] = (
         rows_dot(dq_buf[...], w_query[...])
         + rows_dot(dkv[mine, :width], w_key[...])
@@ -2087,8 +2093,6 @@
     gain_ref[2:3, :] = gain10
     dpassed = (dmiddle + dpassed).astype(BF).astype(F32)
 
-    if plan.late:
-        scatter.stage(0)
     upstream0 = mask * dpassed
     give[5] = upstream0.astype(BF)
     copy = push(give.at[5], take.at[5], send.at[5], recv.at[5], sibling)
@@ -2113,11 +2117,11 @@
     for cross in crossing:
         cross.start()
     if plan.late:
-        scatter.stage(1)
+        scatter.stage(0)
     both = jnp.concatenate([give[5], take[5]], 0)
     dnormed = feed_back(0, pair0, layer0, (gate0_g, up0_g, down0_g), both, 6)
     if plan.late:
-        for number in range(2, plan.depth + 1):
+        for number in range(1, plan.depth + 1):
             scatter.stage(number)
     middle0 = dmid_ref[...]
     dmiddle, gain01 = norm_back(middle0, factor0, gains_ref[1:2, :], dnormed)

time: 310 us -> 305 us (0.984)
  Pallas kernels: 300 us -> 294 us
    pallas_call x1, Pallas kernels: 109 us -> 103 us  [middle_call(): pl.pallas_call(functools.partial(middle_kernel, plan), out_shape=[jax.Sha...]
where the time goes in v7:
time: 305 us; the launch traced here: 304 us
  Pallas kernels  294 us (96%)
  local copies, waits for them, and re-layouts  6.81 us (2%)
    pallas_call x1, Pallas kernels, middle_call(): pl.pallas_call(functools.partial(middle_kernel, plan), out_shape=[jax.Sha...  103 us
    pallas_call x1, Pallas kernels, backward_call(): pl.pallas_call(functools.partial(backward_kernel, plan, len(grads)), out_...  101 us
    pallas_call x1, Pallas kernels, forward_call(): pl.pallas_call(functools.partial(forward_kernel, plan), out_shape=[jax.Sh...  89.8 us

profile of v7, /device:TPU:0, one launch (start us, length us, event | category | flops | bytes accessed | tf_op | source)
XLA Modules:
  0.0 304.4 jit_solution(10909080465688773017)
XLA Ops:
  0.6 1.4 copy.18.refs_2_
  2.0 89.8 %spectral_forward.1 = (bf16[4,2,2,32,1024]{4,3,2,1,0:T(8,128)(2,1)}, bf16[4,2,2,32,1024]{4,3,2,1,0:T(8,128)(2,1)}, bf16[4,2,2,64,512]{4,3,2,1,0:T(8,128)(2,1)}, ...) custom-call(bf16[2,128,512]{2,1,0:T(8,128)(2,1)} %bitcast.38, ...), custom_call_target="tpu_custom_call" | custom-call | tf_op jit(solution)/shard_map/spectral_forward/pallas_call | solution.py:1105
  91.8 103.3 %middle.1 = (bf16[128,512]{1,0:T(8,128)(2,1)}, bf16[128,512]{1,0:T(8,128)(2,1)}, f32[128,512]{1,0:T(8,128)}, f32[8,512]{1,0:T(8,128)}, bf16[512,1024]{1,0:T(8,12...) custom-call(f32[128,512]{1,0:T(8,128)} %bitcast.33, ...), custom_call_target="tpu_custom_call" | custom-call | tf_op jit(solution)/shard_map/middle/pallas_call | solution.py:2199
  195.2 101.1 %spectral_backward.1 = (bf16[2,128,512]{2,1,0:T(8,128)(2,1)}, f32[32,2048]{1,0:T(8,128)}, f32[32,2048]{1,0:T(8,128)}, f32[128,512]{1,0:T(8,128)}, f32[48,512]{1,...) custom-call(bf16[2,64,512]{2,1,0:T(8,128)(2,1)} %bitcast.39, ...), custom_call_target="tpu_custom_call" | custom-call | tf_op jit(solution)/shard_map/spectral_backward/pallas_call | solution.py:1602
  296.3 0.0 copy-start.3
  296.3 0.0 copy-start.4
  296.3 0.0 copy-start.5
  296.3 0.0 copy-start.2
  296.3 0.0 copy-start.1
  296.3 0.0 copy-start
  296.4 2.6 convert_element_type.3
  299.0 1.3 dynamic-slice_bitcast_fusion
  300.3 0.0 copy-done.3
  300.3 0.7 copy.25
  301.0 0.0 copy-done.4
  301.0 0.6 copy.26
  301.7 0.0 copy-done.5
  301.7 0.6 copy.27
  302.3 0.0 copy-done.2
  302.3 0.7 copy.28
  303.0 0.0 copy-done.1
  303.0 0.7 copy.29
  303.7 0.0 copy-done
  303.7 0.7 copy.30
Async XLA Ops:
  296.3 4.0 %copy-start.3 = (bf16[2,128,512]{2,1,0:T(8,128)(2,1)S(1)}, bf16[2,128,512]{2,1,0:T(8,128)(2,1)}, u32[]{:S(2)}) copy-start(bf16[2,128,512]{2,1,0:T(8,128)(2,1)} %get-tuple-element.80) | copy-start | bytes 786436
  296.3 4.7 %copy-start.4 = (f32[48,512]{1,0:T(8,128)S(1)}, f32[48,512]{1,0:T(8,128)}, u32[]{:S(2)}) copy-start(f32[48,512]{1,0:T(8,128)} %get-tuple-element.98) | copy-start | bytes 294916
  296.3 5.3 %copy-start.5 = (f32[16,512]{1,0:T(8,128)S(1)}, f32[16,512]{1,0:T(8,128)}, u32[]{:S(2)}) copy-start(f32[16,512]{1,0:T(8,128)} %get-tuple-element.99) | copy-start | bytes 98308
  296.3 5.9 %copy-start.2 = (f32[32,2048]{1,0:T(8,128)S(1)}, f32[32,2048]{1,0:T(8,128)}, u32[]{:S(2)}) copy-start(f32[32,2048]{1,0:T(8,128)} %get-tuple-element.85) | copy-start | bytes 786436
  296.3 6.6 %copy-start.1 = (f32[32,2048]{1,0:T(8,128)S(1)}, f32[32,2048]{1,0:T(8,128)}, u32[]{:S(2)}) copy-start(f32[32,2048]{1,0:T(8,128)} %get-tuple-element.86) | copy-start | bytes 786436
  296.3 7.3 %copy-start = (f32[128,512]{1,0:T(8,128)S(1)}, f32[128,512]{1,0:T(8,128)}, u32[]{:S(2)}) copy-start(f32[128,512]{1,0:T(8,128)} %get-tuple-element.87) | copy-start | bytes 786436

commit v8 on v7

--- a/solution.py
+++ b/solution.py
@@ -942,12 +942,8 @@
             attention.stage(1)
         if i == 2:
             layer0.stage(4)
+        if i == 3:
             attention.stage(2)
-            layer1.second(1)
-        if i == 3:
-            attention.stage(3)
-            attention.stage(4)
-            layer1.second(2)
         rows = slice(BLOCK * i, BLOCK * (i + 1))
         depth = BLOCK * (i + 1)
         offset = plan.length - depth
@@ -1024,7 +1020,10 @@
 
         lax.fori_loop(0, BLOCK // half, give, 0)
 
-    layer1.second(3)
+    attention.stage(3)
+    attention.stage(4)
+    for number in range(1, plan.depth):
+        layer1.second(number)
     if not plan.late:
         for number in range(plan.depth):
             layer1.third(number)

time: 305 us -> 302 us (level)
  no operation moved by 1% of the time
where the time goes in v8:
time: 302 us
  Pallas kernels  292 us (97%)
  local copies, waits for them, and re-layouts  6.81 us (2%)
    pallas_call x1, Pallas kernels, middle_call(): pl.pallas_call(functools.partial(middle_kernel, plan), out_shape=[jax.Sha...  102 us
    pallas_call x1, Pallas kernels, backward_call(): pl.pallas_call(functools.partial(backward_kernel, plan, len(grads)), out_...  100 us
    pallas_call x1, Pallas kernels, forward_call(): pl.pallas_call(functools.partial(forward_kernel, plan), out_shape=[jax.Sh...  89.5 us

profile of v8, /device:TPU:0, one launch (start us, length us, event | category | flops | bytes accessed | tf_op | source)
XLA Modules:
  0.0 301.7 jit_solution(10139956960384250486)
XLA Ops:
  0.6 1.4 copy.18.refs_2_
  2.0 89.5 %spectral_forward.1 = (bf16[4,2,2,32,1024]{4,3,2,1,0:T(8,128)(2,1)}, bf16[4,2,2,32,1024]{4,3,2,1,0:T(8,128)(2,1)}, bf16[4,2,2,64,512]{4,3,2,1,0:T(8,128)(2,1)}, ...) custom-call(bf16[2,128,512]{2,1,0:T(8,128)(2,1)} %bitcast.38, ...), custom_call_target="tpu_custom_call" | custom-call | tf_op jit(solution)/shard_map/spectral_forward/pallas_call | solution.py:1104
  91.6 101.6 %middle.1 = (bf16[128,512]{1,0:T(8,128)(2,1)}, bf16[128,512]{1,0:T(8,128)(2,1)}, f32[128,512]{1,0:T(8,128)}, f32[8,512]{1,0:T(8,128)}, bf16[512,1024]{1,0:T(8,12...) custom-call(f32[128,512]{1,0:T(8,128)} %bitcast.33, ...), custom_call_target="tpu_custom_call" | custom-call | tf_op jit(solution)/shard_map/middle/pallas_call | solution.py:2198
  193.2 100.4 %spectral_backward.1 = (bf16[2,128,512]{2,1,0:T(8,128)(2,1)}, f32[32,2048]{1,0:T(8,128)}, f32[32,2048]{1,0:T(8,128)}, f32[128,512]{1,0:T(8,128)}, f32[48,512]{1,...) custom-call(bf16[2,64,512]{2,1,0:T(8,128)(2,1)} %bitcast.39, ...), custom_call_target="tpu_custom_call" | custom-call | tf_op jit(solution)/shard_map/spectral_backward/pallas_call | solution.py:1601
  293.6 0.0 copy-start.3
  293.6 0.0 copy-start.4
  293.6 0.0 copy-start.5
  293.6 0.0 copy-start.2
  293.6 0.0 copy-start.1
  293.7 0.0 copy-start
  293.7 2.6 convert_element_type.3
  296.3 1.3 dynamic-slice_bitcast_fusion
  297.6 0.0 copy-done.3
  297.6 0.7 copy.25
  298.3 0.0 copy-done.4
  298.3 0.6 copy.26
  299.0 0.0 copy-done.5
  299.0 0.6 copy.27
  299.6 0.0 copy-done.2
  299.6 0.7 copy.28
  300.3 0.0 copy-done.1
  300.3 0.7 copy.29
  301.0 0.0 copy-done
  301.0 0.7 copy.30
Async XLA Ops:
  293.6 4.0 %copy-start.3 = (bf16[2,128,512]{2,1,0:T(8,128)(2,1)S(1)}, bf16[2,128,512]{2,1,0:T(8,128)(2,1)}, u32[]{:S(2)}) copy-start(bf16[2,128,512]{2,1,0:T(8,128)(2,1)} %get-tuple-element.80) | copy-start | bytes 786436
  293.6 4.7 %copy-start.4 = (f32[48,512]{1,0:T(8,128)S(1)}, f32[48,512]{1,0:T(8,128)}, u32[]{:S(2)}) copy-start(f32[48,512]{1,0:T(8,128)} %get-tuple-element.98) | copy-start | bytes 294916
  293.6 5.3 %copy-start.5 = (f32[16,512]{1,0:T(8,128)S(1)}, f32[16,512]{1,0:T(8,128)}, u32[]{:S(2)}) copy-start(f32[16,512]{1,0:T(8,128)} %get-tuple-element.99) | copy-start | bytes 98308
  293.6 5.9 %copy-start.2 = (f32[32,2048]{1,0:T(8,128)S(1)}, f32[32,2048]{1,0:T(8,128)}, u32[]{:S(2)}) copy-start(f32[32,2048]{1,0:T(8,128)} %get-tuple-element.85) | copy-start | bytes 786436
  293.6 6.6 %copy-start.1 = (f32[32,2048]{1,0:T(8,128)S(1)}, f32[32,2048]{1,0:T(8,128)}, u32[]{:S(2)}) copy-start(f32[32,2048]{1,0:T(8,128)} %get-tuple-element.86) | copy-start | bytes 786436
  293.7 7.3 %copy-start = (f32[128,512]{1,0:T(8,128)S(1)}, f32[128,512]{1,0:T(8,128)}, u32[]{:S(2)}) copy-start(f32[128,512]{1,0:T(8,128)} %get-tuple-element.87) | copy-start | bytes 786436
